TPU v7x, 512 devices: a whole 4x4x16 slice. The times are simulated.
512 devices in a mesh: shot: 16 (over z), row: 8 (over y, core), col: 4 (over x).
Axes of the slice: x: 4, y: 4, z: 16, core: 2. Of those that a mesh axis runs over, the one named last changes fastest.
Arguments:
- soft: bfloat16 [12288, 32768], P('shot', ('row', 'col')), may hold values from 0.1 to 0.9, as said below
- partners: int32 [128, 4], P(('row', 'col')), may hold values from -1 to 127, as said below
- incidence: int32 [3, 128, 512], P(None, ('row', 'col')), may hold values from 0 to 255, as said below
- edge_prob: float32 [128, 512], P(('row', 'col')), may hold values from 0.002 to 0.05
Outputs:
- pair_prob: bfloat16 [128, 4, 256, 256], P(('row', 'col'), None, 'shot')
- gradient: float32 [128, 512], P(('row', 'col'))
Inputs may be any that keep to these rules, and one draw needn't show every extreme that they name: Slot 0 of block b holds b itself; a live partner lies within 2 blocks of b and the live partners of a block differ. `soft`: each entry lies between 0 and 1 - 0.2 / 2, so gram / 12288 exceeds 0.01. incidence[0] and incidence[2] lie in 0 to 255, incidence[1] in 0 to 3.
All inputs are finite; a program needn't handle non-finite values.
Results may differ from a plain program's by a relative error of at most 0.001.
Values may be sent and summed in bfloat16 or wider, within the bound.
No kernel may reach another device: no remote copies, remote signals or barrier semaphores. Data moves between devices by JAX's collectives and lax.ppermute only.
A program may use at most 64 MiB of HBM per device.

v0:
```python
import jax
import jax.numpy as jnp
from jax import lax
from jax.sharding import PartitionSpec as P

HALO = 2


NOISE_SPREAD = 0.05


def padded(cells, sides, width):
    for axis, dim in sides:
        count = lax.axis_size(axis)
        ends = count - 1
        head = lax.slice_in_dim(cells, 0, width, axis=dim)
        tail = lax.slice_in_dim(cells, cells.shape[dim] - width, cells.shape[dim], axis=dim)
        cells = jnp.concatenate(
            [
                lax.ppermute(tail, axis, [(i, (i + 1) % count) for i in range(ends)]),
                cells,
                lax.ppermute(head, axis, [((i + 1) % count, i) for i in range(ends)]),
            ],
            axis=dim,
        )
    return cells


def pairwise_probability(summed_gram, row_average, column_average, activity_mask, count_of_shots):
    quotient_value = (
        row_average[..., :, None] * column_average[..., None, :] * count_of_shots / summed_gram
    )
    return (0.5 - 0.5 * jnp.sqrt(quotient_value)) * activity_mask[:, :, None, None]


def local(soft, partners, incidence, edge_prob):
    shots_local, width_local = soft.shape
    blocks_local, slot_count = partners.shape
    block_width = width_local // blocks_local
    groups = lax.axis_size("shot")
    count_of_shots = float(shots_local * groups)
    first_block = lax.axis_index(("row", "col")) * blocks_local
    extended = padded(soft, ((("row", "col"), 1),), HALO * block_width)
    column_sums = jnp.sum(extended, axis=0, dtype=jnp.float32)
    means = lax.psum(column_sums, "shot") / count_of_shots
    own_ids = first_block + jnp.arange(blocks_local, dtype=jnp.int32)
    active_flags = partners >= 0
    chosen = jnp.where(active_flags, partners, own_ids[:, None])
    local_index = (chosen - first_block + HALO).reshape(-1)
    reached = extended.reshape(shots_local, blocks_local + 2 * HALO, block_width)
    partner_cols = jnp.take(reached, local_index, axis=1).reshape(
        shots_local, blocks_local, slot_count, block_width
    )
    own_cols = soft.reshape(shots_local, blocks_local, block_width)
    partial_gram = jnp.einsum(
        "sbi,sbkj->bkij", own_cols, partner_cols, preferred_element_type=jnp.float32
    )
    mean_blocks = means.reshape(blocks_local + 2 * HALO, block_width)
    local_average = mean_blocks[HALO : HALO + blocks_local]
    partial_average = jnp.take(mean_blocks, local_index, axis=0).reshape(
        blocks_local, slot_count, block_width
    )
    activity_mask = active_flags.astype(jnp.float32)
    rows_x = incidence[0]
    slot_x = incidence[1]
    cols_x = incidence[2]
    block_rows = jnp.broadcast_to(jnp.arange(blocks_local, dtype=jnp.int32)[:, None], rows_x.shape)
    summed_gram = lax.psum(partial_gram, "shot")
    pairwise_entry = pairwise_probability(
        summed_gram, local_average[:, None, :], partial_average, activity_mask, count_of_shots
    )
    fitted_values = (
        jnp.zeros(pairwise_entry.shape, jnp.float32)
        .at[block_rows, slot_x, rows_x, cols_x]
        .add(edge_prob)
    )
    fit_residual = activity_mask[:, :, None, None] * (pairwise_entry - fitted_values) / NOISE_SPREAD
    gradient = -fit_residual[block_rows, slot_x, rows_x, cols_x] / NOISE_SPREAD
    row_share = block_width // groups
    row_start = lax.axis_index("shot") * row_share
    pair_out = lax.dynamic_slice_in_dim(pairwise_entry, row_start, row_share, 2).astype(
        jnp.bfloat16
    )
    return (pair_out, gradient)


def solution(mesh):
    placed = (
        P("shot", ("row", "col")),
        P(("row", "col"), None),
        P(None, ("row", "col"), None),
        P(("row", "col"), None),
    )
    return jax.shard_map(
        local,
        mesh=mesh,
        in_specs=placed,
        out_specs=(P(("row", "col"), None, "shot", None), P(("row", "col"), None)),
        check_vma=False,
    )
```

profile of v0, /device:TPU:24, one launch (start us, length us, event | category | flops | bytes accessed | tf_op | source)
XLA Modules:
  0.0 266.5 jit_solution(888900097400583340)
XLA Ops:
  7.2 1.8 copy.13
  9.1 1.2 fusion.14
  10.3 3.4 %collective-permute-start = (bf16[768,512]{0,1:T(8,128)(2,1)}, bf16[768,512]{0,1:T(8,128)(2,1)}, u32[]{:S(2)}, u32[]{:S(2)}) collective-permute-start(bf16[768,512]{0,1:T(8,128)(2,1)} %get-tuple-element.12), channel_id=1, source_target_pairs={{0,1},{1,2},{2,3},{3,4},{4,5},{5,6},{6,7},{7,8},{8,9},{9,10},{10,1... | collective-permute-start | bytes 2359304 | tf_op jit(solution)/shard_map/ppermute | solution.py:20
  13.7 4.3 %collective-permute-start.1 = (bf16[768,512]{0,1:T(8,128)(2,1)}, bf16[768,512]{0,1:T(8,128)(2,1)}, u32[]{:S(2)}, u32[]{:S(2)}) collective-permute-start(bf16[768,512]{0,1:T(8,128)(2,1)} %get-tuple-element.13), channel_id=1, source_target_pairs={{1,0},{2,1},{3,2},{4,3},{5,4},{6,5},{7,6},{8,7},{9,8},{10,9},{11,1... | collective-permute-start | bytes 2359304 | tf_op jit(solution)/shard_map/ppermute | solution.py:22
  18.0 2.4 reshape.179
  20.6 13.2 %collective-permute-done = bf16[768,512]{0,1:T(8,128)(2,1)} collective-permute-done((bf16[768,512]{0,1:T(8,128)(2,1)}, bf16[768,512]{0,1:T(8,128)(2,1)}, u32[]{:S(2)}, u32[]{:S(2)}) %collective-permute-start) | collective-permute-done | bytes 786464 | tf_op jit(solution)/shard_map/ppermute | solution.py:20
  33.8 1.1 collective-permute-done.1
  34.9 3.1 %convert_reduce_fusion = (f32[2048]{0:T(1024)S(1)}, bf16[768,2048]{0,1:T(8,128)(2,1)}) fusion(bf16[768,512]{0,1:T(8,128)(2,1)} %collective-permute-done.1, bf16[768,1024]{0,1:T(8,128)(2,1)S(1)} %copy.13, bf16[768,512]{0,1:T(8,128)(2,1)} %collective-permute-done), kind=kLoop, calls=%fused_computation.6 | loop fusion | flops 12580864 | bytes 6299648 | tf_op jit(solution)/shard_map/reduce_sum | solution.py:44
  38.0 3.2 %copy.16 = bf16[768,8,256]{2,0,1:T(8,128)(2,1)S(1)} copy(bf16[768,8,256]{0,2,1:T(8,128)(2,1)} %bitcast.32) | data formatting | bytes 6291456 | tf_op jit(solution)/shard_map/reshape | solution.py:50
  41.1 3.6 %gather_fusion.1 = bf16[16,768,256]{2,1,0:T(8,128)(2,1)} fusion(bf16[768,8,256]{2,0,1:T(8,128)(2,1)S(1)} %copy.16, s32[1024]{0:T(1024)S(1)} %pad_clamp_fusion), kind=kCustom, calls=%fused_computation.1 | custom fusion | bytes 12582976 | tf_op jit(solution)/shard_map/jit(_take)/gather | solution.py:51
  44.7 8.7 %copy.17 = bf16[768,4,4,256]{0,3,2,1:T(8,128)(2,1)} copy(bf16[768,4,4,256]{3,0,2,1:T(8,128)(2,1)} %bitcast.31) | data formatting | bytes 12582912 | tf_op jit(solution)/shard_map/jit(_take)/gather | solution.py:51
  53.4 6.6 %fusion.4 = f32[4,4,256,256]{2,3,1,0:T(8,128)} fusion(bf16[768,4,4,256]{0,3,2,1:T(8,128)(2,1)} %copy.17, pred[4,4]{1,0:T(4,128)(4,1)S(1)} %get-tuple-element.18, bf16[768,4,256,1]{2,1,0,3:T(4,128)(2,1)S(1)} %bitcast.33), kind=kOutput, calls=%fused_computation.12 | convolution fusion | flops 1613758464 | bytes 12058640 | tf_op jit(solution)/shard_map/sbi,sbkj->bkij/dot_general | solution.py:55
  60.0 0.7 copy-done.2
  61.0 13.4 %scatter_custom_fusion = f32[1048576]{0:T(1024)} fusion(s32[2048]{0:T(1024)S(1)} %bitcast.35, f32[2048]{0:T(1024)S(1)} %bitcast.36, f32[]{:T(128)} %constant.23.clone.1), kind=kCustom, calls=%fused_computation.13 | custom fusion | flops 2048 | bytes 4194308
  74.5 5.2 %reshape.183 = f32[4,4,256,256]{3,2,1,0:T(8,128)} reshape(f32[1048576]{0:T(1024)} %scatter_custom_fusion) | data formatting | bytes 8388608 | tf_op jit(solution)/shard_map/scatter-add | solution.py:75
  79.7 5.3 %copy.19 = f32[4,4,256,256]{2,3,1,0:T(8,128)} copy(f32[4,4,256,256]{3,2,1,0:T(8,128)} %reshape.183) | data formatting | bytes 8388608 | tf_op jit(solution)/shard_map/scatter-add | solution.py:75
  85.0 37.2 %psum.14 = f32[2048]{0:T(1024)S(1)} all-reduce(f32[2048]{0:T(1024)S(1)} %get-tuple-element.10), channel_id=1, replica_groups=mesh['shot'=16,'row'=8,'col'=4] {'shot'}, use_global_device_ids=true, to_apply=%region_1.0 | all-reduce | flops 2048 | bytes 16384 | tf_op jit(solution)/shard_map/psum | solution.py:45
  122.3 0.6 gather_fusion
  123.0 98.7 %all-reduce.2.cloned.1.call-done = f32[4,4,256,256]{2,3,1,0:T(8,128)} async-done(((f32[4,4,256,256]{2,3,1,0:T(8,128)}), f32[4,4,256,256]{2,3,1,0:T(8,128)}) %all-reduce.2.cloned.1.call-update) | async-done | bytes 4194320 | tf_op jit(solution)/shard_map/psum | solution.py:68
  221.6 6.1 %multiply_multiply_fusion = (f32[4,4,256,256]{2,3,1,0:T(8,128)}, bf16[4,4,256,256]{2,3,1,0:T(8,128)(2,1)S(1)}) fusion(f32[4,4,256,256]{2,3,1,0:T(8,128)} %copy.19, f32[4,4]{1,0:T(4,128)S(1)} %get-tuple-element.19, f32[4,4,256,256]{2,3,1,0:T(8,128)} %all-reduce.2.cloned.1.call-done, f32[4,4,256]{2,1,0:T(4,128)S(1)} %broadcast_select_fusion, f32[4,256]{1,0:T(4,128)S(1)} %slice.32), kind=kLoop, calls=%fused_computation.8 | loop fusion | flops 10485760 | bytes 14700608 | tf_op jit(solution)/shard_map/div | solution.py:77
  227.7 0.4 dynamic-slice_convert_fusion
  228.1 1.0 copy.20
  229.0 30.0 %gather_fusion.2 = f32[2048]{0:T(1024)S(1)} fusion(f32[4,4,256,256]{2,3,1,0:T(8,128)} %get-tuple-element.8, s32[2048]{0:T(1024)S(1)} %bitcast.30), kind=kCustom, calls=%fused_computation.2 | custom fusion | bytes 49152 | tf_op jit(solution)/shard_map/gather | solution.py:78
  259.0 0.6 reshape.214
  (36 shorter events, 0.7 us)
Async XLA Ops:
  7.2 10.8 %copy-start = (bf16[768,1024]{1,0:T(8,128)(2,1)S(1)}, bf16[768,1024]{1,0:T(8,128)(2,1)}, u32[]{:S(2)}) copy-start(bf16[768,1024]{1,0:T(8,128)(2,1)} %param.4) | copy-start | bytes 4718596
  7.2 13.2 %copy-start.4 = (s32[4,4]{1,0:T(4,128)S(1)}, s32[4,4]{1,0:T(4,128)}, u32[]{:S(2)}) copy-start(s32[4,4]{1,0:T(4,128)} %param.5) | copy-start | bytes 196
  7.2 214.4 %all-reduce.2.cloned.1.call-start = ((), (), s32[]{:S(2)}) async-start(), calls=%async_computation | async-start | bytes 8388608 | tf_op jit(solution)/shard_map/psum | solution.py:68
  10.3 23.5 %collective-permute-start = (bf16[768,512]{0,1:T(8,128)(2,1)}, bf16[768,512]{0,1:T(8,128)(2,1)}, u32[]{:S(2)}, u32[]{:S(2)}) collective-permute-start(bf16[768,512]{0,1:T(8,128)(2,1)} %get-tuple-element.12), channel_id=1, source_target_pairs={{0,1},{1,2},{2,3},{3,4},{4,5},{5,6},{6,7},{7,8},{8,9},{9,10},{10,1... | collective-permute-start | bytes 2359304 | tf_op jit(solution)/shard_map/ppermute | solution.py:20
  13.7 21.2 %collective-permute-start.1 = (bf16[768,512]{0,1:T(8,128)(2,1)}, bf16[768,512]{0,1:T(8,128)(2,1)}, u32[]{:S(2)}, u32[]{:S(2)}) collective-permute-start(bf16[768,512]{0,1:T(8,128)(2,1)} %get-tuple-element.13), channel_id=1, source_target_pairs={{1,0},{2,1},{3,2},{4,3},{5,4},{6,5},{7,6},{8,7},{9,8},{10,9},{11,1... | collective-permute-start | bytes 2359304 | tf_op jit(solution)/shard_map/ppermute | solution.py:22
  44.7 8.7 %copy-start.1 = (bf16[768,4,256]{2,1,0:T(4,128)(2,1)S(1)}, bf16[768,4,256]{2,1,0:T(4,128)(2,1)}, u32[]{:S(2)}) copy-start(bf16[768,4,256]{2,1,0:T(4,128)(2,1)} %reshape.179) | copy-start | bytes 4718596
  60.0 0.7 copy-start.2
  60.0 0.8 copy-start.6
  60.0 0.9 copy-start.5
  60.0 1.0 copy-start.3
Sparse Core Ops, SparseCore 0:
  60.2 161.4 all-reduce.1
where the time goes:
time: 268 us; the launch traced here: 266 us
  waiting for transfers between devices  113 us (42%)
  local copies, waits for them, and re-layouts  64.7 us (24%)
  blocking collectives  37.2 us (14%)
  other arithmetic  23 us (9%)
  between operations  14.2 us (5%)
  starting transfers between devices  7.7 us (3%)
  matrix products  6.6 us (2%)
    psum x1, waiting for transfers between devices, local(): summed_gram = lax.psum(partial_gram, 'shot')  98.7 us
    psum x1, blocking collectives, local(): means = lax.psum(column_sums, 'shot') / count_of_shots  37.2 us
    gather x1, local copies, waits for them, and re-layouts, local(): gradient = -fit_residual[block_rows, slot_x, rows_x, cols_x] / NOISE_SPREAD  30 us
    unnamed x5, other arithmetic  13.7 us
    ppermute x1, waiting for transfers between devices, padded(): lax.ppermute(tail, axis, [(i, (i + 1) % count) for i in range(ends)])  13.2 us
    gather x2, local copies, waits for them, and re-layouts, local(): jnp.take(reached, local_index, axis=1)  12.3 us
    scatter-add x2, local copies, waits for them, and re-layouts, local(): fitted_values = jnp.zeros(pairwise_entry.shape, jnp.float32).at[block_row...  10.5 us
    dot_general x1, matrix products, local(): jnp.einsum('sbi,sbkj->bkij', own_cols, partner_cols, preferred_element_ty...  6.6 us
  transfers between devices with their start and end apart: 3, of which 3 were waited for; matrix products, arithmetic and copies ran while one was open for 10% of the time, Pallas kernels for 0%

commit v1 on v0

v1 whole, which is shorter than its diff:
```python
import functools

import jax
import jax.numpy as jnp
from jax import lax
from jax.experimental import pallas as pl
from jax.experimental.pallas import tpu as pltpu
from jax.sharding import PartitionSpec as P

HALO = 2
NOISE_SPREAD = 0.05


def gram_kernel(
    blocks, slots, width, local_ref, left_ref, own_ref, right_ref, inc_ref, keyt_ref, probt_ref,
    gram_ref, small_ref, fit_ref, ext, sems,
):
    shots = own_ref.shape[0]
    halo = left_ref.shape[1]
    own_width = own_ref.shape[1]
    parts = (
        (left_ref, 0, halo),
        (own_ref, halo, own_width),
        (right_ref, halo + own_width, halo),
    )
    copies = [
        pltpu.make_async_copy(ref, ext.at[:, pl.ds(start, size)], sems.at[n])
        for n, (ref, start, size) in enumerate(parts)
    ]
    for copy in copies:
        copy.start()
    edges = inc_ref.shape[2]
    groups = gram_ref.shape[0]
    share = width // groups
    for b in range(blocks):
        key = inc_ref[1, b : b + 1, :] * (width * width) + inc_ref[0, b : b + 1, :] * width + inc_ref[2, b : b + 1, :]
        same = keyt_ref[:, b : b + 1] == key
        fit_ref[b : b + 1, :] = jnp.sum(jnp.where(same, probt_ref[:, b : b + 1], 0.0), axis=0, keepdims=True)
    for copy in copies:
        copy.wait()
    ones = jnp.ones((8, shots), jnp.bfloat16)
    small_ref[0:1, :] = jnp.dot(ones, ext[...], preferred_element_type=jnp.float32)[0:1, :]
    for b in range(blocks):
        own = ext[:, halo + b * width : halo + (b + 1) * width]
        chosen = []
        for k in range(slots):
            start = pl.multiple_of(local_ref[b * slots + k] * width, width)
            chosen.append(ext[:, pl.ds(start, width)])
        chosen = jnp.concatenate(chosen, axis=1)
        tile = lax.dot_general(own, chosen, (((0,), (0,)), ((), ())), preferred_element_type=jnp.float32)
        for k in range(slots):
            gram_ref[:, b, k] = tile[:, k * width : (k + 1) * width].reshape(groups, share, width)
        row_hot = lax.broadcasted_iota(jnp.int32, (width, edges), 0) == inc_ref[0, b : b + 1, :]
        col_hot = lax.broadcasted_iota(jnp.int32, (slots * width, edges), 0) == (
            inc_ref[1, b : b + 1, :] * width + inc_ref[2, b : b + 1, :]
        )
        row_vals = jnp.dot(own, row_hot.astype(jnp.bfloat16), preferred_element_type=jnp.float32)
        col_vals = jnp.dot(chosen, col_hot.astype(jnp.bfloat16), preferred_element_type=jnp.float32)
        at = slice(b * edges, (b + 1) * edges)
        small_ref[1:2, at] = jnp.sum(row_vals, axis=0, keepdims=True)
        small_ref[2:3, at] = jnp.sum(col_vals, axis=0, keepdims=True)
        small_ref[3:4, at] = jnp.sum(row_vals * col_vals, axis=0, keepdims=True)


def gram_call(local_index, left, own, right, incidence, keys_t, prob_t, groups, slots, width):
    shots, own_width = own.shape
    blocks = own_width // width
    edges = incidence.shape[2]
    any_spec = pl.BlockSpec(memory_space=pl.ANY)
    vmem = pl.BlockSpec(memory_space=pltpu.VMEM)
    ext_width = own_width + 2 * left.shape[1]
    return pl.pallas_call(
        functools.partial(gram_kernel, blocks, slots, width),
        out_shape=(
            jax.ShapeDtypeStruct((groups, blocks, slots, width // groups, width), jnp.float32),
            jax.ShapeDtypeStruct((4, max(ext_width, blocks * edges)), jnp.float32),
            jax.ShapeDtypeStruct((blocks, edges), jnp.float32),
        ),
        in_specs=[pl.BlockSpec(memory_space=pltpu.SMEM), any_spec, any_spec, any_spec, vmem, vmem, vmem],
        out_specs=(vmem, vmem, vmem),
        scratch_shapes=[pltpu.VMEM((shots, ext_width), jnp.bfloat16), pltpu.SemaphoreType.DMA((3,))],
        compiler_params=pltpu.CompilerParams(vmem_limit_bytes=40 * 1024 * 1024),
        cost_estimate=pl.CostEstimate(flops=6_500_000_000, bytes_accessed=8_000_000, transcendentals=0),
    )(local_index, left, own, right, incidence, keys_t, prob_t)


def local(soft, partners, incidence, edge_prob):
    shots, own_width = soft.shape
    blocks, slots = partners.shape
    width = own_width // blocks
    groups = lax.axis_size("shot")
    count = float(shots * groups)
    first = lax.axis_index(("row", "col")) * blocks
    sides = lax.axis_size(("row", "col"))
    reach = HALO * width

    left = lax.ppermute(soft[:, own_width - reach :], ("row", "col"), [(i, (i + 1) % sides) for i in range(sides)])
    right = lax.ppermute(soft[:, :reach], ("row", "col"), [((i + 1) % sides, i) for i in range(sides)])

    own_ids = first + jnp.arange(blocks, dtype=jnp.int32)
    live = partners >= 0
    local_index = (jnp.where(live, partners, own_ids[:, None]) - first + HALO).reshape(-1)
    keys = incidence[1] * (width * width) + incidence[0] * width + incidence[2]
    gram, small, fitted = gram_call(
        local_index, left, soft, right, incidence, keys.T, edge_prob.T, groups, slots, width
    )
    small = lax.psum(small, "shot")
    total = lax.psum_scatter(gram, "shot", scatter_dimension=0, tiled=False)

    mean_blocks = small[0].reshape(blocks + 2 * HALO, width) / count
    share = width // groups
    row_mean = lax.dynamic_slice_in_dim(
        mean_blocks[HALO : HALO + blocks], lax.axis_index("shot") * share, share, 1
    )
    col_mean = jnp.take(mean_blocks, local_index, axis=0).reshape(blocks, slots, width)
    mask = live.astype(jnp.float32)
    quotient = row_mean[:, None, :, None] * col_mean[:, :, None, :] * count / total
    pair = ((0.5 - 0.5 * jnp.sqrt(quotient)) * mask[:, :, None, None]).astype(jnp.bfloat16)

    edge = small[1:].reshape(3, blocks, -1)
    at_edge = (edge[0] / count) * (edge[1] / count) * count / edge[2]
    edge_live = jnp.zeros(edge_prob.shape, jnp.float32)
    for k in range(slots):
        edge_live = edge_live + jnp.where(incidence[1] == k, mask[:, k : k + 1], 0.0)
    residual = edge_live * ((0.5 - 0.5 * jnp.sqrt(at_edge)) * edge_live - fitted) / NOISE_SPREAD
    return (pair, -residual / NOISE_SPREAD)


def solution(mesh):
    placed = (
        P("shot", ("row", "col")),
        P(("row", "col"), None),
        P(None, ("row", "col"), None),
        P(("row", "col"), None),
    )
    return jax.shard_map(
        local,
        mesh=mesh,
        in_specs=placed,
        out_specs=(P(("row", "col"), None, "shot", None), P(("row", "col"), None)),
        check_vma=False,
    )
```

time: 268 us -> 140 us (0.52)
  waiting for transfers between devices: 113 us -> 37.4 us
  local copies, waits for them, and re-layouts: 64.7 us -> 6.04 us
  blocking collectives: 37.2 us -> 62.1 us
  other arithmetic: 23 us -> 2.81 us
  Pallas kernels: 0 us -> 9.13 us
  matrix products: 6.6 us -> 0 us
    psum x1 -> x0, waiting for transfers between devices: 98.7 us -> none  [local(): summed_gram = lax.psum(partial_gram, 'shot')]
    gather x5 -> x2, local copies, waits for them, and re-layouts: 42.8 us -> 0.59 us  [local(): jnp.take(mean_blocks, local_index, axis=0).reshape(blocks, slots, width)]
    psum x1, blocking collectives: 37.2 us -> 62.1 us  [local(): small = lax.psum(small, 'shot')]
    reduce_scatter x0 -> x1, waiting for transfers between devices: none -> 20.9 us  [local(): total = lax.psum_scatter(gram, 'shot', scatter_dimension=0, tiled=False)]
    unnamed x5 -> x0, other arithmetic: 13.7 us -> none
    scatter-add x2 -> x0, local copies, waits for them, and re-layouts: 10.5 us -> none  [local(): fitted_values = jnp.zeros(pairwise_entry.shape, jnp.float32).at[block_row...]
    pallas_call x0 -> x1, Pallas kernels: none -> 9.13 us  [gram_call(): pl.pallas_call(functools.partial(gram_kernel, blocks, slots, width), out_...]
    dot_general x1 -> x0, matrix products: 6.6 us -> none  [local(): jnp.einsum('sbi,sbkj->bkij', own_cols, partner_cols, preferred_element_ty...]
  transfers between devices with their start and end apart: 3 -> 3, of which waited for: 3 -> 3; matrix products, arithmetic and copies ran while one was open for 10% -> 2% of each run, Pallas kernels for 0% -> 0%
where the time goes in v1:
time: 140 us; the launch traced here: 139 us
  blocking collectives  62.1 us (44%)
  waiting for transfers between devices  37.4 us (27%)
  between operations  14.2 us (10%)
  Pallas kernels  9.13 us (7%)
  starting transfers between devices  7.7 us (6%)
  local copies, waits for them, and re-layouts  6.04 us (4%)
  other arithmetic  2.81 us (2%)
    psum x1, blocking collectives, local(): small = lax.psum(small, 'shot')  62.1 us
    reduce_scatter x1, waiting for transfers between devices, local(): total = lax.psum_scatter(gram, 'shot', scatter_dimension=0, tiled=False)  20.9 us
    ppermute x1, waiting for transfers between devices, local(): lax.ppermute(soft[:, own_width - reach:], ('row', 'col'), [(i, (i + 1) %...  15.2 us
    pallas_call x1, Pallas kernels, gram_call(): pl.pallas_call(functools.partial(gram_kernel, blocks, slots, width), out_...  9.13 us
    ppermute x1, starting transfers between devices, local(): lax.ppermute(soft[:, :reach], ('row', 'col'), [((i + 1) % sides, i) for i...  4.27 us
    ppermute x1, starting transfers between devices, local(): lax.ppermute(soft[:, own_width - reach:], ('row', 'col'), [(i, (i + 1) %...  3.39 us
  transfers between devices with their start and end apart: 3, of which 3 were waited for; matrix products, arithmetic and copies ran while one was open for 2% of the time, Pallas kernels for 0%

profile of v1, /device:TPU:24, one launch (start us, length us, event | category | flops | bytes accessed | tf_op | source)
XLA Modules:
  0.0 139.3 jit_solution(5583177082921985743)
XLA Ops:
  7.2 0.0 reduce-scatter.2.cloned.1.call-start
  7.2 2.7 %fusion.10 = (bf16[768,512]{1,0:T(8,128)(2,1)}, bf16[768,512]{1,0:T(8,128)(2,1)}) fusion(bf16[768,1024]{1,0:T(8,128)(2,1)} %own_ref.1), kind=kLoop, calls=%fused_computation.33 | loop fusion | bytes 3145728 | tf_op jit(solution)/shard_map/slice | solution.py:98
  10.0 3.4 %collective-permute-start = (bf16[768,512]{1,0:T(8,128)(2,1)}, bf16[768,512]{1,0:T(8,128)(2,1)S(1)}, u32[]{:S(2)}, u32[]{:S(2)}) collective-permute-start(bf16[768,512]{1,0:T(8,128)(2,1)} %get-tuple-element.19), channel_id=1, source_target_pairs={{0,1},{1,2},{2,3},{3,4},{4,5},{5,6},{6,7},{7,8},{8,9},{9,10},{10,1... | collective-permute-start | bytes 2359304 | tf_op jit(solution)/shard_map/ppermute | solution.py:97
  13.4 4.3 %collective-permute-start.1 = (bf16[768,512]{1,0:T(8,128)(2,1)}, bf16[768,512]{1,0:T(8,128)(2,1)}, u32[]{:S(2)}, u32[]{:S(2)}) collective-permute-start(bf16[768,512]{1,0:T(8,128)(2,1)} %get-tuple-element.18), channel_id=1, source_target_pairs={{1,0},{2,1},{3,2},{4,3},{5,4},{6,5},{7,6},{8,7},{9,8},{10,9},{11,1... | collective-permute-start | bytes 2359304 | tf_op jit(solution)/shard_map/ppermute | solution.py:98
  17.7 0.1 fusion.7
  17.8 0.1 reshape.92.local_ref
  17.9 0.1 copy.23
  18.0 0.1 copy.24
  18.2 15.2 %collective-permute-done.left_ref = bf16[768,512]{1,0:T(8,128)(2,1)S(1)} collective-permute-done((bf16[768,512]{1,0:T(8,128)(2,1)}, bf16[768,512]{1,0:T(8,128)(2,1)S(1)}, u32[]{:S(2)}, u32[]{:S(2)}) %collective-permute-start) | collective-permute-done | bytes 786464 | tf_op jit(solution)/shard_map/ppermute | solution.py:97
  33.4 1.2 collective-permute-done.1.right_ref
  34.6 9.1 %shard_map.59 = (f32[16,4,4,16,256]{4,3,2,1,0:T(8,128)S(1)}, f32[4,2048]{1,0:T(4,128)S(1)}, f32[4,512]{1,0:T(4,128)S(1)}) custom-call(s32[16]{0:T(128)S(1)} %reshape.92.local_ref, bf16[768,512]{1,0:T(8,128)(2,1)S(1)} %collective-permute-done.left_ref, bf16[768,1024]{1,0:T(8,128)(2,1)S(1)} %copy-done.1, bf16[768,512]{1,0:T(8,128)(2,1)} %collective-permute-done.1.right_ref, ...), custom_call_target="tpu_custom_call" | custom-call | flops 6499999744 | bytes 8000000 | tf_op jit(solution)/shard_map/pallas_call | solution.py:72
  43.7 1.9 %copy-done = f32[16,4,4,16,256]{4,3,2,1,0:T(8,128)} copy-done((f32[16,4,4,16,256]{4,3,2,1,0:T(8,128)}, f32[16,4,4,16,256]{4,3,2,1,0:T(8,128)S(1)}, u32[]{:S(2)}) %copy-start) | copy-done | bytes 4194328
  45.7 0.0 reduce-scatter.2.cloned.1.call-update
  45.7 0.1 reshape.93
  45.8 0.1 compare_and_fusion
  45.9 0.2 slice_reduce_fusion.4
  46.1 62.1 %psum.7 = f32[4,2048]{1,0:T(4,128)S(1)} all-reduce(f32[4,2048]{1,0:T(4,128)S(1)} %get-tuple-element.5), channel_id=1, replica_groups=mesh['shot'=16,'row'=8,'col'=4] {'shot'}, use_global_device_ids=true, to_apply=%region_0.1 | all-reduce | flops 8192 | bytes 65536 | tf_op jit(solution)/shard_map/psum | solution.py:107
  108.2 0.1 subtract_reduce_fusion
  108.3 0.6 gather_fusion
  108.9 0.1 constant_dynamic-slice_fusion
  109.0 0.1 broadcast_select_fusion
  109.1 0.7 negate_multiply_fusion
  109.8 20.9 %reduce-scatter.2.cloned.1.call-done = f32[1,4,4,16,256]{4,3,2,1,0:T(8,128)} async-done(((f32[16,4,4,16,256]{4,3,2,1,0:T(8,128)}), f32[1,4,4,16,256]{4,3,2,1,0:T(8,128)}) %reduce-scatter.2.cloned.1.call-update) | async-done | bytes 262160 | tf_op jit(solution)/shard_map/reduce_scatter | solution.py:108
  130.7 1.8 %fusion.4 = bf16[4,4,16,256]{3,2,1,0:T(8,128)(2,1)} fusion(f32[1,4,4,16,256]{4,3,2,1,0:T(8,128)} %reduce-scatter.2.cloned.1.call-done, f32[4,4]{1,0:T(4,128)S(1)} %get-tuple-element.22, f32[4,4,256]{2,1,0:T(4,128)S(1)} %broadcast_select_fusion, f32[4,16]{1,0:T(4,128)S(1)} %constant_dynamic-slice_fusion), kind=kLoop, calls=%fused_computation.6 | loop fusion | flops 458752 | bytes 409920 | tf_op jit(solution)/shard_map/convert_element_type | solution.py:118
  (18 shorter events, 0.1 us)
Async XLA Ops:
  7.2 27.4 %copy-start.1 = (bf16[768,1024]{1,0:T(8,128)(2,1)S(1)}, bf16[768,1024]{1,0:T(8,128)(2,1)}, u32[]{:S(2)}) copy-start(bf16[768,1024]{1,0:T(8,128)(2,1)} %own_ref.1) | copy-start | bytes 4718596
  7.2 10.5 %copy-start.4 = (s32[4,4]{1,0:T(4,128)S(1)}, s32[4,4]{1,0:T(4,128)}, u32[]{:S(2)}) copy-start(s32[4,4]{1,0:T(4,128)} %param.5) | copy-start | bytes 196
  7.2 10.7 %copy-start.2 = (s32[3,4,512]{2,1,0:T(4,128)S(1)}, s32[3,4,512]{2,1,0:T(4,128)}, u32[]{:S(2)}) copy-start(s32[3,4,512]{2,1,0:T(4,128)} %inc_ref.1) | copy-start | bytes 73732
  7.2 10.8 %copy-start.3 = (f32[4,512]{1,0:T(4,128)S(1)}, f32[4,512]{1,0:T(4,128)}, u32[]{:S(2)}) copy-start(f32[4,512]{1,0:T(4,128)} %param.7) | copy-start | bytes 24580
  7.2 123.5 %reduce-scatter.2.cloned.1.call-start = ((), (), s32[]{:S(2)}) async-start(), calls=%async_computation.1 | async-start | bytes 4456448 | tf_op jit(solution)/shard_map/reduce_scatter | solution.py:108
  10.0 23.4 %collective-permute-start = (bf16[768,512]{1,0:T(8,128)(2,1)}, bf16[768,512]{1,0:T(8,128)(2,1)S(1)}, u32[]{:S(2)}, u32[]{:S(2)}) collective-permute-start(bf16[768,512]{1,0:T(8,128)(2,1)} %get-tuple-element.19), channel_id=1, source_target_pairs={{0,1},{1,2},{2,3},{3,4},{4,5},{5,6},{6,7},{7,8},{8,9},{9,10},{10,1... | collective-permute-start | bytes 2359304 | tf_op jit(solution)/shard_map/ppermute | solution.py:97
  13.4 21.2 %collective-permute-start.1 = (bf16[768,512]{1,0:T(8,128)(2,1)}, bf16[768,512]{1,0:T(8,128)(2,1)}, u32[]{:S(2)}, u32[]{:S(2)}) collective-permute-start(bf16[768,512]{1,0:T(8,128)(2,1)} %get-tuple-element.18), channel_id=1, source_target_pairs={{1,0},{2,1},{3,2},{4,3},{5,4},{6,5},{7,6},{8,7},{9,8},{10,9},{11,1... | collective-permute-start | bytes 2359304 | tf_op jit(solution)/shard_map/ppermute | solution.py:98
  43.7 1.9 %copy-start = (f32[16,4,4,16,256]{4,3,2,1,0:T(8,128)}, f32[16,4,4,16,256]{4,3,2,1,0:T(8,128)S(1)}, u32[]{:S(2)}) copy-start(f32[16,4,4,16,256]{4,3,2,1,0:T(8,128)S(1)} %get-tuple-element.6) | copy-start | bytes 12582916
Sparse Core Ops, SparseCore 0:
  45.8 84.8 reduce-scatter.1

commit v2 on v1

--- a/solution.py
+++ b/solution.py
@@ -84,6 +84,26 @@
     )(local_index, left, own, right, incidence, keys_t, prob_t)
 
 
+def arcs_sum(parts, axis, count):
+    me = lax.axis_index(axis)
+
+    def mine(shift):
+        return lax.dynamic_index_in_dim(parts, lax.rem(me + shift + count, count), 0, keepdims=False)
+
+    lower = [((i + 1) % count, i) for i in range(count)]
+    upper = [(i, (i + 1) % count) for i in range(count)]
+    half = count // 2
+    down, up = mine(-half), mine(half - 1)
+    for step in range(half):
+        down = lax.ppermute(down, axis, lower)
+        if step < half - 1:
+            down = down + mine(step + 1 - half)
+            up = lax.ppermute(up, axis, upper)
+            if step < half - 2:
+                up = up + mine(half - 2 - step)
+    return mine(0) + down + up
+
+
 def local(soft, partners, incidence, edge_prob):
     shots, own_width = soft.shape
     blocks, slots = partners.shape
@@ -104,8 +124,8 @@
     gram, small, fitted = gram_call(
         local_index, left, soft, right, incidence, keys.T, edge_prob.T, groups, slots, width
     )
-    small = lax.psum(small, "shot")
-    total = lax.psum_scatter(gram, "shot", scatter_dimension=0, tiled=False)
+    small = jnp.sum(lax.all_gather(small, "shot"), axis=0)
+    total = arcs_sum(gram, "shot", groups)
 
     mean_blocks = small[0].reshape(blocks + 2 * HALO, width) / count
     share = width // groups

time: 140 us -> 180 us (1.29)
  the two profiles are of different devices: /device:TPU:24 before, /device:TPU:6 now
where the time goes in v2:
time: 180 us; the launch traced here: 179 us
  starting transfers between devices  62.7 us (35%)
  waiting for transfers between devices  55.2 us (31%)
  blocking collectives  30.5 us (17%)
  other arithmetic  12.7 us (7%)
  local copies, waits for them, and re-layouts  8.55 us (5%)
  Pallas kernels  8.22 us (5%)
    ppermute x8, starting transfers between devices, arcs_sum(): down = lax.ppermute(down, axis, lower)  37.7 us
    all_gather x1, blocking collectives, local(): small = jnp.sum(lax.all_gather(small, 'shot'), axis=0)  30.5 us
    ppermute x8, waiting for transfers between devices, arcs_sum(): down = lax.ppermute(down, axis, lower)  22.6 us
    ppermute x7, starting transfers between devices, arcs_sum(): up = lax.ppermute(up, axis, upper)  19.2 us
    ppermute x7, waiting for transfers between devices, arcs_sum(): up = lax.ppermute(up, axis, upper)  18.5 us
    ppermute x1, waiting for transfers between devices, local(): lax.ppermute(soft[:, own_width - reach:], ('row', 'col'), [(i, (i + 1) %...  12.9 us
    pallas_call x1, Pallas kernels, gram_call(): pl.pallas_call(functools.partial(gram_kernel, blocks, slots, width), out_...  8.22 us
    add x7, other arithmetic, arcs_sum(): down = down + mine(step + 1 - half)  7.67 us
  transfers between devices with their start and end apart: 17, of which 14 were waited for; matrix products, arithmetic and copies ran while one was open for 4% of the time, Pallas kernels for 0%

profile of v2, /device:TPU:6, one launch (start us, length us, event | category | flops | bytes accessed | tf_op | source)
XLA Modules:
  0.0 178.9 jit_solution(12967207039076214547)
XLA Ops:
  0.6 2.4 %fusion.12 = (bf16[768,512]{1,0:T(8,128)(2,1)S(1)}, bf16[768,512]{1,0:T(8,128)(2,1)}) fusion(bf16[768,1024]{1,0:T(8,128)(2,1)} %own_ref.1), kind=kLoop, calls=%fused_computation.50 | loop fusion | bytes 3145728 | tf_op jit(solution)/shard_map/slice | solution.py:118
  4.9 3.9 %collective-permute-start.1 = (bf16[768,512]{1,0:T(8,128)(2,1)S(1)}, bf16[768,512]{1,0:T(8,128)(2,1)S(1)}, u32[]{:S(2)}, u32[]{:S(2)}) collective-permute-start(bf16[768,512]{1,0:T(8,128)(2,1)S(1)} %get-tuple-element.34), channel_id=1, source_target_pairs={{1,0},{2,1},{3,2},{4,3},{5,4},{6,5},{7,6},{8,7},{9,8},{10,9},{11,1... | collective-permute-start | bytes 2359304 | tf_op jit(solution)/shard_map/ppermute | solution.py:118
  11.5 12.9 %collective-permute-done.left_ref = bf16[768,512]{1,0:T(8,128)(2,1)S(1)} collective-permute-done((bf16[768,512]{1,0:T(8,128)(2,1)}, bf16[768,512]{1,0:T(8,128)(2,1)S(1)}, u32[]{:S(2)}, u32[]{:S(2)}) %collective-permute-start) | collective-permute-done | bytes 786464 | tf_op jit(solution)/shard_map/ppermute | solution.py:117
  27.8 8.2 %shard_map.59 = (f32[16,4,4,16,256]{4,3,2,1,0:T(8,128)S(1)}, f32[4,2048]{1,0:T(4,128)S(1)}, f32[4,512]{1,0:T(4,128)S(1)}) custom-call(s32[16]{0:T(128)S(1)} %reshape.92.local_ref, bf16[768,512]{1,0:T(8,128)(2,1)S(1)} %collective-permute-done.left_ref, bf16[768,1024]{1,0:T(8,128)(2,1)S(1)} %copy-done.1, ...), custom_call_target="tpu_custom_call" | custom-call | flops 6499999744 | bytes 8000000 | tf_op jit(solution)/shard_map/pallas_call | solution.py:72
  38.0 11.4 %collective-permute-start.2 = (f32[4,4,16,256]{3,2,1,0:T(8,128)S(1)}, f32[4,4,16,256]{3,2,1,0:T(8,128)S(1)}, u32[]{:S(2)}, u32[]{:S(2)}) collective-permute-start(f32[4,4,16,256]{3,2,1,0:T(8,128)S(1)} %get-tuple-element.32), channel_id=1, source_target_pairs={{32,0},{64,32},{96,64},{128,96},{160,128},{192,160},{224,192},{256... | collective-permute-start | bytes 786440 | tf_op jit(solution)/shard_map/ppermute | solution.py:98
  51.4 2.6 %collective-permute-done.2 = f32[4,4,16,256]{3,2,1,0:T(8,128)S(1)} collective-permute-done((f32[4,4,16,256]{3,2,1,0:T(8,128)S(1)}, f32[4,4,16,256]{3,2,1,0:T(8,128)S(1)}, u32[]{:S(2)}, u32[]{:S(2)}) %collective-permute-start.2) | collective-permute-done | bytes 262176 | tf_op jit(solution)/shard_map/ppermute | solution.py:98
  55.0 5.6 %collective-permute-start.3 = (f32[4,4,16,256]{3,2,1,0:T(8,128)S(1)}, f32[4,4,16,256]{3,2,1,0:T(8,128)S(1)}, u32[]{:S(2)}, u32[]{:S(2)}) collective-permute-start(f32[4,4,16,256]{3,2,1,0:T(8,128)S(1)} %bitcast_add_fusion.12), channel_id=1, source_target_pairs={{32,0},{64,32},{96,64},{128,96},{160,128},{192,160},{224,192},{256... | collective-permute-start | bytes 786440 | tf_op jit(solution)/shard_map/ppermute | solution.py:98
  60.6 5.7 %collective-permute-done.3 = f32[4,4,16,256]{3,2,1,0:T(8,128)S(1)} collective-permute-done((f32[4,4,16,256]{3,2,1,0:T(8,128)S(1)}, f32[4,4,16,256]{3,2,1,0:T(8,128)S(1)}, u32[]{:S(2)}, u32[]{:S(2)}) %collective-permute-start.3) | collective-permute-done | bytes 262176 | tf_op jit(solution)/shard_map/ppermute | solution.py:98
  67.5 5.6 %collective-permute-start.4 = (f32[4,4,16,256]{3,2,1,0:T(8,128)S(1)}, f32[4,4,16,256]{3,2,1,0:T(8,128)S(1)}, u32[]{:S(2)}, u32[]{:S(2)}) collective-permute-start(f32[4,4,16,256]{3,2,1,0:T(8,128)S(1)} %get-tuple-element.30), channel_id=1, source_target_pairs={{32,0},{64,32},{96,64},{128,96},{160,128},{192,160},{224,192},{256... | collective-permute-start | bytes 786440 | tf_op jit(solution)/shard_map/ppermute | solution.py:98
  75.0 4.5 %collective-permute-done.4 = f32[4,4,16,256]{3,2,1,0:T(8,128)S(1)} collective-permute-done((f32[4,4,16,256]{3,2,1,0:T(8,128)S(1)}, f32[4,4,16,256]{3,2,1,0:T(8,128)S(1)}, u32[]{:S(2)}, u32[]{:S(2)}) %collective-permute-start.4) | collective-permute-done | bytes 262176 | tf_op jit(solution)/shard_map/ppermute | solution.py:98
  79.5 5.3 %collective-permute-done.11 = f32[4,4,16,256]{3,2,1,0:T(8,128)S(1)} collective-permute-done((f32[4,4,16,256]{3,2,1,0:T(8,128)S(1)}, f32[4,4,16,256]{3,2,1,0:T(8,128)S(1)}, u32[]{:S(2)}, u32[]{:S(2)}) %collective-permute-start.11) | collective-permute-done | bytes 262176 | tf_op jit(solution)/shard_map/ppermute | solution.py:101
  87.9 3.9 %collective-permute-start.12 = (f32[4,4,16,256]{3,2,1,0:T(8,128)S(1)}, f32[4,4,16,256]{3,2,1,0:T(8,128)S(1)}, u32[]{:S(2)}, u32[]{:S(2)}) collective-permute-start(f32[4,4,16,256]{3,2,1,0:T(8,128)S(1)} %get-tuple-element.29), channel_id=1, source_target_pairs={{0,32},{32,64},{64,96},{96,128},{128,160},{160,192},{192,224},{224... | collective-permute-start | bytes 786440 | tf_op jit(solution)/shard_map/ppermute | solution.py:101
  92.0 3.8 %collective-permute-done.5 = f32[4,4,16,256]{3,2,1,0:T(8,128)S(1)} collective-permute-done((f32[4,4,16,256]{3,2,1,0:T(8,128)S(1)}, f32[4,4,16,256]{3,2,1,0:T(8,128)S(1)}, u32[]{:S(2)}, u32[]{:S(2)}) %collective-permute-start.5) | collective-permute-done | bytes 262176 | tf_op jit(solution)/shard_map/ppermute | solution.py:98
  95.8 3.1 %collective-permute-done.12 = f32[4,4,16,256]{3,2,1,0:T(8,128)S(1)} collective-permute-done((f32[4,4,16,256]{3,2,1,0:T(8,128)S(1)}, f32[4,4,16,256]{3,2,1,0:T(8,128)S(1)}, u32[]{:S(2)}, u32[]{:S(2)}) %collective-permute-start.12) | collective-permute-done | bytes 262176 | tf_op jit(solution)/shard_map/ppermute | solution.py:101
  102.0 3.9 %collective-permute-start.13 = (f32[4,4,16,256]{3,2,1,0:T(8,128)S(1)}, f32[4,4,16,256]{3,2,1,0:T(8,128)S(1)}, u32[]{:S(2)}, u32[]{:S(2)}) collective-permute-start(f32[4,4,16,256]{3,2,1,0:T(8,128)S(1)} %get-tuple-element.27), channel_id=1, source_target_pairs={{0,32},{32,64},{64,96},{96,128},{128,160},{160,192},{192,224},{224... | collective-permute-start | bytes 786440 | tf_op jit(solution)/shard_map/ppermute | solution.py:101
  106.2 2.8 %collective-permute-done.6 = f32[4,4,16,256]{3,2,1,0:T(8,128)S(1)} collective-permute-done((f32[4,4,16,256]{3,2,1,0:T(8,128)S(1)}, f32[4,4,16,256]{3,2,1,0:T(8,128)S(1)}, u32[]{:S(2)}, u32[]{:S(2)}) %collective-permute-start.6) | collective-permute-done | bytes 262176 | tf_op jit(solution)/shard_map/ppermute | solution.py:98
  109.0 3.1 %collective-permute-done.13 = f32[4,4,16,256]{3,2,1,0:T(8,128)S(1)} collective-permute-done((f32[4,4,16,256]{3,2,1,0:T(8,128)S(1)}, f32[4,4,16,256]{3,2,1,0:T(8,128)S(1)}, u32[]{:S(2)}, u32[]{:S(2)}) %collective-permute-start.13) | collective-permute-done | bytes 262176 | tf_op jit(solution)/shard_map/ppermute | solution.py:101
  113.2 2.4 %collective-permute-start.7 = (f32[4,4,16,256]{3,2,1,0:T(8,128)S(1)}, f32[4,4,16,256]{3,2,1,0:T(8,128)S(1)}, u32[]{:S(2)}, u32[]{:S(2)}) collective-permute-start(f32[4,4,16,256]{3,2,1,0:T(8,128)S(1)} %get-tuple-element.24), channel_id=1, source_target_pairs={{32,0},{64,32},{96,64},{128,96},{160,128},{192,160},{224,192},{256... | collective-permute-start | bytes 786440 | tf_op jit(solution)/shard_map/ppermute | solution.py:98
  115.6 3.5 %collective-permute-start.14 = (f32[4,4,16,256]{3,2,1,0:T(8,128)S(1)}, f32[4,4,16,256]{3,2,1,0:T(8,128)S(1)}, u32[]{:S(2)}, u32[]{:S(2)}) collective-permute-start(f32[4,4,16,256]{3,2,1,0:T(8,128)S(1)} %get-tuple-element.25), channel_id=1, source_target_pairs={{0,32},{32,64},{64,96},{96,128},{128,160},{160,192},{192,224},{224... | collective-permute-start | bytes 786440 | tf_op jit(solution)/shard_map/ppermute | solution.py:101
  119.1 30.5 %all-gather.1 = f32[16,4,2048]{2,1,0:T(4,128)S(1)} all-gather(f32[1,4,2048]{2,1,0:T(4,128)S(1)} %bitcast.63), channel_id=2, replica_groups=mesh['shot'=16,'row'=8,'col'=4] {'shot'}, dimensions={0}, use_global_device_ids=true | all-gather | bytes 557056 | tf_op jit(solution)/shard_map/all_gather | solution.py:127
  150.9 3.7 %collective-permute-start.8 = (f32[4,4,16,256]{3,2,1,0:T(8,128)S(1)}, f32[4,4,16,256]{3,2,1,0:T(8,128)S(1)}, u32[]{:S(2)}, u32[]{:S(2)}) collective-permute-start(f32[4,4,16,256]{3,2,1,0:T(8,128)S(1)} %get-tuple-element.22), channel_id=1, source_target_pairs={{32,0},{64,32},{96,64},{128,96},{160,128},{192,160},{224,192},{256... | collective-permute-start | bytes 786440 | tf_op jit(solution)/shard_map/ppermute | solution.py:98
  154.6 2.1 %collective-permute-start.15 = (f32[4,4,16,256]{3,2,1,0:T(8,128)S(1)}, f32[4,4,16,256]{3,2,1,0:T(8,128)S(1)}, u32[]{:S(2)}, u32[]{:S(2)}) collective-permute-start(f32[4,4,16,256]{3,2,1,0:T(8,128)S(1)} %get-tuple-element.23), channel_id=1, source_target_pairs={{0,32},{32,64},{64,96},{96,128},{128,160},{160,192},{192,224},{224... | collective-permute-start | bytes 786440 | tf_op jit(solution)/shard_map/ppermute | solution.py:101
  159.1 5.9 %collective-permute-done.15 = f32[4,4,16,256]{3,2,1,0:T(8,128)S(1)} collective-permute-done((f32[4,4,16,256]{3,2,1,0:T(8,128)S(1)}, f32[4,4,16,256]{3,2,1,0:T(8,128)S(1)}, u32[]{:S(2)}, u32[]{:S(2)}) %collective-permute-start.15) | collective-permute-done | bytes 262176 | tf_op jit(solution)/shard_map/ppermute | solution.py:101
  168.1 5.1 %collective-permute-start.9 = (f32[4,4,16,256]{3,2,1,0:T(8,128)S(1)}, f32[4,4,16,256]{3,2,1,0:T(8,128)S(1)}, u32[]{:S(2)}, u32[]{:S(2)}) collective-permute-start(f32[4,4,16,256]{3,2,1,0:T(8,128)S(1)} %get-tuple-element.20), channel_id=1, source_target_pairs={{32,0},{64,32},{96,64},{128,96},{160,128},{192,160},{224,192},{256... | collective-permute-start | bytes 786440 | tf_op jit(solution)/shard_map/ppermute | solution.py:98
  (52 shorter events, 35.8 us)
Async XLA Ops:
  3.0 21.4 %collective-permute-start = (bf16[768,512]{1,0:T(8,128)(2,1)}, bf16[768,512]{1,0:T(8,128)(2,1)S(1)}, u32[]{:S(2)}, u32[]{:S(2)}) collective-permute-start(bf16[768,512]{1,0:T(8,128)(2,1)} %get-tuple-element.35), channel_id=1, source_target_pairs={{0,1},{1,2},{2,3},{3,4},{4,5},{5,6},{6,7},{7,8},{8,9},{9,10},{10,1... | collective-permute-start | bytes 2359304 | tf_op jit(solution)/shard_map/ppermute | solution.py:117
  4.9 20.7 %collective-permute-start.1 = (bf16[768,512]{1,0:T(8,128)(2,1)S(1)}, bf16[768,512]{1,0:T(8,128)(2,1)S(1)}, u32[]{:S(2)}, u32[]{:S(2)}) collective-permute-start(bf16[768,512]{1,0:T(8,128)(2,1)S(1)} %get-tuple-element.34), channel_id=1, source_target_pairs={{1,0},{2,1},{3,2},{4,3},{5,4},{6,5},{7,6},{8,7},{9,8},{10,9},{11,1... | collective-permute-start | bytes 2359304 | tf_op jit(solution)/shard_map/ppermute | solution.py:118
  25.6 1.4 copy-start.1
  27.1 0.7 copy-start.2
  36.0 1.9 %copy-start = (f32[16,4,4,16,256]{4,3,2,1,0:T(8,128)}, f32[16,4,4,16,256]{4,3,2,1,0:T(8,128)S(1)}, u32[]{:S(2)}) copy-start(f32[16,4,4,16,256]{4,3,2,1,0:T(8,128)S(1)} %get-tuple-element.6) | copy-start | bytes 12582916
  36.0 55.9 %copy-start.3 = (s32[4,4]{1,0:T(4,128)S(1)}, s32[4,4]{1,0:T(4,128)}, u32[]{:S(2)}) copy-start(s32[4,4]{1,0:T(4,128)} %param.5) | copy-start | bytes 196
  38.0 16.0 %collective-permute-start.2 = (f32[4,4,16,256]{3,2,1,0:T(8,128)S(1)}, f32[4,4,16,256]{3,2,1,0:T(8,128)S(1)}, u32[]{:S(2)}, u32[]{:S(2)}) collective-permute-start(f32[4,4,16,256]{3,2,1,0:T(8,128)S(1)} %get-tuple-element.32), channel_id=1, source_target_pairs={{32,0},{64,32},{96,64},{128,96},{160,128},{192,160},{224,192},{256... | collective-permute-start | bytes 786440 | tf_op jit(solution)/shard_map/ppermute | solution.py:98
  49.4 11.2 %collective-permute-start.10 = (f32[4,4,16,256]{3,2,1,0:T(8,128)S(1)}, f32[4,4,16,256]{3,2,1,0:T(8,128)S(1)}, u32[]{:S(2)}, u32[]{:S(2)}) collective-permute-start(f32[4,4,16,256]{3,2,1,0:T(8,128)S(1)} %get-tuple-element.33), channel_id=1, source_target_pairs={{0,32},{32,64},{64,96},{96,128},{128,160},{160,192},{192,224},{224... | collective-permute-start | bytes 786440 | tf_op jit(solution)/shard_map/ppermute | solution.py:101
  55.0 11.3 %collective-permute-start.3 = (f32[4,4,16,256]{3,2,1,0:T(8,128)S(1)}, f32[4,4,16,256]{3,2,1,0:T(8,128)S(1)}, u32[]{:S(2)}, u32[]{:S(2)}) collective-permute-start(f32[4,4,16,256]{3,2,1,0:T(8,128)S(1)} %bitcast_add_fusion.12), channel_id=1, source_target_pairs={{32,0},{64,32},{96,64},{128,96},{160,128},{192,160},{224,192},{256... | collective-permute-start | bytes 786440 | tf_op jit(solution)/shard_map/ppermute | solution.py:98
  67.5 12.1 %collective-permute-start.4 = (f32[4,4,16,256]{3,2,1,0:T(8,128)S(1)}, f32[4,4,16,256]{3,2,1,0:T(8,128)S(1)}, u32[]{:S(2)}, u32[]{:S(2)}) collective-permute-start(f32[4,4,16,256]{3,2,1,0:T(8,128)S(1)} %get-tuple-element.30), channel_id=1, source_target_pairs={{32,0},{64,32},{96,64},{128,96},{160,128},{192,160},{224,192},{256... | collective-permute-start | bytes 786440 | tf_op jit(solution)/shard_map/ppermute | solution.py:98
  73.1 11.8 %collective-permute-start.11 = (f32[4,4,16,256]{3,2,1,0:T(8,128)S(1)}, f32[4,4,16,256]{3,2,1,0:T(8,128)S(1)}, u32[]{:S(2)}, u32[]{:S(2)}) collective-permute-start(f32[4,4,16,256]{3,2,1,0:T(8,128)S(1)} %get-tuple-element.31), channel_id=1, source_target_pairs={{0,32},{32,64},{64,96},{96,128},{128,160},{160,192},{192,224},{224... | collective-permute-start | bytes 786440 | tf_op jit(solution)/shard_map/ppermute | solution.py:101
  86.0 9.8 %collective-permute-start.5 = (f32[4,4,16,256]{3,2,1,0:T(8,128)S(1)}, f32[4,4,16,256]{3,2,1,0:T(8,128)S(1)}, u32[]{:S(2)}, u32[]{:S(2)}) collective-permute-start(f32[4,4,16,256]{3,2,1,0:T(8,128)S(1)} %get-tuple-element.28), channel_id=1, source_target_pairs={{32,0},{64,32},{96,64},{128,96},{160,128},{192,160},{224,192},{256... | collective-permute-start | bytes 786440 | tf_op jit(solution)/shard_map/ppermute | solution.py:98
  87.9 11.0 %collective-permute-start.12 = (f32[4,4,16,256]{3,2,1,0:T(8,128)S(1)}, f32[4,4,16,256]{3,2,1,0:T(8,128)S(1)}, u32[]{:S(2)}, u32[]{:S(2)}) collective-permute-start(f32[4,4,16,256]{3,2,1,0:T(8,128)S(1)} %get-tuple-element.29), channel_id=1, source_target_pairs={{0,32},{32,64},{64,96},{96,128},{128,160},{160,192},{192,224},{224... | collective-permute-start | bytes 786440 | tf_op jit(solution)/shard_map/ppermute | solution.py:101
  100.0 8.9 %collective-permute-start.6 = (f32[4,4,16,256]{3,2,1,0:T(8,128)S(1)}, f32[4,4,16,256]{3,2,1,0:T(8,128)S(1)}, u32[]{:S(2)}, u32[]{:S(2)}) collective-permute-start(f32[4,4,16,256]{3,2,1,0:T(8,128)S(1)} %get-tuple-element.26), channel_id=1, source_target_pairs={{32,0},{64,32},{96,64},{128,96},{160,128},{192,160},{224,192},{256... | collective-permute-start | bytes 786440 | tf_op jit(solution)/shard_map/ppermute | solution.py:98
  102.0 10.1 %collective-permute-start.13 = (f32[4,4,16,256]{3,2,1,0:T(8,128)S(1)}, f32[4,4,16,256]{3,2,1,0:T(8,128)S(1)}, u32[]{:S(2)}, u32[]{:S(2)}) collective-permute-start(f32[4,4,16,256]{3,2,1,0:T(8,128)S(1)} %get-tuple-element.27), channel_id=1, source_target_pairs={{0,32},{32,64},{64,96},{96,128},{128,160},{160,192},{192,224},{224... | collective-permute-start | bytes 786440 | tf_op jit(solution)/shard_map/ppermute | solution.py:101
  113.2 36.5 %collective-permute-start.7 = (f32[4,4,16,256]{3,2,1,0:T(8,128)S(1)}, f32[4,4,16,256]{3,2,1,0:T(8,128)S(1)}, u32[]{:S(2)}, u32[]{:S(2)}) collective-permute-start(f32[4,4,16,256]{3,2,1,0:T(8,128)S(1)} %get-tuple-element.24), channel_id=1, source_target_pairs={{32,0},{64,32},{96,64},{128,96},{160,128},{192,160},{224,192},{256... | collective-permute-start | bytes 786440 | tf_op jit(solution)/shard_map/ppermute | solution.py:98
  115.6 34.1 %collective-permute-start.14 = (f32[4,4,16,256]{3,2,1,0:T(8,128)S(1)}, f32[4,4,16,256]{3,2,1,0:T(8,128)S(1)}, u32[]{:S(2)}, u32[]{:S(2)}) collective-permute-start(f32[4,4,16,256]{3,2,1,0:T(8,128)S(1)} %get-tuple-element.25), channel_id=1, source_target_pairs={{0,32},{32,64},{64,96},{96,128},{128,160},{160,192},{192,224},{224... | collective-permute-start | bytes 786440 | tf_op jit(solution)/shard_map/ppermute | solution.py:101
  150.9 8.3 %collective-permute-start.8 = (f32[4,4,16,256]{3,2,1,0:T(8,128)S(1)}, f32[4,4,16,256]{3,2,1,0:T(8,128)S(1)}, u32[]{:S(2)}, u32[]{:S(2)}) collective-permute-start(f32[4,4,16,256]{3,2,1,0:T(8,128)S(1)} %get-tuple-element.22), channel_id=1, source_target_pairs={{32,0},{64,32},{96,64},{128,96},{160,128},{192,160},{224,192},{256... | collective-permute-start | bytes 786440 | tf_op jit(solution)/shard_map/ppermute | solution.py:98
  154.6 10.4 %collective-permute-start.15 = (f32[4,4,16,256]{3,2,1,0:T(8,128)S(1)}, f32[4,4,16,256]{3,2,1,0:T(8,128)S(1)}, u32[]{:S(2)}, u32[]{:S(2)}) collective-permute-start(f32[4,4,16,256]{3,2,1,0:T(8,128)S(1)} %get-tuple-element.23), channel_id=1, source_target_pairs={{0,32},{32,64},{64,96},{96,128},{128,160},{160,192},{192,224},{224... | collective-permute-start | bytes 786440 | tf_op jit(solution)/shard_map/ppermute | solution.py:101
  166.2 9.5 %collective-permute-start.16 = (f32[4,4,16,256]{3,2,1,0:T(8,128)S(1)}, f32[4,4,16,256]{3,2,1,0:T(8,128)S(1)}, u32[]{:S(2)}, u32[]{:S(2)}) collective-permute-start(f32[4,4,16,256]{3,2,1,0:T(8,128)S(1)} %get-tuple-element.21), channel_id=1, source_target_pairs={{0,32},{32,64},{64,96},{96,128},{128,160},{160,192},{192,224},{224... | collective-permute-start | bytes 786440 | tf_op jit(solution)/shard_map/ppermute | solution.py:101
  168.1 9.0 %collective-permute-start.9 = (f32[4,4,16,256]{3,2,1,0:T(8,128)S(1)}, f32[4,4,16,256]{3,2,1,0:T(8,128)S(1)}, u32[]{:S(2)}, u32[]{:S(2)}) collective-permute-start(f32[4,4,16,256]{3,2,1,0:T(8,128)S(1)} %get-tuple-element.20), channel_id=1, source_target_pairs={{32,0},{64,32},{96,64},{128,96},{160,128},{192,160},{224,192},{256... | collective-permute-start | bytes 786440 | tf_op jit(solution)/shard_map/ppermute | solution.py:98

commit v3 on v0

v3 whole, which is shorter than its diff:
```python
import functools

import jax
import jax.numpy as jnp
from jax import lax
from jax.experimental import pallas as pl
from jax.experimental.pallas import tpu as pltpu
from jax.sharding import PartitionSpec as P

HALO = 2
NOISE_SPREAD = 0.05
SCALE = 131072.0
VMEM = pl.BlockSpec(memory_space=pltpu.VMEM)
ANY = pl.BlockSpec(memory_space=pl.ANY)
SMEM = pl.BlockSpec(memory_space=pltpu.SMEM)
PARAMS = pltpu.CompilerParams(vmem_limit_bytes=40 * 1024 * 1024)


def fixed(values):
    return jnp.floor(values * SCALE + 0.5).astype(jnp.int32)


def place():
    me = lax.axis_index("shot")
    way = 1 - 2 * lax.rem(lax.axis_index("row"), 2)
    first = (lax.axis_index("row") * lax.axis_size("col") + lax.axis_index("col"))
    return me, way, first


def spread(tile, slot, stage, first_ref, keep_ref, give_ref, me, way, groups):
    share = tile.shape[0] // groups
    stage[...] = tile.reshape(groups, share, tile.shape[1])
    half = groups // 2

    def rows(hop):
        return fixed(stage[lax.rem(me + way * hop + 2 * groups, groups)])

    for hop in range(half):
        keep_ref[hop, slot] = rows(hop)
    first_ref[slot] = rows(half)
    for hop in range(1, half):
        give_ref[hop - 1, slot] = rows(-hop)


def self_kernel(width, groups, own_ref, _, first_ref, keep_ref, give_ref, stage):
    me, way, _ = place()
    for b in range(own_ref.shape[1] // width):
        own = own_ref[:, b * width : (b + 1) * width]
        tile = lax.dot_general(own, own, (((0,), (0,)), ((), ())), preferred_element_type=jnp.float32)
        spread(tile, b, stage, first_ref, keep_ref, give_ref, me, way, groups)


def pair_kernel(
    upper, width, groups, partners_ref, halo_ref, own_ref, inc_ref, keyt_ref, probt_ref, _,
    first_ref, keep_ref, give_ref, fit_ref, win, stage,
):
    blocks, slots = partners_ref.shape
    mine = blocks // 2
    low = mine * upper
    edges = inc_ref.shape[2]
    reach = HALO * width
    own_width = own_ref.shape[1]
    me, way, group = place()
    base = group * blocks
    if upper:
        win[:, 0:own_width] = own_ref[...]
        win[:, own_width:] = halo_ref[...]
        window_first = base + low - HALO
    else:
        win[:, 0:reach] = halo_ref[...]
        win[:, reach:] = own_ref[...]
        window_first = base - HALO
    at_own = HALO * width
    share = width // groups
    pieces = edges // width
    small = [[], [], [], []]
    for b in range(mine):
        block = low + b
        own = win[:, at_own + b * width : at_own + (b + 1) * width]
        chosen = [own]
        for k in range(1, slots):
            partner = partners_ref[block, k]
            partner = jnp.where(partner >= 0, partner, base + block)
            start = pl.multiple_of((partner - window_first) * width, width)
            chosen.append(win[:, pl.ds(start, width)])
        chosen = jnp.concatenate(chosen, axis=1)
        tiles = lax.dot_general(
            own, chosen[:, width:], (((0,), (0,)), ((), ())), preferred_element_type=jnp.float32
        )
        for k in range(1, slots):
            spread(
                tiles[:, (k - 1) * width : k * width], b * (slots - 1) + k - 1, stage,
                first_ref, keep_ref, give_ref, me, way, groups,
            )
        rows_x = inc_ref[0, block : block + 1, :]
        slot_x = inc_ref[1, block : block + 1, :]
        cols_x = inc_ref[2, block : block + 1, :]
        row_hot = lax.broadcasted_iota(jnp.int32, (width, edges), 0) == rows_x
        col_hot = lax.broadcasted_iota(jnp.int32, (slots * width, edges), 0) == slot_x * width + cols_x
        row_vals = jnp.dot(own, row_hot.astype(jnp.bfloat16), preferred_element_type=jnp.float32)
        col_vals = jnp.dot(chosen, col_hot.astype(jnp.bfloat16), preferred_element_type=jnp.float32)
        sums = (row_vals * col_vals, row_vals, col_vals)
        for n, values in enumerate(sums):
            total = jnp.sum(values, axis=0, keepdims=True)
            small[n] += [total[:, p * width : (p + 1) * width] for p in range(pieces)]
        key = slot_x * (width * width) + rows_x * width + cols_x
        same = keyt_ref[:, block : block + 1] == key
        fit_ref[b : b + 1, :] = jnp.sum(jnp.where(same, probt_ref[:, block : block + 1], 0.0), axis=0, keepdims=True)
    ones = jnp.ones((8, win.shape[0]), jnp.bfloat16)
    low_col = reach if upper else 0
    columns = jnp.dot(ones, win[:, low_col : low_col + 4 * width], preferred_element_type=jnp.float32)
    small[3] = [columns[0:1, p * width : (p + 1) * width] for p in range(4)]
    rest = fixed(jnp.concatenate(small[0] + small[1] + small[2] + small[3], axis=0))
    last = mine * (slots - 1)
    first_ref[last] = rest
    for hop in range(groups // 2):
        keep_ref[hop, last] = rest
    for hop in range(1, groups // 2):
        give_ref[hop - 1, last] = rest


def pieces_of(slots, groups, share, width):
    shape = (slots, share, width)
    return [
        jax.ShapeDtypeStruct(shape, jnp.int32),
        jax.ShapeDtypeStruct((groups // 2,) + shape, jnp.int32),
        jax.ShapeDtypeStruct((groups // 2 - 1,) + shape, jnp.int32),
    ]


def self_call(soft, after, width, groups):
    blocks = soft.shape[1] // width
    share = width // groups
    return pl.pallas_call(
        functools.partial(self_kernel, width, groups),
        out_shape=pieces_of(blocks, groups, share, width),
        in_specs=[VMEM, ANY],
        out_specs=[VMEM] * 3,
        scratch_shapes=[pltpu.VMEM((groups, share, width), jnp.float32)],
        compiler_params=PARAMS,
        cost_estimate=pl.CostEstimate(flops=400_000_000, bytes_accessed=3_000_000, transcendentals=0),
    )(soft, after)


def pair_call(upper, partners, halo, after, soft, incidence, keys_t, prob_t, width, groups):
    blocks, slots = partners.shape
    share = width // groups
    edges = incidence.shape[2]
    return pl.pallas_call(
        functools.partial(pair_kernel, upper, width, groups),
        out_shape=pieces_of((blocks // 2) * (slots - 1) + 1, groups, share, width)
        + [jax.ShapeDtypeStruct((blocks // 2, edges), jnp.float32)],
        in_specs=[SMEM] + [VMEM] * 5 + [ANY],
        out_specs=[VMEM] * 4,
        scratch_shapes=[
            pltpu.VMEM((soft.shape[0], soft.shape[1] + halo.shape[1]), jnp.bfloat16),
            pltpu.VMEM((groups, share, width), jnp.float32),
        ],
        compiler_params=PARAMS,
        cost_estimate=pl.CostEstimate(flops=3_200_000_000, bytes_accessed=4_000_000, transcendentals=0),
    )(partners, halo, soft, incidence, keys_t, prob_t, after)


def hop_kernel(hop, came_ref, keep_ref, got_ref, *refs):
    out_ref = refs[-1]
    if len(came_ref.shape) == 3:
        out_ref[0] = came_ref[...] + keep_ref[hop]
        out_ref[1] = got_ref[hop - 1]
    else:
        out_ref[0] = came_ref[0] + keep_ref[hop]
        out_ref[1] = came_ref[1] + got_ref[hop - 1]


def hop_call(hop, came, keep, got, after):
    return pl.pallas_call(
        functools.partial(hop_kernel, hop),
        out_shape=jax.ShapeDtypeStruct((2,) + keep.shape[1:], jnp.int32),
        in_specs=[VMEM] * 3 + [ANY] * len(after),
        out_specs=VMEM,
        compiler_params=PARAMS,
        cost_estimate=pl.CostEstimate(flops=100_000, bytes_accessed=600_000, transcendentals=0),
    )(came, keep, got, *after)


def swap(values):
    rows = lax.axis_size("row")
    return lax.ppermute(values, "row", [(r, r ^ 1) for r in range(rows)])


def onward(values):
    groups, rows = lax.axis_size("shot"), lax.axis_size("row")
    pairs = []
    for z in range(groups):
        for r in range(rows):
            pairs.append((z * rows + r, ((z + 1 - 2 * (r % 2)) % groups) * rows + r))
    return lax.ppermute(values, ("shot", "row"), pairs)


def final_kernel(
    width, groups, count, partners_ref, inc_ref, *refs,
):
    (keep_a, came_a, back_a, keep_l, came_l, back_l, keep_u, came_u, back_u, fit_l, fit_u,
     pair_ref, grad_ref, total_l, total_u, means) = refs
    blocks, slots = partners_ref.shape
    mine = blocks // 2
    share = width // groups
    me, _, group = place()
    base = group * blocks
    total_l[...] = (keep_l[0] + came_l[0] + back_l[...]).astype(jnp.float32) * (1.0 / SCALE)
    total_u[...] = (keep_u[0] + came_u[0] + back_u[...]).astype(jnp.float32) * (1.0 / SCALE)
    last = mine * (slots - 1)
    means[0:4, :] = total_l[last, 12:16, :] / count
    means[4:8, :] = total_u[last, 12:16, :] / count
    spot = lax.broadcasted_iota(jnp.int32, (share, width), 1) == (
        lax.broadcasted_iota(jnp.int32, (share, width), 0) + me * share
    )
    for block in range(blocks):
        b = block % mine
        total, fit = (total_l, fit_l) if block < mine else (total_u, fit_u)
        row_mean = jnp.sum(
            jnp.where(spot, means[block + HALO : block + HALO + 1, :], 0.0), axis=1, keepdims=True
        )
        for k in range(slots):
            if k == 0:
                gram = (keep_a[0, block] + came_a[0, block] + back_a[block]).astype(jnp.float32) * (1.0 / SCALE)
                at = block + HALO
                live = jnp.float32(1.0)
            else:
                gram = total[b * (slots - 1) + k - 1]
                partner = partners_ref[block, k]
                live = jnp.where(partner >= 0, 1.0, 0.0)
                at = jnp.where(partner >= 0, partner - base + HALO, block + HALO)
            quotient = row_mean * means[pl.ds(at, 1), :] * count / gram
            pair_ref[block, k] = ((0.5 - 0.5 * jnp.sqrt(quotient)) * live).astype(jnp.bfloat16)
        pieces = inc_ref.shape[2] // width
        for p in range(pieces):
            n = b * pieces + p
            gram = total[last, n : n + 1, :]
            row_mean_x = total[last, 4 + n : 5 + n, :] / count
            col_mean_x = total[last, 8 + n : 9 + n, :] / count
            at = slice(p * width, (p + 1) * width)
            slot_x = inc_ref[1, block : block + 1, at]
            live = jnp.where(slot_x == 0, 1.0, 0.0)
            for k in range(1, slots):
                live = live + jnp.where((slot_x == k) & (partners_ref[block, k] >= 0), 1.0, 0.0)
            quotient = row_mean_x * col_mean_x * count / gram
            entry = (0.5 - 0.5 * jnp.sqrt(quotient)) * live
            residual = live * (entry - fit[b : b + 1, at]) / NOISE_SPREAD
            grad_ref[block : block + 1, at] = -residual / NOISE_SPREAD


def final_call(partners, incidence, sums, fits, width, groups, count):
    blocks, slots = partners.shape
    share = width // groups
    rows = (blocks // 2) * (slots - 1) + 1
    flat = [array for triple in sums for array in triple]
    return pl.pallas_call(
        functools.partial(final_kernel, width, groups, count),
        out_shape=[
            jax.ShapeDtypeStruct((blocks, slots, share, width), jnp.bfloat16),
            jax.ShapeDtypeStruct((blocks, incidence.shape[2]), jnp.float32),
        ],
        in_specs=[SMEM] + [VMEM] * (1 + len(flat) + len(fits)),
        out_specs=[VMEM] * 2,
        scratch_shapes=[
            pltpu.VMEM((rows, share, width), jnp.float32),
            pltpu.VMEM((rows, share, width), jnp.float32),
            pltpu.VMEM((blocks + 2 * HALO, width), jnp.float32),
        ],
        compiler_params=PARAMS,
        cost_estimate=pl.CostEstimate(flops=1_000_000, bytes_accessed=2_000_000, transcendentals=100_000),
    )(partners, incidence, *flat, *fits)


def local(soft, partners, incidence, edge_prob):
    shots, own_width = soft.shape
    blocks, slots = partners.shape
    width = own_width // blocks
    groups = lax.axis_size("shot")
    count = float(shots * groups)
    sides = lax.axis_size(("row", "col"))
    reach = HALO * width

    tail, head = soft[:, own_width - reach :], soft[:, :reach]
    left = lax.ppermute(tail, ("row", "col"), [(i, (i + 1) % sides) for i in range(sides)])
    right = lax.ppermute(head, ("row", "col"), [((i + 1) % sides, i) for i in range(sides)])

    keys = incidence[1] * (width * width) + incidence[0] * width + incidence[2]
    args = (soft, incidence, keys.T, edge_prob.T, width, groups)
    half = groups // 2

    def around(first, keep, give, order):
        steps = [onward(first)]
        got = swap(give)
        for hop in range(half - 1, 0, -1):
            steps.append(onward(hop_call(hop, steps[-1], keep, got, order.get(hop, ()))))
        return steps, (keep, steps[-1], swap(steps[-1][1]))

    early, alone = around(*self_call(soft, tail, width, groups), {})
    lower = pair_call(0, partners, left, early[4], *args)
    upper = pair_call(1, partners, right, early[5], *args)
    order = {half - 2: (early[6],), half - 3: (early[7],), half - 4: (alone[2],)}
    sums = (alone, around(*lower[:3], order)[1], around(*upper[:3], {})[1])
    return final_call(partners, incidence, sums, (lower[3], upper[3]), width, groups, count)


def solution(mesh):
    placed = (
        P("shot", ("row", "col")),
        P(("row", "col"), None),
        P(None, ("row", "col"), None),
        P(("row", "col"), None),
    )
    return jax.shard_map(
        local,
        mesh=mesh,
        in_specs=placed,
        out_specs=(P(("row", "col"), None, "shot", None), P(("row", "col"), None)),
        check_vma=False,
    )
```

time: 268 us -> 167 us (0.62)
  starting transfers between devices: 7.7 us -> 81.7 us
  local copies, waits for them, and re-layouts: 64.7 us -> 6.16 us
  waiting for transfers between devices: 113 us -> 62.9 us
  blocking collectives: 37.2 us -> 0 us
  other arithmetic: 23 us -> 0.01 us
  between operations: 14.2 us -> 1.17 us
  Pallas kernels: 0 us -> 12.7 us
  matrix products: 6.6 us -> 0 us
    psum x1 -> x0, waiting for transfers between devices: 98.7 us -> none  [local(): summed_gram = lax.psum(partial_gram, 'shot')]
    ppermute x2 -> x32, starting transfers between devices: 7.66 us -> 81.7 us  [the longest x24 61.4 us: onward(): return lax.ppermute(values, ('shot', 'row'), pairs)]
    ppermute x2 -> x32, waiting for transfers between devices: 14.3 us -> 62.9 us  [the longest x24 61.6 us: onward(): return lax.ppermute(values, ('shot', 'row'), pairs)]
    gather x5 -> x0, local copies, waits for them, and re-layouts: 42.8 us -> none  [the longest x1 30 us: local(): gradient = -fit_residual[block_rows, slot_x, rows_x, cols_x] / NOISE_SPREAD]
    psum x1 -> x0, blocking collectives: 37.2 us -> none  [local(): means = lax.psum(column_sums, 'shot') / count_of_shots]
    unnamed x5 -> x0, other arithmetic: 13.7 us -> none
    pallas_call x0 -> x25, Pallas kernels: none -> 12.7 us  [the longest x2 9.19 us: pair_call(): pl.pallas_call(functools.partial(pair_kernel, upper, width, groups), out_...]
    scatter-add x2 -> x0, local copies, waits for them, and re-layouts: 10.5 us -> none  [local(): fitted_values = jnp.zeros(pairwise_entry.shape, jnp.float32).at[block_row...]
  transfers between devices with their start and end apart: 3 -> 32, of which waited for: 3 -> 18; matrix products, arithmetic and copies ran while one was open for 10% -> 1% of each run, Pallas kernels for 0% -> 6%
where the time goes in v3:
time: 167 us; the launch traced here: 165 us
  starting transfers between devices  81.7 us (49%)
  waiting for transfers between devices  62.9 us (38%)
  Pallas kernels  12.7 us (8%)
  local copies, waits for them, and re-layouts  6.16 us (4%)
    ppermute x24, waiting for transfers between devices, onward(): return lax.ppermute(values, ('shot', 'row'), pairs)  61.6 us
    ppermute x24, starting transfers between devices, onward(): return lax.ppermute(values, ('shot', 'row'), pairs)  61.4 us
    ppermute x6, starting transfers between devices, swap(): return lax.ppermute(values, 'row', [(r, r ^ 1) for r in range(rows)])  12 us
    pallas_call x2, Pallas kernels, pair_call(): pl.pallas_call(functools.partial(pair_kernel, upper, width, groups), out_...  9.19 us
    ppermute x1, starting transfers between devices, local(): lax.ppermute(head, ('row', 'col'), [((i + 1) % sides, i) for i in range(s...  4.9 us
    ppermute x1, starting transfers between devices, local(): lax.ppermute(tail, ('row', 'col'), [(i, (i + 1) % sides) for i in range(s...  3.39 us
  transfers between devices with their start and end apart: 32, of which 18 were waited for; matrix products, arithmetic and copies ran while one was open for 1% of the time, Pallas kernels for 6%

profile of v3, /device:TPU:24, one launch (start us, length us, event | category | flops | bytes accessed | tf_op | source)
XLA Modules:
  0.0 164.6 jit_solution(17985847730850125357)
XLA Ops:
  0.6 2.5 %fusion = (bf16[768,512]{1,0:T(8,128)(2,1)}, bf16[768,512]{1,0:T(8,128)(2,1)S(1)}) fusion(bf16[768,1024]{1,0:T(8,128)(2,1)} %own_ref.5), kind=kLoop, calls=%fused_computation.4 | loop fusion | bytes 3145728 | tf_op jit(solution)/shard_map/slice | solution.py:284
  5.9 3.4 %collective-permute-start.10 = (bf16[768,512]{1,0:T(8,128)(2,1)S(1)}, bf16[768,512]{1,0:T(8,128)(2,1)}, u32[]{:S(2)}, u32[]{:S(2)}) collective-permute-start(bf16[768,512]{1,0:T(8,128)(2,1)S(1)} %get-tuple-element.25._), channel_id=1, source_target_pairs={{0,1},{1,2},{2,3},{3,4},{4,5},{5,6},{6,7},{7,8},{8,9},{9,10},{10,1... | collective-permute-start | bytes 2359304 | tf_op jit(solution)/shard_map/ppermute | solution.py:285
  9.3 3.8 %collective-permute-start = (s32[4,16,256]{2,1,0:T(8,128)S(1)}, s32[4,16,256]{2,1,0:T(8,128)S(1)}, u32[]{:S(2)}, u32[]{:S(2)}) collective-permute-start(s32[4,16,256]{2,1,0:T(8,128)S(1)} %get-tuple-element.14), channel_id=1, source_target_pairs={{0,32},{4,484},{8,40},{12,492},{16,48},{20,500},{24,56},{28,508},{... | collective-permute-start | bytes 196616 | tf_op jit(solution)/shard_map/ppermute | solution.py:196
  13.1 9.8 %collective-permute-done.came_ref = s32[4,16,256]{2,1,0:T(8,128)S(1)} collective-permute-done((s32[4,16,256]{2,1,0:T(8,128)S(1)}, s32[4,16,256]{2,1,0:T(8,128)S(1)}, u32[]{:S(2)}, u32[]{:S(2)}) %collective-permute-start) | collective-permute-done | bytes 65568 | tf_op jit(solution)/shard_map/ppermute | solution.py:196
  24.9 6.1 %collective-permute-done.2.came_ref = s32[2,4,16,256]{3,2,1,0:T(8,128)S(1)} collective-permute-done((s32[2,4,16,256]{3,2,1,0:T(8,128)S(1)}, s32[2,4,16,256]{3,2,1,0:T(8,128)S(1)}, u32[]{:S(2)}, u32[]{:S(2)}) %collective-permute-start.2) | collective-permute-done | bytes 131104 | tf_op jit(solution)/shard_map/ppermute | solution.py:196
  33.0 4.9 %collective-permute-start.21 = (bf16[768,512]{1,0:T(8,128)(2,1)}, bf16[768,512]{1,0:T(8,128)(2,1)}, u32[]{:S(2)}, u32[]{:S(2)}) collective-permute-start(bf16[768,512]{1,0:T(8,128)(2,1)} %get-tuple-element.24), channel_id=1, source_target_pairs={{1,0},{2,1},{3,2},{4,3},{5,4},{6,5},{7,6},{8,7},{9,8},{10,9},{11,1... | collective-permute-start | bytes 2359304 | tf_op jit(solution)/shard_map/ppermute | solution.py:286
  41.1 6.1 %collective-permute-done.4.came_ref = s32[2,4,16,256]{3,2,1,0:T(8,128)S(1)} collective-permute-done((s32[2,4,16,256]{3,2,1,0:T(8,128)S(1)}, s32[2,4,16,256]{3,2,1,0:T(8,128)S(1)}, u32[]{:S(2)}, u32[]{:S(2)}) %collective-permute-start.4) | collective-permute-done | bytes 131104 | tf_op jit(solution)/shard_map/ppermute | solution.py:196
  51.6 4.6 %collective-permute-done.5.came_ref._ = s32[2,4,16,256]{3,2,1,0:T(8,128)S(1)} collective-permute-done((s32[2,4,16,256]{3,2,1,0:T(8,128)}, s32[2,4,16,256]{3,2,1,0:T(8,128)S(1)}, u32[]{:S(2)}, u32[]{:S(2)}) %collective-permute-start.5) | collective-permute-done | bytes 131104 | tf_op jit(solution)/shard_map/ppermute | solution.py:196
  60.1 4.6 %shard_map.67 = (s32[7,16,256]{2,1,0:T(8,128)S(1)}, s32[8,7,16,256]{3,2,1,0:T(8,128)S(1)}, s32[7,7,16,256]{3,2,1,0:T(8,128)S(1)}, f32[2,512]{1,0:T(2,128)S(1)}) custom-call(s32[4,4]{1,0:T(4,128)S(1)} %copy-done.6, bf16[768,512]{1,0:T(8,128)(2,1)} %collective-permute-done.10.halo_ref, bf16[768,1024]{1,0:T(8,128)(2,1)S(1)} %copy-done, ...), custom_call_target="tpu_custom_call" | custom-call | flops 3200000000 | bytes 4000000 | tf_op jit(solution)/shard_map/pallas_call | solution.py:149
  66.7 4.6 %shard_map.75 = (s32[7,16,256]{2,1,0:T(8,128)S(1)}, s32[8,7,16,256]{3,2,1,0:T(8,128)S(1)}, s32[7,7,16,256]{3,2,1,0:T(8,128)S(1)}, f32[2,512]{1,0:T(2,128)S(1)}) custom-call(s32[4,4]{1,0:T(4,128)S(1)} %copy-done.6, bf16[768,512]{1,0:T(8,128)(2,1)} %collective-permute-done.21.halo_ref, bf16[768,1024]{1,0:T(8,128)(2,1)S(1)} %copy-done, ...), custom_call_target="tpu_custom_call" | custom-call | flops 3200000000 | bytes 4000000 | tf_op jit(solution)/shard_map/pallas_call | solution.py:149
  75.6 6.0 %collective-permute-done.11.came_ref = s32[7,16,256]{2,1,0:T(8,128)S(1)} collective-permute-done((s32[7,16,256]{2,1,0:T(8,128)S(1)}, s32[7,16,256]{2,1,0:T(8,128)S(1)}, u32[]{:S(2)}, u32[]{:S(2)}) %collective-permute-start.11) | collective-permute-done | bytes 114720 | tf_op jit(solution)/shard_map/ppermute | solution.py:196
  85.4 3.3 %collective-permute-start.22 = (s32[7,16,256]{2,1,0:T(8,128)S(1)}, s32[7,16,256]{2,1,0:T(8,128)S(1)}, u32[]{:S(2)}, u32[]{:S(2)}) collective-permute-start(s32[7,16,256]{2,1,0:T(8,128)S(1)} %get-tuple-element.20), channel_id=1, source_target_pairs={{0,32},{4,484},{8,40},{12,492},{16,48},{20,500},{24,56},{28,508},{... | collective-permute-start | bytes 344072 | tf_op jit(solution)/shard_map/ppermute | solution.py:196
  88.7 4.6 %collective-permute-done.22.came_ref = s32[7,16,256]{2,1,0:T(8,128)S(1)} collective-permute-done((s32[7,16,256]{2,1,0:T(8,128)S(1)}, s32[7,16,256]{2,1,0:T(8,128)S(1)}, u32[]{:S(2)}, u32[]{:S(2)}) %collective-permute-start.22) | collective-permute-done | bytes 114720 | tf_op jit(solution)/shard_map/ppermute | solution.py:196
  95.5 3.1 %collective-permute-start.14 = (s32[2,7,16,256]{3,2,1,0:T(8,128)S(1)}, s32[2,7,16,256]{3,2,1,0:T(8,128)S(1)}, u32[]{:S(2)}, u32[]{:S(2)}) collective-permute-start(s32[2,7,16,256]{3,2,1,0:T(8,128)S(1)} %shard_map.69), channel_id=1, source_target_pairs={{0,32},{4,484},{8,40},{12,492},{16,48},{20,500},{24,56},{28,508},{... | collective-permute-start | bytes 688136 | tf_op jit(solution)/shard_map/ppermute | solution.py:196
  98.6 4.7 %collective-permute-start.8 = (s32[2,4,16,256]{3,2,1,0:T(8,128)S(1)}, s32[2,4,16,256]{3,2,1,0:T(8,128)S(1)}, u32[]{:S(2)}, u32[]{:S(2)}) collective-permute-start(s32[2,4,16,256]{3,2,1,0:T(8,128)S(1)} %shard_map.66), channel_id=1, source_target_pairs={{0,32},{4,484},{8,40},{12,492},{16,48},{20,500},{24,56},{28,508},{... | collective-permute-start | bytes 393224 | tf_op jit(solution)/shard_map/ppermute | solution.py:196
  103.4 5.5 %collective-permute-start.25 = (s32[2,7,16,256]{3,2,1,0:T(8,128)S(1)}, s32[2,7,16,256]{3,2,1,0:T(8,128)S(1)}, u32[]{:S(2)}, u32[]{:S(2)}) collective-permute-start(s32[2,7,16,256]{3,2,1,0:T(8,128)S(1)} %shard_map.77), channel_id=1, source_target_pairs={{0,32},{4,484},{8,40},{12,492},{16,48},{20,500},{24,56},{28,508},{... | collective-permute-start | bytes 688136 | tf_op jit(solution)/shard_map/ppermute | solution.py:196
  109.0 3.1 %collective-permute-start.15 = (s32[2,7,16,256]{3,2,1,0:T(8,128)S(1)}, s32[2,7,16,256]{3,2,1,0:T(8,128)S(1)}, u32[]{:S(2)}, u32[]{:S(2)}) collective-permute-start(s32[2,7,16,256]{3,2,1,0:T(8,128)S(1)} %shard_map.70), channel_id=1, source_target_pairs={{0,32},{4,484},{8,40},{12,492},{16,48},{20,500},{24,56},{28,508},{... | collective-permute-start | bytes 688136 | tf_op jit(solution)/shard_map/ppermute | solution.py:196
  114.1 3.7 %collective-permute-start.26 = (s32[2,7,16,256]{3,2,1,0:T(8,128)S(1)}, s32[2,7,16,256]{3,2,1,0:T(8,128)S(1)}, u32[]{:S(2)}, u32[]{:S(2)}) collective-permute-start(s32[2,7,16,256]{3,2,1,0:T(8,128)S(1)} %shard_map.78), channel_id=1, source_target_pairs={{0,32},{4,484},{8,40},{12,492},{16,48},{20,500},{24,56},{28,508},{... | collective-permute-start | bytes 688136 | tf_op jit(solution)/shard_map/ppermute | solution.py:196
  118.2 2.8 %collective-permute-start.16 = (s32[2,7,16,256]{3,2,1,0:T(8,128)S(1)}, s32[2,7,16,256]{3,2,1,0:T(8,128)S(1)}, u32[]{:S(2)}, u32[]{:S(2)}) collective-permute-start(s32[2,7,16,256]{3,2,1,0:T(8,128)S(1)} %shard_map.71), channel_id=1, source_target_pairs={{0,32},{4,484},{8,40},{12,492},{16,48},{20,500},{24,56},{28,508},{... | collective-permute-start | bytes 688136 | tf_op jit(solution)/shard_map/ppermute | solution.py:196
  123.3 2.4 %collective-permute-start.27 = (s32[2,7,16,256]{3,2,1,0:T(8,128)S(1)}, s32[2,7,16,256]{3,2,1,0:T(8,128)S(1)}, u32[]{:S(2)}, u32[]{:S(2)}) collective-permute-start(s32[2,7,16,256]{3,2,1,0:T(8,128)S(1)} %shard_map.79), channel_id=1, source_target_pairs={{0,32},{4,484},{8,40},{12,492},{16,48},{20,500},{24,56},{28,508},{... | collective-permute-start | bytes 688136 | tf_op jit(solution)/shard_map/ppermute | solution.py:196
  129.3 3.2 %collective-permute-done.27.came_ref = s32[2,7,16,256]{3,2,1,0:T(8,128)S(1)} collective-permute-done((s32[2,7,16,256]{3,2,1,0:T(8,128)S(1)}, s32[2,7,16,256]{3,2,1,0:T(8,128)S(1)}, u32[]{:S(2)}, u32[]{:S(2)}) %collective-permute-start.27) | collective-permute-done | bytes 229408 | tf_op jit(solution)/shard_map/ppermute | solution.py:196
  138.4 3.2 %collective-permute-done.28.came_ref = s32[2,7,16,256]{3,2,1,0:T(8,128)S(1)} collective-permute-done((s32[2,7,16,256]{3,2,1,0:T(8,128)S(1)}, s32[2,7,16,256]{3,2,1,0:T(8,128)S(1)}, u32[]{:S(2)}, u32[]{:S(2)}) %collective-permute-start.28) | collective-permute-done | bytes 229408 | tf_op jit(solution)/shard_map/ppermute | solution.py:196
  147.6 3.2 %collective-permute-done.29.came_ref = s32[2,7,16,256]{3,2,1,0:T(8,128)S(1)} collective-permute-done((s32[2,7,16,256]{3,2,1,0:T(8,128)S(1)}, s32[2,7,16,256]{3,2,1,0:T(8,128)S(1)}, u32[]{:S(2)}, u32[]{:S(2)}) %collective-permute-start.29) | collective-permute-done | bytes 229408 | tf_op jit(solution)/shard_map/ppermute | solution.py:196
  156.7 3.2 %collective-permute-done.30.refs_7_ = s32[2,7,16,256]{3,2,1,0:T(8,128)S(1)} collective-permute-done((s32[2,7,16,256]{3,2,1,0:T(8,128)S(1)}, s32[2,7,16,256]{3,2,1,0:T(8,128)S(1)}, u32[]{:S(2)}, u32[]{:S(2)}) %collective-permute-start.30) | collective-permute-done | bytes 229408 | tf_op jit(solution)/shard_map/ppermute | solution.py:196
  (88 shorter events, 61.0 us)
Async XLA Ops:
  4.0 19.0 %collective-permute-start.1 = (s32[7,4,16,256]{3,2,1,0:T(8,128)S(1)}, s32[7,4,16,256]{3,2,1,0:T(8,128)S(1)}, u32[]{:S(2)}, u32[]{:S(2)}) collective-permute-start(s32[7,4,16,256]{3,2,1,0:T(8,128)S(1)} %get-tuple-element.15), channel_id=1, source_target_pairs={{0,4},{4,0},{8,12},{12,8},{16,20},{20,16},{24,28},{28,24},{1,5},{5... | collective-permute-start | bytes 1376264 | tf_op jit(solution)/shard_map/ppermute | solution.py:187
  5.9 52.3 %collective-permute-start.10 = (bf16[768,512]{1,0:T(8,128)(2,1)S(1)}, bf16[768,512]{1,0:T(8,128)(2,1)}, u32[]{:S(2)}, u32[]{:S(2)}) collective-permute-start(bf16[768,512]{1,0:T(8,128)(2,1)S(1)} %get-tuple-element.25._), channel_id=1, source_target_pairs={{0,1},{1,2},{2,3},{3,4},{4,5},{5,6},{6,7},{7,8},{8,9},{9,10},{10,1... | collective-permute-start | bytes 2359304 | tf_op jit(solution)/shard_map/ppermute | solution.py:285
  9.3 13.6 %collective-permute-start = (s32[4,16,256]{2,1,0:T(8,128)S(1)}, s32[4,16,256]{2,1,0:T(8,128)S(1)}, u32[]{:S(2)}, u32[]{:S(2)}) collective-permute-start(s32[4,16,256]{2,1,0:T(8,128)S(1)} %get-tuple-element.14), channel_id=1, source_target_pairs={{0,32},{4,484},{8,40},{12,492},{16,48},{20,500},{24,56},{28,508},{... | collective-permute-start | bytes 196616 | tf_op jit(solution)/shard_map/ppermute | solution.py:196
  33.0 33.6 %collective-permute-start.21 = (bf16[768,512]{1,0:T(8,128)(2,1)}, bf16[768,512]{1,0:T(8,128)(2,1)}, u32[]{:S(2)}, u32[]{:S(2)}) collective-permute-start(bf16[768,512]{1,0:T(8,128)(2,1)} %get-tuple-element.24), channel_id=1, source_target_pairs={{1,0},{2,1},{3,2},{4,3},{5,4},{6,5},{7,6},{8,7},{9,8},{10,9},{11,1... | collective-permute-start | bytes 2359304 | tf_op jit(solution)/shard_map/ppermute | solution.py:286
  47.9 8.3 %collective-permute-start.5 = (s32[2,4,16,256]{3,2,1,0:T(8,128)}, s32[2,4,16,256]{3,2,1,0:T(8,128)S(1)}, u32[]{:S(2)}, u32[]{:S(2)}) collective-permute-start(s32[2,4,16,256]{3,2,1,0:T(8,128)} %shard_map.63), channel_id=1, source_target_pairs={{0,32},{4,484},{8,40},{12,492},{16,48},{20,500},{24,56},{28,508},{... | collective-permute-start | bytes 393224 | tf_op jit(solution)/shard_map/ppermute | solution.py:196
  56.2 10.4 %collective-permute-start.6 = (s32[2,4,16,256]{3,2,1,0:T(8,128)S(1)}, s32[2,4,16,256]{3,2,1,0:T(8,128)S(1)}, u32[]{:S(2)}, u32[]{:S(2)}) collective-permute-start(s32[2,4,16,256]{3,2,1,0:T(8,128)S(1)} %shard_map.64), channel_id=1, source_target_pairs={{0,32},{4,484},{8,40},{12,492},{16,48},{20,500},{24,56},{28,508},{... | collective-permute-start | bytes 393224 | tf_op jit(solution)/shard_map/ppermute | solution.py:196
  64.7 16.8 %collective-permute-start.12 = (s32[7,7,16,256]{3,2,1,0:T(8,128)S(1)}, s32[7,7,16,256]{3,2,1,0:T(8,128)S(1)}, u32[]{:S(2)}, u32[]{:S(2)}) collective-permute-start(s32[7,7,16,256]{3,2,1,0:T(8,128)S(1)} %get-tuple-element.18), channel_id=1, source_target_pairs={{0,4},{4,0},{8,12},{12,8},{16,20},{20,16},{24,28},{28,24},{1,5},{5... | collective-permute-start | bytes 2408456 | tf_op jit(solution)/shard_map/ppermute | solution.py:187
  71.2 22.1 %collective-permute-start.23 = (s32[7,7,16,256]{3,2,1,0:T(8,128)S(1)}, s32[7,7,16,256]{3,2,1,0:T(8,128)S(1)}, u32[]{:S(2)}, u32[]{:S(2)}) collective-permute-start(s32[7,7,16,256]{3,2,1,0:T(8,128)S(1)} %get-tuple-element.21), channel_id=1, source_target_pairs={{0,4},{4,0},{8,12},{12,8},{16,20},{20,16},{24,28},{28,24},{1,5},{5... | collective-permute-start | bytes 2408456 | tf_op jit(solution)/shard_map/ppermute | solution.py:187
  81.5 13.9 %collective-permute-start.13 = (s32[2,7,16,256]{3,2,1,0:T(8,128)S(1)}, s32[2,7,16,256]{3,2,1,0:T(8,128)S(1)}, u32[]{:S(2)}, u32[]{:S(2)}) collective-permute-start(s32[2,7,16,256]{3,2,1,0:T(8,128)S(1)} %shard_map.68), channel_id=1, source_target_pairs={{0,32},{4,484},{8,40},{12,492},{16,48},{20,500},{24,56},{28,508},{... | collective-permute-start | bytes 688136 | tf_op jit(solution)/shard_map/ppermute | solution.py:196
  83.5 11.9 %collective-permute-start.7 = (s32[2,4,16,256]{3,2,1,0:T(8,128)S(1)}, s32[2,4,16,256]{3,2,1,0:T(8,128)S(1)}, u32[]{:S(2)}, u32[]{:S(2)}) collective-permute-start(s32[2,4,16,256]{3,2,1,0:T(8,128)S(1)} %shard_map.65), channel_id=1, source_target_pairs={{0,32},{4,484},{8,40},{12,492},{16,48},{20,500},{24,56},{28,508},{... | collective-permute-start | bytes 393224 | tf_op jit(solution)/shard_map/ppermute | solution.py:196
  93.4 10.0 %collective-permute-start.24 = (s32[2,7,16,256]{3,2,1,0:T(8,128)S(1)}, s32[2,7,16,256]{3,2,1,0:T(8,128)S(1)}, u32[]{:S(2)}, u32[]{:S(2)}) collective-permute-start(s32[2,7,16,256]{3,2,1,0:T(8,128)S(1)} %shard_map.76), channel_id=1, source_target_pairs={{0,32},{4,484},{8,40},{12,492},{16,48},{20,500},{24,56},{28,508},{... | collective-permute-start | bytes 688136 | tf_op jit(solution)/shard_map/ppermute | solution.py:196
  95.5 13.5 %collective-permute-start.14 = (s32[2,7,16,256]{3,2,1,0:T(8,128)S(1)}, s32[2,7,16,256]{3,2,1,0:T(8,128)S(1)}, u32[]{:S(2)}, u32[]{:S(2)}) collective-permute-start(s32[2,7,16,256]{3,2,1,0:T(8,128)S(1)} %shard_map.69), channel_id=1, source_target_pairs={{0,32},{4,484},{8,40},{12,492},{16,48},{20,500},{24,56},{28,508},{... | collective-permute-start | bytes 688136 | tf_op jit(solution)/shard_map/ppermute | solution.py:196
  98.6 10.3 %collective-permute-start.8 = (s32[2,4,16,256]{3,2,1,0:T(8,128)S(1)}, s32[2,4,16,256]{3,2,1,0:T(8,128)S(1)}, u32[]{:S(2)}, u32[]{:S(2)}) collective-permute-start(s32[2,4,16,256]{3,2,1,0:T(8,128)S(1)} %shard_map.66), channel_id=1, source_target_pairs={{0,32},{4,484},{8,40},{12,492},{16,48},{20,500},{24,56},{28,508},{... | collective-permute-start | bytes 393224 | tf_op jit(solution)/shard_map/ppermute | solution.py:196
  103.4 10.7 %collective-permute-start.25 = (s32[2,7,16,256]{3,2,1,0:T(8,128)S(1)}, s32[2,7,16,256]{3,2,1,0:T(8,128)S(1)}, u32[]{:S(2)}, u32[]{:S(2)}) collective-permute-start(s32[2,7,16,256]{3,2,1,0:T(8,128)S(1)} %shard_map.77), channel_id=1, source_target_pairs={{0,32},{4,484},{8,40},{12,492},{16,48},{20,500},{24,56},{28,508},{... | collective-permute-start | bytes 688136 | tf_op jit(solution)/shard_map/ppermute | solution.py:196
  109.0 9.1 %collective-permute-start.15 = (s32[2,7,16,256]{3,2,1,0:T(8,128)S(1)}, s32[2,7,16,256]{3,2,1,0:T(8,128)S(1)}, u32[]{:S(2)}, u32[]{:S(2)}) collective-permute-start(s32[2,7,16,256]{3,2,1,0:T(8,128)S(1)} %shard_map.70), channel_id=1, source_target_pairs={{0,32},{4,484},{8,40},{12,492},{16,48},{20,500},{24,56},{28,508},{... | collective-permute-start | bytes 688136 | tf_op jit(solution)/shard_map/ppermute | solution.py:196
  114.1 9.1 %collective-permute-start.26 = (s32[2,7,16,256]{3,2,1,0:T(8,128)S(1)}, s32[2,7,16,256]{3,2,1,0:T(8,128)S(1)}, u32[]{:S(2)}, u32[]{:S(2)}) collective-permute-start(s32[2,7,16,256]{3,2,1,0:T(8,128)S(1)} %shard_map.78), channel_id=1, source_target_pairs={{0,32},{4,484},{8,40},{12,492},{16,48},{20,500},{24,56},{28,508},{... | collective-permute-start | bytes 688136 | tf_op jit(solution)/shard_map/ppermute | solution.py:196
  118.2 9.1 %collective-permute-start.16 = (s32[2,7,16,256]{3,2,1,0:T(8,128)S(1)}, s32[2,7,16,256]{3,2,1,0:T(8,128)S(1)}, u32[]{:S(2)}, u32[]{:S(2)}) collective-permute-start(s32[2,7,16,256]{3,2,1,0:T(8,128)S(1)} %shard_map.71), channel_id=1, source_target_pairs={{0,32},{4,484},{8,40},{12,492},{16,48},{20,500},{24,56},{28,508},{... | collective-permute-start | bytes 688136 | tf_op jit(solution)/shard_map/ppermute | solution.py:196
  123.3 9.1 %collective-permute-start.27 = (s32[2,7,16,256]{3,2,1,0:T(8,128)S(1)}, s32[2,7,16,256]{3,2,1,0:T(8,128)S(1)}, u32[]{:S(2)}, u32[]{:S(2)}) collective-permute-start(s32[2,7,16,256]{3,2,1,0:T(8,128)S(1)} %shard_map.79), channel_id=1, source_target_pairs={{0,32},{4,484},{8,40},{12,492},{16,48},{20,500},{24,56},{28,508},{... | collective-permute-start | bytes 688136 | tf_op jit(solution)/shard_map/ppermute | solution.py:196
  127.3 9.1 %collective-permute-start.17 = (s32[2,7,16,256]{3,2,1,0:T(8,128)S(1)}, s32[2,7,16,256]{3,2,1,0:T(8,128)S(1)}, u32[]{:S(2)}, u32[]{:S(2)}) collective-permute-start(s32[2,7,16,256]{3,2,1,0:T(8,128)S(1)} %shard_map.72), channel_id=1, source_target_pairs={{0,32},{4,484},{8,40},{12,492},{16,48},{20,500},{24,56},{28,508},{... | collective-permute-start | bytes 688136 | tf_op jit(solution)/shard_map/ppermute | solution.py:196
  132.4 9.1 %collective-permute-start.28 = (s32[2,7,16,256]{3,2,1,0:T(8,128)S(1)}, s32[2,7,16,256]{3,2,1,0:T(8,128)S(1)}, u32[]{:S(2)}, u32[]{:S(2)}) collective-permute-start(s32[2,7,16,256]{3,2,1,0:T(8,128)S(1)} %shard_map.80), channel_id=1, source_target_pairs={{0,32},{4,484},{8,40},{12,492},{16,48},{20,500},{24,56},{28,508},{... | collective-permute-start | bytes 688136 | tf_op jit(solution)/shard_map/ppermute | solution.py:196
  136.5 9.1 %collective-permute-start.18 = (s32[2,7,16,256]{3,2,1,0:T(8,128)S(1)}, s32[2,7,16,256]{3,2,1,0:T(8,128)S(1)}, u32[]{:S(2)}, u32[]{:S(2)}) collective-permute-start(s32[2,7,16,256]{3,2,1,0:T(8,128)S(1)} %shard_map.73), channel_id=1, source_target_pairs={{0,32},{4,484},{8,40},{12,492},{16,48},{20,500},{24,56},{28,508},{... | collective-permute-start | bytes 688136 | tf_op jit(solution)/shard_map/ppermute | solution.py:196
  141.6 9.1 %collective-permute-start.29 = (s32[2,7,16,256]{3,2,1,0:T(8,128)S(1)}, s32[2,7,16,256]{3,2,1,0:T(8,128)S(1)}, u32[]{:S(2)}, u32[]{:S(2)}) collective-permute-start(s32[2,7,16,256]{3,2,1,0:T(8,128)S(1)} %shard_map.81), channel_id=1, source_target_pairs={{0,32},{4,484},{8,40},{12,492},{16,48},{20,500},{24,56},{28,508},{... | collective-permute-start | bytes 688136 | tf_op jit(solution)/shard_map/ppermute | solution.py:196
  145.6 9.1 %collective-permute-start.19 = (s32[2,7,16,256]{3,2,1,0:T(8,128)S(1)}, s32[2,7,16,256]{3,2,1,0:T(8,128)S(1)}, u32[]{:S(2)}, u32[]{:S(2)}) collective-permute-start(s32[2,7,16,256]{3,2,1,0:T(8,128)S(1)} %shard_map.74), channel_id=1, source_target_pairs={{0,32},{4,484},{8,40},{12,492},{16,48},{20,500},{24,56},{28,508},{... | collective-permute-start | bytes 688136 | tf_op jit(solution)/shard_map/ppermute | solution.py:196
  150.8 9.1 %collective-permute-start.30 = (s32[2,7,16,256]{3,2,1,0:T(8,128)S(1)}, s32[2,7,16,256]{3,2,1,0:T(8,128)S(1)}, u32[]{:S(2)}, u32[]{:S(2)}) collective-permute-start(s32[2,7,16,256]{3,2,1,0:T(8,128)S(1)} %shard_map.82), channel_id=1, source_target_pairs={{0,32},{4,484},{8,40},{12,492},{16,48},{20,500},{24,56},{28,508},{... | collective-permute-start | bytes 688136 | tf_op jit(solution)/shard_map/ppermute | solution.py:196
  (16 other events, 139.0 us)

commit v4 on v1

v4 whole, which is shorter than its diff:
```python
import functools

import jax
import jax.numpy as jnp
from jax import lax
from jax.experimental import pallas as pl
from jax.experimental.pallas import tpu as pltpu
from jax.sharding import PartitionSpec as P

HALO = 2
NOISE_SPREAD = 0.05
SCALE = 131072.0
PAIR_SCALE = 1638.0
LOW = (1 << 24) - 1
ANY = pl.BlockSpec(memory_space=pl.ANY)
VMEM = pl.BlockSpec(memory_space=pltpu.VMEM)
SMEM = pl.BlockSpec(memory_space=pltpu.SMEM)
PARAMS = pltpu.CompilerParams(vmem_limit_bytes=48 * 1024 * 1024)


def fixed(values, scale):
    return jnp.floor(values * scale + 0.5).astype(jnp.int32)


def packed(parts):
    a, b, c, d = parts
    return (
        a | ((d & 255) << 24),
        b | (((d >> 8) & 255) << 24),
        c | ((d >> 16) << 24),
    )


def unpacked(words):
    tops = [lax.shift_right_logical(word, 24) for word in words]
    return [word & LOW for word in words] + [tops[0] | (tops[1] << 8) | (tops[2] << 16)]


def group_index():
    return lax.axis_index("row") * lax.axis_size("col") + lax.axis_index("col")


def cut_kernel(soft_ref, head_ref, tail_ref, sems):
    width = soft_ref.shape[1]
    reach = head_ref.shape[1]
    copies = [
        pltpu.make_async_copy(soft_ref.at[:, pl.ds(width - reach, reach)], tail_ref, sems.at[0]),
        pltpu.make_async_copy(soft_ref.at[:, pl.ds(0, reach)], head_ref, sems.at[1]),
    ]
    for copy in copies:
        copy.start()
    for copy in copies:
        copy.wait()


def cut_call(soft, reach):
    shape = jax.ShapeDtypeStruct((soft.shape[0], reach), soft.dtype)
    return pl.pallas_call(
        cut_kernel,
        out_shape=[shape, shape],
        in_specs=[ANY],
        out_specs=[VMEM, VMEM],
        scratch_shapes=[pltpu.SemaphoreType.DMA((2,))],
        compiler_params=PARAMS,
        cost_estimate=pl.CostEstimate(flops=0, bytes_accessed=3_000_000, transcendentals=0),
    )(soft)


def ready_kernel(
    width, slots, own_ref, inc_ref, keyt_ref, probt_ref, _,
    fit_ref, vals_ref, hot_ref, self_ref, small_ref,
):
    blocks = own_ref.shape[1] // width
    edges = inc_ref.shape[2]
    pieces = edges // width
    for b in range(blocks):
        own = own_ref[:, b * width : (b + 1) * width]
        tile = lax.dot_general(own, own, (((0,), (0,)), ((), ())), preferred_element_type=jnp.float32)
        self_ref[b] = fixed(tile, PAIR_SCALE)
        rows_x = inc_ref[0, b : b + 1, :]
        slot_x = inc_ref[1, b : b + 1, :]
        cols_x = inc_ref[2, b : b + 1, :]
        lines = lax.broadcasted_iota(jnp.int32, (width, edges), 0)
        row_hot = (lines == rows_x).astype(jnp.bfloat16)
        for k in range(slots):
            hot_ref[b, k * width : (k + 1) * width, :] = (
                lines == jnp.where(slot_x == k, cols_x, -1)
            ).astype(jnp.bfloat16)
        vals = jnp.dot(own, row_hot, preferred_element_type=jnp.float32)
        vals_ref[b] = vals.astype(jnp.bfloat16)
        total = jnp.sum(vals, axis=0, keepdims=True)
        for p in range(pieces):
            n = b * pieces + p
            small_ref[n : n + 1, :] = total[:, p * width : (p + 1) * width]
        key = slot_x * (width * width) + rows_x * width + cols_x
        same = keyt_ref[:, b : b + 1] == key
        fit_ref[b : b + 1, :] = jnp.sum(jnp.where(same, probt_ref[:, b : b + 1], 0.0), axis=0, keepdims=True)


def ready_call(soft, incidence, keys_t, prob_t, after, width, slots):
    shots, own_width = soft.shape
    blocks = own_width // width
    edges = incidence.shape[2]
    return pl.pallas_call(
        functools.partial(ready_kernel, width, slots),
        out_shape=[
            jax.ShapeDtypeStruct((blocks, edges), jnp.float32),
            jax.ShapeDtypeStruct((blocks, shots, edges), jnp.bfloat16),
            jax.ShapeDtypeStruct((blocks, slots * width, edges), jnp.bfloat16),
            jax.ShapeDtypeStruct((blocks, width, width), jnp.int32),
            jax.ShapeDtypeStruct((blocks * edges // width, width), jnp.float32),
        ],
        in_specs=[VMEM] * 4 + [ANY],
        out_specs=[VMEM] * 5,
        compiler_params=PARAMS,
        cost_estimate=pl.CostEstimate(flops=20_000_000_000, bytes_accessed=12_000_000, transcendentals=0),
    )(soft, incidence, keys_t, prob_t, after)


def pair_kernel(
    upper, width, groups, partners_ref, halo_ref, own_ref, vals_ref, hot_ref, self_ref, early_ref, _,
    first_ref, parts_ref, win,
):
    blocks, slots = partners_ref.shape
    mine = blocks // 2
    low = mine * upper
    reach = HALO * width
    own_width = own_ref.shape[1]
    share = width // groups
    pieces = hot_ref.shape[2] // width
    me = lax.axis_index("shot")
    base = group_index() * blocks
    if upper:
        win[:, 0:own_width] = own_ref[...]
        win[:, own_width:] = halo_ref[...]
        window_first = base + low - HALO
    else:
        win[:, 0:reach] = halo_ref[...]
        win[:, reach:] = own_ref[...]
        window_first = base - HALO
    products, others = [], []
    for b in range(mine):
        block = low + b
        own = win[:, reach + b * width : reach + (b + 1) * width]
        chosen = [own]
        for k in range(1, slots):
            partner = partners_ref[block, k]
            partner = jnp.where(partner >= 0, partner, base + block)
            start = pl.multiple_of((partner - window_first) * width, width)
            chosen.append(win[:, pl.ds(start, width)])
        chosen = jnp.concatenate(chosen, axis=1)
        tiles = lax.dot_general(
            own, chosen[:, width:], (((0,), (0,)), ((), ())), preferred_element_type=jnp.float32
        )
        tiles = fixed(tiles, PAIR_SCALE)
        for d in range(groups):
            rows = slice(d * share, (d + 1) * share)
            values = [self_ref[block, rows, :]]
            values += [tiles[rows, k * width : (k + 1) * width] for k in range(slots - 1)]
            at = lax.rem(d - me + groups, groups)
            for n, word in enumerate(packed(values)):
                parts_ref[at, b * (slots - 1) + n] = word
        other = jnp.dot(chosen, hot_ref[block], preferred_element_type=jnp.float32)
        product = jnp.sum(vals_ref[block].astype(jnp.float32) * other, axis=0, keepdims=True)
        other = jnp.sum(other, axis=0, keepdims=True)
        products += [product[:, p * width : (p + 1) * width] for p in range(pieces)]
        others += [other[:, p * width : (p + 1) * width] for p in range(pieces)]
    ones = jnp.ones((8, win.shape[0]), jnp.bfloat16)
    low_col = reach if upper else 0
    columns = jnp.dot(ones, win[:, low_col : low_col + 4 * width], preferred_element_type=jnp.float32)
    columns = [columns[0:1, p * width : (p + 1) * width] for p in range(4)]
    early = early_ref[upper * mine * pieces : (upper + 1) * mine * pieces, :]
    rest = fixed(jnp.concatenate(products + [early] + others + columns, axis=0), SCALE)
    last = mine * (slots - 1)
    for at in range(groups):
        parts_ref[at, last] = rest
    first_ref[...] = parts_ref[groups // 2]


def pair_call(upper, partners, halo, soft, vals, hot, selfs, early, after, width, groups):
    blocks, slots = partners.shape
    shape = ((blocks // 2) * (slots - 1) + 1, width // groups, width)
    return pl.pallas_call(
        functools.partial(pair_kernel, upper, width, groups),
        out_shape=[
            jax.ShapeDtypeStruct(shape, jnp.int32),
            jax.ShapeDtypeStruct((groups,) + shape, jnp.int32),
        ],
        in_specs=[SMEM] + [VMEM] * 6 + [ANY],
        out_specs=[VMEM] * 2,
        scratch_shapes=[pltpu.VMEM((soft.shape[0], soft.shape[1] + halo.shape[1]), jnp.bfloat16)],
        compiler_params=PARAMS,
        cost_estimate=pl.CostEstimate(flops=3_000_000_000, bytes_accessed=4_000_000, transcendentals=0),
    )(partners, halo, soft, vals, hot, selfs, early, after)


def plus(a, b):
    words = a.shape[0] - 1
    out = []
    for n in range(0, words, 3):
        one, two = unpacked([a[n + i] for i in range(3)]), unpacked([b[n + i] for i in range(3)])
        out += packed([x + y for x, y in zip(one, two)])
    return out + [a[words] + b[words]]


def hop_kernel(at, start, came_ref, lower_ref, upper_ref, _, out_ref):
    half = lower_ref.shape[1]
    if start == 0:
        sources = ((came_ref, 0), (None, 0))
    elif start == 1:
        sources = ((None, 0), (came_ref, 0))
    else:
        sources = ((came_ref, 0), (came_ref, half))
    for (came, low), mine, base in zip(sources, (lower_ref, upper_ref), (0, half)):
        if came is None:
            out_ref[base : base + half] = mine[at]
        else:
            for n, word in enumerate(plus(came[low : low + half], mine[at])):
                out_ref[base + n] = word


def hop_call(at, start, came, lower, upper, after):
    return pl.pallas_call(
        functools.partial(hop_kernel, at, start),
        out_shape=jax.ShapeDtypeStruct((2 * lower.shape[1],) + lower.shape[2:], jnp.int32),
        in_specs=[VMEM] * 3 + [ANY],
        out_specs=VMEM,
        compiler_params=PARAMS,
        cost_estimate=pl.CostEstimate(flops=100_000, bytes_accessed=600_000, transcendentals=0),
    )(came, lower, upper, after)


def final_kernel(
    count, partners_ref, inc_ref, lower_ref, upper_ref, rising_ref, falling_ref, fit_ref,
    pair_ref, grad_ref, means,
):
    blocks, slots = partners_ref.shape
    mine = blocks // 2
    half, share, width = lower_ref.shape[1:]
    pieces = inc_ref.shape[2] // width
    me = lax.axis_index("shot")
    base = group_index() * blocks
    last = half - 1
    grams, smalls = [], []
    for part, low in ((lower_ref, 0), (upper_ref, half)):
        sources = (part[0], rising_ref[low : low + half], falling_ref[low : low + half])
        for b in range(mine):
            parts = [unpacked([source[b * (slots - 1) + n] for n in range(3)]) for source in sources]
            grams.append([
                (x + y + z).astype(jnp.float32) * (1.0 / PAIR_SCALE) for x, y, z in zip(*parts)
            ])
        smalls.append((sources[0][last] + sources[1][last] + sources[2][last]).astype(jnp.float32) * (1.0 / SCALE))
    means[0:4, :] = smalls[0][12:16] / count
    means[4:8, :] = smalls[1][12:16] / count
    spot = lax.broadcasted_iota(jnp.int32, (share, width), 1) == (
        lax.broadcasted_iota(jnp.int32, (share, width), 0) + me * share
    )
    for block in range(blocks):
        small = smalls[block // mine]
        row_mean = jnp.sum(
            jnp.where(spot, means[block + HALO : block + HALO + 1, :], 0.0), axis=1, keepdims=True
        )
        for k in range(slots):
            partner = partners_ref[block, k]
            live = jnp.where(partner >= 0, 1.0, 0.0)
            at = jnp.where(partner >= 0, partner - base, block) + HALO
            quotient = row_mean * means[pl.ds(at, 1), :] * count / grams[block][k]
            pair_ref[block, k] = ((0.5 - 0.5 * jnp.sqrt(quotient)) * live).astype(jnp.bfloat16)
        for p in range(pieces):
            n = (block % mine) * pieces + p
            at = slice(p * width, (p + 1) * width)
            slot_x = inc_ref[1, block : block + 1, at]
            live = jnp.zeros((1, width), jnp.float32)
            for k in range(slots):
                live = live + jnp.where((slot_x == k) & (partners_ref[block, k] >= 0), 1.0, 0.0)
            quotient = (small[4 + n : 5 + n] / count) * (small[8 + n : 9 + n] / count) * count / small[n : n + 1]
            entry = (0.5 - 0.5 * jnp.sqrt(quotient)) * live
            residual = live * (entry - fit_ref[block : block + 1, at]) / NOISE_SPREAD
            grad_ref[block : block + 1, at] = -residual / NOISE_SPREAD


def final_call(partners, incidence, lower, upper, rising, falling, fit, count):
    blocks, slots = partners.shape
    share, width = lower.shape[2:]
    return pl.pallas_call(
        functools.partial(final_kernel, count),
        out_shape=[
            jax.ShapeDtypeStruct((blocks, slots, share, width), jnp.bfloat16),
            jax.ShapeDtypeStruct((blocks, incidence.shape[2]), jnp.float32),
        ],
        in_specs=[SMEM] + [VMEM] * 6,
        out_specs=[VMEM] * 2,
        scratch_shapes=[pltpu.VMEM((blocks + 2 * HALO, width), jnp.float32)],
        compiler_params=PARAMS,
        cost_estimate=pl.CostEstimate(flops=1_000_000, bytes_accessed=2_000_000, transcendentals=100_000),
    )(partners, incidence, lower, upper, rising, falling, fit)


def local(soft, partners, incidence, edge_prob):
    shots, own_width = soft.shape
    blocks, slots = partners.shape
    width = own_width // blocks
    groups = lax.axis_size("shot")
    count = float(shots * groups)
    sides = lax.axis_size(("row", "col"))

    head, tail = cut_call(soft, HALO * width)
    left = lax.ppermute(tail, ("row", "col"), [(i, (i + 1) % sides) for i in range(sides)])
    right = lax.ppermute(head, ("row", "col"), [((i + 1) % sides, i) for i in range(sides)])

    keys = incidence[1] * (width * width) + incidence[0] * width + incidence[2]
    fit, vals, hot, selfs, early = ready_call(soft, incidence, keys.T, edge_prob.T, tail, width, slots)
    args = (soft, vals, hot, selfs, early)
    first_up, lower = pair_call(0, partners, left, *args, early, width, groups)
    first_down, upper = pair_call(1, partners, right, *args, first_up, width, groups)

    half = groups // 2
    rise = [(i, (i + 1) % groups) for i in range(groups)]
    fall = [((i + 1) % groups, i) for i in range(groups)]
    rising = lax.ppermute(first_up, "shot", rise)
    falling = lax.ppermute(first_down, "shot", fall)
    order = first_down
    for step in range(1, half):
        start = 0 if step == 1 else 2
        order = hop_call(half - step, start, rising, lower, upper, order)
        rising = lax.ppermute(order, "shot", rise)
        start = 1 if step == 1 else 2
        order = hop_call(half + step, start, falling, lower, upper, order)
        falling = lax.ppermute(order, "shot", fall)
    return final_call(partners, incidence, lower, upper, rising, falling, fit, count)


def solution(mesh):
    placed = (
        P("shot", ("row", "col")),
        P(("row", "col"), None),
        P(None, ("row", "col"), None),
        P(("row", "col"), None),
    )
    return jax.shard_map(
        local,
        mesh=mesh,
        in_specs=placed,
        out_specs=(P(("row", "col"), None, "shot", None), P(("row", "col"), None)),
        check_vma=False,
    )
```

time: 140 us -> 137 us (0.979)
  starting transfers between devices: 7.7 us -> 72.1 us
  blocking collectives: 62.1 us -> 0 us
  between operations: 14.2 us -> 0.93 us
  Pallas kernels: 9.13 us -> 21.3 us
  local copies, waits for them, and re-layouts: 6.04 us -> 1.71 us
  waiting for transfers between devices: 37.4 us -> 39.7 us
  other arithmetic: 2.81 us -> 0.74 us
    ppermute x2 -> x18, starting transfers between devices: 7.66 us -> 72.1 us  [the longest x7 39.1 us: local(): falling = lax.ppermute(order, 'shot', fall)]
    psum x1 -> x0, blocking collectives: 62.1 us -> none  [local(): small = lax.psum(small, 'shot')]
    ppermute x2 -> x18, waiting for transfers between devices: 16.4 us -> 39.7 us  [the longest x1 15.9 us: local(): lax.ppermute(tail, ('row', 'col'), [(i, (i + 1) % sides) for i in range(s...]
    reduce_scatter x1 -> x0, waiting for transfers between devices: 20.9 us -> none  [local(): total = lax.psum_scatter(gram, 'shot', scatter_dimension=0, tiled=False)]
    pallas_call x1 -> x19, Pallas kernels: 9.13 us -> 21.3 us  [the longest x2 12.2 us: pair_call(): pl.pallas_call(functools.partial(pair_kernel, upper, width, groups), out_...]
    slice x4 -> x0, local copies, waits for them, and re-layouts: 2.97 us -> none  [the longest x1 2.73 us: local(): soft[:, :reach]]
    convert_element_type x1 -> x0, other arithmetic: 1.79 us -> none  [local(): ((0.5 - 0.5 * jnp.sqrt(quotient)) * mask[:, :, None, None]).astype(jnp.bf...]
  transfers between devices with their start and end apart: 3 -> 18, of which waited for: 3 -> 15; matrix products, arithmetic and copies ran while one was open for 2% -> 1% of each run, Pallas kernels for 0% -> 13%
where the time goes in v4:
time: 137 us
  starting transfers between devices  72.1 us (53%)
  waiting for transfers between devices  39.7 us (29%)
  Pallas kernels  21.3 us (16%)
  local copies, waits for them, and re-layouts  1.71 us (1%)
    ppermute x7, starting transfers between devices, local(): falling = lax.ppermute(order, 'shot', fall)  39.1 us
    ppermute x1, waiting for transfers between devices, local(): lax.ppermute(tail, ('row', 'col'), [(i, (i + 1) % sides) for i in range(s...  15.9 us
    ppermute x7, starting transfers between devices, local(): rising = lax.ppermute(order, 'shot', rise)  13.4 us
    ppermute x7, waiting for transfers between devices, local(): rising = lax.ppermute(order, 'shot', rise)  12.7 us
    pallas_call x2, Pallas kernels, pair_call(): pl.pallas_call(functools.partial(pair_kernel, upper, width, groups), out_...  12.2 us
    ppermute x7, waiting for transfers between devices, local(): falling = lax.ppermute(order, 'shot', fall)  10.7 us
    ppermute x1, starting transfers between devices, local(): falling = lax.ppermute(first_down, 'shot', fall)  9.5 us
    pallas_call x1, Pallas kernels, ready_call(): pl.pallas_call(functools.partial(ready_kernel, width, slots), out_shape=[...  5.18 us
  transfers between devices with their start and end apart: 18, of which 15 were waited for; matrix products, arithmetic and copies ran while one was open for 1% of the time, Pallas kernels for 13%

profile of v4, /device:TPU:24, one launch (start us, length us, event | category | flops | bytes accessed | tf_op | source)
XLA Modules:
  0.0 136.5 jit_solution(15575601448486074134)
XLA Ops:
  3.5 4.3 %collective-permute-start.1 = (bf16[768,512]{1,0:T(8,128)(2,1)}, bf16[768,512]{1,0:T(8,128)(2,1)S(1)}, u32[]{:S(2)}, u32[]{:S(2)}) collective-permute-start(bf16[768,512]{1,0:T(8,128)(2,1)} %get-tuple-element.19), channel_id=1, source_target_pairs={{1,0},{2,1},{3,2},{4,3},{5,4},{6,5},{7,6},{8,7},{9,8},{10,9},{11,1... | collective-permute-start | bytes 2359304 | tf_op jit(solution)/shard_map/ppermute | solution.py:309
  7.8 1.9 %collective-permute-start = (bf16[768,512]{1,0:T(8,128)(2,1)}, bf16[768,512]{1,0:T(8,128)(2,1)}, u32[]{:S(2)}, u32[]{:S(2)}) collective-permute-start(bf16[768,512]{1,0:T(8,128)(2,1)} %get-tuple-element.13._), channel_id=1, source_target_pairs={{0,1},{1,2},{2,3},{3,4},{4,5},{5,6},{6,7},{7,8},{8,9},{9,10},{10,1... | collective-permute-start | bytes 2359304 | tf_op jit(solution)/shard_map/ppermute | solution.py:308
  10.8 5.2 %shard_map.60 = (f32[4,512]{1,0:T(4,128)S(1)}, bf16[4,768,512]{2,1,0:T(8,128)(2,1)}, bf16[4,1024,512]{2,1,0:T(8,128)(2,1)}, s32[4,256,256]{2,1,0:T(8,128)S(1)}, f32[8,256]{1,0:T(8,128)S(1)}) custom-call(bf16[768,1024]{1,0:T(8,128)(2,1)S(1)} %copy-done.1, s32[3,4,512]{2,1,0:T(4,128)S(1)} %copy-done.2, s32[512,4]{1,0:T(8,128)S(1)} %bitcast.4, ...), custom_call_target="tpu_custom_call" | custom-call | flops 20000000000 | bytes 12000000 | tf_op jit(solution)/shard_map/pallas_call | solution.py:104
  16.0 15.9 %collective-permute-done.halo_ref = bf16[768,512]{1,0:T(8,128)(2,1)} collective-permute-done((bf16[768,512]{1,0:T(8,128)(2,1)}, bf16[768,512]{1,0:T(8,128)(2,1)}, u32[]{:S(2)}, u32[]{:S(2)}) %collective-permute-start) | collective-permute-done | bytes 786464 | tf_op jit(solution)/shard_map/ppermute | solution.py:308
  31.9 6.2 %shard_map.61 = (s32[7,16,256]{2,1,0:T(8,128)S(1)}, s32[16,7,16,256]{3,2,1,0:T(8,128)S(1)}) custom-call(s32[4,4]{1,0:T(4,128)S(1)} %copy-done.3, bf16[768,512]{1,0:T(8,128)(2,1)} %collective-permute-done.halo_ref, bf16[768,1024]{1,0:T(8,128)(2,1)S(1)} %copy-done.1, bf16[4,768,512]{2,1,0:T(8,128)(2,1)} %get-tuple-element.14.vals_ref, ...), custom_call_target="tpu_custom_call" | custom-call | flops 3000000000 | bytes 4000000 | tf_op jit(solution)/shard_map/pallas_call | solution.py:183
  38.1 3.8 %collective-permute-start.2 = (s32[7,16,256]{2,1,0:T(8,128)S(1)}, s32[7,16,256]{2,1,0:T(8,128)S(1)}, u32[]{:S(2)}, u32[]{:S(2)}) collective-permute-start(s32[7,16,256]{2,1,0:T(8,128)S(1)} %get-tuple-element.20._), channel_id=1, source_target_pairs={{0,32},{32,64},{64,96},{96,128},{128,160},{160,192},{192,224},{224... | collective-permute-start | bytes 344072 | tf_op jit(solution)/shard_map/ppermute | solution.py:320
  42.0 6.0 %shard_map.62 = (s32[7,16,256]{2,1,0:T(8,128)S(1)}, s32[16,7,16,256]{3,2,1,0:T(8,128)S(1)}) custom-call(s32[4,4]{1,0:T(4,128)S(1)} %copy-done.3, bf16[768,512]{1,0:T(8,128)(2,1)S(1)} %collective-permute-done.1.halo_ref, bf16[768,1024]{1,0:T(8,128)(2,1)S(1)} %copy-done.1, bf16[4,768,512]{2,1,0:T(8,128)(2,1)} %get-tuple-element.14.vals_ref, ...), custom_call_target="tpu_custom_call" | custom-call | flops 3000000000 | bytes 4000000 | tf_op jit(solution)/shard_map/pallas_call | solution.py:183
  47.9 9.5 %collective-permute-start.4 = (s32[7,16,256]{2,1,0:T(8,128)S(1)}, s32[7,16,256]{2,1,0:T(8,128)S(1)}, u32[]{:S(2)}, u32[]{:S(2)}) collective-permute-start(s32[7,16,256]{2,1,0:T(8,128)S(1)} %get-tuple-element.22._), channel_id=1, source_target_pairs={{32,0},{64,32},{96,64},{128,96},{160,128},{192,160},{224,192},{256... | collective-permute-start | bytes 344072 | tf_op jit(solution)/shard_map/ppermute | solution.py:321
  57.5 1.9 %collective-permute-start.3 = (s32[14,16,256]{2,1,0:T(8,128)S(1)}, s32[14,16,256]{2,1,0:T(8,128)S(1)}, u32[]{:S(2)}, u32[]{:S(2)}) collective-permute-start(s32[14,16,256]{2,1,0:T(8,128)S(1)} %shard_map.63._), channel_id=1, source_target_pairs={{0,32},{32,64},{64,96},{96,128},{128,160},{160,192},{192,224},{224... | collective-permute-start | bytes 688136 | tf_op jit(solution)/shard_map/ppermute | solution.py:326
  59.8 5.5 %collective-permute-start.6 = (s32[14,16,256]{2,1,0:T(8,128)S(1)}, s32[14,16,256]{2,1,0:T(8,128)S(1)}, u32[]{:S(2)}, u32[]{:S(2)}) collective-permute-start(s32[14,16,256]{2,1,0:T(8,128)S(1)} %shard_map.64._), channel_id=1, source_target_pairs={{32,0},{64,32},{96,64},{128,96},{160,128},{192,160},{224,192},{256... | collective-permute-start | bytes 688136 | tf_op jit(solution)/shard_map/ppermute | solution.py:329
  66.7 1.9 %collective-permute-start.5 = (s32[14,16,256]{2,1,0:T(8,128)S(1)}, s32[14,16,256]{2,1,0:T(8,128)S(1)}, u32[]{:S(2)}, u32[]{:S(2)}) collective-permute-start(s32[14,16,256]{2,1,0:T(8,128)S(1)} %shard_map.65._), channel_id=1, source_target_pairs={{0,32},{32,64},{64,96},{96,128},{128,160},{160,192},{192,224},{224... | collective-permute-start | bytes 688136 | tf_op jit(solution)/shard_map/ppermute | solution.py:326
  69.0 5.6 %collective-permute-start.8 = (s32[14,16,256]{2,1,0:T(8,128)S(1)}, s32[14,16,256]{2,1,0:T(8,128)S(1)}, u32[]{:S(2)}, u32[]{:S(2)}) collective-permute-start(s32[14,16,256]{2,1,0:T(8,128)S(1)} %shard_map.66._), channel_id=1, source_target_pairs={{32,0},{64,32},{96,64},{128,96},{160,128},{192,160},{224,192},{256... | collective-permute-start | bytes 688136 | tf_op jit(solution)/shard_map/ppermute | solution.py:329
  75.9 1.9 %collective-permute-start.7 = (s32[14,16,256]{2,1,0:T(8,128)S(1)}, s32[14,16,256]{2,1,0:T(8,128)S(1)}, u32[]{:S(2)}, u32[]{:S(2)}) collective-permute-start(s32[14,16,256]{2,1,0:T(8,128)S(1)} %shard_map.67._), channel_id=1, source_target_pairs={{0,32},{32,64},{64,96},{96,128},{128,160},{160,192},{192,224},{224... | collective-permute-start | bytes 688136 | tf_op jit(solution)/shard_map/ppermute | solution.py:326
  78.2 5.6 %collective-permute-start.10 = (s32[14,16,256]{2,1,0:T(8,128)S(1)}, s32[14,16,256]{2,1,0:T(8,128)S(1)}, u32[]{:S(2)}, u32[]{:S(2)}) collective-permute-start(s32[14,16,256]{2,1,0:T(8,128)S(1)} %shard_map.68._), channel_id=1, source_target_pairs={{32,0},{64,32},{96,64},{128,96},{160,128},{192,160},{224,192},{256... | collective-permute-start | bytes 688136 | tf_op jit(solution)/shard_map/ppermute | solution.py:329
  85.1 1.9 %collective-permute-start.9 = (s32[14,16,256]{2,1,0:T(8,128)S(1)}, s32[14,16,256]{2,1,0:T(8,128)S(1)}, u32[]{:S(2)}, u32[]{:S(2)}) collective-permute-start(s32[14,16,256]{2,1,0:T(8,128)S(1)} %shard_map.69._), channel_id=1, source_target_pairs={{0,32},{32,64},{64,96},{96,128},{128,160},{160,192},{192,224},{224... | collective-permute-start | bytes 688136 | tf_op jit(solution)/shard_map/ppermute | solution.py:326
  87.5 5.6 %collective-permute-start.12 = (s32[14,16,256]{2,1,0:T(8,128)S(1)}, s32[14,16,256]{2,1,0:T(8,128)S(1)}, u32[]{:S(2)}, u32[]{:S(2)}) collective-permute-start(s32[14,16,256]{2,1,0:T(8,128)S(1)} %shard_map.70._), channel_id=1, source_target_pairs={{32,0},{64,32},{96,64},{128,96},{160,128},{192,160},{224,192},{256... | collective-permute-start | bytes 688136 | tf_op jit(solution)/shard_map/ppermute | solution.py:329
  94.7 1.9 %collective-permute-start.11 = (s32[14,16,256]{2,1,0:T(8,128)S(1)}, s32[14,16,256]{2,1,0:T(8,128)S(1)}, u32[]{:S(2)}, u32[]{:S(2)}) collective-permute-start(s32[14,16,256]{2,1,0:T(8,128)S(1)} %shard_map.71._), channel_id=1, source_target_pairs={{0,32},{32,64},{64,96},{96,128},{128,160},{160,192},{192,224},{224... | collective-permute-start | bytes 688136 | tf_op jit(solution)/shard_map/ppermute | solution.py:326
  97.9 5.6 %collective-permute-start.14 = (s32[14,16,256]{2,1,0:T(8,128)S(1)}, s32[14,16,256]{2,1,0:T(8,128)S(1)}, u32[]{:S(2)}, u32[]{:S(2)}) collective-permute-start(s32[14,16,256]{2,1,0:T(8,128)S(1)} %shard_map.72._), channel_id=1, source_target_pairs={{32,0},{64,32},{96,64},{128,96},{160,128},{192,160},{224,192},{256... | collective-permute-start | bytes 688136 | tf_op jit(solution)/shard_map/ppermute | solution.py:329
  105.4 1.9 %collective-permute-start.13 = (s32[14,16,256]{2,1,0:T(8,128)S(1)}, s32[14,16,256]{2,1,0:T(8,128)S(1)}, u32[]{:S(2)}, u32[]{:S(2)}) collective-permute-start(s32[14,16,256]{2,1,0:T(8,128)S(1)} %shard_map.73._), channel_id=1, source_target_pairs={{0,32},{32,64},{64,96},{96,128},{128,160},{160,192},{192,224},{224... | collective-permute-start | bytes 688136 | tf_op jit(solution)/shard_map/ppermute | solution.py:326
  107.4 2.0 %collective-permute-done.14.came_ref = s32[14,16,256]{2,1,0:T(8,128)S(1)} collective-permute-done((s32[14,16,256]{2,1,0:T(8,128)S(1)}, s32[14,16,256]{2,1,0:T(8,128)S(1)}, u32[]{:S(2)}, u32[]{:S(2)}) %collective-permute-start.14) | collective-permute-done | bytes 229408 | tf_op jit(solution)/shard_map/ppermute | solution.py:329
  109.5 5.6 %collective-permute-start.16 = (s32[14,16,256]{2,1,0:T(8,128)S(1)}, s32[14,16,256]{2,1,0:T(8,128)S(1)}, u32[]{:S(2)}, u32[]{:S(2)}) collective-permute-start(s32[14,16,256]{2,1,0:T(8,128)S(1)} %shard_map.74._), channel_id=1, source_target_pairs={{32,0},{64,32},{96,64},{128,96},{160,128},{192,160},{224,192},{256... | collective-permute-start | bytes 688136 | tf_op jit(solution)/shard_map/ppermute | solution.py:329
  115.2 5.0 %collective-permute-done.16.came_ref = s32[14,16,256]{2,1,0:T(8,128)S(1)} collective-permute-done((s32[14,16,256]{2,1,0:T(8,128)S(1)}, s32[14,16,256]{2,1,0:T(8,128)S(1)}, u32[]{:S(2)}, u32[]{:S(2)}) %collective-permute-start.16) | collective-permute-done | bytes 229408 | tf_op jit(solution)/shard_map/ppermute | solution.py:329
  120.3 5.6 %collective-permute-start.17 = (s32[14,16,256]{2,1,0:T(8,128)S(1)}, s32[14,16,256]{2,1,0:T(8,128)S(1)}, u32[]{:S(2)}, u32[]{:S(2)}) collective-permute-start(s32[14,16,256]{2,1,0:T(8,128)S(1)} %shard_map.76), channel_id=1, source_target_pairs={{32,0},{64,32},{96,64},{128,96},{160,128},{192,160},{224,192},{256... | collective-permute-start | bytes 688136 | tf_op jit(solution)/shard_map/ppermute | solution.py:329
  129.4 5.6 %collective-permute-done.15.rising_ref = s32[14,16,256]{2,1,0:T(8,128)S(1)} collective-permute-done((s32[14,16,256]{2,1,0:T(8,128)S(1)}, s32[14,16,256]{2,1,0:T(8,128)S(1)}, u32[]{:S(2)}, u32[]{:S(2)}) %collective-permute-start.15) | collective-permute-done | bytes 229408 | tf_op jit(solution)/shard_map/ppermute | solution.py:326
  (44 shorter events, 19.5 us)
Async XLA Ops:
  0.6 1.4 %copy-start = (bf16[768,1024]{1,0:T(8,128)(2,1)S(1)}, bf16[768,1024]{1,0:T(8,128)(2,1)}, u32[]{:S(2)}) copy-start(bf16[768,1024]{1,0:T(8,128)(2,1)} %own_ref.5) | copy-start | bytes 4718596
  2.0 8.6 %copy-start.4 = (f32[4,512]{1,0:T(4,128)S(1)}, f32[4,512]{1,0:T(4,128)}, u32[]{:S(2)}) copy-start(f32[4,512]{1,0:T(4,128)} %param.7) | copy-start | bytes 24580
  2.0 8.7 %copy-start.1 = (bf16[768,1024]{1,0:T(8,128)(2,1)S(1)}, bf16[768,1024]{1,0:T(8,128)(2,1)}, u32[]{:S(2)}) copy-start(bf16[768,1024]{1,0:T(8,128)(2,1)} %own_ref.5) | copy-start | bytes 4718596
  2.0 8.7 %copy-start.2 = (s32[3,4,512]{2,1,0:T(4,128)S(1)}, s32[3,4,512]{2,1,0:T(4,128)}, u32[]{:S(2)}) copy-start(s32[3,4,512]{2,1,0:T(4,128)} %inc_ref.3) | copy-start | bytes 73732
  3.5 38.5 %collective-permute-start.1 = (bf16[768,512]{1,0:T(8,128)(2,1)}, bf16[768,512]{1,0:T(8,128)(2,1)S(1)}, u32[]{:S(2)}, u32[]{:S(2)}) collective-permute-start(bf16[768,512]{1,0:T(8,128)(2,1)} %get-tuple-element.19), channel_id=1, source_target_pairs={{1,0},{2,1},{3,2},{4,3},{5,4},{6,5},{7,6},{8,7},{9,8},{10,9},{11,1... | collective-permute-start | bytes 2359304 | tf_op jit(solution)/shard_map/ppermute | solution.py:309
  7.8 24.1 %collective-permute-start = (bf16[768,512]{1,0:T(8,128)(2,1)}, bf16[768,512]{1,0:T(8,128)(2,1)}, u32[]{:S(2)}, u32[]{:S(2)}) collective-permute-start(bf16[768,512]{1,0:T(8,128)(2,1)} %get-tuple-element.13._), channel_id=1, source_target_pairs={{0,1},{1,2},{2,3},{3,4},{4,5},{5,6},{6,7},{7,8},{8,9},{9,10},{10,1... | collective-permute-start | bytes 2359304 | tf_op jit(solution)/shard_map/ppermute | solution.py:308
  10.8 21.1 %copy-start.3 = (s32[4,4]{1,0:T(4,128)S(1)}, s32[4,4]{1,0:T(4,128)}, u32[]{:S(2)}) copy-start(s32[4,4]{1,0:T(4,128)} %partners_ref.5) | copy-start | bytes 196
  38.1 19.3 %collective-permute-start.2 = (s32[7,16,256]{2,1,0:T(8,128)S(1)}, s32[7,16,256]{2,1,0:T(8,128)S(1)}, u32[]{:S(2)}, u32[]{:S(2)}) collective-permute-start(s32[7,16,256]{2,1,0:T(8,128)S(1)} %get-tuple-element.20._), channel_id=1, source_target_pairs={{0,32},{32,64},{64,96},{96,128},{128,160},{160,192},{192,224},{224... | collective-permute-start | bytes 344072 | tf_op jit(solution)/shard_map/ppermute | solution.py:320
  47.9 11.9 %collective-permute-start.4 = (s32[7,16,256]{2,1,0:T(8,128)S(1)}, s32[7,16,256]{2,1,0:T(8,128)S(1)}, u32[]{:S(2)}, u32[]{:S(2)}) collective-permute-start(s32[7,16,256]{2,1,0:T(8,128)S(1)} %get-tuple-element.22._), channel_id=1, source_target_pairs={{32,0},{64,32},{96,64},{128,96},{160,128},{192,160},{224,192},{256... | collective-permute-start | bytes 344072 | tf_op jit(solution)/shard_map/ppermute | solution.py:321
  57.5 9.1 %collective-permute-start.3 = (s32[14,16,256]{2,1,0:T(8,128)S(1)}, s32[14,16,256]{2,1,0:T(8,128)S(1)}, u32[]{:S(2)}, u32[]{:S(2)}) collective-permute-start(s32[14,16,256]{2,1,0:T(8,128)S(1)} %shard_map.63._), channel_id=1, source_target_pairs={{0,32},{32,64},{64,96},{96,128},{128,160},{160,192},{192,224},{224... | collective-permute-start | bytes 688136 | tf_op jit(solution)/shard_map/ppermute | solution.py:326
  59.8 9.1 %collective-permute-start.6 = (s32[14,16,256]{2,1,0:T(8,128)S(1)}, s32[14,16,256]{2,1,0:T(8,128)S(1)}, u32[]{:S(2)}, u32[]{:S(2)}) collective-permute-start(s32[14,16,256]{2,1,0:T(8,128)S(1)} %shard_map.64._), channel_id=1, source_target_pairs={{32,0},{64,32},{96,64},{128,96},{160,128},{192,160},{224,192},{256... | collective-permute-start | bytes 688136 | tf_op jit(solution)/shard_map/ppermute | solution.py:329
  66.7 9.1 %collective-permute-start.5 = (s32[14,16,256]{2,1,0:T(8,128)S(1)}, s32[14,16,256]{2,1,0:T(8,128)S(1)}, u32[]{:S(2)}, u32[]{:S(2)}) collective-permute-start(s32[14,16,256]{2,1,0:T(8,128)S(1)} %shard_map.65._), channel_id=1, source_target_pairs={{0,32},{32,64},{64,96},{96,128},{128,160},{160,192},{192,224},{224... | collective-permute-start | bytes 688136 | tf_op jit(solution)/shard_map/ppermute | solution.py:326
  69.0 9.1 %collective-permute-start.8 = (s32[14,16,256]{2,1,0:T(8,128)S(1)}, s32[14,16,256]{2,1,0:T(8,128)S(1)}, u32[]{:S(2)}, u32[]{:S(2)}) collective-permute-start(s32[14,16,256]{2,1,0:T(8,128)S(1)} %shard_map.66._), channel_id=1, source_target_pairs={{32,0},{64,32},{96,64},{128,96},{160,128},{192,160},{224,192},{256... | collective-permute-start | bytes 688136 | tf_op jit(solution)/shard_map/ppermute | solution.py:329
  75.9 9.1 %collective-permute-start.7 = (s32[14,16,256]{2,1,0:T(8,128)S(1)}, s32[14,16,256]{2,1,0:T(8,128)S(1)}, u32[]{:S(2)}, u32[]{:S(2)}) collective-permute-start(s32[14,16,256]{2,1,0:T(8,128)S(1)} %shard_map.67._), channel_id=1, source_target_pairs={{0,32},{32,64},{64,96},{96,128},{128,160},{160,192},{192,224},{224... | collective-permute-start | bytes 688136 | tf_op jit(solution)/shard_map/ppermute | solution.py:326
  78.2 9.2 %collective-permute-start.10 = (s32[14,16,256]{2,1,0:T(8,128)S(1)}, s32[14,16,256]{2,1,0:T(8,128)S(1)}, u32[]{:S(2)}, u32[]{:S(2)}) collective-permute-start(s32[14,16,256]{2,1,0:T(8,128)S(1)} %shard_map.68._), channel_id=1, source_target_pairs={{32,0},{64,32},{96,64},{128,96},{160,128},{192,160},{224,192},{256... | collective-permute-start | bytes 688136 | tf_op jit(solution)/shard_map/ppermute | solution.py:329
  85.1 9.5 %collective-permute-start.9 = (s32[14,16,256]{2,1,0:T(8,128)S(1)}, s32[14,16,256]{2,1,0:T(8,128)S(1)}, u32[]{:S(2)}, u32[]{:S(2)}) collective-permute-start(s32[14,16,256]{2,1,0:T(8,128)S(1)} %shard_map.69._), channel_id=1, source_target_pairs={{0,32},{32,64},{64,96},{96,128},{128,160},{160,192},{192,224},{224... | collective-permute-start | bytes 688136 | tf_op jit(solution)/shard_map/ppermute | solution.py:326
  87.5 10.3 %collective-permute-start.12 = (s32[14,16,256]{2,1,0:T(8,128)S(1)}, s32[14,16,256]{2,1,0:T(8,128)S(1)}, u32[]{:S(2)}, u32[]{:S(2)}) collective-permute-start(s32[14,16,256]{2,1,0:T(8,128)S(1)} %shard_map.70._), channel_id=1, source_target_pairs={{32,0},{64,32},{96,64},{128,96},{160,128},{192,160},{224,192},{256... | collective-permute-start | bytes 688136 | tf_op jit(solution)/shard_map/ppermute | solution.py:329
  94.7 10.7 %collective-permute-start.11 = (s32[14,16,256]{2,1,0:T(8,128)S(1)}, s32[14,16,256]{2,1,0:T(8,128)S(1)}, u32[]{:S(2)}, u32[]{:S(2)}) collective-permute-start(s32[14,16,256]{2,1,0:T(8,128)S(1)} %shard_map.71._), channel_id=1, source_target_pairs={{0,32},{32,64},{64,96},{96,128},{128,160},{160,192},{192,224},{224... | collective-permute-start | bytes 688136 | tf_op jit(solution)/shard_map/ppermute | solution.py:326
  97.9 11.5 %collective-permute-start.14 = (s32[14,16,256]{2,1,0:T(8,128)S(1)}, s32[14,16,256]{2,1,0:T(8,128)S(1)}, u32[]{:S(2)}, u32[]{:S(2)}) collective-permute-start(s32[14,16,256]{2,1,0:T(8,128)S(1)} %shard_map.72._), channel_id=1, source_target_pairs={{32,0},{64,32},{96,64},{128,96},{160,128},{192,160},{224,192},{256... | collective-permute-start | bytes 688136 | tf_op jit(solution)/shard_map/ppermute | solution.py:329
  105.4 9.7 %collective-permute-start.13 = (s32[14,16,256]{2,1,0:T(8,128)S(1)}, s32[14,16,256]{2,1,0:T(8,128)S(1)}, u32[]{:S(2)}, u32[]{:S(2)}) collective-permute-start(s32[14,16,256]{2,1,0:T(8,128)S(1)} %shard_map.73._), channel_id=1, source_target_pairs={{0,32},{32,64},{64,96},{96,128},{128,160},{160,192},{192,224},{224... | collective-permute-start | bytes 688136 | tf_op jit(solution)/shard_map/ppermute | solution.py:326
  109.5 10.7 %collective-permute-start.16 = (s32[14,16,256]{2,1,0:T(8,128)S(1)}, s32[14,16,256]{2,1,0:T(8,128)S(1)}, u32[]{:S(2)}, u32[]{:S(2)}) collective-permute-start(s32[14,16,256]{2,1,0:T(8,128)S(1)} %shard_map.74._), channel_id=1, source_target_pairs={{32,0},{64,32},{96,64},{128,96},{160,128},{192,160},{224,192},{256... | collective-permute-start | bytes 688136 | tf_op jit(solution)/shard_map/ppermute | solution.py:329
  120.3 9.1 %collective-permute-start.17 = (s32[14,16,256]{2,1,0:T(8,128)S(1)}, s32[14,16,256]{2,1,0:T(8,128)S(1)}, u32[]{:S(2)}, u32[]{:S(2)}) collective-permute-start(s32[14,16,256]{2,1,0:T(8,128)S(1)} %shard_map.76), channel_id=1, source_target_pairs={{32,0},{64,32},{96,64},{128,96},{160,128},{192,160},{224,192},{256... | collective-permute-start | bytes 688136 | tf_op jit(solution)/shard_map/ppermute | solution.py:329
  125.9 9.1 %collective-permute-start.15 = (s32[14,16,256]{2,1,0:T(8,128)S(1)}, s32[14,16,256]{2,1,0:T(8,128)S(1)}, u32[]{:S(2)}, u32[]{:S(2)}) collective-permute-start(s32[14,16,256]{2,1,0:T(8,128)S(1)} %shard_map.75._), channel_id=1, source_target_pairs={{0,32},{32,64},{64,96},{96,128},{128,160},{160,192},{192,224},{224... | collective-permute-start | bytes 688136 | tf_op jit(solution)/shard_map/ppermute | solution.py:326

commit v5 on v4

--- a/solution.py
+++ b/solution.py
@@ -34,6 +34,14 @@
 def unpacked(words):
     tops = [lax.shift_right_logical(word, 24) for word in words]
     return [word & LOW for word in words] + [tops[0] | (tops[1] << 8) | (tops[2] << 16)]
+
+
+def ring_place(z, count):
+    return jnp.where(lax.rem(z, 2) == 0, z // 2, count - 1 - z // 2)
+
+
+def ring_order(count):
+    return list(range(0, count, 2)) + list(range(count - 1, 0, -2))
 
 
 def group_index():
@@ -128,7 +136,8 @@
     own_width = own_ref.shape[1]
     share = width // groups
     pieces = hot_ref.shape[2] // width
-    me = lax.axis_index("shot")
+    place = ring_place(lax.axis_index("shot"), groups)
+    places = ring_order(groups)
     base = group_index() * blocks
     if upper:
         win[:, 0:own_width] = own_ref[...]
@@ -157,7 +166,7 @@
             rows = slice(d * share, (d + 1) * share)
             values = [self_ref[block, rows, :]]
             values += [tiles[rows, k * width : (k + 1) * width] for k in range(slots - 1)]
-            at = lax.rem(d - me + groups, groups)
+            at = lax.rem(places.index(d) - place + groups, groups)
             for n, word in enumerate(packed(values)):
                 parts_ref[at, b * (slots - 1) + n] = word
         other = jnp.dot(chosen, hot_ref[block], preferred_element_type=jnp.float32)
@@ -315,8 +324,9 @@
     first_down, upper = pair_call(1, partners, right, *args, first_up, width, groups)
 
     half = groups // 2
-    rise = [(i, (i + 1) % groups) for i in range(groups)]
-    fall = [((i + 1) % groups, i) for i in range(groups)]
+    places = ring_order(groups)
+    rise = [(places[i], places[(i + 1) % groups]) for i in range(groups)]
+    fall = [(b, a) for a, b in rise]
     rising = lax.ppermute(first_up, "shot", rise)
     falling = lax.ppermute(first_down, "shot", fall)
     order = first_down

time: 137 us -> 163 us (1.19)
  the two profiles are of different devices: /device:TPU:24 before, /device:TPU:248 now
where the time goes in v5:
time: 163 us
  starting transfers between devices  81.3 us (50%)
  waiting for transfers between devices  56.8 us (35%)
  Pallas kernels  21.4 us (13%)
  local copies, waits for them, and re-layouts  1.71 us (1%)
    ppermute x7, starting transfers between devices, local(): falling = lax.ppermute(order, 'shot', fall)  53.3 us
    ppermute x7, waiting for transfers between devices, local(): falling = lax.ppermute(order, 'shot', fall)  24.7 us
    ppermute x1, waiting for transfers between devices, local(): lax.ppermute(tail, ('row', 'col'), [(i, (i + 1) % sides) for i in range(s...  15.9 us
    ppermute x7, waiting for transfers between devices, local(): rising = lax.ppermute(order, 'shot', rise)  15.7 us
    ppermute x7, starting transfers between devices, local(): rising = lax.ppermute(order, 'shot', rise)  13.8 us
    pallas_call x2, Pallas kernels, pair_call(): pl.pallas_call(functools.partial(pair_kernel, upper, width, groups), out_...  12.2 us
    ppermute x1, starting transfers between devices, local(): falling = lax.ppermute(first_down, 'shot', fall)  6.03 us
    pallas_call x1, Pallas kernels, ready_call(): pl.pallas_call(functools.partial(ready_kernel, width, slots), out_shape=[...  5.19 us
  transfers between devices with their start and end apart: 18, of which 15 were waited for; matrix products, arithmetic and copies ran while one was open for 1% of the time, Pallas kernels for 11%

profile of v5, /device:TPU:248, one launch (start us, length us, event | category | flops | bytes accessed | tf_op | source)
XLA Modules:
  0.0 162.8 jit_solution(3940331459221635372)
XLA Ops:
  3.5 4.3 %collective-permute-start.1 = (bf16[768,512]{1,0:T(8,128)(2,1)}, bf16[768,512]{1,0:T(8,128)(2,1)S(1)}, u32[]{:S(2)}, u32[]{:S(2)}) collective-permute-start(bf16[768,512]{1,0:T(8,128)(2,1)} %get-tuple-element.19), channel_id=1, source_target_pairs={{1,0},{2,1},{3,2},{4,3},{5,4},{6,5},{7,6},{8,7},{9,8},{10,9},{11,1... | collective-permute-start | bytes 2359304 | tf_op jit(solution)/shard_map/ppermute | solution.py:318
  7.8 1.9 %collective-permute-start = (bf16[768,512]{1,0:T(8,128)(2,1)}, bf16[768,512]{1,0:T(8,128)(2,1)}, u32[]{:S(2)}, u32[]{:S(2)}) collective-permute-start(bf16[768,512]{1,0:T(8,128)(2,1)} %get-tuple-element.13._), channel_id=1, source_target_pairs={{0,1},{1,2},{2,3},{3,4},{4,5},{5,6},{6,7},{7,8},{8,9},{9,10},{10,1... | collective-permute-start | bytes 2359304 | tf_op jit(solution)/shard_map/ppermute | solution.py:317
  10.8 5.2 %shard_map.60 = (f32[4,512]{1,0:T(4,128)S(1)}, bf16[4,768,512]{2,1,0:T(8,128)(2,1)}, bf16[4,1024,512]{2,1,0:T(8,128)(2,1)}, s32[4,256,256]{2,1,0:T(8,128)S(1)}, f32[8,256]{1,0:T(8,128)S(1)}) custom-call(bf16[768,1024]{1,0:T(8,128)(2,1)S(1)} %copy-done.1, s32[3,4,512]{2,1,0:T(4,128)S(1)} %copy-done.2, s32[512,4]{1,0:T(8,128)S(1)} %bitcast.4, ...), custom_call_target="tpu_custom_call" | custom-call | flops 20000000000 | bytes 12000000 | tf_op jit(solution)/shard_map/pallas_call | solution.py:112
  16.0 15.9 %collective-permute-done.halo_ref = bf16[768,512]{1,0:T(8,128)(2,1)} collective-permute-done((bf16[768,512]{1,0:T(8,128)(2,1)}, bf16[768,512]{1,0:T(8,128)(2,1)}, u32[]{:S(2)}, u32[]{:S(2)}) %collective-permute-start) | collective-permute-done | bytes 786464 | tf_op jit(solution)/shard_map/ppermute | solution.py:317
  31.9 6.2 %shard_map.61 = (s32[7,16,256]{2,1,0:T(8,128)S(1)}, s32[16,7,16,256]{3,2,1,0:T(8,128)S(1)}) custom-call(s32[4,4]{1,0:T(4,128)S(1)} %copy-done.3, bf16[768,512]{1,0:T(8,128)(2,1)} %collective-permute-done.halo_ref, bf16[768,1024]{1,0:T(8,128)(2,1)S(1)} %copy-done.1, bf16[4,768,512]{2,1,0:T(8,128)(2,1)} %get-tuple-element.14.vals_ref, ...), custom_call_target="tpu_custom_call" | custom-call | flops 3000000000 | bytes 4000000 | tf_op jit(solution)/shard_map/pallas_call | solution.py:192
  40.1 6.0 %shard_map.62 = (s32[7,16,256]{2,1,0:T(8,128)S(1)}, s32[16,7,16,256]{3,2,1,0:T(8,128)S(1)}) custom-call(s32[4,4]{1,0:T(4,128)S(1)} %copy-done.3, bf16[768,512]{1,0:T(8,128)(2,1)S(1)} %collective-permute-done.1.halo_ref, bf16[768,1024]{1,0:T(8,128)(2,1)S(1)} %copy-done.1, bf16[4,768,512]{2,1,0:T(8,128)(2,1)} %get-tuple-element.14.vals_ref, ...), custom_call_target="tpu_custom_call" | custom-call | flops 3000000000 | bytes 4000000 | tf_op jit(solution)/shard_map/pallas_call | solution.py:192
  46.0 6.0 %collective-permute-start.4 = (s32[7,16,256]{2,1,0:T(8,128)S(1)}, s32[7,16,256]{2,1,0:T(8,128)S(1)}, u32[]{:S(2)}, u32[]{:S(2)}) collective-permute-start(s32[7,16,256]{2,1,0:T(8,128)S(1)} %get-tuple-element.22._), channel_id=1, source_target_pairs={{64,0},{128,64},{192,128},{256,192},{320,256},{384,320},{448,384},... | collective-permute-start | bytes 344072 | tf_op jit(solution)/shard_map/ppermute | solution.py:331
  52.1 1.9 %collective-permute-start.3 = (s32[14,16,256]{2,1,0:T(8,128)S(1)}, s32[14,16,256]{2,1,0:T(8,128)S(1)}, u32[]{:S(2)}, u32[]{:S(2)}) collective-permute-start(s32[14,16,256]{2,1,0:T(8,128)S(1)} %shard_map.63._), channel_id=1, source_target_pairs={{0,64},{64,128},{128,192},{192,256},{256,320},{320,384},{384,448},... | collective-permute-start | bytes 688136 | tf_op jit(solution)/shard_map/ppermute | solution.py:336
  54.5 6.5 %collective-permute-start.6 = (s32[14,16,256]{2,1,0:T(8,128)S(1)}, s32[14,16,256]{2,1,0:T(8,128)S(1)}, u32[]{:S(2)}, u32[]{:S(2)}) collective-permute-start(s32[14,16,256]{2,1,0:T(8,128)S(1)} %shard_map.64._), channel_id=1, source_target_pairs={{64,0},{128,64},{192,128},{256,192},{320,256},{384,320},{448,384},... | collective-permute-start | bytes 688136 | tf_op jit(solution)/shard_map/ppermute | solution.py:339
  62.8 2.3 %collective-permute-start.5 = (s32[14,16,256]{2,1,0:T(8,128)S(1)}, s32[14,16,256]{2,1,0:T(8,128)S(1)}, u32[]{:S(2)}, u32[]{:S(2)}) collective-permute-start(s32[14,16,256]{2,1,0:T(8,128)S(1)} %shard_map.65._), channel_id=1, source_target_pairs={{0,64},{64,128},{128,192},{192,256},{256,320},{320,384},{384,448},... | collective-permute-start | bytes 688136 | tf_op jit(solution)/shard_map/ppermute | solution.py:336
  67.0 6.5 %collective-permute-start.8 = (s32[14,16,256]{2,1,0:T(8,128)S(1)}, s32[14,16,256]{2,1,0:T(8,128)S(1)}, u32[]{:S(2)}, u32[]{:S(2)}) collective-permute-start(s32[14,16,256]{2,1,0:T(8,128)S(1)} %shard_map.66._), channel_id=1, source_target_pairs={{64,0},{128,64},{192,128},{256,192},{320,256},{384,320},{448,384},... | collective-permute-start | bytes 688136 | tf_op jit(solution)/shard_map/ppermute | solution.py:339
  76.2 4.0 %collective-permute-done.8.came_ref = s32[14,16,256]{2,1,0:T(8,128)S(1)} collective-permute-done((s32[14,16,256]{2,1,0:T(8,128)S(1)}, s32[14,16,256]{2,1,0:T(8,128)S(1)}, u32[]{:S(2)}, u32[]{:S(2)}) %collective-permute-start.8) | collective-permute-done | bytes 229408 | tf_op jit(solution)/shard_map/ppermute | solution.py:339
  80.2 6.5 %collective-permute-start.10 = (s32[14,16,256]{2,1,0:T(8,128)S(1)}, s32[14,16,256]{2,1,0:T(8,128)S(1)}, u32[]{:S(2)}, u32[]{:S(2)}) collective-permute-start(s32[14,16,256]{2,1,0:T(8,128)S(1)} %shard_map.68._), channel_id=1, source_target_pairs={{64,0},{128,64},{192,128},{256,192},{320,256},{384,320},{448,384},... | collective-permute-start | bytes 688136 | tf_op jit(solution)/shard_map/ppermute | solution.py:339
  92.2 7.4 %collective-permute-start.12 = (s32[14,16,256]{2,1,0:T(8,128)S(1)}, s32[14,16,256]{2,1,0:T(8,128)S(1)}, u32[]{:S(2)}, u32[]{:S(2)}) collective-permute-start(s32[14,16,256]{2,1,0:T(8,128)S(1)} %shard_map.70._), channel_id=1, source_target_pairs={{64,0},{128,64},{192,128},{256,192},{320,256},{384,320},{448,384},... | collective-permute-start | bytes 688136 | tf_op jit(solution)/shard_map/ppermute | solution.py:339
  99.7 4.8 %collective-permute-done.9.came_ref = s32[14,16,256]{2,1,0:T(8,128)S(1)} collective-permute-done((s32[14,16,256]{2,1,0:T(8,128)S(1)}, s32[14,16,256]{2,1,0:T(8,128)S(1)}, u32[]{:S(2)}, u32[]{:S(2)}) %collective-permute-start.9) | collective-permute-done | bytes 229408 | tf_op jit(solution)/shard_map/ppermute | solution.py:336
  104.5 1.9 %collective-permute-start.11 = (s32[14,16,256]{2,1,0:T(8,128)S(1)}, s32[14,16,256]{2,1,0:T(8,128)S(1)}, u32[]{:S(2)}, u32[]{:S(2)}) collective-permute-start(s32[14,16,256]{2,1,0:T(8,128)S(1)} %shard_map.71._), channel_id=1, source_target_pairs={{0,64},{64,128},{128,192},{192,256},{256,320},{320,384},{384,448},... | collective-permute-start | bytes 688136 | tf_op jit(solution)/shard_map/ppermute | solution.py:336
  106.5 2.6 %collective-permute-done.12.came_ref = s32[14,16,256]{2,1,0:T(8,128)S(1)} collective-permute-done((s32[14,16,256]{2,1,0:T(8,128)S(1)}, s32[14,16,256]{2,1,0:T(8,128)S(1)}, u32[]{:S(2)}, u32[]{:S(2)}) %collective-permute-start.12) | collective-permute-done | bytes 229408 | tf_op jit(solution)/shard_map/ppermute | solution.py:339
  109.1 13.3 %collective-permute-start.14 = (s32[14,16,256]{2,1,0:T(8,128)S(1)}, s32[14,16,256]{2,1,0:T(8,128)S(1)}, u32[]{:S(2)}, u32[]{:S(2)}) collective-permute-start(s32[14,16,256]{2,1,0:T(8,128)S(1)} %shard_map.72._), channel_id=1, source_target_pairs={{64,0},{128,64},{192,128},{256,192},{320,256},{384,320},{448,384},... | collective-permute-start | bytes 688136 | tf_op jit(solution)/shard_map/ppermute | solution.py:339
  122.9 1.9 %collective-permute-start.13 = (s32[14,16,256]{2,1,0:T(8,128)S(1)}, s32[14,16,256]{2,1,0:T(8,128)S(1)}, u32[]{:S(2)}, u32[]{:S(2)}) collective-permute-start(s32[14,16,256]{2,1,0:T(8,128)S(1)} %shard_map.73._), channel_id=1, source_target_pairs={{0,64},{64,128},{128,192},{192,256},{256,320},{320,384},{384,448},... | collective-permute-start | bytes 688136 | tf_op jit(solution)/shard_map/ppermute | solution.py:336
  124.9 5.6 %collective-permute-done.14.came_ref = s32[14,16,256]{2,1,0:T(8,128)S(1)} collective-permute-done((s32[14,16,256]{2,1,0:T(8,128)S(1)}, s32[14,16,256]{2,1,0:T(8,128)S(1)}, u32[]{:S(2)}, u32[]{:S(2)}) %collective-permute-start.14) | collective-permute-done | bytes 229408 | tf_op jit(solution)/shard_map/ppermute | solution.py:339
  130.6 6.5 %collective-permute-start.16 = (s32[14,16,256]{2,1,0:T(8,128)S(1)}, s32[14,16,256]{2,1,0:T(8,128)S(1)}, u32[]{:S(2)}, u32[]{:S(2)}) collective-permute-start(s32[14,16,256]{2,1,0:T(8,128)S(1)} %shard_map.74._), channel_id=1, source_target_pairs={{64,0},{128,64},{192,128},{256,192},{320,256},{384,320},{448,384},... | collective-permute-start | bytes 688136 | tf_op jit(solution)/shard_map/ppermute | solution.py:339
  137.2 7.4 %collective-permute-done.16.came_ref = s32[14,16,256]{2,1,0:T(8,128)S(1)} collective-permute-done((s32[14,16,256]{2,1,0:T(8,128)S(1)}, s32[14,16,256]{2,1,0:T(8,128)S(1)}, u32[]{:S(2)}, u32[]{:S(2)}) %collective-permute-start.16) | collective-permute-done | bytes 229408 | tf_op jit(solution)/shard_map/ppermute | solution.py:339
  144.6 6.6 %collective-permute-start.17 = (s32[14,16,256]{2,1,0:T(8,128)S(1)}, s32[14,16,256]{2,1,0:T(8,128)S(1)}, u32[]{:S(2)}, u32[]{:S(2)}) collective-permute-start(s32[14,16,256]{2,1,0:T(8,128)S(1)} %shard_map.76), channel_id=1, source_target_pairs={{64,0},{128,64},{192,128},{256,192},{320,256},{384,320},{448,384},... | collective-permute-start | bytes 688136 | tf_op jit(solution)/shard_map/ppermute | solution.py:339
  154.8 6.5 %collective-permute-done.15.rising_ref = s32[14,16,256]{2,1,0:T(8,128)S(1)} collective-permute-done((s32[14,16,256]{2,1,0:T(8,128)S(1)}, s32[14,16,256]{2,1,0:T(8,128)S(1)}, u32[]{:S(2)}, u32[]{:S(2)}) %collective-permute-start.15) | collective-permute-done | bytes 229408 | tf_op jit(solution)/shard_map/ppermute | solution.py:336
  (44 shorter events, 24.1 us)
Async XLA Ops:
  0.6 1.4 copy-start
  2.0 8.6 %copy-start.4 = (f32[4,512]{1,0:T(4,128)S(1)}, f32[4,512]{1,0:T(4,128)}, u32[]{:S(2)}) copy-start(f32[4,512]{1,0:T(4,128)} %param.7) | copy-start | bytes 24580
  2.0 8.7 %copy-start.1 = (bf16[768,1024]{1,0:T(8,128)(2,1)S(1)}, bf16[768,1024]{1,0:T(8,128)(2,1)}, u32[]{:S(2)}) copy-start(bf16[768,1024]{1,0:T(8,128)(2,1)} %own_ref.5) | copy-start | bytes 4718596
  2.0 8.7 %copy-start.2 = (s32[3,4,512]{2,1,0:T(4,128)S(1)}, s32[3,4,512]{2,1,0:T(4,128)}, u32[]{:S(2)}) copy-start(s32[3,4,512]{2,1,0:T(4,128)} %inc_ref.3) | copy-start | bytes 73732
  3.5 36.6 %collective-permute-start.1 = (bf16[768,512]{1,0:T(8,128)(2,1)}, bf16[768,512]{1,0:T(8,128)(2,1)S(1)}, u32[]{:S(2)}, u32[]{:S(2)}) collective-permute-start(bf16[768,512]{1,0:T(8,128)(2,1)} %get-tuple-element.19), channel_id=1, source_target_pairs={{1,0},{2,1},{3,2},{4,3},{5,4},{6,5},{7,6},{8,7},{9,8},{10,9},{11,1... | collective-permute-start | bytes 2359304 | tf_op jit(solution)/shard_map/ppermute | solution.py:318
  7.8 24.1 %collective-permute-start = (bf16[768,512]{1,0:T(8,128)(2,1)}, bf16[768,512]{1,0:T(8,128)(2,1)}, u32[]{:S(2)}, u32[]{:S(2)}) collective-permute-start(bf16[768,512]{1,0:T(8,128)(2,1)} %get-tuple-element.13._), channel_id=1, source_target_pairs={{0,1},{1,2},{2,3},{3,4},{4,5},{5,6},{6,7},{7,8},{8,9},{9,10},{10,1... | collective-permute-start | bytes 2359304 | tf_op jit(solution)/shard_map/ppermute | solution.py:317
  10.8 21.1 %copy-start.3 = (s32[4,4]{1,0:T(4,128)S(1)}, s32[4,4]{1,0:T(4,128)}, u32[]{:S(2)}) copy-start(s32[4,4]{1,0:T(4,128)} %partners_ref.5) | copy-start | bytes 196
  38.1 14.0 %collective-permute-start.2 = (s32[7,16,256]{2,1,0:T(8,128)S(1)}, s32[7,16,256]{2,1,0:T(8,128)S(1)}, u32[]{:S(2)}, u32[]{:S(2)}) collective-permute-start(s32[7,16,256]{2,1,0:T(8,128)S(1)} %get-tuple-element.20._), channel_id=1, source_target_pairs={{0,64},{64,128},{128,192},{192,256},{256,320},{320,384},{384,448},... | collective-permute-start | bytes 344072 | tf_op jit(solution)/shard_map/ppermute | solution.py:330
  46.0 8.4 %collective-permute-start.4 = (s32[7,16,256]{2,1,0:T(8,128)S(1)}, s32[7,16,256]{2,1,0:T(8,128)S(1)}, u32[]{:S(2)}, u32[]{:S(2)}) collective-permute-start(s32[7,16,256]{2,1,0:T(8,128)S(1)} %get-tuple-element.22._), channel_id=1, source_target_pairs={{64,0},{128,64},{192,128},{256,192},{320,256},{384,320},{448,384},... | collective-permute-start | bytes 344072 | tf_op jit(solution)/shard_map/ppermute | solution.py:331
  52.1 10.6 %collective-permute-start.3 = (s32[14,16,256]{2,1,0:T(8,128)S(1)}, s32[14,16,256]{2,1,0:T(8,128)S(1)}, u32[]{:S(2)}, u32[]{:S(2)}) collective-permute-start(s32[14,16,256]{2,1,0:T(8,128)S(1)} %shard_map.63._), channel_id=1, source_target_pairs={{0,64},{64,128},{128,192},{192,256},{256,320},{320,384},{384,448},... | collective-permute-start | bytes 688136 | tf_op jit(solution)/shard_map/ppermute | solution.py:336
  54.5 12.5 %collective-permute-start.6 = (s32[14,16,256]{2,1,0:T(8,128)S(1)}, s32[14,16,256]{2,1,0:T(8,128)S(1)}, u32[]{:S(2)}, u32[]{:S(2)}) collective-permute-start(s32[14,16,256]{2,1,0:T(8,128)S(1)} %shard_map.64._), channel_id=1, source_target_pairs={{64,0},{128,64},{192,128},{256,192},{320,256},{384,320},{448,384},... | collective-permute-start | bytes 688136 | tf_op jit(solution)/shard_map/ppermute | solution.py:339
  62.8 11.4 %collective-permute-start.5 = (s32[14,16,256]{2,1,0:T(8,128)S(1)}, s32[14,16,256]{2,1,0:T(8,128)S(1)}, u32[]{:S(2)}, u32[]{:S(2)}) collective-permute-start(s32[14,16,256]{2,1,0:T(8,128)S(1)} %shard_map.65._), channel_id=1, source_target_pairs={{0,64},{64,128},{128,192},{192,256},{256,320},{320,384},{384,448},... | collective-permute-start | bytes 688136 | tf_op jit(solution)/shard_map/ppermute | solution.py:336
  67.0 13.1 %collective-permute-start.8 = (s32[14,16,256]{2,1,0:T(8,128)S(1)}, s32[14,16,256]{2,1,0:T(8,128)S(1)}, u32[]{:S(2)}, u32[]{:S(2)}) collective-permute-start(s32[14,16,256]{2,1,0:T(8,128)S(1)} %shard_map.66._), channel_id=1, source_target_pairs={{64,0},{128,64},{192,128},{256,192},{320,256},{384,320},{448,384},... | collective-permute-start | bytes 688136 | tf_op jit(solution)/shard_map/ppermute | solution.py:339
  74.3 14.1 %collective-permute-start.7 = (s32[14,16,256]{2,1,0:T(8,128)S(1)}, s32[14,16,256]{2,1,0:T(8,128)S(1)}, u32[]{:S(2)}, u32[]{:S(2)}) collective-permute-start(s32[14,16,256]{2,1,0:T(8,128)S(1)} %shard_map.67._), channel_id=1, source_target_pairs={{0,64},{64,128},{128,192},{192,256},{256,320},{320,384},{384,448},... | collective-permute-start | bytes 688136 | tf_op jit(solution)/shard_map/ppermute | solution.py:336
  80.2 11.9 %collective-permute-start.10 = (s32[14,16,256]{2,1,0:T(8,128)S(1)}, s32[14,16,256]{2,1,0:T(8,128)S(1)}, u32[]{:S(2)}, u32[]{:S(2)}) collective-permute-start(s32[14,16,256]{2,1,0:T(8,128)S(1)} %shard_map.68._), channel_id=1, source_target_pairs={{64,0},{128,64},{192,128},{256,192},{320,256},{384,320},{448,384},... | collective-permute-start | bytes 688136 | tf_op jit(solution)/shard_map/ppermute | solution.py:339
  88.5 16.0 %collective-permute-start.9 = (s32[14,16,256]{2,1,0:T(8,128)S(1)}, s32[14,16,256]{2,1,0:T(8,128)S(1)}, u32[]{:S(2)}, u32[]{:S(2)}) collective-permute-start(s32[14,16,256]{2,1,0:T(8,128)S(1)} %shard_map.69._), channel_id=1, source_target_pairs={{0,64},{64,128},{128,192},{192,256},{256,320},{320,384},{384,448},... | collective-permute-start | bytes 688136 | tf_op jit(solution)/shard_map/ppermute | solution.py:336
  92.2 16.8 %collective-permute-start.12 = (s32[14,16,256]{2,1,0:T(8,128)S(1)}, s32[14,16,256]{2,1,0:T(8,128)S(1)}, u32[]{:S(2)}, u32[]{:S(2)}) collective-permute-start(s32[14,16,256]{2,1,0:T(8,128)S(1)} %shard_map.70._), channel_id=1, source_target_pairs={{64,0},{128,64},{192,128},{256,192},{320,256},{384,320},{448,384},... | collective-permute-start | bytes 688136 | tf_op jit(solution)/shard_map/ppermute | solution.py:339
  104.5 18.3 %collective-permute-start.11 = (s32[14,16,256]{2,1,0:T(8,128)S(1)}, s32[14,16,256]{2,1,0:T(8,128)S(1)}, u32[]{:S(2)}, u32[]{:S(2)}) collective-permute-start(s32[14,16,256]{2,1,0:T(8,128)S(1)} %shard_map.71._), channel_id=1, source_target_pairs={{0,64},{64,128},{128,192},{192,256},{256,320},{320,384},{384,448},... | collective-permute-start | bytes 688136 | tf_op jit(solution)/shard_map/ppermute | solution.py:336
  109.1 21.4 %collective-permute-start.14 = (s32[14,16,256]{2,1,0:T(8,128)S(1)}, s32[14,16,256]{2,1,0:T(8,128)S(1)}, u32[]{:S(2)}, u32[]{:S(2)}) collective-permute-start(s32[14,16,256]{2,1,0:T(8,128)S(1)} %shard_map.72._), channel_id=1, source_target_pairs={{64,0},{128,64},{192,128},{256,192},{320,256},{384,320},{448,384},... | collective-permute-start | bytes 688136 | tf_op jit(solution)/shard_map/ppermute | solution.py:339
  122.9 14.1 %collective-permute-start.13 = (s32[14,16,256]{2,1,0:T(8,128)S(1)}, s32[14,16,256]{2,1,0:T(8,128)S(1)}, u32[]{:S(2)}, u32[]{:S(2)}) collective-permute-start(s32[14,16,256]{2,1,0:T(8,128)S(1)} %shard_map.73._), channel_id=1, source_target_pairs={{0,64},{64,128},{128,192},{192,256},{256,320},{320,384},{384,448},... | collective-permute-start | bytes 688136 | tf_op jit(solution)/shard_map/ppermute | solution.py:336
  130.6 14.0 %collective-permute-start.16 = (s32[14,16,256]{2,1,0:T(8,128)S(1)}, s32[14,16,256]{2,1,0:T(8,128)S(1)}, u32[]{:S(2)}, u32[]{:S(2)}) collective-permute-start(s32[14,16,256]{2,1,0:T(8,128)S(1)} %shard_map.74._), channel_id=1, source_target_pairs={{64,0},{128,64},{192,128},{256,192},{320,256},{384,320},{448,384},... | collective-permute-start | bytes 688136 | tf_op jit(solution)/shard_map/ppermute | solution.py:339
  144.6 10.1 %collective-permute-start.17 = (s32[14,16,256]{2,1,0:T(8,128)S(1)}, s32[14,16,256]{2,1,0:T(8,128)S(1)}, u32[]{:S(2)}, u32[]{:S(2)}) collective-permute-start(s32[14,16,256]{2,1,0:T(8,128)S(1)} %shard_map.76), channel_id=1, source_target_pairs={{64,0},{128,64},{192,128},{256,192},{320,256},{384,320},{448,384},... | collective-permute-start | bytes 688136 | tf_op jit(solution)/shard_map/ppermute | solution.py:339
  151.2 10.0 %collective-permute-start.15 = (s32[14,16,256]{2,1,0:T(8,128)S(1)}, s32[14,16,256]{2,1,0:T(8,128)S(1)}, u32[]{:S(2)}, u32[]{:S(2)}) collective-permute-start(s32[14,16,256]{2,1,0:T(8,128)S(1)} %shard_map.75._), channel_id=1, source_target_pairs={{0,64},{64,128},{128,192},{192,256},{256,320},{320,384},{384,448},... | collective-permute-start | bytes 688136 | tf_op jit(solution)/shard_map/ppermute | solution.py:336

commit v6 on v4

v6 whole, which is shorter than its diff:
```python
import functools

import jax
import jax.numpy as jnp
from jax import lax
from jax.experimental import pallas as pl
from jax.experimental.pallas import tpu as pltpu
from jax.sharding import PartitionSpec as P

HALO = 2
NOISE_SPREAD = 0.05
SCALE = 131072.0
UNIT = 1600.0 / 65535.0
SHOTS = 768
TAIL = 40
ANY = pl.BlockSpec(memory_space=pl.ANY)
VMEM = pl.BlockSpec(memory_space=pltpu.VMEM)
SMEM = pl.BlockSpec(memory_space=pltpu.SMEM)
PARAMS = pltpu.CompilerParams(vmem_limit_bytes=48 * 1024 * 1024)


def fixed(values):
    return jnp.floor(values * SCALE + 0.5).astype(jnp.int32)


def coded(values):
    top = jnp.max(jnp.abs(values), axis=0, keepdims=True)
    scale = jnp.floor(top * (1.0 / UNIT)).astype(jnp.int32) + 1
    steps = jnp.floor(values * (32767.0 / (scale.astype(jnp.float32) * UNIT)) + 0.5)
    return steps.astype(jnp.int32), scale


def decoded(steps, scale):
    return steps.astype(jnp.float32) * (scale.astype(jnp.float32) * (UNIT / 32767.0))


def column_of(row, first, count):
    spot = lax.broadcasted_iota(jnp.int32, (count, row.shape[1]), 1) == (
        lax.broadcasted_iota(jnp.int32, (count, row.shape[1]), 0) + first
    )
    return jnp.sum(jnp.where(spot, row, 0.0), axis=1, keepdims=True)


def group_index():
    return lax.axis_index("row") * lax.axis_size("col") + lax.axis_index("col")


def row_sums(values):
    ones = jnp.ones((8, values.shape[0]), jnp.bfloat16)
    return jnp.dot(ones, values, preferred_element_type=jnp.float32)[0:1, :]


def sums_of(values):
    ones = jnp.ones((values.shape[0], 128), jnp.bfloat16)
    return lax.dot_general(values, ones, (((0,), (0,)), ((), ())), preferred_element_type=jnp.float32)[:, 0:1]


def cut_kernel(soft_ref, head_ref, tail_ref, sems):
    width = soft_ref.shape[1]
    reach = head_ref.shape[1]
    copies = [
        pltpu.make_async_copy(soft_ref.at[:, pl.ds(width - reach, reach)], tail_ref, sems.at[0]),
        pltpu.make_async_copy(soft_ref.at[:, pl.ds(0, reach)], head_ref, sems.at[1]),
    ]
    for copy in copies:
        copy.start()
    for copy in copies:
        copy.wait()


def cut_call(soft, reach):
    shape = jax.ShapeDtypeStruct((soft.shape[0], reach), soft.dtype)
    return pl.pallas_call(
        cut_kernel,
        out_shape=[shape, shape],
        in_specs=[ANY],
        out_specs=[VMEM, VMEM],
        scratch_shapes=[pltpu.SemaphoreType.DMA((2,))],
        compiler_params=PARAMS,
        cost_estimate=pl.CostEstimate(flops=0, bytes_accessed=3_000_000, transcendentals=0),
    )(soft)


def ready_kernel(
    width, slots, own_ref, inc_ref, keyt_ref, probt_ref, _,
    fit_ref, vals_ref, hot_ref, self_ref, small_ref,
):
    blocks = own_ref.shape[1] // width
    edges = inc_ref.shape[2]
    pieces = edges // width
    for b in range(blocks):
        own = own_ref[:, b * width : (b + 1) * width]
        tile = lax.dot_general(own, own, (((0,), (0,)), ((), ())), preferred_element_type=jnp.float32)
        self_ref[b] = tile - sums_of(own) * row_sums(own) * (1.0 / own.shape[0])
        rows_x = inc_ref[0, b : b + 1, :]
        slot_x = inc_ref[1, b : b + 1, :]
        cols_x = inc_ref[2, b : b + 1, :]
        lines = lax.broadcasted_iota(jnp.int32, (width, edges), 0)
        row_hot = (lines == rows_x).astype(jnp.bfloat16)
        for k in range(slots):
            hot_ref[b, k * width : (k + 1) * width, :] = (
                lines == jnp.where(slot_x == k, cols_x, -1)
            ).astype(jnp.bfloat16)
        vals = jnp.dot(own, row_hot, preferred_element_type=jnp.float32)
        vals_ref[b] = vals.astype(jnp.bfloat16)
        total = jnp.sum(vals, axis=0, keepdims=True)
        for p in range(pieces):
            n = b * pieces + p
            small_ref[n : n + 1, :] = total[:, p * width : (p + 1) * width]
        key = slot_x * (width * width) + rows_x * width + cols_x
        same = keyt_ref[:, b : b + 1] == key
        fit_ref[b : b + 1, :] = jnp.sum(jnp.where(same, probt_ref[:, b : b + 1], 0.0), axis=0, keepdims=True)


def ready_call(soft, incidence, keys_t, prob_t, after, width, slots):
    shots, own_width = soft.shape
    blocks = own_width // width
    edges = incidence.shape[2]
    return pl.pallas_call(
        functools.partial(ready_kernel, width, slots),
        out_shape=[
            jax.ShapeDtypeStruct((blocks, edges), jnp.float32),
            jax.ShapeDtypeStruct((blocks, shots, edges), jnp.bfloat16),
            jax.ShapeDtypeStruct((blocks, slots * width, edges), jnp.bfloat16),
            jax.ShapeDtypeStruct((blocks, width, width), jnp.float32),
            jax.ShapeDtypeStruct((blocks * edges // width, width), jnp.float32),
        ],
        in_specs=[VMEM] * 4 + [ANY],
        out_specs=[VMEM] * 5,
        compiler_params=PARAMS,
        cost_estimate=pl.CostEstimate(flops=20_000_000_000, bytes_accessed=12_000_000, transcendentals=0),
    )(soft, incidence, keys_t, prob_t, after)


def pair_kernel(
    upper, width, groups, partners_ref, halo_ref, own_ref, vals_ref, hot_ref, self_ref, early_ref, _,
    cov_ref, edge_ref, sums_ref, win,
):
    blocks, slots = partners_ref.shape
    mine = blocks // 2
    low = mine * upper
    reach = HALO * width
    own_width = own_ref.shape[1]
    shots = own_ref.shape[0]
    share = width // groups
    pieces = hot_ref.shape[2] // width
    me = lax.axis_index("shot")
    base = group_index() * blocks
    if upper:
        win[:, 0:own_width] = own_ref[...]
        win[:, own_width:] = halo_ref[...]
        window_first = base + low - HALO
    else:
        win[:, 0:reach] = halo_ref[...]
        win[:, reach:] = own_ref[...]
        window_first = base - HALO
    products, others = [], []
    for b in range(mine):
        block = low + b
        own = win[:, reach + b * width : reach + (b + 1) * width]
        chosen = [own]
        for k in range(1, slots):
            partner = partners_ref[block, k]
            partner = jnp.where(partner >= 0, partner, base + block)
            start = pl.multiple_of((partner - window_first) * width, width)
            chosen.append(win[:, pl.ds(start, width)])
        chosen = jnp.concatenate(chosen, axis=1)
        tiles = lax.dot_general(
            own, chosen[:, width:], (((0,), (0,)), ((), ())), preferred_element_type=jnp.float32
        )
        tiles = tiles - sums_of(own) * (row_sums(chosen[:, width:]) * (1.0 / shots))
        for d in range(groups):
            rows = slice(d * share, (d + 1) * share)
            at = lax.rem(d - me + groups, groups)
            cov_ref[at, b * slots] = self_ref[block, rows, :]
            for k in range(1, slots):
                cov_ref[at, b * slots + k] = tiles[rows, (k - 1) * width : k * width]
        other = jnp.dot(chosen, hot_ref[block], preferred_element_type=jnp.float32)
        product = jnp.sum(vals_ref[block].astype(jnp.float32) * other, axis=0, keepdims=True)
        other = jnp.sum(other, axis=0, keepdims=True)
        products += [product[:, p * width : (p + 1) * width] for p in range(pieces)]
        others += [other[:, p * width : (p + 1) * width] for p in range(pieces)]
    low_col = reach if upper else 0
    columns = row_sums(win[:, low_col : low_col + 4 * width])
    sums_ref[...] = fixed(jnp.concatenate([columns[:, p * width : (p + 1) * width] for p in range(4)], axis=0))
    early = early_ref[upper * mine * pieces : (upper + 1) * mine * pieces, :]
    edge_ref[...] = fixed(jnp.concatenate(products + [early] + others, axis=0))


def pair_call(upper, partners, halo, soft, vals, hot, selfs, early, after, width, groups):
    blocks, slots = partners.shape
    mine = blocks // 2
    return pl.pallas_call(
        functools.partial(pair_kernel, upper, width, groups),
        out_shape=[
            jax.ShapeDtypeStruct((groups, mine * slots, width // groups, width), jnp.float32),
            jax.ShapeDtypeStruct((3 * mine * hot.shape[2] // width, width), jnp.int32),
            jax.ShapeDtypeStruct((mine + HALO, width), jnp.int32),
        ],
        in_specs=[SMEM] + [VMEM] * 6 + [ANY],
        out_specs=[VMEM] * 3,
        scratch_shapes=[pltpu.VMEM((soft.shape[0], soft.shape[1] + halo.shape[1]), jnp.bfloat16)],
        compiler_params=PARAMS,
        cost_estimate=pl.CostEstimate(flops=3_000_000_000, bytes_accessed=4_000_000, transcendentals=0),
    )(partners, halo, soft, vals, hot, selfs, early, after)


def partner_row(partners_ref, block, k, base):
    partner = partners_ref[block, k]
    return jnp.where(partner >= 0, partner - base, block) + HALO


def words_of(came_ref, word, share):
    words = came_ref[word * share : (word + 1) * share, :]
    at = came_ref.shape[0] - TAIL + word
    scales = came_ref[at : at + 1, :]
    low = decoded(lax.shift_right_arithmetic(words << 16, 16), scales & 65535)
    high = decoded(lax.shift_right_arithmetic(words, 16), lax.shift_right_logical(scales, 16))
    return low, high


def hop_kernel(at, seen, partners_ref, *refs):
    came_ref = refs[0] if seen else None
    cov_l, cov_u, edge_l, edge_u, sums_l, sums_u, _, out_ref, own_means, shift = refs[-10:]
    blocks, slots = partners_ref.shape
    share, width = cov_l.shape[2:]
    mine = blocks // 2
    groups = cov_l.shape[0]
    base = group_index() * blocks
    words = blocks * slots // 2
    body = words * share
    quarter = edge_l.shape[0] // 3
    shots = SHOTS
    sums = jnp.concatenate([sums_l[...], sums_u[...]], axis=0)
    edges = jnp.concatenate(
        [part[n * quarter : (n + 1) * quarter, :] for n in range(3) for part in (edge_l, edge_u)], axis=0
    )
    if seen:
        old = came_ref[body + words : body + words + 8, :]
        shift[...] = old.astype(jnp.float32) * (1.0 / (SCALE * shots * seen)) - sums.astype(jnp.float32) * (
            1.0 / (SCALE * shots)
        )
        sums = sums + old
        edges = edges + came_ref[body + words + 8 :, :]
        weight = float(shots) * seen / (seen + 1)
    dest = lax.rem(lax.axis_index("shot") + at, groups)
    for block in range(blocks):
        cov_ref, b = (cov_l, block) if block < mine else (cov_u, block - mine)
        if seen:
            column = column_of(shift[block + HALO : block + HALO + 1, :], dest * share, share) * weight
        for pair in range(slots // 2):
            word = block * (slots // 2) + pair
            values = [cov_ref[at, b * slots + 2 * pair + i] for i in range(2)]
            if seen:
                came = words_of(came_ref, word, share)
                for i in range(2):
                    row = shift[pl.ds(partner_row(partners_ref, block, 2 * pair + i, base), 1), :]
                    values[i] = values[i] + came[i] + column * row
            (low, low_scale), (high, high_scale) = coded(values[0]), coded(values[1])
            out_ref[word * share : (word + 1) * share, :] = (high << 16) | (low & 65535)
            out_ref[body + word : body + word + 1, :] = (high_scale << 16) | low_scale
    out_ref[body + words : body + words + 8, :] = sums
    out_ref[body + words + 8 :, :] = edges


def hop_call(at, seen, partners, came, parts, after):
    (cov_l, edge_l, sums_l), (cov_u, edge_u, sums_u) = parts
    share, width = cov_l.shape[2:]
    body = 2 * cov_l.shape[1] * share // 2
    came = (came,) if seen else ()
    return pl.pallas_call(
        functools.partial(hop_kernel, at, seen),
        out_shape=jax.ShapeDtypeStruct((body + TAIL, width), jnp.int32),
        in_specs=[SMEM] + [VMEM] * (6 + len(came)) + [ANY],
        out_specs=VMEM,
        scratch_shapes=[pltpu.VMEM((8, width), jnp.float32), pltpu.VMEM((8, width), jnp.float32)],
        compiler_params=PARAMS,
        cost_estimate=pl.CostEstimate(flops=1_000_000, bytes_accessed=600_000, transcendentals=0),
    )(partners, *came, cov_l, cov_u, edge_l, edge_u, sums_l, sums_u, after)


def final_kernel(
    rises, falls, partners_ref, inc_ref, rising_ref, falling_ref,
    cov_l, cov_u, edge_l, edge_u, sums_l, sums_u, fit_ref,
    pair_ref, grad_ref, first_shift, second_shift, totals,
):
    blocks, slots = partners_ref.shape
    mine = blocks // 2
    groups = cov_l.shape[0]
    share, width = cov_l.shape[2:]
    pieces = inc_ref.shape[2] // width
    quarter = edge_l.shape[0] // 3
    words = blocks * slots // 2
    body = words * share
    shots = SHOTS
    count = float(shots * groups)
    base = group_index() * blocks
    start = lax.axis_index("shot") * share
    sums = jnp.concatenate([sums_l[...], sums_u[...]], axis=0)
    rise_sums = rising_ref[body + words : body + words + 8, :]
    fall_sums = falling_ref[body + words : body + words + 8, :]

    def mean(values, sources):
        return values.astype(jnp.float32) * (1.0 / (SCALE * shots * sources))

    first_shift[...] = mean(rise_sums, rises) - mean(sums, 1)
    second_shift[...] = mean(fall_sums, falls) - mean(sums + rise_sums, rises + 1)
    totals[...] = (sums + rise_sums + fall_sums).astype(jnp.float32) * (1.0 / SCALE)
    first_weight = float(shots) * rises / (rises + 1)
    second_weight = float(shots) * falls * (rises + 1) / (rises + 1 + falls)
    edges = jnp.concatenate(
        [part[n * quarter : (n + 1) * quarter, :] for n in range(3) for part in (edge_l, edge_u)], axis=0
    )
    edges = edges + rising_ref[body + words + 8 :, :] + falling_ref[body + words + 8 :, :]
    edges = edges.astype(jnp.float32) * (1.0 / SCALE)
    for block in range(blocks):
        cov_ref, b = (cov_l, block) if block < mine else (cov_u, block - mine)
        own = slice(block + HALO, block + HALO + 1)
        first_column = column_of(first_shift[own, :], start, share) * first_weight
        second_column = column_of(second_shift[own, :], start, share) * second_weight
        total_column = column_of(totals[own, :], start, share) * (1.0 / count)
        for pair in range(slots // 2):
            word = block * (slots // 2) + pair
            risen, fallen = words_of(rising_ref, word, share), words_of(falling_ref, word, share)
            for i in range(2):
                k = 2 * pair + i
                at = pl.ds(partner_row(partners_ref, block, k, base), 1)
                live = jnp.where(partners_ref[block, k] >= 0, 1.0, 0.0)
                cov = cov_ref[0, b * slots + k] + risen[i] + first_column * first_shift[at, :]
                cov = cov + fallen[i] + second_column * second_shift[at, :]
                alone = total_column * totals[at, :]
                entry = 0.5 - 0.5 * jnp.sqrt(alone / (alone + cov))
                pair_ref[block, k] = (entry * live).astype(jnp.bfloat16)
        for p in range(pieces):
            n = block * pieces + p
            at = slice(p * width, (p + 1) * width)
            slot_x = inc_ref[1, block : block + 1, at]
            live = jnp.zeros((1, width), jnp.float32)
            for k in range(slots):
                live = live + jnp.where((slot_x == k) & (partners_ref[block, k] >= 0), 1.0, 0.0)
            rows = 2 * quarter
            quotient = (edges[rows + n : rows + n + 1] / count) * (
                edges[2 * rows + n : 2 * rows + n + 1] / count
            ) * count / edges[n : n + 1]
            entry = (0.5 - 0.5 * jnp.sqrt(quotient)) * live
            residual = live * (entry - fit_ref[block : block + 1, at]) / NOISE_SPREAD
            grad_ref[block : block + 1, at] = -residual / NOISE_SPREAD


def final_call(partners, incidence, rising, falling, parts, fit):
    (cov_l, edge_l, sums_l), (cov_u, edge_u, sums_u) = parts
    blocks, slots = partners.shape
    groups, _, share, width = cov_l.shape
    half = groups // 2
    return pl.pallas_call(
        functools.partial(final_kernel, half, groups - 1 - half),
        out_shape=[
            jax.ShapeDtypeStruct((blocks, slots, share, width), jnp.bfloat16),
            jax.ShapeDtypeStruct((blocks, incidence.shape[2]), jnp.float32),
        ],
        in_specs=[SMEM] + [VMEM] * 10,
        out_specs=[VMEM] * 2,
        scratch_shapes=[pltpu.VMEM((8, width), jnp.float32)] * 3,
        compiler_params=PARAMS,
        cost_estimate=pl.CostEstimate(flops=1_000_000, bytes_accessed=2_000_000, transcendentals=100_000),
    )(partners, incidence, rising, falling, cov_l, cov_u, edge_l, edge_u, sums_l, sums_u, fit)


def local(soft, partners, incidence, edge_prob):
    shots, own_width = soft.shape
    blocks, slots = partners.shape
    width = own_width // blocks
    groups = lax.axis_size("shot")
    sides = lax.axis_size(("row", "col"))

    head, tail = cut_call(soft, HALO * width)
    left = lax.ppermute(tail, ("row", "col"), [(i, (i + 1) % sides) for i in range(sides)])
    right = lax.ppermute(head, ("row", "col"), [((i + 1) % sides, i) for i in range(sides)])

    keys = incidence[1] * (width * width) + incidence[0] * width + incidence[2]
    fit, vals, hot, selfs, early = ready_call(soft, incidence, keys.T, edge_prob.T, tail, width, slots)
    args = (soft, vals, hot, selfs, early)
    lower = pair_call(0, partners, left, *args, early, width, groups)
    upper = pair_call(1, partners, right, *args, lower[1], width, groups)
    parts = (lower, upper)

    half = groups // 2
    rise = [(i, (i + 1) % groups) for i in range(groups)]
    fall = [(b, a) for a, b in rise]
    rising = falling = None
    order = early
    for step in range(half):
        order = hop_call(half - step, step, partners, rising, parts, order)
        rising = lax.ppermute(order, "shot", rise)
        if step < half - 1:
            order = hop_call(half + 1 + step, step, partners, falling, parts, order)
            falling = lax.ppermute(order, "shot", fall)
    return final_call(partners, incidence, rising, falling, parts, fit)


def solution(mesh):
    placed = (
        P("shot", ("row", "col")),
        P(("row", "col"), None),
        P(None, ("row", "col"), None),
        P(("row", "col"), None),
    )
    return jax.shard_map(
        local,
        mesh=mesh,
        in_specs=placed,
        out_specs=(P(("row", "col"), None, "shot", None), P(("row", "col"), None)),
        check_vma=False,
    )
```

time: 137 us -> 131 us (0.956)
  Pallas kernels: 21.3 us -> 34.8 us
  waiting for transfers between devices: 39.7 us -> 26.5 us
  starting transfers between devices: 72.1 us -> 65.2 us
    ppermute x2 -> x0, starting transfers between devices: 13.3 us -> none  [the longest x1 9.5 us: local(): falling = lax.ppermute(first_down, 'shot', fall)]
    pallas_call x15 -> x16, Pallas kernels: 2.55 us -> 14 us  [the longest x15 12.4 us: hop_call(): pl.pallas_call(functools.partial(hop_kernel, at, seen), out_shape=jax.Sha...]
    ppermute x7, waiting for transfers between devices: 10.7 us -> 0.72 us  [local(): falling = lax.ppermute(order, 'shot', fall)]
    ppermute x7 -> x8, starting transfers between devices: 13.4 us -> 17.3 us  [local(): rising = lax.ppermute(order, 'shot', rise)]
    ppermute x7, starting transfers between devices: 39.1 us -> 41.8 us  [local(): falling = lax.ppermute(order, 'shot', fall)]
    ppermute x7 -> x8, waiting for transfers between devices: 12.7 us -> 11.2 us  [local(): rising = lax.ppermute(order, 'shot', rise)]
    pallas_call x2, Pallas kernels: 12.2 us -> 13.6 us  [pair_call(): pl.pallas_call(functools.partial(pair_kernel, upper, width, groups), out_...]
  transfers between devices with their start and end apart: 18 -> 17, of which waited for: 15 -> 11; matrix products, arithmetic and copies ran while one was open for 1% -> 1% of each run, Pallas kernels for 13% -> 19%
where the time goes in v6:
time: 131 us
  starting transfers between devices  65.2 us (50%)
  Pallas kernels  34.8 us (27%)
  waiting for transfers between devices  26.5 us (20%)
  local copies, waits for them, and re-layouts  2.4 us (2%)
    ppermute x7, starting transfers between devices, local(): falling = lax.ppermute(order, 'shot', fall)  41.8 us
    ppermute x8, starting transfers between devices, local(): rising = lax.ppermute(order, 'shot', rise)  17.3 us
    ppermute x1, waiting for transfers between devices, local(): lax.ppermute(tail, ('row', 'col'), [(i, (i + 1) % sides) for i in range(s...  14.6 us
    pallas_call x2, Pallas kernels, pair_call(): pl.pallas_call(functools.partial(pair_kernel, upper, width, groups), out_...  13.6 us
    pallas_call x15, Pallas kernels, hop_call(): pl.pallas_call(functools.partial(hop_kernel, at, seen), out_shape=jax.Sha...  12.4 us
    ppermute x8, waiting for transfers between devices, local(): rising = lax.ppermute(order, 'shot', rise)  11.2 us
    pallas_call x1, Pallas kernels, ready_call(): pl.pallas_call(functools.partial(ready_kernel, width, slots), out_shape=[...  5.77 us
    ppermute x1, starting transfers between devices, local(): lax.ppermute(head, ('row', 'col'), [((i + 1) % sides, i) for i in range(s...  4.29 us
  transfers between devices with their start and end apart: 17, of which 11 were waited for; matrix products, arithmetic and copies ran while one was open for 1% of the time, Pallas kernels for 19%

profile of v6, /device:TPU:24, one launch (start us, length us, event | category | flops | bytes accessed | tf_op | source)
XLA Modules:
  0.0 130.7 jit_solution(6223211261427083927)
XLA Ops:
  2.0 1.4 %shard_map.59 = (bf16[768,512]{1,0:T(8,128)(2,1)}, bf16[768,512]{1,0:T(8,128)(2,1)}) custom-call(bf16[768,1024]{1,0:T(8,128)(2,1)S(1)} %copy-done), custom_call_target="tpu_custom_call" | custom-call | bytes 3000000 | tf_op jit(solution)/shard_map/pallas_call | solution.py:73
  3.5 4.3 %collective-permute-start.1 = (bf16[768,512]{1,0:T(8,128)(2,1)}, bf16[768,512]{1,0:T(8,128)(2,1)S(1)}, u32[]{:S(2)}, u32[]{:S(2)}) collective-permute-start(bf16[768,512]{1,0:T(8,128)(2,1)} %get-tuple-element.21), channel_id=1, source_target_pairs={{1,0},{2,1},{3,2},{4,3},{5,4},{6,5},{7,6},{8,7},{9,8},{10,9},{11,1... | collective-permute-start | bytes 2359304 | tf_op jit(solution)/shard_map/ppermute | solution.py:378
  7.8 1.9 %collective-permute-start = (bf16[768,512]{1,0:T(8,128)(2,1)}, bf16[768,512]{1,0:T(8,128)(2,1)}, u32[]{:S(2)}, u32[]{:S(2)}) collective-permute-start(bf16[768,512]{1,0:T(8,128)(2,1)} %get-tuple-element.15._), channel_id=1, source_target_pairs={{0,1},{1,2},{2,3},{3,4},{4,5},{5,6},{6,7},{7,8},{8,9},{9,10},{10,1... | collective-permute-start | bytes 2359304 | tf_op jit(solution)/shard_map/ppermute | solution.py:377
  11.5 5.8 %shard_map.60 = (f32[4,512]{1,0:T(4,128)S(1)}, bf16[4,768,512]{2,1,0:T(8,128)(2,1)}, bf16[4,1024,512]{2,1,0:T(8,128)(2,1)}, f32[4,256,256]{2,1,0:T(8,128)S(1)}, f32[8,256]{1,0:T(8,128)S(1)}) custom-call(bf16[768,1024]{1,0:T(8,128)(2,1)S(1)} %copy-done.1, s32[3,4,512]{2,1,0:T(4,128)S(1)} %copy-done.3, s32[512,4]{1,0:T(8,128)S(1)} %bitcast.4, ...), custom_call_target="tpu_custom_call" | custom-call | flops 20000000000 | bytes 12000000 | tf_op jit(solution)/shard_map/pallas_call | solution.py:119
  17.3 14.6 %collective-permute-done.halo_ref = bf16[768,512]{1,0:T(8,128)(2,1)} collective-permute-done((bf16[768,512]{1,0:T(8,128)(2,1)}, bf16[768,512]{1,0:T(8,128)(2,1)}, u32[]{:S(2)}, u32[]{:S(2)}) %collective-permute-start) | collective-permute-done | bytes 786464 | tf_op jit(solution)/shard_map/ppermute | solution.py:377
  31.9 6.9 %shard_map.61 = (f32[16,8,16,256]{3,2,1,0:T(8,128)S(1)}, s32[12,256]{1,0:T(8,128)S(1)}, s32[4,256]{1,0:T(4,128)S(1)}) custom-call(s32[4,4]{1,0:T(4,128)S(1)} %copy-done.2, bf16[768,512]{1,0:T(8,128)(2,1)} %collective-permute-done.halo_ref, bf16[768,1024]{1,0:T(8,128)(2,1)S(1)} %copy-done.1, bf16[4,768,512]{2,1,0:T(8,128)(2,1)} %get-tuple-element.16.vals_ref, ...), custom_call_target="tpu_custom_call" | custom-call | flops 3000000000 | bytes 4000000 | tf_op jit(solution)/shard_map/pallas_call | solution.py:193
  38.9 6.7 %shard_map.62 = (f32[16,8,16,256]{3,2,1,0:T(8,128)S(1)}, s32[12,256]{1,0:T(8,128)S(1)}, s32[4,256]{1,0:T(4,128)S(1)}) custom-call(s32[4,4]{1,0:T(4,128)S(1)} %copy-done.2, bf16[768,512]{1,0:T(8,128)(2,1)S(1)} %collective-permute-done.1.halo_ref, bf16[768,1024]{1,0:T(8,128)(2,1)S(1)} %copy-done.1, bf16[4,768,512]{2,1,0:T(8,128)(2,1)} %get-tuple-element.16.vals_ref, ...), custom_call_target="tpu_custom_call" | custom-call | flops 3000000000 | bytes 4000000 | tf_op jit(solution)/shard_map/pallas_call | solution.py:193
  46.3 3.8 %collective-permute-start.2 = (s32[168,256]{1,0:T(8,128)S(1)}, s32[168,256]{1,0:T(8,128)S(1)}, u32[]{:S(2)}, u32[]{:S(2)}) collective-permute-start(s32[168,256]{1,0:T(8,128)S(1)} %shard_map.63.refs_6_), channel_id=1, source_target_pairs={{0,32},{32,64},{64,96},{96,128},{128,160},{160,192},{192,224},{224... | collective-permute-start | bytes 516104 | tf_op jit(solution)/shard_map/ppermute | solution.py:394
  50.8 9.5 %collective-permute-start.4 = (s32[168,256]{1,0:T(8,128)S(1)}, s32[168,256]{1,0:T(8,128)S(1)}, u32[]{:S(2)}, u32[]{:S(2)}) collective-permute-start(s32[168,256]{1,0:T(8,128)S(1)} %shard_map.64.refs_7_), channel_id=1, source_target_pairs={{32,0},{64,32},{96,64},{128,96},{160,128},{192,160},{224,192},{256... | collective-permute-start | bytes 516104 | tf_op jit(solution)/shard_map/ppermute | solution.py:397
  61.9 1.9 %collective-permute-start.3 = (s32[168,256]{1,0:T(8,128)S(1)}, s32[168,256]{1,0:T(8,128)S(1)}, u32[]{:S(2)}, u32[]{:S(2)}) collective-permute-start(s32[168,256]{1,0:T(8,128)S(1)} %shard_map.65.refs_7_), channel_id=1, source_target_pairs={{0,32},{32,64},{64,96},{96,128},{128,160},{160,192},{192,224},{224... | collective-permute-start | bytes 516104 | tf_op jit(solution)/shard_map/ppermute | solution.py:394
  64.7 5.1 %collective-permute-start.6 = (s32[168,256]{1,0:T(8,128)S(1)}, s32[168,256]{1,0:T(8,128)S(1)}, u32[]{:S(2)}, u32[]{:S(2)}) collective-permute-start(s32[168,256]{1,0:T(8,128)S(1)} %shard_map.66.refs_7_), channel_id=1, source_target_pairs={{32,0},{64,32},{96,64},{128,96},{160,128},{192,160},{224,192},{256... | collective-permute-start | bytes 516104 | tf_op jit(solution)/shard_map/ppermute | solution.py:397
  71.2 1.9 %collective-permute-start.5 = (s32[168,256]{1,0:T(8,128)S(1)}, s32[168,256]{1,0:T(8,128)S(1)}, u32[]{:S(2)}, u32[]{:S(2)}) collective-permute-start(s32[168,256]{1,0:T(8,128)S(1)} %shard_map.67.refs_7_), channel_id=1, source_target_pairs={{0,32},{32,64},{64,96},{96,128},{128,160},{160,192},{192,224},{224... | collective-permute-start | bytes 516104 | tf_op jit(solution)/shard_map/ppermute | solution.py:394
  74.0 5.3 %collective-permute-start.8 = (s32[168,256]{1,0:T(8,128)S(1)}, s32[168,256]{1,0:T(8,128)S(1)}, u32[]{:S(2)}, u32[]{:S(2)}) collective-permute-start(s32[168,256]{1,0:T(8,128)S(1)} %shard_map.68.refs_7_), channel_id=1, source_target_pairs={{32,0},{64,32},{96,64},{128,96},{160,128},{192,160},{224,192},{256... | collective-permute-start | bytes 516104 | tf_op jit(solution)/shard_map/ppermute | solution.py:397
  80.6 1.9 %collective-permute-start.7 = (s32[168,256]{1,0:T(8,128)S(1)}, s32[168,256]{1,0:T(8,128)S(1)}, u32[]{:S(2)}, u32[]{:S(2)}) collective-permute-start(s32[168,256]{1,0:T(8,128)S(1)} %shard_map.69.refs_7_), channel_id=1, source_target_pairs={{0,32},{32,64},{64,96},{96,128},{128,160},{160,192},{192,224},{224... | collective-permute-start | bytes 516104 | tf_op jit(solution)/shard_map/ppermute | solution.py:394
  83.4 5.3 %collective-permute-start.10 = (s32[168,256]{1,0:T(8,128)S(1)}, s32[168,256]{1,0:T(8,128)S(1)}, u32[]{:S(2)}, u32[]{:S(2)}) collective-permute-start(s32[168,256]{1,0:T(8,128)S(1)} %shard_map.70.refs_7_), channel_id=1, source_target_pairs={{32,0},{64,32},{96,64},{128,96},{160,128},{192,160},{224,192},{256... | collective-permute-start | bytes 516104 | tf_op jit(solution)/shard_map/ppermute | solution.py:397
  90.0 1.9 %collective-permute-start.9 = (s32[168,256]{1,0:T(8,128)S(1)}, s32[168,256]{1,0:T(8,128)S(1)}, u32[]{:S(2)}, u32[]{:S(2)}) collective-permute-start(s32[168,256]{1,0:T(8,128)S(1)} %shard_map.71.refs_7_), channel_id=1, source_target_pairs={{0,32},{32,64},{64,96},{96,128},{128,160},{160,192},{192,224},{224... | collective-permute-start | bytes 516104 | tf_op jit(solution)/shard_map/ppermute | solution.py:394
  92.8 5.3 %collective-permute-start.12 = (s32[168,256]{1,0:T(8,128)S(1)}, s32[168,256]{1,0:T(8,128)S(1)}, u32[]{:S(2)}, u32[]{:S(2)}) collective-permute-start(s32[168,256]{1,0:T(8,128)S(1)} %shard_map.72.refs_7_), channel_id=1, source_target_pairs={{32,0},{64,32},{96,64},{128,96},{160,128},{192,160},{224,192},{256... | collective-permute-start | bytes 516104 | tf_op jit(solution)/shard_map/ppermute | solution.py:397
  99.3 1.9 %collective-permute-start.11 = (s32[168,256]{1,0:T(8,128)S(1)}, s32[168,256]{1,0:T(8,128)S(1)}, u32[]{:S(2)}, u32[]{:S(2)}) collective-permute-start(s32[168,256]{1,0:T(8,128)S(1)} %shard_map.73.refs_7_), channel_id=1, source_target_pairs={{0,32},{32,64},{64,96},{96,128},{128,160},{160,192},{192,224},{224... | collective-permute-start | bytes 516104 | tf_op jit(solution)/shard_map/ppermute | solution.py:394
  102.3 5.6 %collective-permute-start.14 = (s32[168,256]{1,0:T(8,128)S(1)}, s32[168,256]{1,0:T(8,128)S(1)}, u32[]{:S(2)}, u32[]{:S(2)}) collective-permute-start(s32[168,256]{1,0:T(8,128)S(1)} %shard_map.74.refs_7_), channel_id=1, source_target_pairs={{32,0},{64,32},{96,64},{128,96},{160,128},{192,160},{224,192},{256... | collective-permute-start | bytes 516104 | tf_op jit(solution)/shard_map/ppermute | solution.py:397
  109.9 1.9 %collective-permute-start.13 = (s32[168,256]{1,0:T(8,128)S(1)}, s32[168,256]{1,0:T(8,128)S(1)}, u32[]{:S(2)}, u32[]{:S(2)}) collective-permute-start(s32[168,256]{1,0:T(8,128)S(1)} %shard_map.75.refs_7_), channel_id=1, source_target_pairs={{0,32},{32,64},{64,96},{96,128},{128,160},{160,192},{192,224},{224... | collective-permute-start | bytes 516104 | tf_op jit(solution)/shard_map/ppermute | solution.py:394
  113.2 5.6 %collective-permute-start.16 = (s32[168,256]{1,0:T(8,128)S(1)}, s32[168,256]{1,0:T(8,128)S(1)}, u32[]{:S(2)}, u32[]{:S(2)}) collective-permute-start(s32[168,256]{1,0:T(8,128)S(1)} %shard_map.76.refs_7_), channel_id=1, source_target_pairs={{32,0},{64,32},{96,64},{128,96},{160,128},{192,160},{224,192},{256... | collective-permute-start | bytes 516104 | tf_op jit(solution)/shard_map/ppermute | solution.py:397
  120.6 1.9 %collective-permute-start.15 = (s32[168,256]{1,0:T(8,128)S(1)}, s32[168,256]{1,0:T(8,128)S(1)}, u32[]{:S(2)}, u32[]{:S(2)}) collective-permute-start(s32[168,256]{1,0:T(8,128)S(1)} %shard_map.77), channel_id=1, source_target_pairs={{0,32},{32,64},{64,96},{96,128},{128,160},{160,192},{192,224},{224... | collective-permute-start | bytes 516104 | tf_op jit(solution)/shard_map/ppermute | solution.py:394
  122.5 6.6 %collective-permute-done.15.rising_ref = s32[168,256]{1,0:T(8,128)S(1)} collective-permute-done((s32[168,256]{1,0:T(8,128)S(1)}, s32[168,256]{1,0:T(8,128)S(1)}, u32[]{:S(2)}, u32[]{:S(2)}) %collective-permute-start.15) | collective-permute-done | bytes 172064 | tf_op jit(solution)/shard_map/ppermute | solution.py:394
  129.1 1.6 %shard_map.78 = (bf16[4,4,16,256]{3,2,1,0:T(8,128)(2,1)}, f32[4,512]{1,0:T(4,128)}) custom-call(s32[4,4]{1,0:T(4,128)S(1)} %copy-done.2, s32[3,4,512]{2,1,0:T(4,128)S(1)} %copy-done.3, s32[168,256]{1,0:T(8,128)S(1)} %collective-permute-done.15.rising_ref, s32[168,256]{1,0:T(8,128)S(1)} %collective-permute-done.16.falling_ref, ...), custom_call_target="tpu_custom_call" | custom-call | flops 1000000 | bytes 2000000 | tf_op jit(solution)/shard_map/pallas_call | solution.py:355
  (41 shorter events, 20.9 us)
Async XLA Ops:
  0.6 1.4 %copy-start = (bf16[768,1024]{1,0:T(8,128)(2,1)S(1)}, bf16[768,1024]{1,0:T(8,128)(2,1)}, u32[]{:S(2)}) copy-start(bf16[768,1024]{1,0:T(8,128)(2,1)} %own_ref.5) | copy-start | bytes 4718596
  2.0 9.4 %copy-start.1 = (bf16[768,1024]{1,0:T(8,128)(2,1)S(1)}, bf16[768,1024]{1,0:T(8,128)(2,1)}, u32[]{:S(2)}) copy-start(bf16[768,1024]{1,0:T(8,128)(2,1)} %own_ref.5) | copy-start | bytes 4718596
  2.0 9.4 %copy-start.3 = (s32[3,4,512]{2,1,0:T(4,128)S(1)}, s32[3,4,512]{2,1,0:T(4,128)}, u32[]{:S(2)}) copy-start(s32[3,4,512]{2,1,0:T(4,128)} %inc_ref.3) | copy-start | bytes 73732
  3.5 35.4 %collective-permute-start.1 = (bf16[768,512]{1,0:T(8,128)(2,1)}, bf16[768,512]{1,0:T(8,128)(2,1)S(1)}, u32[]{:S(2)}, u32[]{:S(2)}) collective-permute-start(bf16[768,512]{1,0:T(8,128)(2,1)} %get-tuple-element.21), channel_id=1, source_target_pairs={{1,0},{2,1},{3,2},{4,3},{5,4},{6,5},{7,6},{8,7},{9,8},{10,9},{11,1... | collective-permute-start | bytes 2359304 | tf_op jit(solution)/shard_map/ppermute | solution.py:378
  7.8 24.1 %collective-permute-start = (bf16[768,512]{1,0:T(8,128)(2,1)}, bf16[768,512]{1,0:T(8,128)(2,1)}, u32[]{:S(2)}, u32[]{:S(2)}) collective-permute-start(bf16[768,512]{1,0:T(8,128)(2,1)} %get-tuple-element.15._), channel_id=1, source_target_pairs={{0,1},{1,2},{2,3},{3,4},{4,5},{5,6},{6,7},{7,8},{8,9},{9,10},{10,1... | collective-permute-start | bytes 2359304 | tf_op jit(solution)/shard_map/ppermute | solution.py:377
  11.5 20.4 %copy-start.2 = (s32[4,4]{1,0:T(4,128)S(1)}, s32[4,4]{1,0:T(4,128)}, u32[]{:S(2)}) copy-start(s32[4,4]{1,0:T(4,128)} %partners_ref.35) | copy-start | bytes 196
  46.3 14.8 %collective-permute-start.2 = (s32[168,256]{1,0:T(8,128)S(1)}, s32[168,256]{1,0:T(8,128)S(1)}, u32[]{:S(2)}, u32[]{:S(2)}) collective-permute-start(s32[168,256]{1,0:T(8,128)S(1)} %shard_map.63.refs_6_), channel_id=1, source_target_pairs={{0,32},{32,64},{64,96},{96,128},{128,160},{160,192},{192,224},{224... | collective-permute-start | bytes 516104 | tf_op jit(solution)/shard_map/ppermute | solution.py:394
  50.8 13.0 %collective-permute-start.4 = (s32[168,256]{1,0:T(8,128)S(1)}, s32[168,256]{1,0:T(8,128)S(1)}, u32[]{:S(2)}, u32[]{:S(2)}) collective-permute-start(s32[168,256]{1,0:T(8,128)S(1)} %shard_map.64.refs_7_), channel_id=1, source_target_pairs={{32,0},{64,32},{96,64},{128,96},{160,128},{192,160},{224,192},{256... | collective-permute-start | bytes 516104 | tf_op jit(solution)/shard_map/ppermute | solution.py:397
  61.9 8.5 %collective-permute-start.3 = (s32[168,256]{1,0:T(8,128)S(1)}, s32[168,256]{1,0:T(8,128)S(1)}, u32[]{:S(2)}, u32[]{:S(2)}) collective-permute-start(s32[168,256]{1,0:T(8,128)S(1)} %shard_map.65.refs_7_), channel_id=1, source_target_pairs={{0,32},{32,64},{64,96},{96,128},{128,160},{160,192},{192,224},{224... | collective-permute-start | bytes 516104 | tf_op jit(solution)/shard_map/ppermute | solution.py:394
  64.7 8.5 %collective-permute-start.6 = (s32[168,256]{1,0:T(8,128)S(1)}, s32[168,256]{1,0:T(8,128)S(1)}, u32[]{:S(2)}, u32[]{:S(2)}) collective-permute-start(s32[168,256]{1,0:T(8,128)S(1)} %shard_map.66.refs_7_), channel_id=1, source_target_pairs={{32,0},{64,32},{96,64},{128,96},{160,128},{192,160},{224,192},{256... | collective-permute-start | bytes 516104 | tf_op jit(solution)/shard_map/ppermute | solution.py:397
  71.2 8.5 %collective-permute-start.5 = (s32[168,256]{1,0:T(8,128)S(1)}, s32[168,256]{1,0:T(8,128)S(1)}, u32[]{:S(2)}, u32[]{:S(2)}) collective-permute-start(s32[168,256]{1,0:T(8,128)S(1)} %shard_map.67.refs_7_), channel_id=1, source_target_pairs={{0,32},{32,64},{64,96},{96,128},{128,160},{160,192},{192,224},{224... | collective-permute-start | bytes 516104 | tf_op jit(solution)/shard_map/ppermute | solution.py:394
  74.0 8.5 %collective-permute-start.8 = (s32[168,256]{1,0:T(8,128)S(1)}, s32[168,256]{1,0:T(8,128)S(1)}, u32[]{:S(2)}, u32[]{:S(2)}) collective-permute-start(s32[168,256]{1,0:T(8,128)S(1)} %shard_map.68.refs_7_), channel_id=1, source_target_pairs={{32,0},{64,32},{96,64},{128,96},{160,128},{192,160},{224,192},{256... | collective-permute-start | bytes 516104 | tf_op jit(solution)/shard_map/ppermute | solution.py:397
  80.6 8.5 %collective-permute-start.7 = (s32[168,256]{1,0:T(8,128)S(1)}, s32[168,256]{1,0:T(8,128)S(1)}, u32[]{:S(2)}, u32[]{:S(2)}) collective-permute-start(s32[168,256]{1,0:T(8,128)S(1)} %shard_map.69.refs_7_), channel_id=1, source_target_pairs={{0,32},{32,64},{64,96},{96,128},{128,160},{160,192},{192,224},{224... | collective-permute-start | bytes 516104 | tf_op jit(solution)/shard_map/ppermute | solution.py:394
  83.4 8.5 %collective-permute-start.10 = (s32[168,256]{1,0:T(8,128)S(1)}, s32[168,256]{1,0:T(8,128)S(1)}, u32[]{:S(2)}, u32[]{:S(2)}) collective-permute-start(s32[168,256]{1,0:T(8,128)S(1)} %shard_map.70.refs_7_), channel_id=1, source_target_pairs={{32,0},{64,32},{96,64},{128,96},{160,128},{192,160},{224,192},{256... | collective-permute-start | bytes 516104 | tf_op jit(solution)/shard_map/ppermute | solution.py:397
  90.0 8.5 %collective-permute-start.9 = (s32[168,256]{1,0:T(8,128)S(1)}, s32[168,256]{1,0:T(8,128)S(1)}, u32[]{:S(2)}, u32[]{:S(2)}) collective-permute-start(s32[168,256]{1,0:T(8,128)S(1)} %shard_map.71.refs_7_), channel_id=1, source_target_pairs={{0,32},{32,64},{64,96},{96,128},{128,160},{160,192},{192,224},{224... | collective-permute-start | bytes 516104 | tf_op jit(solution)/shard_map/ppermute | solution.py:394
  92.8 8.7 %collective-permute-start.12 = (s32[168,256]{1,0:T(8,128)S(1)}, s32[168,256]{1,0:T(8,128)S(1)}, u32[]{:S(2)}, u32[]{:S(2)}) collective-permute-start(s32[168,256]{1,0:T(8,128)S(1)} %shard_map.72.refs_7_), channel_id=1, source_target_pairs={{32,0},{64,32},{96,64},{128,96},{160,128},{192,160},{224,192},{256... | collective-permute-start | bytes 516104 | tf_op jit(solution)/shard_map/ppermute | solution.py:397
  99.3 9.7 %collective-permute-start.11 = (s32[168,256]{1,0:T(8,128)S(1)}, s32[168,256]{1,0:T(8,128)S(1)}, u32[]{:S(2)}, u32[]{:S(2)}) collective-permute-start(s32[168,256]{1,0:T(8,128)S(1)} %shard_map.73.refs_7_), channel_id=1, source_target_pairs={{0,32},{32,64},{64,96},{96,128},{128,160},{160,192},{192,224},{224... | collective-permute-start | bytes 516104 | tf_op jit(solution)/shard_map/ppermute | solution.py:394
  102.3 10.1 %collective-permute-start.14 = (s32[168,256]{1,0:T(8,128)S(1)}, s32[168,256]{1,0:T(8,128)S(1)}, u32[]{:S(2)}, u32[]{:S(2)}) collective-permute-start(s32[168,256]{1,0:T(8,128)S(1)} %shard_map.74.refs_7_), channel_id=1, source_target_pairs={{32,0},{64,32},{96,64},{128,96},{160,128},{192,160},{224,192},{256... | collective-permute-start | bytes 516104 | tf_op jit(solution)/shard_map/ppermute | solution.py:397
  109.9 9.9 %collective-permute-start.13 = (s32[168,256]{1,0:T(8,128)S(1)}, s32[168,256]{1,0:T(8,128)S(1)}, u32[]{:S(2)}, u32[]{:S(2)}) collective-permute-start(s32[168,256]{1,0:T(8,128)S(1)} %shard_map.75.refs_7_), channel_id=1, source_target_pairs={{0,32},{32,64},{64,96},{96,128},{128,160},{160,192},{192,224},{224... | collective-permute-start | bytes 516104 | tf_op jit(solution)/shard_map/ppermute | solution.py:394
  113.2 9.3 %collective-permute-start.16 = (s32[168,256]{1,0:T(8,128)S(1)}, s32[168,256]{1,0:T(8,128)S(1)}, u32[]{:S(2)}, u32[]{:S(2)}) collective-permute-start(s32[168,256]{1,0:T(8,128)S(1)} %shard_map.76.refs_7_), channel_id=1, source_target_pairs={{32,0},{64,32},{96,64},{128,96},{160,128},{192,160},{224,192},{256... | collective-permute-start | bytes 516104 | tf_op jit(solution)/shard_map/ppermute | solution.py:397
  120.6 8.5 %collective-permute-start.15 = (s32[168,256]{1,0:T(8,128)S(1)}, s32[168,256]{1,0:T(8,128)S(1)}, u32[]{:S(2)}, u32[]{:S(2)}) collective-permute-start(s32[168,256]{1,0:T(8,128)S(1)} %shard_map.77), channel_id=1, source_target_pairs={{0,32},{32,64},{64,96},{96,128},{128,160},{160,192},{192,224},{224... | collective-permute-start | bytes 516104 | tf_op jit(solution)/shard_map/ppermute | solution.py:394

commit v7 on v6

v7 whole, which is shorter than its diff:
```python
import functools

import jax
import jax.numpy as jnp
from jax import lax
from jax.experimental import pallas as pl
from jax.experimental.pallas import tpu as pltpu
from jax.sharding import PartitionSpec as P

HALO = 2
NOISE_SPREAD = 0.05
SCALE = 131072.0
UNIT = 1600.0 / 65535.0
SHOTS = 768
TAIL = 40
ANY = pl.BlockSpec(memory_space=pl.ANY)
VMEM = pl.BlockSpec(memory_space=pltpu.VMEM)
SMEM = pl.BlockSpec(memory_space=pltpu.SMEM)
HBM = pl.BlockSpec(memory_space=pltpu.HBM)
PARAMS = pltpu.CompilerParams(vmem_limit_bytes=20 * 1024 * 1024)


def fixed(values):
    return jnp.floor(values * SCALE + 0.5).astype(jnp.int32)


def column_of(row, first, count):
    spot = lax.broadcasted_iota(jnp.int32, (count, row.shape[1]), 1) == (
        lax.broadcasted_iota(jnp.int32, (count, row.shape[1]), 0) + first
    )
    return jnp.sum(jnp.where(spot, row, 0.0), axis=1, keepdims=True)


def group_index():
    return lax.axis_index("row") * lax.axis_size("col") + lax.axis_index("col")


def row_sums(values):
    ones = jnp.ones((8, values.shape[0]), jnp.bfloat16)
    return jnp.dot(ones, values, preferred_element_type=jnp.float32)[0:1, :]


def sums_of(values):
    ones = jnp.ones((values.shape[0], 128), jnp.bfloat16)
    return lax.dot_general(values, ones, (((0,), (0,)), ((), ())), preferred_element_type=jnp.float32)[:, 0:1]


def cut_kernel(soft_ref, head_ref, tail_ref, done_ref, sems):
    width = soft_ref.shape[1]
    reach = head_ref.shape[1]
    copies = [
        pltpu.make_async_copy(soft_ref.at[:, pl.ds(width - reach, reach)], tail_ref, sems.at[0]),
        pltpu.make_async_copy(soft_ref.at[:, pl.ds(0, reach)], head_ref, sems.at[1]),
    ]
    for copy in copies:
        copy.start()
    done_ref[...] = jnp.zeros_like(done_ref)
    for copy in copies:
        copy.wait()


def cut_call(soft, reach):
    shape = jax.ShapeDtypeStruct((soft.shape[0], reach), soft.dtype)
    return pl.pallas_call(
        cut_kernel,
        out_shape=[shape, shape, jax.ShapeDtypeStruct((8, 128), jnp.float32)],
        in_specs=[HBM],
        out_specs=[VMEM, VMEM, VMEM],
        scratch_shapes=[pltpu.SemaphoreType.DMA((2,))],
        compiler_params=pltpu.CompilerParams(vmem_limit_bytes=58 * 1024 * 1024),
        cost_estimate=pl.CostEstimate(flops=0, bytes_accessed=3_000_000, transcendentals=0),
    )(soft)


def spread(cov_ref, slot, tile, me):
    groups, _, share, _ = cov_ref.shape
    for d in range(groups):
        at = lax.rem(d - me + groups, groups)
        cov_ref[at, slot] = tile[d * share : (d + 1) * share, :]


def rows_of(row, pieces):
    width = row.shape[1] // pieces
    return [row[:, p * width : (p + 1) * width] for p in range(pieces)]


def ready_kernel(
    width, partners_ref, own_ref, inc_ref, keyt_ref, probt_ref, _,
    fit_ref, vals_ref, hot_ref, lower_ref, upper_ref, early_ref, sums_ref,
):
    blocks, slots = partners_ref.shape
    mine = blocks // 2
    shots = own_ref.shape[0]
    edges = inc_ref.shape[2]
    pieces = edges // width
    me = lax.axis_index("shot")
    base = group_index() * blocks
    lines = lax.broadcasted_iota(jnp.int32, (width, edges), 0)
    products, firsts, others = [], [], []
    for b in range(blocks):
        own = own_ref[:, b * width : (b + 1) * width]
        rows_x = inc_ref[0, b : b + 1, :]
        slot_x = inc_ref[1, b : b + 1, :]
        cols_x = inc_ref[2, b : b + 1, :]
        halo_first = base - HALO if b < mine else base + blocks
        chosen, hot = [], []
        far = [jnp.full((1, edges), -1, jnp.int32) for _ in range(HALO)]
        for k in range(slots):
            partner = partners_ref[b, k]
            partner = jnp.where(partner >= 0, partner, base + b)
            inside = (partner >= base) & (partner < base + blocks)
            start = pl.multiple_of(jnp.where(inside, partner - base, b) * width, width)
            chosen.append(own_ref[:, pl.ds(start, width)])
            here = slot_x == k
            hot.append((lines == jnp.where(here & inside, cols_x, -1)).astype(jnp.bfloat16))
            for w in range(HALO):
                there = here & (partner == halo_first + w) & jnp.logical_not(inside)
                far[w] = jnp.where(there, cols_x, far[w])
        for w in range(HALO):
            hot_ref[b, w * width : (w + 1) * width, :] = (lines == far[w]).astype(jnp.bfloat16)
        chosen = jnp.concatenate(chosen, axis=1)
        tiles = lax.dot_general(own, chosen, (((0,), (0,)), ((), ())), preferred_element_type=jnp.float32)
        tiles = tiles - sums_of(own) * (row_sums(chosen) * (1.0 / shots))
        for k in range(slots):
            spread(
                lower_ref if b < mine else upper_ref, (b % mine) * slots + k,
                tiles[:, k * width : (k + 1) * width], me,
            )
        vals = jnp.dot(own, (lines == rows_x).astype(jnp.bfloat16), preferred_element_type=jnp.float32)
        vals_ref[b] = vals.astype(jnp.bfloat16)
        other = jnp.dot(chosen, jnp.concatenate(hot, axis=0), preferred_element_type=jnp.float32)
        products += rows_of(jnp.sum(vals * other, axis=0, keepdims=True), pieces)
        firsts += rows_of(jnp.sum(vals, axis=0, keepdims=True), pieces)
        others += rows_of(jnp.sum(other, axis=0, keepdims=True), pieces)
        key = slot_x * (width * width) + rows_x * width + cols_x
        same = keyt_ref[:, b : b + 1] == key
        fit_ref[b : b + 1, :] = jnp.sum(jnp.where(same, probt_ref[:, b : b + 1], 0.0), axis=0, keepdims=True)
    early_ref[...] = jnp.concatenate(products + firsts + others, axis=0)
    sums_ref[...] = jnp.concatenate(rows_of(row_sums(own_ref[...]), blocks), axis=0)


def ready_call(partners, soft, incidence, keys_t, prob_t, after, width, groups):
    shots = soft.shape[0]
    blocks, slots = partners.shape
    edges = incidence.shape[2]
    cov = jax.ShapeDtypeStruct((groups, blocks // 2 * slots, width // groups, width), jnp.float32)
    return pl.pallas_call(
        functools.partial(ready_kernel, width),
        out_shape=[
            jax.ShapeDtypeStruct((blocks, edges), jnp.float32),
            jax.ShapeDtypeStruct((blocks, shots, edges), jnp.bfloat16),
            jax.ShapeDtypeStruct((blocks, HALO * width, edges), jnp.bfloat16),
            cov,
            cov,
            jax.ShapeDtypeStruct((3 * blocks * edges // width, width), jnp.float32),
            jax.ShapeDtypeStruct((blocks, width), jnp.float32),
        ],
        in_specs=[SMEM] + [VMEM] * 4 + [ANY],
        out_specs=[VMEM] * 7,
        compiler_params=PARAMS,
        cost_estimate=pl.CostEstimate(flops=20_000_000_000, bytes_accessed=12_000_000, transcendentals=0),
    )(partners, soft, incidence, keys_t, prob_t, after)


def pair_kernel(
    upper, partners_ref, halo_ref, own_ref, vals_ref, hot_ref, early_ref, own_sums_ref, _, _after,
    cov_ref, edge_ref, sums_ref,
):
    blocks, slots = partners_ref.shape
    mine = blocks // 2
    low = mine * upper
    shots = own_ref.shape[0]
    width = cov_ref.shape[3]
    pieces = hot_ref.shape[2] // width
    me = lax.axis_index("shot")
    base = group_index() * blocks
    halo_first = base + blocks if upper else base - HALO
    halo = halo_ref[...]
    halo_sums = row_sums(halo)
    products, others = [], []
    for b in range(mine):
        block = low + b
        own = own_ref[:, block * width : (block + 1) * width]
        reached = [w for w in range(HALO) if abs(block - (blocks + w if upper else w - HALO)) <= HALO]
        first, last = reached[0] * width, (reached[-1] + 1) * width
        tiles = lax.dot_general(
            own, halo[:, first:last], (((0,), (0,)), ((), ())), preferred_element_type=jnp.float32
        )
        tiles = tiles - sums_of(own) * (halo_sums[:, first:last] * (1.0 / shots))
        for n, w in enumerate(reached):
            for k in range(1, slots):
                partner = partners_ref[block, k]

                @pl.when((partner >= 0) & (partner == halo_first + w))
                def _():
                    spread(cov_ref, b * slots + k, tiles[:, n * width : (n + 1) * width], me)

        other = jnp.dot(halo, hot_ref[block], preferred_element_type=jnp.float32)
        product = jnp.sum(vals_ref[block].astype(jnp.float32) * other, axis=0, keepdims=True)
        products += rows_of(product, pieces)
        others += rows_of(jnp.sum(other, axis=0, keepdims=True), pieces)
    count = mine * pieces
    early = [early_ref[n * 2 * count + upper * count : n * 2 * count + (upper + 1) * count, :] for n in range(3)]
    own_sums = [own_sums_ref[low : low + mine, :]]
    side = rows_of(halo_sums, HALO)
    sums_ref[...] = fixed(jnp.concatenate(own_sums + side if upper else side + own_sums, axis=0))
    edge_ref[...] = fixed(
        jnp.concatenate(
            [early[0] + jnp.concatenate(products, axis=0), early[1], early[2] + jnp.concatenate(others, axis=0)],
            axis=0,
        )
    )


def pair_call(upper, partners, halo, soft, vals, hot, early, own_sums, cov, after):
    blocks = partners.shape[0]
    mine = blocks // 2
    width = cov.shape[3]
    return pl.pallas_call(
        functools.partial(pair_kernel, upper),
        out_shape=[
            jax.ShapeDtypeStruct(cov.shape, jnp.float32),
            jax.ShapeDtypeStruct((3 * mine * hot.shape[2] // width, width), jnp.int32),
            jax.ShapeDtypeStruct((mine + HALO, width), jnp.int32),
        ],
        in_specs=[SMEM] + [VMEM] * 7 + [ANY],
        out_specs=[VMEM] * 3,
        input_output_aliases={7: 0},
        compiler_params=PARAMS,
        cost_estimate=pl.CostEstimate(flops=1_000_000_000, bytes_accessed=4_000_000, transcendentals=0),
    )(partners, halo, soft, vals, hot, early, own_sums, cov, after)


def partner_row(partners_ref, block, k, base):
    partner = partners_ref[block, k]
    return jnp.where(partner >= 0, partner - base, block) + HALO


def factors_of(came_ref, words):
    scales = came_ref[came_ref.shape[0] - TAIL : came_ref.shape[0] - TAIL + words, :]
    step = UNIT / 32767.0
    low = (scales & 65535).astype(jnp.float32) * step
    return low, lax.shift_right_logical(scales, 16).astype(jnp.float32) * step


def words_of(came_ref, word, share, factors):
    words = came_ref[word * share : (word + 1) * share, :]
    low = lax.shift_right_arithmetic(words << 16, 16).astype(jnp.float32)
    high = lax.shift_right_arithmetic(words, 16).astype(jnp.float32)
    return low * factors[0][word : word + 1, :], high * factors[1][word : word + 1, :]


def hop_kernel(at, seen, partners_ref, *refs):
    came_ref = refs[0] if seen else None
    cov_l, cov_u, edge_l, edge_u, sums_l, sums_u, _, out_ref, shift, exact = refs[-10:]
    blocks, slots = partners_ref.shape
    share, width = cov_l.shape[2:]
    mine = blocks // 2
    groups = cov_l.shape[0]
    base = group_index() * blocks
    words = blocks * slots // 2
    body = words * share
    quarter = edge_l.shape[0] // 3
    shots = SHOTS
    sums = jnp.concatenate([sums_l[...], sums_u[...]], axis=0)
    edges = jnp.concatenate(
        [part[n * quarter : (n + 1) * quarter, :] for n in range(3) for part in (edge_l, edge_u)], axis=0
    )
    if seen:
        old = came_ref[body + words : body + words + 8, :]
        shift[...] = old.astype(jnp.float32) * (1.0 / (SCALE * shots * seen)) - sums.astype(jnp.float32) * (
            1.0 / (SCALE * shots)
        )
        sums = sums + old
        edges = edges + came_ref[body + words + 8 :, :]
        weight = float(shots) * seen / (seen + 1)
        factors = factors_of(came_ref, words)
    out_ref[body + words : body + words + 8, :] = sums
    out_ref[body + words + 8 :, :] = edges
    dest = lax.rem(lax.axis_index("shot") + at, groups)
    tops = [[], []]
    for block in range(blocks):
        cov_ref, b = (cov_l, block) if block < mine else (cov_u, block - mine)
        if seen:
            column = column_of(shift[block + HALO : block + HALO + 1, :], dest * share, share) * weight
        for pair in range(slots // 2):
            word = block * (slots // 2) + pair
            if seen:
                came = words_of(came_ref, word, share, factors)
            for i in range(2):
                value = cov_ref[at, b * slots + 2 * pair + i]
                if seen:
                    row = shift[pl.ds(partner_row(partners_ref, block, 2 * pair + i, base), 1), :]
                    value = value + came[i] + column * row
                exact[i, word] = value
                tops[i].append(jnp.max(jnp.abs(value), axis=0, keepdims=True))
    scales, steps = [], []
    for i in range(2):
        scale = jnp.floor(jnp.concatenate(tops[i], axis=0) * (1.0 / UNIT)).astype(jnp.int32) + 1
        scales.append(scale)
        steps.append(32767.0 / (scale.astype(jnp.float32) * UNIT))
    out_ref[body : body + words, :] = (scales[1] << 16) | scales[0]
    for word in range(words):
        low, high = [
            jnp.floor(exact[i, word] * steps[i][word : word + 1, :] + 0.5).astype(jnp.int32) for i in range(2)
        ]
        out_ref[word * share : (word + 1) * share, :] = (high << 16) | (low & 65535)


def hop_call(at, seen, partners, came, parts, after):
    (cov_l, edge_l, sums_l), (cov_u, edge_u, sums_u) = parts
    share, width = cov_l.shape[2:]
    body = 2 * cov_l.shape[1] * share // 2
    came = (came,) if seen else ()
    return pl.pallas_call(
        functools.partial(hop_kernel, at, seen),
        out_shape=jax.ShapeDtypeStruct((body + TAIL, width), jnp.int32),
        in_specs=[SMEM] + [VMEM] * (6 + len(came)) + [ANY],
        out_specs=VMEM,
        scratch_shapes=[
            pltpu.VMEM((8, width), jnp.float32),
            pltpu.VMEM((2, body // share, share, width), jnp.float32),
        ],
        compiler_params=PARAMS,
        cost_estimate=pl.CostEstimate(flops=1_000_000, bytes_accessed=600_000, transcendentals=0),
    )(partners, *came, cov_l, cov_u, edge_l, edge_u, sums_l, sums_u, after)


def final_kernel(
    rises, falls, partners_ref, inc_ref, rising_ref, falling_ref,
    cov_l, cov_u, edge_l, edge_u, sums_l, sums_u, fit_ref,
    pair_ref, grad_ref, first_shift, second_shift, totals,
):
    blocks, slots = partners_ref.shape
    mine = blocks // 2
    groups = cov_l.shape[0]
    share, width = cov_l.shape[2:]
    pieces = inc_ref.shape[2] // width
    quarter = edge_l.shape[0] // 3
    words = blocks * slots // 2
    body = words * share
    shots = SHOTS
    count = float(shots * groups)
    base = group_index() * blocks
    start = lax.axis_index("shot") * share
    sums = jnp.concatenate([sums_l[...], sums_u[...]], axis=0)
    rise_sums = rising_ref[body + words : body + words + 8, :]
    fall_sums = falling_ref[body + words : body + words + 8, :]

    def mean(values, sources):
        return values.astype(jnp.float32) * (1.0 / (SCALE * shots * sources))

    first_shift[...] = mean(rise_sums, rises) - mean(sums, 1)
    second_shift[...] = mean(fall_sums, falls) - mean(sums + rise_sums, rises + 1)
    totals[...] = (sums + rise_sums + fall_sums).astype(jnp.float32) * (1.0 / SCALE)
    first_weight = float(shots) * rises / (rises + 1)
    second_weight = float(shots) * falls * (rises + 1) / (rises + 1 + falls)
    edges = jnp.concatenate(
        [part[n * quarter : (n + 1) * quarter, :] for n in range(3) for part in (edge_l, edge_u)], axis=0
    )
    edges = edges + rising_ref[body + words + 8 :, :] + falling_ref[body + words + 8 :, :]
    edges = edges.astype(jnp.float32) * (1.0 / SCALE)
    risen_factors, fallen_factors = factors_of(rising_ref, words), factors_of(falling_ref, words)
    for block in range(blocks):
        cov_ref, b = (cov_l, block) if block < mine else (cov_u, block - mine)
        own = slice(block + HALO, block + HALO + 1)
        first_column = column_of(first_shift[own, :], start, share) * first_weight
        second_column = column_of(second_shift[own, :], start, share) * second_weight
        total_column = column_of(totals[own, :], start, share) * (1.0 / count)
        for pair in range(slots // 2):
            word = block * (slots // 2) + pair
            risen = words_of(rising_ref, word, share, risen_factors)
            fallen = words_of(falling_ref, word, share, fallen_factors)
            for i in range(2):
                k = 2 * pair + i
                at = pl.ds(partner_row(partners_ref, block, k, base), 1)
                live = jnp.where(partners_ref[block, k] >= 0, 1.0, 0.0)
                cov = cov_ref[0, b * slots + k] + risen[i] + first_column * first_shift[at, :]
                cov = cov + fallen[i] + second_column * second_shift[at, :]
                alone = total_column * totals[at, :]
                entry = 0.5 - 0.5 * jnp.sqrt(alone / (alone + cov))
                pair_ref[block, k] = (entry * live).astype(jnp.bfloat16)
        for p in range(pieces):
            n = block * pieces + p
            at = slice(p * width, (p + 1) * width)
            slot_x = inc_ref[1, block : block + 1, at]
            live = jnp.zeros((1, width), jnp.float32)
            for k in range(slots):
                live = live + jnp.where((slot_x == k) & (partners_ref[block, k] >= 0), 1.0, 0.0)
            rows = 2 * quarter
            quotient = (edges[rows + n : rows + n + 1] / count) * (
                edges[2 * rows + n : 2 * rows + n + 1] / count
            ) * count / edges[n : n + 1]
            entry = (0.5 - 0.5 * jnp.sqrt(quotient)) * live
            residual = live * (entry - fit_ref[block : block + 1, at]) / NOISE_SPREAD
            grad_ref[block : block + 1, at] = -residual / NOISE_SPREAD


def final_call(partners, incidence, rising, falling, parts, fit):
    (cov_l, edge_l, sums_l), (cov_u, edge_u, sums_u) = parts
    blocks, slots = partners.shape
    groups, _, share, width = cov_l.shape
    half = groups // 2
    return pl.pallas_call(
        functools.partial(final_kernel, half, groups - 1 - half),
        out_shape=[
            jax.ShapeDtypeStruct((blocks, slots, share, width), jnp.bfloat16),
            jax.ShapeDtypeStruct((blocks, incidence.shape[2]), jnp.float32),
        ],
        in_specs=[SMEM] + [VMEM] * 10,
        out_specs=[VMEM] * 2,
        scratch_shapes=[pltpu.VMEM((8, width), jnp.float32)] * 3,
        compiler_params=PARAMS,
        cost_estimate=pl.CostEstimate(flops=1_000_000, bytes_accessed=2_000_000, transcendentals=100_000),
    )(partners, incidence, rising, falling, cov_l, cov_u, edge_l, edge_u, sums_l, sums_u, fit)


def local(soft, partners, incidence, edge_prob):
    shots, own_width = soft.shape
    blocks, slots = partners.shape
    width = own_width // blocks
    groups = lax.axis_size("shot")
    sides = lax.axis_size(("row", "col"))

    head, tail, cut = cut_call(soft, HALO * width)
    left = lax.ppermute(tail, ("row", "col"), [(i, (i + 1) % sides) for i in range(sides)])
    right = lax.ppermute(head, ("row", "col"), [((i + 1) % sides, i) for i in range(sides)])

    keys = incidence[1] * (width * width) + incidence[0] * width + incidence[2]
    fit, vals, hot, cov_l, cov_u, early, own_sums = ready_call(
        partners, soft, incidence, keys.T, edge_prob.T, cut, width, groups
    )
    args = (soft, vals, hot, early, own_sums)
    lower = pair_call(0, partners, left, *args, cov_l, early)
    upper = pair_call(1, partners, right, *args, cov_u, lower[1])
    parts = (lower, upper)

    half = groups // 2
    rise = [(i, (i + 1) % groups) for i in range(groups)]
    fall = [(b, a) for a, b in rise]
    rising = falling = None
    order = early
    for step in range(half):
        order = hop_call(half - step, step, partners, rising, parts, order)
        rising = lax.ppermute(order, "shot", rise)
        if step < half - 1:
            order = hop_call(half + 1 + step, step, partners, falling, parts, order)
            falling = lax.ppermute(order, "shot", fall)
    return final_call(partners, incidence, rising, falling, parts, fit)


def solution(mesh):
    placed = (
        P("shot", ("row", "col")),
        P(("row", "col"), None),
        P(None, ("row", "col"), None),
        P(("row", "col"), None),
    )
    return jax.shard_map(
        local,
        mesh=mesh,
        in_specs=placed,
        out_specs=(P(("row", "col"), None, "shot", None), P(("row", "col"), None)),
        check_vma=False,
    )
```

time: 131 us -> 118 us (0.901)
  waiting for transfers between devices: 26.5 us -> 15.7 us
  Pallas kernels: 34.8 us -> 30.8 us
    ppermute x1, waiting for transfers between devices: 14.6 us -> 2.45 us  [local(): lax.ppermute(tail, ('row', 'col'), [(i, (i + 1) % sides) for i in range(s...]
    pallas_call x4, Pallas kernels: 20.8 us -> 17.5 us  [the longest x1 9.2 us: ready_call(): pl.pallas_call(functools.partial(ready_kernel, width), out_shape=[jax.Sha...]
    ppermute x8, waiting for transfers between devices: 11.2 us -> 13.3 us  [local(): rising = lax.ppermute(order, 'shot', rise)]
    ppermute x1, starting transfers between devices: 1.92 us -> 3.4 us  [local(): lax.ppermute(tail, ('row', 'col'), [(i, (i + 1) % sides) for i in range(s...]
    unnamed x9 -> x11, local copies, waits for them, and re-layouts: 2.26 us -> 3.21 us
  transfers between devices with their start and end apart: 17 -> 17, of which waited for: 11 -> 9; matrix products, arithmetic and copies ran while one was open for 1% -> 2% of each run, Pallas kernels for 19% -> 20%
where the time goes in v7:
time: 118 us; the launch traced here: 117 us
  starting transfers between devices  65.5 us (56%)
  Pallas kernels  30.8 us (26%)
  waiting for transfers between devices  15.7 us (13%)
  local copies, waits for them, and re-layouts  3.35 us (3%)
    ppermute x7, starting transfers between devices, local(): falling = lax.ppermute(order, 'shot', fall)  40.6 us
    ppermute x8, starting transfers between devices, local(): rising = lax.ppermute(order, 'shot', rise)  17.3 us
    ppermute x8, waiting for transfers between devices, local(): rising = lax.ppermute(order, 'shot', rise)  13.3 us
    pallas_call x15, Pallas kernels, hop_call(): pl.pallas_call(functools.partial(hop_kernel, at, seen), out_shape=jax.Sha...  11.7 us
    pallas_call x1, Pallas kernels, ready_call(): pl.pallas_call(functools.partial(ready_kernel, width), out_shape=[jax.Sha...  9.2 us
    pallas_call x2, Pallas kernels, pair_call(): pl.pallas_call(functools.partial(pair_kernel, upper), out_shape=[jax.Shap...  5.7 us
    ppermute x1, starting transfers between devices, local(): lax.ppermute(head, ('row', 'col'), [((i + 1) % sides, i) for i in range(s...  4.27 us
    ppermute x1, starting transfers between devices, local(): lax.ppermute(tail, ('row', 'col'), [(i, (i + 1) % sides) for i in range(s...  3.4 us
  transfers between devices with their start and end apart: 17, of which 9 were waited for; matrix products, arithmetic and copies ran while one was open for 2% of the time, Pallas kernels for 20%

profile of v7, /device:TPU:24, one launch (start us, length us, event | category | flops | bytes accessed | tf_op | source)
XLA Modules:
  0.0 117.1 jit_solution(14844267708382601913)
XLA Ops:
  0.7 2.6 %shard_map.59 = (bf16[768,512]{1,0:T(8,128)(2,1)}, bf16[768,512]{1,0:T(8,128)(2,1)}, f32[8,128]{1,0:T(8,128)}) custom-call(bf16[768,1024]{1,0:T(8,128)(2,1)} %own_ref.5), custom_call_target="tpu_custom_call" | custom-call | bytes 3000000 | tf_op jit(solution)/shard_map/pallas_call | solution.py:64
  3.3 3.4 %collective-permute-start = (bf16[768,512]{1,0:T(8,128)(2,1)}, bf16[768,512]{1,0:T(8,128)(2,1)S(1)}, u32[]{:S(2)}, u32[]{:S(2)}) collective-permute-start(bf16[768,512]{1,0:T(8,128)(2,1)} %get-tuple-element.18), channel_id=1, source_target_pairs={{0,1},{1,2},{2,3},{3,4},{4,5},{5,6},{6,7},{7,8},{8,9},{9,10},{10,1... | collective-permute-start | bytes 2359304 | tf_op jit(solution)/shard_map/ppermute | solution.py:426
  6.7 4.3 %collective-permute-start.1 = (bf16[768,512]{1,0:T(8,128)(2,1)}, bf16[768,512]{1,0:T(8,128)(2,1)S(1)}, u32[]{:S(2)}, u32[]{:S(2)}) collective-permute-start(bf16[768,512]{1,0:T(8,128)(2,1)} %get-tuple-element.26), channel_id=1, source_target_pairs={{1,0},{2,1},{3,2},{4,3},{5,4},{6,5},{7,6},{8,7},{9,8},{10,9},{11,1... | collective-permute-start | bytes 2359304 | tf_op jit(solution)/shard_map/ppermute | solution.py:427
  15.1 9.2 %shard_map.60 = (f32[4,512]{1,0:T(4,128)S(1)}, bf16[4,768,512]{2,1,0:T(8,128)(2,1)S(1)}, bf16[4,512,512]{2,1,0:T(8,128)(2,1)S(1)}, f32[16,8,16,256]{3,2,1,0:T(8,...) custom-call(s32[4,4]{1,0:T(4,128)S(1)} %copy-done.1, ...), custom_call_target="tpu_custom_call" | custom-call | flops 20000000000 | bytes 12000000 | tf_op jit(solution)/shard_map/pallas_call | solution.py:147
  24.3 2.5 %collective-permute-done.halo_ref = bf16[768,512]{1,0:T(8,128)(2,1)S(1)} collective-permute-done((bf16[768,512]{1,0:T(8,128)(2,1)}, bf16[768,512]{1,0:T(8,128)(2,1)S(1)}, u32[]{:S(2)}, u32[]{:S(2)}) %collective-permute-start) | collective-permute-done | bytes 786464 | tf_op jit(solution)/shard_map/ppermute | solution.py:426
  26.7 2.8 %shard_map.61 = (f32[16,8,16,256]{3,2,1,0:T(8,128)S(1)}, s32[12,256]{1,0:T(8,128)S(1)}, s32[4,256]{1,0:T(4,128)S(1)}) custom-call(s32[4,4]{1,0:T(4,128)S(1)} %copy-done.1, bf16[768,512]{1,0:T(8,128)(2,1)S(1)} %collective-permute-done.halo_ref, bf16[768,1024]{1,0:T(8,128)(2,1)S(1)} %copy-done, ...), custom_call_target="tpu_custom_call", output_to_operand_aliasing={{0}: (7, {})} | custom-call | flops 1000000000 | bytes 4000000 | tf_op jit(solution)/shard_map/pallas_call | solution.py:219
  29.5 2.9 %shard_map.62 = (f32[16,8,16,256]{3,2,1,0:T(8,128)S(1)}, s32[12,256]{1,0:T(8,128)S(1)}, s32[4,256]{1,0:T(4,128)S(1)}) custom-call(s32[4,4]{1,0:T(4,128)S(1)} %copy-done.1, bf16[768,512]{1,0:T(8,128)(2,1)S(1)} %collective-permute-done.1.halo_ref, bf16[768,1024]{1,0:T(8,128)(2,1)S(1)} %copy-done, ...), custom_call_target="tpu_custom_call", output_to_operand_aliasing={{0}: (7, {})} | custom-call | flops 1000000000 | bytes 4000000 | tf_op jit(solution)/shard_map/pallas_call | solution.py:219
  33.2 3.8 %collective-permute-start.2 = (s32[168,256]{1,0:T(8,128)S(1)}, s32[168,256]{1,0:T(8,128)S(1)}, u32[]{:S(2)}, u32[]{:S(2)}) collective-permute-start(s32[168,256]{1,0:T(8,128)S(1)} %shard_map.63.refs_6_), channel_id=1, source_target_pairs={{0,32},{32,64},{64,96},{96,128},{128,160},{160,192},{192,224},{224... | collective-permute-start | bytes 516104 | tf_op jit(solution)/shard_map/ppermute | solution.py:445
  37.7 9.5 %collective-permute-start.4 = (s32[168,256]{1,0:T(8,128)S(1)}, s32[168,256]{1,0:T(8,128)S(1)}, u32[]{:S(2)}, u32[]{:S(2)}) collective-permute-start(s32[168,256]{1,0:T(8,128)S(1)} %shard_map.64.refs_7_), channel_id=1, source_target_pairs={{32,0},{64,32},{96,64},{128,96},{160,128},{192,160},{224,192},{256... | collective-permute-start | bytes 516104 | tf_op jit(solution)/shard_map/ppermute | solution.py:448
  49.3 1.9 %collective-permute-start.3 = (s32[168,256]{1,0:T(8,128)S(1)}, s32[168,256]{1,0:T(8,128)S(1)}, u32[]{:S(2)}, u32[]{:S(2)}) collective-permute-start(s32[168,256]{1,0:T(8,128)S(1)} %shard_map.65.refs_7_), channel_id=1, source_target_pairs={{0,32},{32,64},{64,96},{96,128},{128,160},{160,192},{192,224},{224... | collective-permute-start | bytes 516104 | tf_op jit(solution)/shard_map/ppermute | solution.py:445
  52.1 5.1 %collective-permute-start.6 = (s32[168,256]{1,0:T(8,128)S(1)}, s32[168,256]{1,0:T(8,128)S(1)}, u32[]{:S(2)}, u32[]{:S(2)}) collective-permute-start(s32[168,256]{1,0:T(8,128)S(1)} %shard_map.66.refs_7_), channel_id=1, source_target_pairs={{32,0},{64,32},{96,64},{128,96},{160,128},{192,160},{224,192},{256... | collective-permute-start | bytes 516104 | tf_op jit(solution)/shard_map/ppermute | solution.py:448
  58.6 1.9 %collective-permute-start.5 = (s32[168,256]{1,0:T(8,128)S(1)}, s32[168,256]{1,0:T(8,128)S(1)}, u32[]{:S(2)}, u32[]{:S(2)}) collective-permute-start(s32[168,256]{1,0:T(8,128)S(1)} %shard_map.67.refs_7_), channel_id=1, source_target_pairs={{0,32},{32,64},{64,96},{96,128},{128,160},{160,192},{192,224},{224... | collective-permute-start | bytes 516104 | tf_op jit(solution)/shard_map/ppermute | solution.py:445
  61.4 5.1 %collective-permute-start.8 = (s32[168,256]{1,0:T(8,128)S(1)}, s32[168,256]{1,0:T(8,128)S(1)}, u32[]{:S(2)}, u32[]{:S(2)}) collective-permute-start(s32[168,256]{1,0:T(8,128)S(1)} %shard_map.68.refs_7_), channel_id=1, source_target_pairs={{32,0},{64,32},{96,64},{128,96},{160,128},{192,160},{224,192},{256... | collective-permute-start | bytes 516104 | tf_op jit(solution)/shard_map/ppermute | solution.py:448
  67.9 1.9 %collective-permute-start.7 = (s32[168,256]{1,0:T(8,128)S(1)}, s32[168,256]{1,0:T(8,128)S(1)}, u32[]{:S(2)}, u32[]{:S(2)}) collective-permute-start(s32[168,256]{1,0:T(8,128)S(1)} %shard_map.69.refs_7_), channel_id=1, source_target_pairs={{0,32},{32,64},{64,96},{96,128},{128,160},{160,192},{192,224},{224... | collective-permute-start | bytes 516104 | tf_op jit(solution)/shard_map/ppermute | solution.py:445
  70.7 5.1 %collective-permute-start.10 = (s32[168,256]{1,0:T(8,128)S(1)}, s32[168,256]{1,0:T(8,128)S(1)}, u32[]{:S(2)}, u32[]{:S(2)}) collective-permute-start(s32[168,256]{1,0:T(8,128)S(1)} %shard_map.70.refs_7_), channel_id=1, source_target_pairs={{32,0},{64,32},{96,64},{128,96},{160,128},{192,160},{224,192},{256... | collective-permute-start | bytes 516104 | tf_op jit(solution)/shard_map/ppermute | solution.py:448
  77.2 1.9 %collective-permute-start.9 = (s32[168,256]{1,0:T(8,128)S(1)}, s32[168,256]{1,0:T(8,128)S(1)}, u32[]{:S(2)}, u32[]{:S(2)}) collective-permute-start(s32[168,256]{1,0:T(8,128)S(1)} %shard_map.71.refs_7_), channel_id=1, source_target_pairs={{0,32},{32,64},{64,96},{96,128},{128,160},{160,192},{192,224},{224... | collective-permute-start | bytes 516104 | tf_op jit(solution)/shard_map/ppermute | solution.py:445
  80.0 5.1 %collective-permute-start.12 = (s32[168,256]{1,0:T(8,128)S(1)}, s32[168,256]{1,0:T(8,128)S(1)}, u32[]{:S(2)}, u32[]{:S(2)}) collective-permute-start(s32[168,256]{1,0:T(8,128)S(1)} %shard_map.72.refs_7_), channel_id=1, source_target_pairs={{32,0},{64,32},{96,64},{128,96},{160,128},{192,160},{224,192},{256... | collective-permute-start | bytes 516104 | tf_op jit(solution)/shard_map/ppermute | solution.py:448
  86.6 1.9 %collective-permute-start.11 = (s32[168,256]{1,0:T(8,128)S(1)}, s32[168,256]{1,0:T(8,128)S(1)}, u32[]{:S(2)}, u32[]{:S(2)}) collective-permute-start(s32[168,256]{1,0:T(8,128)S(1)} %shard_map.73.refs_7_), channel_id=1, source_target_pairs={{0,32},{32,64},{64,96},{96,128},{128,160},{160,192},{192,224},{224... | collective-permute-start | bytes 516104 | tf_op jit(solution)/shard_map/ppermute | solution.py:445
  89.3 5.1 %collective-permute-start.14 = (s32[168,256]{1,0:T(8,128)S(1)}, s32[168,256]{1,0:T(8,128)S(1)}, u32[]{:S(2)}, u32[]{:S(2)}) collective-permute-start(s32[168,256]{1,0:T(8,128)S(1)} %shard_map.74.refs_7_), channel_id=1, source_target_pairs={{32,0},{64,32},{96,64},{128,96},{160,128},{192,160},{224,192},{256... | collective-permute-start | bytes 516104 | tf_op jit(solution)/shard_map/ppermute | solution.py:448
  96.2 1.9 %collective-permute-start.13 = (s32[168,256]{1,0:T(8,128)S(1)}, s32[168,256]{1,0:T(8,128)S(1)}, u32[]{:S(2)}, u32[]{:S(2)}) collective-permute-start(s32[168,256]{1,0:T(8,128)S(1)} %shard_map.75.refs_7_), channel_id=1, source_target_pairs={{0,32},{32,64},{64,96},{96,128},{128,160},{160,192},{192,224},{224... | collective-permute-start | bytes 516104 | tf_op jit(solution)/shard_map/ppermute | solution.py:445
  99.0 5.5 %collective-permute-start.16 = (s32[168,256]{1,0:T(8,128)S(1)}, s32[168,256]{1,0:T(8,128)S(1)}, u32[]{:S(2)}, u32[]{:S(2)}) collective-permute-start(s32[168,256]{1,0:T(8,128)S(1)} %shard_map.76.refs_7_), channel_id=1, source_target_pairs={{32,0},{64,32},{96,64},{128,96},{160,128},{192,160},{224,192},{256... | collective-permute-start | bytes 516104 | tf_op jit(solution)/shard_map/ppermute | solution.py:448
  104.4 1.8 %collective-permute-done.13.refs_0_ = s32[168,256]{1,0:T(8,128)S(1)} collective-permute-done((s32[168,256]{1,0:T(8,128)S(1)}, s32[168,256]{1,0:T(8,128)S(1)}, u32[]{:S(2)}, u32[]{:S(2)}) %collective-permute-start.13) | collective-permute-done | bytes 172064 | tf_op jit(solution)/shard_map/ppermute | solution.py:445
  107.1 1.9 %collective-permute-start.15 = (s32[168,256]{1,0:T(8,128)S(1)}, s32[168,256]{1,0:T(8,128)S(1)}, u32[]{:S(2)}, u32[]{:S(2)}) collective-permute-start(s32[168,256]{1,0:T(8,128)S(1)} %shard_map.77), channel_id=1, source_target_pairs={{0,32},{32,64},{64,96},{96,128},{128,160},{160,192},{192,224},{224... | collective-permute-start | bytes 516104 | tf_op jit(solution)/shard_map/ppermute | solution.py:445
  109.0 6.6 %collective-permute-done.15.rising_ref = s32[168,256]{1,0:T(8,128)S(1)} collective-permute-done((s32[168,256]{1,0:T(8,128)S(1)}, s32[168,256]{1,0:T(8,128)S(1)}, u32[]{:S(2)}, u32[]{:S(2)}) %collective-permute-start.15) | collective-permute-done | bytes 172064 | tf_op jit(solution)/shard_map/ppermute | solution.py:445
  (43 shorter events, 22.2 us)
Async XLA Ops:
  0.6 12.8 %copy-start = (bf16[768,1024]{1,0:T(8,128)(2,1)S(1)}, bf16[768,1024]{1,0:T(8,128)(2,1)}, u32[]{:S(2)}) copy-start(bf16[768,1024]{1,0:T(8,128)(2,1)} %own_ref.5) | copy-start | bytes 4718596
  0.6 12.8 %copy-start.3 = (s32[3,4,512]{2,1,0:T(4,128)S(1)}, s32[3,4,512]{2,1,0:T(4,128)}, u32[]{:S(2)}) copy-start(s32[3,4,512]{2,1,0:T(4,128)} %inc_ref.3) | copy-start | bytes 73732
  0.7 12.8 %copy-start.1 = (s32[4,4]{1,0:T(4,128)S(1)}, s32[4,4]{1,0:T(4,128)}, u32[]{:S(2)}) copy-start(s32[4,4]{1,0:T(4,128)} %partners_ref.37) | copy-start | bytes 196
  3.3 23.4 %collective-permute-start = (bf16[768,512]{1,0:T(8,128)(2,1)}, bf16[768,512]{1,0:T(8,128)(2,1)S(1)}, u32[]{:S(2)}, u32[]{:S(2)}) collective-permute-start(bf16[768,512]{1,0:T(8,128)(2,1)} %get-tuple-element.18), channel_id=1, source_target_pairs={{0,1},{1,2},{2,3},{3,4},{4,5},{5,6},{6,7},{7,8},{8,9},{9,10},{10,1... | collective-permute-start | bytes 2359304 | tf_op jit(solution)/shard_map/ppermute | solution.py:426
  6.7 22.8 %collective-permute-start.1 = (bf16[768,512]{1,0:T(8,128)(2,1)}, bf16[768,512]{1,0:T(8,128)(2,1)S(1)}, u32[]{:S(2)}, u32[]{:S(2)}) collective-permute-start(bf16[768,512]{1,0:T(8,128)(2,1)} %get-tuple-element.26), channel_id=1, source_target_pairs={{1,0},{2,1},{3,2},{4,3},{5,4},{6,5},{7,6},{8,7},{9,8},{10,9},{11,1... | collective-permute-start | bytes 2359304 | tf_op jit(solution)/shard_map/ppermute | solution.py:427
  13.5 1.0 copy-start.2
  14.4 0.7 copy-start.4
  33.2 15.4 %collective-permute-start.2 = (s32[168,256]{1,0:T(8,128)S(1)}, s32[168,256]{1,0:T(8,128)S(1)}, u32[]{:S(2)}, u32[]{:S(2)}) collective-permute-start(s32[168,256]{1,0:T(8,128)S(1)} %shard_map.63.refs_6_), channel_id=1, source_target_pairs={{0,32},{32,64},{64,96},{96,128},{128,160},{160,192},{192,224},{224... | collective-permute-start | bytes 516104 | tf_op jit(solution)/shard_map/ppermute | solution.py:445
  37.7 13.6 %collective-permute-start.4 = (s32[168,256]{1,0:T(8,128)S(1)}, s32[168,256]{1,0:T(8,128)S(1)}, u32[]{:S(2)}, u32[]{:S(2)}) collective-permute-start(s32[168,256]{1,0:T(8,128)S(1)} %shard_map.64.refs_7_), channel_id=1, source_target_pairs={{32,0},{64,32},{96,64},{128,96},{160,128},{192,160},{224,192},{256... | collective-permute-start | bytes 516104 | tf_op jit(solution)/shard_map/ppermute | solution.py:448
  49.3 8.5 %collective-permute-start.3 = (s32[168,256]{1,0:T(8,128)S(1)}, s32[168,256]{1,0:T(8,128)S(1)}, u32[]{:S(2)}, u32[]{:S(2)}) collective-permute-start(s32[168,256]{1,0:T(8,128)S(1)} %shard_map.65.refs_7_), channel_id=1, source_target_pairs={{0,32},{32,64},{64,96},{96,128},{128,160},{160,192},{192,224},{224... | collective-permute-start | bytes 516104 | tf_op jit(solution)/shard_map/ppermute | solution.py:445
  52.1 8.5 %collective-permute-start.6 = (s32[168,256]{1,0:T(8,128)S(1)}, s32[168,256]{1,0:T(8,128)S(1)}, u32[]{:S(2)}, u32[]{:S(2)}) collective-permute-start(s32[168,256]{1,0:T(8,128)S(1)} %shard_map.66.refs_7_), channel_id=1, source_target_pairs={{32,0},{64,32},{96,64},{128,96},{160,128},{192,160},{224,192},{256... | collective-permute-start | bytes 516104 | tf_op jit(solution)/shard_map/ppermute | solution.py:448
  58.6 8.5 %collective-permute-start.5 = (s32[168,256]{1,0:T(8,128)S(1)}, s32[168,256]{1,0:T(8,128)S(1)}, u32[]{:S(2)}, u32[]{:S(2)}) collective-permute-start(s32[168,256]{1,0:T(8,128)S(1)} %shard_map.67.refs_7_), channel_id=1, source_target_pairs={{0,32},{32,64},{64,96},{96,128},{128,160},{160,192},{192,224},{224... | collective-permute-start | bytes 516104 | tf_op jit(solution)/shard_map/ppermute | solution.py:445
  61.4 8.5 %collective-permute-start.8 = (s32[168,256]{1,0:T(8,128)S(1)}, s32[168,256]{1,0:T(8,128)S(1)}, u32[]{:S(2)}, u32[]{:S(2)}) collective-permute-start(s32[168,256]{1,0:T(8,128)S(1)} %shard_map.68.refs_7_), channel_id=1, source_target_pairs={{32,0},{64,32},{96,64},{128,96},{160,128},{192,160},{224,192},{256... | collective-permute-start | bytes 516104 | tf_op jit(solution)/shard_map/ppermute | solution.py:448
  67.9 8.5 %collective-permute-start.7 = (s32[168,256]{1,0:T(8,128)S(1)}, s32[168,256]{1,0:T(8,128)S(1)}, u32[]{:S(2)}, u32[]{:S(2)}) collective-permute-start(s32[168,256]{1,0:T(8,128)S(1)} %shard_map.69.refs_7_), channel_id=1, source_target_pairs={{0,32},{32,64},{64,96},{96,128},{128,160},{160,192},{192,224},{224... | collective-permute-start | bytes 516104 | tf_op jit(solution)/shard_map/ppermute | solution.py:445
  70.7 8.5 %collective-permute-start.10 = (s32[168,256]{1,0:T(8,128)S(1)}, s32[168,256]{1,0:T(8,128)S(1)}, u32[]{:S(2)}, u32[]{:S(2)}) collective-permute-start(s32[168,256]{1,0:T(8,128)S(1)} %shard_map.70.refs_7_), channel_id=1, source_target_pairs={{32,0},{64,32},{96,64},{128,96},{160,128},{192,160},{224,192},{256... | collective-permute-start | bytes 516104 | tf_op jit(solution)/shard_map/ppermute | solution.py:448
  77.2 8.5 %collective-permute-start.9 = (s32[168,256]{1,0:T(8,128)S(1)}, s32[168,256]{1,0:T(8,128)S(1)}, u32[]{:S(2)}, u32[]{:S(2)}) collective-permute-start(s32[168,256]{1,0:T(8,128)S(1)} %shard_map.71.refs_7_), channel_id=1, source_target_pairs={{0,32},{32,64},{64,96},{96,128},{128,160},{160,192},{192,224},{224... | collective-permute-start | bytes 516104 | tf_op jit(solution)/shard_map/ppermute | solution.py:445
  80.0 8.5 %collective-permute-start.12 = (s32[168,256]{1,0:T(8,128)S(1)}, s32[168,256]{1,0:T(8,128)S(1)}, u32[]{:S(2)}, u32[]{:S(2)}) collective-permute-start(s32[168,256]{1,0:T(8,128)S(1)} %shard_map.72.refs_7_), channel_id=1, source_target_pairs={{32,0},{64,32},{96,64},{128,96},{160,128},{192,160},{224,192},{256... | collective-permute-start | bytes 516104 | tf_op jit(solution)/shard_map/ppermute | solution.py:448
  86.6 8.9 %collective-permute-start.11 = (s32[168,256]{1,0:T(8,128)S(1)}, s32[168,256]{1,0:T(8,128)S(1)}, u32[]{:S(2)}, u32[]{:S(2)}) collective-permute-start(s32[168,256]{1,0:T(8,128)S(1)} %shard_map.73.refs_7_), channel_id=1, source_target_pairs={{0,32},{32,64},{64,96},{96,128},{128,160},{160,192},{192,224},{224... | collective-permute-start | bytes 516104 | tf_op jit(solution)/shard_map/ppermute | solution.py:445
  89.3 8.9 %collective-permute-start.14 = (s32[168,256]{1,0:T(8,128)S(1)}, s32[168,256]{1,0:T(8,128)S(1)}, u32[]{:S(2)}, u32[]{:S(2)}) collective-permute-start(s32[168,256]{1,0:T(8,128)S(1)} %shard_map.74.refs_7_), channel_id=1, source_target_pairs={{32,0},{64,32},{96,64},{128,96},{160,128},{192,160},{224,192},{256... | collective-permute-start | bytes 516104 | tf_op jit(solution)/shard_map/ppermute | solution.py:448
  96.2 10.0 %collective-permute-start.13 = (s32[168,256]{1,0:T(8,128)S(1)}, s32[168,256]{1,0:T(8,128)S(1)}, u32[]{:S(2)}, u32[]{:S(2)}) collective-permute-start(s32[168,256]{1,0:T(8,128)S(1)} %shard_map.75.refs_7_), channel_id=1, source_target_pairs={{0,32},{32,64},{64,96},{96,128},{128,160},{160,192},{192,224},{224... | collective-permute-start | bytes 516104 | tf_op jit(solution)/shard_map/ppermute | solution.py:445
  99.0 10.0 %collective-permute-start.16 = (s32[168,256]{1,0:T(8,128)S(1)}, s32[168,256]{1,0:T(8,128)S(1)}, u32[]{:S(2)}, u32[]{:S(2)}) collective-permute-start(s32[168,256]{1,0:T(8,128)S(1)} %shard_map.76.refs_7_), channel_id=1, source_target_pairs={{32,0},{64,32},{96,64},{128,96},{160,128},{192,160},{224,192},{256... | collective-permute-start | bytes 516104 | tf_op jit(solution)/shard_map/ppermute | solution.py:448
  107.1 8.5 %collective-permute-start.15 = (s32[168,256]{1,0:T(8,128)S(1)}, s32[168,256]{1,0:T(8,128)S(1)}, u32[]{:S(2)}, u32[]{:S(2)}) collective-permute-start(s32[168,256]{1,0:T(8,128)S(1)} %shard_map.77), channel_id=1, source_target_pairs={{0,32},{32,64},{64,96},{96,128},{128,160},{160,192},{192,224},{224... | collective-permute-start | bytes 516104 | tf_op jit(solution)/shard_map/ppermute | solution.py:445

commit v8 on v7

v8 whole, which is shorter than its diff:
```python
import functools

import jax
import jax.numpy as jnp
from jax import lax
from jax.experimental import pallas as pl
from jax.experimental.pallas import tpu as pltpu
from jax.sharding import PartitionSpec as P

HALO = 2
REACH = 8
NOISE_SPREAD = 0.05
SCALE = 131072.0
UNIT = 1600.0 / 65535.0
SHOTS = 768
TAIL = 40
ANY = pl.BlockSpec(memory_space=pl.ANY)
VMEM = pl.BlockSpec(memory_space=pltpu.VMEM)
SMEM = pl.BlockSpec(memory_space=pltpu.SMEM)
HBM = pl.BlockSpec(memory_space=pltpu.HBM)
PARAMS = pltpu.CompilerParams(vmem_limit_bytes=20 * 1024 * 1024)


def fixed(values):
    return jnp.floor(values * SCALE + 0.5).astype(jnp.int32)


def column_of(row, first, count):
    spot = lax.broadcasted_iota(jnp.int32, (count, row.shape[1]), 1) == (
        lax.broadcasted_iota(jnp.int32, (count, row.shape[1]), 0) + first
    )
    return jnp.sum(jnp.where(spot, row, 0.0), axis=1, keepdims=True)


def group_index():
    return lax.axis_index("row") * lax.axis_size("col") + lax.axis_index("col")


def row_sums(values):
    ones = jnp.ones((8, values.shape[0]), jnp.bfloat16)
    return jnp.dot(ones, values, preferred_element_type=jnp.float32)[0:1, :]


def sums_of(values):
    ones = jnp.ones((values.shape[0], 128), jnp.bfloat16)
    return lax.dot_general(values, ones, (((0,), (0,)), ((), ())), preferred_element_type=jnp.float32)[:, 0:1]


def cut_kernel(soft_ref, head_ref, tail_ref, done_ref, sems):
    width = soft_ref.shape[1]
    reach = head_ref.shape[1]
    copies = [
        pltpu.make_async_copy(soft_ref.at[:, pl.ds(width - reach, reach)], tail_ref, sems.at[0]),
        pltpu.make_async_copy(soft_ref.at[:, pl.ds(0, reach)], head_ref, sems.at[1]),
    ]
    for copy in copies:
        copy.start()
    done_ref[...] = jnp.zeros_like(done_ref)
    for copy in copies:
        copy.wait()


def cut_call(soft, reach):
    shape = jax.ShapeDtypeStruct((soft.shape[0], reach), soft.dtype)
    return pl.pallas_call(
        cut_kernel,
        out_shape=[shape, shape, jax.ShapeDtypeStruct((8, 128), jnp.float32)],
        in_specs=[HBM],
        out_specs=[VMEM, VMEM, VMEM],
        scratch_shapes=[pltpu.SemaphoreType.DMA((2,))],
        compiler_params=pltpu.CompilerParams(vmem_limit_bytes=58 * 1024 * 1024),
        cost_estimate=pl.CostEstimate(flops=0, bytes_accessed=3_000_000, transcendentals=0),
    )(soft)


def spread(cov_ref, slot, tile, me):
    groups, _, share, _ = cov_ref.shape
    for d in range(groups):
        at = lax.rem(d - me + groups, groups)
        cov_ref[at, slot] = tile[d * share : (d + 1) * share, :]


def rows_of(row, pieces):
    width = row.shape[1] // pieces
    return [row[:, p * width : (p + 1) * width] for p in range(pieces)]


def ready_kernel(
    width, partners_ref, own_ref, inc_ref, keyt_ref, probt_ref, _,
    fit_ref, vals_ref, hot_ref, cov_ref, early_ref, sums_ref, pick_ref,
):
    blocks, slots = partners_ref.shape
    mine = blocks // 2
    shots = own_ref.shape[0]
    edges = inc_ref.shape[2]
    pieces = edges // width
    me = lax.axis_index("shot")
    base = group_index() * blocks
    lines = lax.broadcasted_iota(jnp.int32, (width, edges), 0)
    products, firsts, others = [], [], []
    for b in range(blocks):
        own = own_ref[:, b * width : (b + 1) * width]
        rows_x = inc_ref[0, b : b + 1, :]
        slot_x = inc_ref[1, b : b + 1, :]
        cols_x = inc_ref[2, b : b + 1, :]
        halo_first = base - HALO if b < mine else base + blocks
        chosen, hot = [], []
        far = [jnp.full((1, edges), -1, jnp.int32) for _ in range(HALO)]
        for k in range(slots):
            partner = partners_ref[b, k]
            tile = b * slots + k
            pick_ref[REACH, tile : tile + 1, :] = jnp.where(
                jnp.full((1, width), partner, jnp.int32) >= 0, 1.0, 0.0
            )
            partner = jnp.where(partner >= 0, partner, base + b)
            for w in range(REACH):
                pick_ref[w, tile : tile + 1, :] = jnp.where(
                    jnp.full((1, width), partner - base + HALO, jnp.int32) == w, 1.0, 0.0
                )
            inside = (partner >= base) & (partner < base + blocks)
            start = pl.multiple_of(jnp.where(inside, partner - base, b) * width, width)
            chosen.append(own_ref[:, pl.ds(start, width)])
            here = slot_x == k
            hot.append((lines == jnp.where(here & inside, cols_x, -1)).astype(jnp.bfloat16))
            for w in range(HALO):
                there = here & (partner == halo_first + w) & jnp.logical_not(inside)
                far[w] = jnp.where(there, cols_x, far[w])
        for w in range(HALO):
            hot_ref[b, w * width : (w + 1) * width, :] = (lines == far[w]).astype(jnp.bfloat16)
        chosen = jnp.concatenate(chosen, axis=1)
        tiles = lax.dot_general(own, chosen, (((0,), (0,)), ((), ())), preferred_element_type=jnp.float32)
        tiles = tiles - sums_of(own) * (row_sums(chosen) * (1.0 / shots))
        for k in range(slots):
            spread(cov_ref, b * slots + k, tiles[:, k * width : (k + 1) * width], me)
        vals = jnp.dot(own, (lines == rows_x).astype(jnp.bfloat16), preferred_element_type=jnp.float32)
        vals_ref[b] = vals.astype(jnp.bfloat16)
        other = jnp.dot(chosen, jnp.concatenate(hot, axis=0), preferred_element_type=jnp.float32)
        products += rows_of(jnp.sum(vals * other, axis=0, keepdims=True), pieces)
        firsts += rows_of(jnp.sum(vals, axis=0, keepdims=True), pieces)
        others += rows_of(jnp.sum(other, axis=0, keepdims=True), pieces)
        key = slot_x * (width * width) + rows_x * width + cols_x
        same = keyt_ref[:, b : b + 1] == key
        fit_ref[b : b + 1, :] = jnp.sum(jnp.where(same, probt_ref[:, b : b + 1], 0.0), axis=0, keepdims=True)
    early_ref[...] = jnp.concatenate(products + firsts + others, axis=0)
    sums_ref[...] = jnp.concatenate(rows_of(row_sums(own_ref[...]), blocks), axis=0)


def ready_call(partners, soft, incidence, keys_t, prob_t, after, width, groups):
    shots = soft.shape[0]
    blocks, slots = partners.shape
    edges = incidence.shape[2]
    return pl.pallas_call(
        functools.partial(ready_kernel, width),
        out_shape=[
            jax.ShapeDtypeStruct((blocks, edges), jnp.float32),
            jax.ShapeDtypeStruct((blocks, shots, edges), jnp.bfloat16),
            jax.ShapeDtypeStruct((blocks, HALO * width, edges), jnp.bfloat16),
            jax.ShapeDtypeStruct((groups, blocks * slots, width // groups, width), jnp.float32),
            jax.ShapeDtypeStruct((3 * blocks * edges // width, width), jnp.float32),
            jax.ShapeDtypeStruct((blocks, width), jnp.float32),
            jax.ShapeDtypeStruct((REACH + 1, blocks * slots, width), jnp.float32),
        ],
        in_specs=[SMEM] + [VMEM] * 4 + [ANY],
        out_specs=[VMEM] * 7,
        compiler_params=PARAMS,
        cost_estimate=pl.CostEstimate(flops=20_000_000_000, bytes_accessed=12_000_000, transcendentals=0),
    )(partners, soft, incidence, keys_t, prob_t, after)


def factors_of(came_ref, words):
    scales = came_ref[came_ref.shape[0] - TAIL : came_ref.shape[0] - TAIL + words, :]
    step = UNIT / 32767.0
    low = (scales & 65535).astype(jnp.float32) * step
    return low, lax.shift_right_logical(scales, 16).astype(jnp.float32) * step


def words_of(came_ref, word, share, factors):
    words = came_ref[word * share : (word + 1) * share, :]
    low = lax.shift_right_arithmetic(words << 16, 16).astype(jnp.float32)
    high = lax.shift_right_arithmetic(words, 16).astype(jnp.float32)
    return low * factors[0][word : word + 1, :], high * factors[1][word : word + 1, :]


def encode(exact, sums, edges, out_ref):
    tiles, share, _ = exact.shape
    words = tiles // 2
    body = words * share
    out_ref[body + words : body + words + REACH, :] = sums
    out_ref[body + words + REACH :, :] = edges
    scales, steps = [], []
    for i in range(2):
        tops = [jnp.max(jnp.abs(exact[2 * word + i]), axis=0, keepdims=True) for word in range(words)]
        scale = jnp.floor(jnp.concatenate(tops, axis=0) * (1.0 / UNIT)).astype(jnp.int32) + 1
        scales.append(scale)
        steps.append(32767.0 / (scale.astype(jnp.float32) * UNIT))
    out_ref[body : body + words, :] = (scales[1] << 16) | scales[0]
    for word in range(words):
        low, high = [
            jnp.floor(exact[2 * word + i] * steps[i][word : word + 1, :] + 0.5).astype(jnp.int32) for i in range(2)
        ]
        out_ref[word * share : (word + 1) * share, :] = (high << 16) | (low & 65535)


def pair_kernel(
    partners_ref, left_ref, right_ref, own_ref, vals_ref, hot_ref, early_ref, own_sums_ref, _,
    cov_ref, edge_ref, sums_ref, up_ref, down_ref,
):
    blocks, slots = partners_ref.shape
    mine = blocks // 2
    shots = own_ref.shape[0]
    groups = cov_ref.shape[0]
    width = cov_ref.shape[3]
    pieces = hot_ref.shape[2] // width
    me = lax.axis_index("shot")
    base = group_index() * blocks
    halves = [ref[...] for ref in (left_ref, right_ref)]
    halo_sums = [row_sums(halo) for halo in halves]
    products, others = [], []
    for block in range(blocks):
        side = block // mine
        halo = halves[side]
        offsets = [w + (blocks if side else -HALO) for w in range(HALO)]
        own = own_ref[:, block * width : (block + 1) * width]
        reached = [w for w in range(HALO) if abs(block - offsets[w]) <= HALO]
        first, last = reached[0] * width, (reached[-1] + 1) * width
        tiles = lax.dot_general(
            own, halo[:, first:last], (((0,), (0,)), ((), ())), preferred_element_type=jnp.float32
        )
        tiles = tiles - sums_of(own) * (halo_sums[side][:, first:last] * (1.0 / shots))
        for n, w in enumerate(reached):
            for k in range(1, slots):
                partner = partners_ref[block, k]

                @pl.when((partner >= 0) & (partner == base + offsets[w]))
                def _():
                    spread(cov_ref, block * slots + k, tiles[:, n * width : (n + 1) * width], me)

        other = jnp.dot(halo, hot_ref[block], preferred_element_type=jnp.float32)
        product = jnp.sum(vals_ref[block].astype(jnp.float32) * other, axis=0, keepdims=True)
        products += rows_of(product, pieces)
        others += rows_of(jnp.sum(other, axis=0, keepdims=True), pieces)
    count = blocks * pieces
    sums = fixed(
        jnp.concatenate(rows_of(halo_sums[0], HALO) + [own_sums_ref[...]] + rows_of(halo_sums[1], HALO), axis=0)
    )
    edges = early_ref[...] + jnp.concatenate(
        products + [jnp.zeros((count, width), jnp.float32)] + others, axis=0
    )
    edges = fixed(edges)
    sums_ref[...] = sums
    edge_ref[...] = edges
    encode(cov_ref.at[groups // 2], sums, edges, up_ref)
    encode(cov_ref.at[groups // 2 + 1], sums, edges, down_ref)


def pair_call(partners, left, right, soft, vals, hot, early, own_sums, cov):
    _, tiles, share, width = cov.shape
    message = jax.ShapeDtypeStruct((tiles // 2 * share + TAIL, width), jnp.int32)
    return pl.pallas_call(
        pair_kernel,
        out_shape=[
            jax.ShapeDtypeStruct(cov.shape, jnp.float32),
            jax.ShapeDtypeStruct(early.shape, jnp.int32),
            jax.ShapeDtypeStruct((REACH, width), jnp.int32),
            message,
            message,
        ],
        in_specs=[SMEM] + [VMEM] * 8,
        out_specs=[VMEM] * 5,
        input_output_aliases={8: 0},
        compiler_params=PARAMS,
        cost_estimate=pl.CostEstimate(flops=2_000_000_000, bytes_accessed=4_000_000, transcendentals=0),
    )(partners, left, right, soft, vals, hot, early, own_sums, cov)


def picked(pick_ref, rows):
    total = pick_ref[0] * rows[0:1, :]
    for w in range(1, REACH):
        total = total + pick_ref[w] * rows[w : w + 1, :]
    return total


def hop_kernel(at, seen, came_ref, cov_ref, edge_ref, sums_ref, pick_ref, _, out_ref, exact):
    groups, tiles, share, width = cov_ref.shape
    words = tiles // 2
    body = words * share
    blocks = REACH - 2 * HALO
    slots = tiles // blocks
    old = came_ref[body + words : body + words + REACH, :]
    sums = sums_ref[...]
    shift = old.astype(jnp.float32) * (1.0 / (SCALE * SHOTS * seen)) - sums.astype(jnp.float32) * (
        1.0 / (SCALE * SHOTS)
    )
    others = picked(pick_ref, shift)
    factors = factors_of(came_ref, words)
    dest = lax.rem(lax.axis_index("shot") + at, groups)
    for block in range(blocks):
        column = column_of(shift[block + HALO : block + HALO + 1, :], dest * share, share)
        column = column * (float(SHOTS) * seen / (seen + 1))
        for pair in range(slots // 2):
            word = block * (slots // 2) + pair
            came = words_of(came_ref, word, share, factors)
            for i in range(2):
                tile = 2 * word + i
                exact[tile] = cov_ref[at, tile] + came[i] + column * others[tile : tile + 1, :]
    encode(exact, sums + old, edge_ref[...] + came_ref[body + words + REACH :, :], out_ref)


def hop_call(at, seen, came, parts, after):
    tiles, share, width = parts[0].shape[1:]
    return pl.pallas_call(
        functools.partial(hop_kernel, at, seen),
        out_shape=jax.ShapeDtypeStruct(came.shape, jnp.int32),
        in_specs=[VMEM] * 5 + [ANY],
        out_specs=VMEM,
        scratch_shapes=[pltpu.VMEM((tiles, share, width), jnp.float32)],
        compiler_params=PARAMS,
        cost_estimate=pl.CostEstimate(flops=1_000_000, bytes_accessed=600_000, transcendentals=0),
    )(came, *parts, after)


def final_kernel(
    rises, falls, inc_ref, rising_ref, falling_ref, cov_ref, edge_ref, sums_ref, pick_ref, fit_ref,
    pair_ref, grad_ref,
):
    groups, tiles, share, width = cov_ref.shape
    words = tiles // 2
    body = words * share
    blocks, slots = pair_ref.shape[:2]
    pieces = inc_ref.shape[2] // width
    count = float(SHOTS * groups)
    start = lax.axis_index("shot") * share
    sums = sums_ref[...]
    rise_sums = rising_ref[body + words : body + words + REACH, :]
    fall_sums = falling_ref[body + words : body + words + REACH, :]

    def mean(values, sources):
        return values.astype(jnp.float32) * (1.0 / (SCALE * SHOTS * sources))

    first_shift = mean(rise_sums, rises) - mean(sums, 1)
    second_shift = mean(fall_sums, falls) - mean(sums + rise_sums, rises + 1)
    totals = (sums + rise_sums + fall_sums).astype(jnp.float32) * (1.0 / SCALE)
    firsts, seconds, alls = picked(pick_ref, first_shift), picked(pick_ref, second_shift), picked(pick_ref, totals)
    first_weight = float(SHOTS) * rises / (rises + 1)
    second_weight = float(SHOTS) * falls * (rises + 1) / (rises + 1 + falls)
    edges = edge_ref[...] + rising_ref[body + words + REACH :, :] + falling_ref[body + words + REACH :, :]
    edges = edges.astype(jnp.float32) * (1.0 / SCALE)
    risen_factors, fallen_factors = factors_of(rising_ref, words), factors_of(falling_ref, words)
    for block in range(blocks):
        own = slice(block + HALO, block + HALO + 1)
        first_column = column_of(first_shift[own, :], start, share) * first_weight
        second_column = column_of(second_shift[own, :], start, share) * second_weight
        total_column = column_of(totals[own, :], start, share) * (1.0 / count)
        for pair in range(slots // 2):
            word = block * (slots // 2) + pair
            risen = words_of(rising_ref, word, share, risen_factors)
            fallen = words_of(falling_ref, word, share, fallen_factors)
            for i in range(2):
                row = slice(2 * word + i, 2 * word + i + 1)
                cov = cov_ref[0, 2 * word + i] + risen[i] + first_column * firsts[row, :]
                cov = cov + fallen[i] + second_column * seconds[row, :]
                alone = total_column * alls[row, :]
                entry = 0.5 - 0.5 * jnp.sqrt(alone / (alone + cov))
                pair_ref[block, 2 * pair + i] = (entry * pick_ref[REACH, row, :]).astype(jnp.bfloat16)
        for p in range(pieces):
            n = block * pieces + p
            at = slice(p * width, (p + 1) * width)
            slot_x = inc_ref[1, block : block + 1, at]
            live = jnp.zeros((1, width), jnp.float32)
            for k in range(slots):
                tile = block * slots + k
                live = live + jnp.where(slot_x == k, pick_ref[REACH, tile : tile + 1, :], 0.0)
            rows = blocks * pieces
            quotient = (edges[rows + n : rows + n + 1] / count) * (
                edges[2 * rows + n : 2 * rows + n + 1] / count
            ) * count / edges[n : n + 1]
            entry = (0.5 - 0.5 * jnp.sqrt(quotient)) * live
            residual = live * (entry - fit_ref[block : block + 1, at]) / NOISE_SPREAD
            grad_ref[block : block + 1, at] = -residual / NOISE_SPREAD


def final_call(slots, incidence, rising, falling, parts, fit):
    groups, tiles, share, width = parts[0].shape
    half = groups // 2
    return pl.pallas_call(
        functools.partial(final_kernel, half, groups - 1 - half),
        out_shape=[
            jax.ShapeDtypeStruct((tiles // slots, slots, share, width), jnp.bfloat16),
            jax.ShapeDtypeStruct((tiles // slots, incidence.shape[2]), jnp.float32),
        ],
        in_specs=[VMEM] * 8,
        out_specs=[VMEM] * 2,
        compiler_params=PARAMS,
        cost_estimate=pl.CostEstimate(flops=1_000_000, bytes_accessed=2_000_000, transcendentals=100_000),
    )(incidence, rising, falling, *parts, fit)


def local(soft, partners, incidence, edge_prob):
    shots, own_width = soft.shape
    blocks, slots = partners.shape
    width = own_width // blocks
    groups = lax.axis_size("shot")
    sides = lax.axis_size(("row", "col"))

    head, tail, cut = cut_call(soft, HALO * width)
    left = lax.ppermute(tail, ("row", "col"), [(i, (i + 1) % sides) for i in range(sides)])
    right = lax.ppermute(head, ("row", "col"), [((i + 1) % sides, i) for i in range(sides)])

    keys = incidence[1] * (width * width) + incidence[0] * width + incidence[2]
    fit, vals, hot, cov, early, own_sums, pick = ready_call(
        partners, soft, incidence, keys.T, edge_prob.T, cut, width, groups
    )
    cov, edges, sums, up, down = pair_call(partners, left, right, soft, vals, hot, early, own_sums, cov)
    parts = (cov, edges, sums, pick)

    half = groups // 2
    rise = [(i, (i + 1) % groups) for i in range(groups)]
    fall = [(b, a) for a, b in rise]
    rising = lax.ppermute(up, "shot", rise)
    falling = lax.ppermute(down, "shot", fall)
    order = down
    for step in range(1, half):
        order = hop_call(half - step, step, rising, parts, order)
        rising = lax.ppermute(order, "shot", rise)
        if step < half - 1:
            order = hop_call(half + 1 + step, step, falling, parts, order)
            falling = lax.ppermute(order, "shot", fall)
    return final_call(slots, incidence, rising, falling, parts, fit)


def solution(mesh):
    placed = (
        P("shot", ("row", "col")),
        P(("row", "col"), None),
        P(None, ("row", "col"), None),
        P(("row", "col"), None),
    )
    return jax.shard_map(
        local,
        mesh=mesh,
        in_specs=placed,
        out_specs=(P(("row", "col"), None, "shot", None), P(("row", "col"), None)),
        check_vma=False,
    )
```

time: 118 us -> 114 us (0.966)
  Pallas kernels: 30.8 us -> 21.1 us
  waiting for transfers between devices: 15.7 us -> 20.5 us
    ppermute x0 -> x2, starting transfers between devices: none -> 13.3 us  [the longest x1 9.5 us: local(): falling = lax.ppermute(down, 'shot', fall)]
    ppermute x7 -> x6, starting transfers between devices: 40.6 us -> 31.1 us  [local(): falling = lax.ppermute(order, 'shot', fall)]
    pallas_call x15 -> x13, Pallas kernels: 11.7 us -> 3.12 us  [hop_call(): pl.pallas_call(functools.partial(hop_kernel, at, seen), out_shape=jax.Sha...]
    ppermute x8 -> x7, starting transfers between devices: 17.3 us -> 13.4 us  [local(): rising = lax.ppermute(order, 'shot', rise)]
    ppermute x8 -> x7, waiting for transfers between devices: 13.3 us -> 16.7 us  [local(): rising = lax.ppermute(order, 'shot', rise)]
    ppermute x0 -> x2, waiting for transfers between devices: none -> 1.44 us  [the longest x1 1.44 us: local(): rising = lax.ppermute(up, 'shot', rise)]
    ppermute x1, waiting for transfers between devices: 2.45 us -> 1.27 us  [local(): lax.ppermute(tail, ('row', 'col'), [(i, (i + 1) % sides) for i in range(s...]
    unnamed x11 -> x9, local copies, waits for them, and re-layouts: 3.21 us -> 4.35 us
  transfers between devices with their start and end apart: 17 -> 17, of which waited for: 9 -> 10; matrix products, arithmetic and copies ran while one was open for 2% -> 2% of each run, Pallas kernels for 20% -> 11%
where the time goes in v8:
time: 114 us; the launch traced here: 113 us
  starting transfers between devices  65.5 us (57%)
  Pallas kernels  21.1 us (19%)
  waiting for transfers between devices  20.5 us (18%)
  local copies, waits for them, and re-layouts  4.5 us (4%)
    ppermute x6, starting transfers between devices, local(): falling = lax.ppermute(order, 'shot', fall)  31.1 us
    ppermute x7, waiting for transfers between devices, local(): rising = lax.ppermute(order, 'shot', rise)  16.7 us
    ppermute x7, starting transfers between devices, local(): rising = lax.ppermute(order, 'shot', rise)  13.4 us
    ppermute x1, starting transfers between devices, local(): falling = lax.ppermute(down, 'shot', fall)  9.5 us
    pallas_call x1, Pallas kernels, ready_call(): pl.pallas_call(functools.partial(ready_kernel, width), out_shape=[jax.Sha...  9.23 us
    pallas_call x1, Pallas kernels, pair_call(): pl.pallas_call(pair_kernel, out_shape=[jax.ShapeDtypeStruct(cov.shape, jn...  5.22 us
    unnamed x9, local copies, waits for them, and re-layouts  4.35 us
    ppermute x1, starting transfers between devices, local(): lax.ppermute(head, ('row', 'col'), [((i + 1) % sides, i) for i in range(s...  4.27 us
  transfers between devices with their start and end apart: 17, of which 10 were waited for; matrix products, arithmetic and copies ran while one was open for 2% of the time, Pallas kernels for 11%

profile of v8, /device:TPU:24, one launch (start us, length us, event | category | flops | bytes accessed | tf_op | source)
XLA Modules:
  0.0 113.3 jit_solution(3605240416369567091)
XLA Ops:
  0.6 2.6 %shard_map.59 = (bf16[768,512]{1,0:T(8,128)(2,1)}, bf16[768,512]{1,0:T(8,128)(2,1)}, f32[8,128]{1,0:T(8,128)}) custom-call(bf16[768,1024]{1,0:T(8,128)(2,1)} %own_ref.3), custom_call_target="tpu_custom_call" | custom-call | bytes 3000000 | tf_op jit(solution)/shard_map/pallas_call | solution.py:65
  3.2 3.4 %collective-permute-start = (bf16[768,512]{1,0:T(8,128)(2,1)}, bf16[768,512]{1,0:T(8,128)(2,1)S(1)}, u32[]{:S(2)}, u32[]{:S(2)}) collective-permute-start(bf16[768,512]{1,0:T(8,128)(2,1)} %get-tuple-element.17), channel_id=1, source_target_pairs={{0,1},{1,2},{2,3},{3,4},{4,5},{5,6},{6,7},{7,8},{8,9},{9,10},{10,1... | collective-permute-start | bytes 2359304 | tf_op jit(solution)/shard_map/ppermute | solution.py:406
  6.6 4.3 %collective-permute-start.1 = (bf16[768,512]{1,0:T(8,128)(2,1)}, bf16[768,512]{1,0:T(8,128)(2,1)S(1)}, u32[]{:S(2)}, u32[]{:S(2)}) collective-permute-start(bf16[768,512]{1,0:T(8,128)(2,1)} %get-tuple-element.18), channel_id=1, source_target_pairs={{1,0},{2,1},{3,2},{4,3},{5,4},{6,5},{7,6},{8,7},{9,8},{10,9},{11,1... | collective-permute-start | bytes 2359304 | tf_op jit(solution)/shard_map/ppermute | solution.py:407
  16.1 9.2 %shard_map.60 = (f32[4,512]{1,0:T(4,128)S(1)}, bf16[4,768,512]{2,1,0:T(8,128)(2,1)S(1)}, bf16[4,512,512]{2,1,0:T(8,128)(2,1)S(1)}, f32[16,16,16,256]{3,2,1,0:T(8...) custom-call(s32[4,4]{1,0:T(4,128)S(1)} %copy-done.2, ...), custom_call_target="tpu_custom_call" | custom-call | flops 20000000000 | bytes 12000000 | tf_op jit(solution)/shard_map/pallas_call | solution.py:152
  27.7 5.2 %shard_map.61 = (f32[16,16,16,256]{3,2,1,0:T(8,128)S(1)}, s32[24,256]{1,0:T(8,128)S(1)}, s32[8,256]{1,0:T(8,128)S(1)}, s32[168,256]{1,0:T(8,128)S(1)}, s32[168,256]{1,0:T(8,128)S(1)}) custom-call(s32[4,4]{1,0:T(4,128)S(1)} %copy-done.2, bf16[768,512]{1,0:T(8,128)(2,1)S(1)} %collective-permute-done.left_ref, ...), custom_call_target="tpu_custom_call", output_to_operand_aliasing={{0}: (8, {})} | custom-call | flops 2000000000 | bytes 4000000 | tf_op jit(solution)/shard_map/pallas_call | solution.py:259
  32.9 3.8 %collective-permute-start.2 = (s32[168,256]{1,0:T(8,128)S(1)}, s32[168,256]{1,0:T(8,128)S(1)}, u32[]{:S(2)}, u32[]{:S(2)}) collective-permute-start(s32[168,256]{1,0:T(8,128)S(1)} %get-tuple-element.25), channel_id=1, source_target_pairs={{0,32},{32,64},{64,96},{96,128},{128,160},{160,192},{192,224},{224... | collective-permute-start | bytes 516104 | tf_op jit(solution)/shard_map/ppermute | solution.py:419
  36.8 9.5 %collective-permute-start.4 = (s32[168,256]{1,0:T(8,128)S(1)}, s32[168,256]{1,0:T(8,128)S(1)}, u32[]{:S(2)}, u32[]{:S(2)}) collective-permute-start(s32[168,256]{1,0:T(8,128)S(1)} %get-tuple-element.30._), channel_id=1, source_target_pairs={{32,0},{64,32},{96,64},{128,96},{160,128},{192,160},{224,192},{256... | collective-permute-start | bytes 516104 | tf_op jit(solution)/shard_map/ppermute | solution.py:420
  48.0 1.9 %collective-permute-start.3 = (s32[168,256]{1,0:T(8,128)S(1)}, s32[168,256]{1,0:T(8,128)S(1)}, u32[]{:S(2)}, u32[]{:S(2)}) collective-permute-start(s32[168,256]{1,0:T(8,128)S(1)} %shard_map.62._), channel_id=1, source_target_pairs={{0,32},{32,64},{64,96},{96,128},{128,160},{160,192},{192,224},{224... | collective-permute-start | bytes 516104 | tf_op jit(solution)/shard_map/ppermute | solution.py:424
  50.1 5.1 %collective-permute-start.6 = (s32[168,256]{1,0:T(8,128)S(1)}, s32[168,256]{1,0:T(8,128)S(1)}, u32[]{:S(2)}, u32[]{:S(2)}) collective-permute-start(s32[168,256]{1,0:T(8,128)S(1)} %shard_map.63._), channel_id=1, source_target_pairs={{32,0},{64,32},{96,64},{128,96},{160,128},{192,160},{224,192},{256... | collective-permute-start | bytes 516104 | tf_op jit(solution)/shard_map/ppermute | solution.py:427
  56.7 1.9 %collective-permute-start.5 = (s32[168,256]{1,0:T(8,128)S(1)}, s32[168,256]{1,0:T(8,128)S(1)}, u32[]{:S(2)}, u32[]{:S(2)}) collective-permute-start(s32[168,256]{1,0:T(8,128)S(1)} %shard_map.64._), channel_id=1, source_target_pairs={{0,32},{32,64},{64,96},{96,128},{128,160},{160,192},{192,224},{224... | collective-permute-start | bytes 516104 | tf_op jit(solution)/shard_map/ppermute | solution.py:424
  58.9 5.1 %collective-permute-start.8 = (s32[168,256]{1,0:T(8,128)S(1)}, s32[168,256]{1,0:T(8,128)S(1)}, u32[]{:S(2)}, u32[]{:S(2)}) collective-permute-start(s32[168,256]{1,0:T(8,128)S(1)} %shard_map.65._), channel_id=1, source_target_pairs={{32,0},{64,32},{96,64},{128,96},{160,128},{192,160},{224,192},{256... | collective-permute-start | bytes 516104 | tf_op jit(solution)/shard_map/ppermute | solution.py:427
  65.5 1.9 %collective-permute-start.7 = (s32[168,256]{1,0:T(8,128)S(1)}, s32[168,256]{1,0:T(8,128)S(1)}, u32[]{:S(2)}, u32[]{:S(2)}) collective-permute-start(s32[168,256]{1,0:T(8,128)S(1)} %shard_map.66._), channel_id=1, source_target_pairs={{0,32},{32,64},{64,96},{96,128},{128,160},{160,192},{192,224},{224... | collective-permute-start | bytes 516104 | tf_op jit(solution)/shard_map/ppermute | solution.py:424
  67.6 5.1 %collective-permute-start.10 = (s32[168,256]{1,0:T(8,128)S(1)}, s32[168,256]{1,0:T(8,128)S(1)}, u32[]{:S(2)}, u32[]{:S(2)}) collective-permute-start(s32[168,256]{1,0:T(8,128)S(1)} %shard_map.67._), channel_id=1, source_target_pairs={{32,0},{64,32},{96,64},{128,96},{160,128},{192,160},{224,192},{256... | collective-permute-start | bytes 516104 | tf_op jit(solution)/shard_map/ppermute | solution.py:427
  74.2 1.9 %collective-permute-start.9 = (s32[168,256]{1,0:T(8,128)S(1)}, s32[168,256]{1,0:T(8,128)S(1)}, u32[]{:S(2)}, u32[]{:S(2)}) collective-permute-start(s32[168,256]{1,0:T(8,128)S(1)} %shard_map.68._), channel_id=1, source_target_pairs={{0,32},{32,64},{64,96},{96,128},{128,160},{160,192},{192,224},{224... | collective-permute-start | bytes 516104 | tf_op jit(solution)/shard_map/ppermute | solution.py:424
  76.4 5.1 %collective-permute-start.12 = (s32[168,256]{1,0:T(8,128)S(1)}, s32[168,256]{1,0:T(8,128)S(1)}, u32[]{:S(2)}, u32[]{:S(2)}) collective-permute-start(s32[168,256]{1,0:T(8,128)S(1)} %shard_map.69._), channel_id=1, source_target_pairs={{32,0},{64,32},{96,64},{128,96},{160,128},{192,160},{224,192},{256... | collective-permute-start | bytes 516104 | tf_op jit(solution)/shard_map/ppermute | solution.py:427
  81.5 2.0 %collective-permute-done.9.came_ref = s32[168,256]{1,0:T(8,128)S(1)} collective-permute-done((s32[168,256]{1,0:T(8,128)S(1)}, s32[168,256]{1,0:T(8,128)S(1)}, u32[]{:S(2)}, u32[]{:S(2)}) %collective-permute-start.9) | collective-permute-done | bytes 172064 | tf_op jit(solution)/shard_map/ppermute | solution.py:424
  83.8 1.9 %collective-permute-start.11 = (s32[168,256]{1,0:T(8,128)S(1)}, s32[168,256]{1,0:T(8,128)S(1)}, u32[]{:S(2)}, u32[]{:S(2)}) collective-permute-start(s32[168,256]{1,0:T(8,128)S(1)} %shard_map.70._), channel_id=1, source_target_pairs={{0,32},{32,64},{64,96},{96,128},{128,160},{160,192},{192,224},{224... | collective-permute-start | bytes 516104 | tf_op jit(solution)/shard_map/ppermute | solution.py:424
  86.0 5.5 %collective-permute-start.14 = (s32[168,256]{1,0:T(8,128)S(1)}, s32[168,256]{1,0:T(8,128)S(1)}, u32[]{:S(2)}, u32[]{:S(2)}) collective-permute-start(s32[168,256]{1,0:T(8,128)S(1)} %shard_map.71._), channel_id=1, source_target_pairs={{32,0},{64,32},{96,64},{128,96},{160,128},{192,160},{224,192},{256... | collective-permute-start | bytes 516104 | tf_op jit(solution)/shard_map/ppermute | solution.py:427
  91.5 2.6 %collective-permute-done.11.came_ref = s32[168,256]{1,0:T(8,128)S(1)} collective-permute-done((s32[168,256]{1,0:T(8,128)S(1)}, s32[168,256]{1,0:T(8,128)S(1)}, u32[]{:S(2)}, u32[]{:S(2)}) %collective-permute-start.11) | collective-permute-done | bytes 172064 | tf_op jit(solution)/shard_map/ppermute | solution.py:424
  94.3 1.9 %collective-permute-start.13 = (s32[168,256]{1,0:T(8,128)S(1)}, s32[168,256]{1,0:T(8,128)S(1)}, u32[]{:S(2)}, u32[]{:S(2)}) collective-permute-start(s32[168,256]{1,0:T(8,128)S(1)} %shard_map.72._), channel_id=1, source_target_pairs={{0,32},{32,64},{64,96},{96,128},{128,160},{160,192},{192,224},{224... | collective-permute-start | bytes 516104 | tf_op jit(solution)/shard_map/ppermute | solution.py:424
  96.4 5.1 %collective-permute-start.16 = (s32[168,256]{1,0:T(8,128)S(1)}, s32[168,256]{1,0:T(8,128)S(1)}, u32[]{:S(2)}, u32[]{:S(2)}) collective-permute-start(s32[168,256]{1,0:T(8,128)S(1)} %shard_map.73._), channel_id=1, source_target_pairs={{32,0},{64,32},{96,64},{128,96},{160,128},{192,160},{224,192},{256... | collective-permute-start | bytes 516104 | tf_op jit(solution)/shard_map/ppermute | solution.py:427
  101.6 2.0 %collective-permute-done.13.came_ref = s32[168,256]{1,0:T(8,128)S(1)} collective-permute-done((s32[168,256]{1,0:T(8,128)S(1)}, s32[168,256]{1,0:T(8,128)S(1)}, u32[]{:S(2)}, u32[]{:S(2)}) %collective-permute-start.13) | collective-permute-done | bytes 172064 | tf_op jit(solution)/shard_map/ppermute | solution.py:424
  103.8 1.9 %collective-permute-start.15 = (s32[168,256]{1,0:T(8,128)S(1)}, s32[168,256]{1,0:T(8,128)S(1)}, u32[]{:S(2)}, u32[]{:S(2)}) collective-permute-start(s32[168,256]{1,0:T(8,128)S(1)} %shard_map.74), channel_id=1, source_target_pairs={{0,32},{32,64},{64,96},{96,128},{128,160},{160,192},{192,224},{224... | collective-permute-start | bytes 516104 | tf_op jit(solution)/shard_map/ppermute | solution.py:424
  105.8 6.6 %collective-permute-done.15.rising_ref = s32[168,256]{1,0:T(8,128)S(1)} collective-permute-done((s32[168,256]{1,0:T(8,128)S(1)}, s32[168,256]{1,0:T(8,128)S(1)}, u32[]{:S(2)}, u32[]{:S(2)}) %collective-permute-start.15) | collective-permute-done | bytes 172064 | tf_op jit(solution)/shard_map/ppermute | solution.py:424
  (38 shorter events, 16.7 us)
Async XLA Ops:
  3.2 23.4 %collective-permute-start = (bf16[768,512]{1,0:T(8,128)(2,1)}, bf16[768,512]{1,0:T(8,128)(2,1)S(1)}, u32[]{:S(2)}, u32[]{:S(2)}) collective-permute-start(bf16[768,512]{1,0:T(8,128)(2,1)} %get-tuple-element.17), channel_id=1, source_target_pairs={{0,1},{1,2},{2,3},{3,4},{4,5},{5,6},{6,7},{7,8},{8,9},{9,10},{10,1... | collective-permute-start | bytes 2359304 | tf_op jit(solution)/shard_map/ppermute | solution.py:406
  6.6 21.1 %collective-permute-start.1 = (bf16[768,512]{1,0:T(8,128)(2,1)}, bf16[768,512]{1,0:T(8,128)(2,1)S(1)}, u32[]{:S(2)}, u32[]{:S(2)}) collective-permute-start(bf16[768,512]{1,0:T(8,128)(2,1)} %get-tuple-element.18), channel_id=1, source_target_pairs={{1,0},{2,1},{3,2},{4,3},{5,4},{6,5},{7,6},{8,7},{9,8},{10,9},{11,1... | collective-permute-start | bytes 2359304 | tf_op jit(solution)/shard_map/ppermute | solution.py:407
  12.6 1.4 %copy-start = (bf16[768,1024]{1,0:T(8,128)(2,1)S(1)}, bf16[768,1024]{1,0:T(8,128)(2,1)}, u32[]{:S(2)}) copy-start(bf16[768,1024]{1,0:T(8,128)(2,1)} %own_ref.3) | copy-start | bytes 4718596
  14.0 0.7 copy-start.1
  14.8 0.7 copy-start.2
  15.5 0.7 copy-start.3
  32.9 14.8 %collective-permute-start.2 = (s32[168,256]{1,0:T(8,128)S(1)}, s32[168,256]{1,0:T(8,128)S(1)}, u32[]{:S(2)}, u32[]{:S(2)}) collective-permute-start(s32[168,256]{1,0:T(8,128)S(1)} %get-tuple-element.25), channel_id=1, source_target_pairs={{0,32},{32,64},{64,96},{96,128},{128,160},{160,192},{192,224},{224... | collective-permute-start | bytes 516104 | tf_op jit(solution)/shard_map/ppermute | solution.py:419
  36.8 13.1 %collective-permute-start.4 = (s32[168,256]{1,0:T(8,128)S(1)}, s32[168,256]{1,0:T(8,128)S(1)}, u32[]{:S(2)}, u32[]{:S(2)}) collective-permute-start(s32[168,256]{1,0:T(8,128)S(1)} %get-tuple-element.30._), channel_id=1, source_target_pairs={{32,0},{64,32},{96,64},{128,96},{160,128},{192,160},{224,192},{256... | collective-permute-start | bytes 516104 | tf_op jit(solution)/shard_map/ppermute | solution.py:420
  48.0 8.5 %collective-permute-start.3 = (s32[168,256]{1,0:T(8,128)S(1)}, s32[168,256]{1,0:T(8,128)S(1)}, u32[]{:S(2)}, u32[]{:S(2)}) collective-permute-start(s32[168,256]{1,0:T(8,128)S(1)} %shard_map.62._), channel_id=1, source_target_pairs={{0,32},{32,64},{64,96},{96,128},{128,160},{160,192},{192,224},{224... | collective-permute-start | bytes 516104 | tf_op jit(solution)/shard_map/ppermute | solution.py:424
  50.1 8.5 %collective-permute-start.6 = (s32[168,256]{1,0:T(8,128)S(1)}, s32[168,256]{1,0:T(8,128)S(1)}, u32[]{:S(2)}, u32[]{:S(2)}) collective-permute-start(s32[168,256]{1,0:T(8,128)S(1)} %shard_map.63._), channel_id=1, source_target_pairs={{32,0},{64,32},{96,64},{128,96},{160,128},{192,160},{224,192},{256... | collective-permute-start | bytes 516104 | tf_op jit(solution)/shard_map/ppermute | solution.py:427
  56.7 8.5 %collective-permute-start.5 = (s32[168,256]{1,0:T(8,128)S(1)}, s32[168,256]{1,0:T(8,128)S(1)}, u32[]{:S(2)}, u32[]{:S(2)}) collective-permute-start(s32[168,256]{1,0:T(8,128)S(1)} %shard_map.64._), channel_id=1, source_target_pairs={{0,32},{32,64},{64,96},{96,128},{128,160},{160,192},{192,224},{224... | collective-permute-start | bytes 516104 | tf_op jit(solution)/shard_map/ppermute | solution.py:424
  58.9 8.5 %collective-permute-start.8 = (s32[168,256]{1,0:T(8,128)S(1)}, s32[168,256]{1,0:T(8,128)S(1)}, u32[]{:S(2)}, u32[]{:S(2)}) collective-permute-start(s32[168,256]{1,0:T(8,128)S(1)} %shard_map.65._), channel_id=1, source_target_pairs={{32,0},{64,32},{96,64},{128,96},{160,128},{192,160},{224,192},{256... | collective-permute-start | bytes 516104 | tf_op jit(solution)/shard_map/ppermute | solution.py:427
  65.5 8.5 %collective-permute-start.7 = (s32[168,256]{1,0:T(8,128)S(1)}, s32[168,256]{1,0:T(8,128)S(1)}, u32[]{:S(2)}, u32[]{:S(2)}) collective-permute-start(s32[168,256]{1,0:T(8,128)S(1)} %shard_map.66._), channel_id=1, source_target_pairs={{0,32},{32,64},{64,96},{96,128},{128,160},{160,192},{192,224},{224... | collective-permute-start | bytes 516104 | tf_op jit(solution)/shard_map/ppermute | solution.py:424
  67.6 8.5 %collective-permute-start.10 = (s32[168,256]{1,0:T(8,128)S(1)}, s32[168,256]{1,0:T(8,128)S(1)}, u32[]{:S(2)}, u32[]{:S(2)}) collective-permute-start(s32[168,256]{1,0:T(8,128)S(1)} %shard_map.67._), channel_id=1, source_target_pairs={{32,0},{64,32},{96,64},{128,96},{160,128},{192,160},{224,192},{256... | collective-permute-start | bytes 516104 | tf_op jit(solution)/shard_map/ppermute | solution.py:427
  74.2 9.4 %collective-permute-start.9 = (s32[168,256]{1,0:T(8,128)S(1)}, s32[168,256]{1,0:T(8,128)S(1)}, u32[]{:S(2)}, u32[]{:S(2)}) collective-permute-start(s32[168,256]{1,0:T(8,128)S(1)} %shard_map.68._), channel_id=1, source_target_pairs={{0,32},{32,64},{64,96},{96,128},{128,160},{160,192},{192,224},{224... | collective-permute-start | bytes 516104 | tf_op jit(solution)/shard_map/ppermute | solution.py:424
  76.4 9.4 %collective-permute-start.12 = (s32[168,256]{1,0:T(8,128)S(1)}, s32[168,256]{1,0:T(8,128)S(1)}, u32[]{:S(2)}, u32[]{:S(2)}) collective-permute-start(s32[168,256]{1,0:T(8,128)S(1)} %shard_map.69._), channel_id=1, source_target_pairs={{32,0},{64,32},{96,64},{128,96},{160,128},{192,160},{224,192},{256... | collective-permute-start | bytes 516104 | tf_op jit(solution)/shard_map/ppermute | solution.py:427
  83.8 10.2 %collective-permute-start.11 = (s32[168,256]{1,0:T(8,128)S(1)}, s32[168,256]{1,0:T(8,128)S(1)}, u32[]{:S(2)}, u32[]{:S(2)}) collective-permute-start(s32[168,256]{1,0:T(8,128)S(1)} %shard_map.70._), channel_id=1, source_target_pairs={{0,32},{32,64},{64,96},{96,128},{128,160},{160,192},{192,224},{224... | collective-permute-start | bytes 516104 | tf_op jit(solution)/shard_map/ppermute | solution.py:424
  86.0 10.2 %collective-permute-start.14 = (s32[168,256]{1,0:T(8,128)S(1)}, s32[168,256]{1,0:T(8,128)S(1)}, u32[]{:S(2)}, u32[]{:S(2)}) collective-permute-start(s32[168,256]{1,0:T(8,128)S(1)} %shard_map.71._), channel_id=1, source_target_pairs={{32,0},{64,32},{96,64},{128,96},{160,128},{192,160},{224,192},{256... | collective-permute-start | bytes 516104 | tf_op jit(solution)/shard_map/ppermute | solution.py:427
  94.3 9.3 %collective-permute-start.13 = (s32[168,256]{1,0:T(8,128)S(1)}, s32[168,256]{1,0:T(8,128)S(1)}, u32[]{:S(2)}, u32[]{:S(2)}) collective-permute-start(s32[168,256]{1,0:T(8,128)S(1)} %shard_map.72._), channel_id=1, source_target_pairs={{0,32},{32,64},{64,96},{96,128},{128,160},{160,192},{192,224},{224... | collective-permute-start | bytes 516104 | tf_op jit(solution)/shard_map/ppermute | solution.py:424
  96.4 9.3 %collective-permute-start.16 = (s32[168,256]{1,0:T(8,128)S(1)}, s32[168,256]{1,0:T(8,128)S(1)}, u32[]{:S(2)}, u32[]{:S(2)}) collective-permute-start(s32[168,256]{1,0:T(8,128)S(1)} %shard_map.73._), channel_id=1, source_target_pairs={{32,0},{64,32},{96,64},{128,96},{160,128},{192,160},{224,192},{256... | collective-permute-start | bytes 516104 | tf_op jit(solution)/shard_map/ppermute | solution.py:427
  103.8 8.5 %collective-permute-start.15 = (s32[168,256]{1,0:T(8,128)S(1)}, s32[168,256]{1,0:T(8,128)S(1)}, u32[]{:S(2)}, u32[]{:S(2)}) collective-permute-start(s32[168,256]{1,0:T(8,128)S(1)} %shard_map.74), channel_id=1, source_target_pairs={{0,32},{32,64},{64,96},{96,128},{128,160},{160,192},{192,224},{224... | collective-permute-start | bytes 516104 | tf_op jit(solution)/shard_map/ppermute | solution.py:424

commit v9 on v8

--- a/solution.py
+++ b/solution.py
@@ -17,7 +17,6 @@
 ANY = pl.BlockSpec(memory_space=pl.ANY)
 VMEM = pl.BlockSpec(memory_space=pltpu.VMEM)
 SMEM = pl.BlockSpec(memory_space=pltpu.SMEM)
-HBM = pl.BlockSpec(memory_space=pltpu.HBM)
 PARAMS = pltpu.CompilerParams(vmem_limit_bytes=20 * 1024 * 1024)
 
 
@@ -65,10 +64,10 @@
     return pl.pallas_call(
         cut_kernel,
         out_shape=[shape, shape, jax.ShapeDtypeStruct((8, 128), jnp.float32)],
-        in_specs=[HBM],
+        in_specs=[ANY],
         out_specs=[VMEM, VMEM, VMEM],
         scratch_shapes=[pltpu.SemaphoreType.DMA((2,))],
-        compiler_params=pltpu.CompilerParams(vmem_limit_bytes=58 * 1024 * 1024),
+        compiler_params=PARAMS,
         cost_estimate=pl.CostEstimate(flops=0, bytes_accessed=3_000_000, transcendentals=0),
     )(soft)
 
@@ -203,7 +202,7 @@
 
 def pair_kernel(
     partners_ref, left_ref, right_ref, own_ref, vals_ref, hot_ref, early_ref, own_sums_ref, _,
-    cov_ref, edge_ref, sums_ref, up_ref, down_ref,
+    cov_ref, edge_ref, sums_ref, up_ref, down_ref, turn_ref,
 ):
     blocks, slots = partners_ref.shape
     mine = blocks // 2
@@ -251,6 +250,7 @@
     edge_ref[...] = edges
     encode(cov_ref.at[groups // 2], sums, edges, up_ref)
     encode(cov_ref.at[groups // 2 + 1], sums, edges, down_ref)
+    turn_ref[...] = jnp.where(me == groups - 1, up_ref[...], down_ref[...])
 
 
 def pair_call(partners, left, right, soft, vals, hot, early, own_sums, cov):
@@ -264,9 +264,10 @@
             jax.ShapeDtypeStruct((REACH, width), jnp.int32),
             message,
             message,
+            message,
         ],
         in_specs=[SMEM] + [VMEM] * 8,
-        out_specs=[VMEM] * 5,
+        out_specs=[VMEM] * 6,
         input_output_aliases={8: 0},
         compiler_params=PARAMS,
         cost_estimate=pl.CostEstimate(flops=2_000_000_000, bytes_accessed=4_000_000, transcendentals=0),
@@ -280,48 +281,60 @@
     return total
 
 
-def hop_kernel(at, seen, came_ref, cov_ref, edge_ref, sums_ref, pick_ref, _, out_ref, exact):
+def hop_kernel(step, up, came_ref, turned_ref, cov_ref, edge_ref, sums_ref, pick_ref, *refs):
+    out_ref = refs[1]
+    came, exact = refs[-2:]
     groups, tiles, share, width = cov_ref.shape
     words = tiles // 2
     body = words * share
     blocks = REACH - 2 * HALO
     slots = tiles // blocks
-    old = came_ref[body + words : body + words + REACH, :]
+    me = lax.axis_index("shot")
+    reach = groups // 2 if up else groups // 2 - 1
+    place = me if up else groups - 1 - me
+    late = jnp.where((place < reach) & (step > 1 + place), 1, 0)
+    hop = reach + 1 - step + late
+    seen = jnp.full((1, width), reach - hop, jnp.int32).astype(jnp.float32)
+    at = hop if up else lax.rem(groups - hop, groups)
+    came[...] = jnp.where(place == 0, turned_ref[...], came_ref[...])
+    old = came[body + words : body + words + REACH, :]
     sums = sums_ref[...]
-    shift = old.astype(jnp.float32) * (1.0 / (SCALE * SHOTS * seen)) - sums.astype(jnp.float32) * (
-        1.0 / (SCALE * SHOTS)
-    )
-    others = picked(pick_ref, shift)
-    factors = factors_of(came_ref, words)
-    dest = lax.rem(lax.axis_index("shot") + at, groups)
+    shift = (
+        old.astype(jnp.float32) * (1.0 / jnp.maximum(seen, 1.0)) - sums.astype(jnp.float32)
+    ) * (1.0 / (SCALE * SHOTS))
+    others = picked(pick_ref, shift * (seen * float(SHOTS) / (seen + 1.0)))
+    factors = factors_of(came, words)
+    dest = lax.rem(me + at, groups)
     for block in range(blocks):
         column = column_of(shift[block + HALO : block + HALO + 1, :], dest * share, share)
-        column = column * (float(SHOTS) * seen / (seen + 1))
         for pair in range(slots // 2):
             word = block * (slots // 2) + pair
-            came = words_of(came_ref, word, share, factors)
+            values = words_of(came, word, share, factors)
             for i in range(2):
                 tile = 2 * word + i
-                exact[tile] = cov_ref[at, tile] + came[i] + column * others[tile : tile + 1, :]
-    encode(exact, sums + old, edge_ref[...] + came_ref[body + words + REACH :, :], out_ref)
-
-
-def hop_call(at, seen, came, parts, after):
+                exact[tile] = cov_ref[at, tile] + values[i] + column * others[tile : tile + 1, :]
+    encode(exact, sums + old, edge_ref[...] + came[body + words + REACH :, :], out_ref)
+    if not up:
+        refs[2][...] = jnp.where(me == groups - 1, refs[0][...], out_ref[...])
+
+
+def hop_call(step, up, came, turned, parts, risen):
     tiles, share, width = parts[0].shape[1:]
+    shape = jax.ShapeDtypeStruct(came.shape, jnp.int32)
     return pl.pallas_call(
-        functools.partial(hop_kernel, at, seen),
-        out_shape=jax.ShapeDtypeStruct(came.shape, jnp.int32),
-        in_specs=[VMEM] * 5 + [ANY],
-        out_specs=VMEM,
-        scratch_shapes=[pltpu.VMEM((tiles, share, width), jnp.float32)],
+        functools.partial(hop_kernel, step, up),
+        out_shape=shape if up else [shape, shape],
+        in_specs=[VMEM] * 6 + [ANY if up else VMEM],
+        out_specs=VMEM if up else [VMEM, VMEM],
+        scratch_shapes=[pltpu.VMEM(came.shape, jnp.int32), pltpu.VMEM((tiles, share, width), jnp.float32)],
         compiler_params=PARAMS,
         cost_estimate=pl.CostEstimate(flops=1_000_000, bytes_accessed=600_000, transcendentals=0),
-    )(came, *parts, after)
+    )(came, turned, *parts, risen)
 
 
 def final_kernel(
-    rises, falls, inc_ref, rising_ref, falling_ref, cov_ref, edge_ref, sums_ref, pick_ref, fit_ref,
-    pair_ref, grad_ref,
+    rises, falls, inc_ref, rising_refs, falling_refs, cov_ref, edge_ref, sums_ref, pick_ref, fit_ref,
+    pair_ref, grad_ref, rising_ref, falling_ref,
 ):
     groups, tiles, share, width = cov_ref.shape
     words = tiles // 2
@@ -329,7 +342,13 @@
     blocks, slots = pair_ref.shape[:2]
     pieces = inc_ref.shape[2] // width
     count = float(SHOTS * groups)
-    start = lax.axis_index("shot") * share
+    me = lax.axis_index("shot")
+    start = me * share
+    for out, refs, place, arc in (
+        (rising_ref, rising_refs, me, rises), (falling_ref, falling_refs, groups - 1 - me, falls),
+    ):
+        late = jnp.where(place < arc, refs[1][...], refs[0][...])
+        out[...] = jnp.where(place == 0, refs[2][...], late)
     sums = sums_ref[...]
     rise_sums = rising_ref[body + words : body + words + REACH, :]
     fall_sums = falling_ref[body + words : body + words + REACH, :]
@@ -382,17 +401,23 @@
 def final_call(slots, incidence, rising, falling, parts, fit):
     groups, tiles, share, width = parts[0].shape
     half = groups // 2
+    message = pltpu.VMEM(rising[0].shape, jnp.int32)
+
+    def kernel(inc_ref, *refs):
+        final_kernel(half, groups - 1 - half, inc_ref, refs[:3], refs[3:6], *refs[6:])
+
     return pl.pallas_call(
-        functools.partial(final_kernel, half, groups - 1 - half),
+        kernel,
         out_shape=[
             jax.ShapeDtypeStruct((tiles // slots, slots, share, width), jnp.bfloat16),
             jax.ShapeDtypeStruct((tiles // slots, incidence.shape[2]), jnp.float32),
         ],
-        in_specs=[VMEM] * 8,
+        in_specs=[VMEM] * 12,
         out_specs=[VMEM] * 2,
+        scratch_shapes=[message, message],
         compiler_params=PARAMS,
         cost_estimate=pl.CostEstimate(flops=1_000_000, bytes_accessed=2_000_000, transcendentals=100_000),
-    )(incidence, rising, falling, *parts, fit)
+    )(incidence, *rising, *falling, *parts, fit)
 
 
 def local(soft, partners, incidence, edge_prob):
@@ -410,21 +435,28 @@
     fit, vals, hot, cov, early, own_sums, pick = ready_call(
         partners, soft, incidence, keys.T, edge_prob.T, cut, width, groups
     )
-    cov, edges, sums, up, down = pair_call(partners, left, right, soft, vals, hot, early, own_sums, cov)
+    cov, edges, sums, up, down, turn = pair_call(
+        partners, left, right, soft, vals, hot, early, own_sums, cov
+    )
     parts = (cov, edges, sums, pick)
 
     half = groups // 2
-    rise = [(i, (i + 1) % groups) for i in range(groups)]
+    rise = [(i, i + 1) for i in range(groups - 1)]
     fall = [(b, a) for a, b in rise]
-    rising = lax.ppermute(up, "shot", rise)
-    falling = lax.ppermute(down, "shot", fall)
-    order = down
-    for step in range(1, half):
-        order = hop_call(half - step, step, rising, parts, order)
-        rising = lax.ppermute(order, "shot", rise)
-        if step < half - 1:
-            order = hop_call(half + 1 + step, step, falling, parts, order)
-            falling = lax.ppermute(order, "shot", fall)
+    ends = [(groups - 1, 0), (0, groups - 1)]
+    rising = [lax.ppermute(up, "shot", rise)]
+    falling = [lax.ppermute(down, "shot", fall)]
+    turned = [lax.ppermute(turn, "shot", ends)]
+    for step in range(2, half + 2):
+        crossed = turned[step - 3] if step > 2 else turn
+        up = hop_call(step, True, rising[-1], crossed, parts, down)
+        rising.append(lax.ppermute(up, "shot", rise))
+        if step <= half:
+            down, turn = hop_call(step, False, falling[-1], crossed, parts, up)
+            falling.append(lax.ppermute(down, "shot", fall))
+            turned.append(lax.ppermute(turn, "shot", ends))
+    rising = (rising[half - 1], rising[half], turned[half - 1])
+    falling = (falling[half - 2], falling[half - 1], turned[half - 2])
     return final_call(slots, incidence, rising, falling, parts, fit)
 
 

time: 114 us -> 117 us (1.026)
  the two profiles are of different devices: /device:TPU:24 before, /device:TPU:384 now
where the time goes in v9:
time: 117 us; the launch traced here: 116 us
  starting transfers between devices  74.4 us (64%)
  Pallas kernels  20.2 us (17%)
  waiting for transfers between devices  14.7 us (13%)
  local copies, waits for them, and re-layouts  5.21 us (4%)
    ppermute x7, starting transfers between devices, local(): falling.append(lax.ppermute(down, 'shot', fall))  37.7 us
    ppermute x8, starting transfers between devices, local(): rising.append(lax.ppermute(up, 'shot', rise))  15.4 us
    ppermute x8, waiting for transfers between devices, local(): rising.append(lax.ppermute(up, 'shot', rise))  10.4 us
    pallas_call x1, Pallas kernels, ready_call(): pl.pallas_call(functools.partial(ready_kernel, width), out_shape=[jax.Sha...  9.24 us
    ppermute x1, starting transfers between devices, local(): lax.ppermute(head, ('row', 'col'), [((i + 1) % sides, i) for i in range(s...  5.48 us
    pallas_call x1, Pallas kernels, pair_call(): pl.pallas_call(pair_kernel, out_shape=[jax.ShapeDtypeStruct(cov.shape, jn...  5.2 us
    unnamed x9, local copies, waits for them, and re-layouts  5.07 us
    ppermute x7, starting transfers between devices, local(): turned.append(lax.ppermute(turn, 'shot', ends))  4.7 us
  transfers between devices with their start and end apart: 27, of which 12 were waited for; matrix products, arithmetic and copies ran while one was open for 1% of the time, Pallas kernels for 11%

profile of v9, /device:TPU:384, one launch (start us, length us, event | category | flops | bytes accessed | tf_op | source)
XLA Modules:
  0.0 116.3 jit_solution(2015357019827386512)
XLA Ops:
  3.2 3.4 %collective-permute-start = (bf16[768,512]{1,0:T(8,128)(2,1)}, bf16[768,512]{1,0:T(8,128)(2,1)S(1)}, u32[]{:S(2)}, u32[]{:S(2)}) collective-permute-start(bf16[768,512]{1,0:T(8,128)(2,1)} %get-tuple-element.32), channel_id=1, source_target_pairs={{0,1},{1,2},{2,3},{3,4},{4,5},{5,6},{6,7},{7,8},{8,9},{9,10},{10,1... | collective-permute-start | bytes 2359304 | tf_op jit(solution)/shard_map/ppermute | solution.py:431
  6.6 5.5 %collective-permute-start.1 = (bf16[768,512]{1,0:T(8,128)(2,1)S(1)}, bf16[768,512]{1,0:T(8,128)(2,1)S(1)}, u32[]{:S(2)}, u32[]{:S(2)}) collective-permute-start(bf16[768,512]{1,0:T(8,128)(2,1)S(1)} %get-tuple-element.33), channel_id=1, source_target_pairs={{1,0},{2,1},{3,2},{4,3},{5,4},{6,5},{7,6},{8,7},{9,8},{10,9},{11,1... | collective-permute-start | bytes 2359304 | tf_op jit(solution)/shard_map/ppermute | solution.py:432
  16.6 9.2 %shard_map.60 = (f32[4,512]{1,0:T(4,128)S(1)}, bf16[4,768,512]{2,1,0:T(8,128)(2,1)S(1)}, bf16[4,512,512]{2,1,0:T(8,128)(2,1)S(1)}, f32[16,16,16,256]{3,2,1,0:T(8...) custom-call(s32[4,4]{1,0:T(4,128)S(1)} %copy-done.3, ...), custom_call_target="tpu_custom_call" | custom-call | flops 20000000000 | bytes 12000000 | tf_op jit(solution)/shard_map/pallas_call | solution.py:151
  25.9 2.2 %collective-permute-done.left_ref = bf16[768,512]{1,0:T(8,128)(2,1)S(1)} collective-permute-done((bf16[768,512]{1,0:T(8,128)(2,1)}, bf16[768,512]{1,0:T(8,128)(2,1)S(1)}, u32[]{:S(2)}, u32[]{:S(2)}) %collective-permute-start) | collective-permute-done | bytes 786464 | tf_op jit(solution)/shard_map/ppermute | solution.py:431
  28.1 5.2 %shard_map.61 = (f32[16,16,16,256]{3,2,1,0:T(8,128)S(1)}, s32[24,256]{1,0:T(8,128)S(1)}, s32[8,256]{1,0:T(8,128)S(1)}, s32[168,256]{1,0:T(8,128)S(1)}, s32[168,256]{1,0:T(8,128)S(1)}, /*index=5*/s32[168,256]{1,0:T(8,128)S(1)}) custom-call(s32[4,4]{1,0:T(4,128)S(1)} %copy-done.3, ...), custom_call_target="tpu_custom_call", output_to_operand_aliasing={{0}: (8, {})} | custom-call | flops 2000000000 | bytes 4000000 | tf_op jit(solution)/shard_map/pallas_call | solution.py:259
  33.3 2.9 %collective-permute-start.2 = (s32[168,256]{1,0:T(8,128)S(1)}, s32[168,256]{1,0:T(8,128)S(1)}, u32[]{:S(2)}, u32[]{:S(2)}) collective-permute-start(s32[168,256]{1,0:T(8,128)S(1)} %get-tuple-element.40), channel_id=1, source_target_pairs={{0,32},{32,64},{64,96},{96,128},{128,160},{160,192},{192,224},{224... | collective-permute-start | bytes 516104 | tf_op jit(solution)/shard_map/ppermute | solution.py:447
  36.2 4.1 %collective-permute-start.5 = (s32[168,256]{1,0:T(8,128)S(1)}, s32[168,256]{1,0:T(8,128)S(1)}, u32[]{:S(2)}, u32[]{:S(2)}) collective-permute-start(s32[168,256]{1,0:T(8,128)S(1)} %get-tuple-element.46.refs_0_), channel_id=1, source_target_pairs={{32,0},{64,32},{96,64},{128,96},{160,128},{192,160},{224,192},{256... | collective-permute-start | bytes 516104 | tf_op jit(solution)/shard_map/ppermute | solution.py:448
  42.0 1.9 %collective-permute-start.3 = (s32[168,256]{1,0:T(8,128)S(1)}, s32[168,256]{1,0:T(8,128)S(1)}, u32[]{:S(2)}, u32[]{:S(2)}) collective-permute-start(s32[168,256]{1,0:T(8,128)S(1)} %shard_map.62.refs_0_), channel_id=1, source_target_pairs={{0,32},{32,64},{64,96},{96,128},{128,160},{160,192},{192,224},{224... | collective-permute-start | bytes 516104 | tf_op jit(solution)/shard_map/ppermute | solution.py:453
  44.2 5.1 %collective-permute-start.8 = (s32[168,256]{1,0:T(8,128)S(1)}, s32[168,256]{1,0:T(8,128)S(1)}, u32[]{:S(2)}, u32[]{:S(2)}) collective-permute-start(s32[168,256]{1,0:T(8,128)S(1)} %get-tuple-element.47.refs_0_), channel_id=1, source_target_pairs={{32,0},{64,32},{96,64},{128,96},{160,128},{192,160},{224,192},{256... | collective-permute-start | bytes 516104 | tf_op jit(solution)/shard_map/ppermute | solution.py:456
  50.8 1.9 %collective-permute-start.6 = (s32[168,256]{1,0:T(8,128)S(1)}, s32[168,256]{1,0:T(8,128)S(1)}, u32[]{:S(2)}, u32[]{:S(2)}) collective-permute-start(s32[168,256]{1,0:T(8,128)S(1)} %shard_map.64.refs_0_), channel_id=1, source_target_pairs={{0,32},{32,64},{64,96},{96,128},{128,160},{160,192},{192,224},{224... | collective-permute-start | bytes 516104 | tf_op jit(solution)/shard_map/ppermute | solution.py:453
  52.9 5.1 %collective-permute-start.11 = (s32[168,256]{1,0:T(8,128)S(1)}, s32[168,256]{1,0:T(8,128)S(1)}, u32[]{:S(2)}, u32[]{:S(2)}) collective-permute-start(s32[168,256]{1,0:T(8,128)S(1)} %get-tuple-element.49.refs_0_), channel_id=1, source_target_pairs={{32,0},{64,32},{96,64},{128,96},{160,128},{192,160},{224,192},{256... | collective-permute-start | bytes 516104 | tf_op jit(solution)/shard_map/ppermute | solution.py:456
  59.5 1.9 %collective-permute-start.9 = (s32[168,256]{1,0:T(8,128)S(1)}, s32[168,256]{1,0:T(8,128)S(1)}, u32[]{:S(2)}, u32[]{:S(2)}) collective-permute-start(s32[168,256]{1,0:T(8,128)S(1)} %shard_map.66.refs_0_), channel_id=1, source_target_pairs={{0,32},{32,64},{64,96},{96,128},{128,160},{160,192},{192,224},{224... | collective-permute-start | bytes 516104 | tf_op jit(solution)/shard_map/ppermute | solution.py:453
  61.7 5.2 %collective-permute-start.14 = (s32[168,256]{1,0:T(8,128)S(1)}, s32[168,256]{1,0:T(8,128)S(1)}, u32[]{:S(2)}, u32[]{:S(2)}) collective-permute-start(s32[168,256]{1,0:T(8,128)S(1)} %get-tuple-element.51.refs_0_), channel_id=1, source_target_pairs={{32,0},{64,32},{96,64},{128,96},{160,128},{192,160},{224,192},{256... | collective-permute-start | bytes 516104 | tf_op jit(solution)/shard_map/ppermute | solution.py:456
  68.4 1.9 %collective-permute-start.12 = (s32[168,256]{1,0:T(8,128)S(1)}, s32[168,256]{1,0:T(8,128)S(1)}, u32[]{:S(2)}, u32[]{:S(2)}) collective-permute-start(s32[168,256]{1,0:T(8,128)S(1)} %shard_map.68.refs_0_), channel_id=1, source_target_pairs={{0,32},{32,64},{64,96},{96,128},{128,160},{160,192},{192,224},{224... | collective-permute-start | bytes 516104 | tf_op jit(solution)/shard_map/ppermute | solution.py:453
  70.6 5.5 %collective-permute-start.17 = (s32[168,256]{1,0:T(8,128)S(1)}, s32[168,256]{1,0:T(8,128)S(1)}, u32[]{:S(2)}, u32[]{:S(2)}) collective-permute-start(s32[168,256]{1,0:T(8,128)S(1)} %get-tuple-element.53.refs_0_), channel_id=1, source_target_pairs={{32,0},{64,32},{96,64},{128,96},{160,128},{192,160},{224,192},{256... | collective-permute-start | bytes 516104 | tf_op jit(solution)/shard_map/ppermute | solution.py:456
  76.8 1.5 %collective-permute-done.12.came_ref = s32[168,256]{1,0:T(8,128)S(1)} collective-permute-done((s32[168,256]{1,0:T(8,128)S(1)}, s32[168,256]{1,0:T(8,128)S(1)}, u32[]{:S(2)}, u32[]{:S(2)}) %collective-permute-start.12) | collective-permute-done | bytes 172064 | tf_op jit(solution)/shard_map/ppermute | solution.py:453
  78.5 1.9 %collective-permute-start.15 = (s32[168,256]{1,0:T(8,128)S(1)}, s32[168,256]{1,0:T(8,128)S(1)}, u32[]{:S(2)}, u32[]{:S(2)}) collective-permute-start(s32[168,256]{1,0:T(8,128)S(1)} %shard_map.70.refs_0_), channel_id=1, source_target_pairs={{0,32},{32,64},{64,96},{96,128},{128,160},{160,192},{192,224},{224... | collective-permute-start | bytes 516104 | tf_op jit(solution)/shard_map/ppermute | solution.py:453
  80.9 5.6 %collective-permute-start.20 = (s32[168,256]{1,0:T(8,128)S(1)}, s32[168,256]{1,0:T(8,128)S(1)}, u32[]{:S(2)}, u32[]{:S(2)}) collective-permute-start(s32[168,256]{1,0:T(8,128)S(1)} %get-tuple-element.55.refs_0_), channel_id=1, source_target_pairs={{32,0},{64,32},{96,64},{128,96},{160,128},{192,160},{224,192},{256... | collective-permute-start | bytes 516104 | tf_op jit(solution)/shard_map/ppermute | solution.py:456
  88.4 1.9 %collective-permute-start.18 = (s32[168,256]{1,0:T(8,128)S(1)}, s32[168,256]{1,0:T(8,128)S(1)}, u32[]{:S(2)}, u32[]{:S(2)}) collective-permute-start(s32[168,256]{1,0:T(8,128)S(1)} %shard_map.72.refs_0_), channel_id=1, source_target_pairs={{0,32},{32,64},{64,96},{96,128},{128,160},{160,192},{192,224},{224... | collective-permute-start | bytes 516104 | tf_op jit(solution)/shard_map/ppermute | solution.py:453
  90.6 5.6 %collective-permute-start.23 = (s32[168,256]{1,0:T(8,128)S(1)}, s32[168,256]{1,0:T(8,128)S(1)}, u32[]{:S(2)}, u32[]{:S(2)}) collective-permute-start(s32[168,256]{1,0:T(8,128)S(1)} %get-tuple-element.57.refs_0_), channel_id=1, source_target_pairs={{32,0},{64,32},{96,64},{128,96},{160,128},{192,160},{224,192},{256... | collective-permute-start | bytes 516104 | tf_op jit(solution)/shard_map/ppermute | solution.py:456
  97.5 1.9 %collective-permute-start.21 = (s32[168,256]{1,0:T(8,128)S(1)}, s32[168,256]{1,0:T(8,128)S(1)}, u32[]{:S(2)}, u32[]{:S(2)}) collective-permute-start(s32[168,256]{1,0:T(8,128)S(1)} %shard_map.74.refs_0_), channel_id=1, source_target_pairs={{0,32},{32,64},{64,96},{96,128},{128,160},{160,192},{192,224},{224... | collective-permute-start | bytes 516104 | tf_op jit(solution)/shard_map/ppermute | solution.py:453
  100.9 5.6 %collective-permute-start.26 = (s32[168,256]{1,0:T(8,128)S(1)}, s32[168,256]{1,0:T(8,128)S(1)}, u32[]{:S(2)}, u32[]{:S(2)}) collective-permute-start(s32[168,256]{1,0:T(8,128)S(1)} %get-tuple-element.59.refs_0_), channel_id=1, source_target_pairs={{32,0},{64,32},{96,64},{128,96},{160,128},{192,160},{224,192},{256... | collective-permute-start | bytes 516104 | tf_op jit(solution)/shard_map/ppermute | solution.py:456
  106.7 1.9 %collective-permute-start.24 = (s32[168,256]{1,0:T(8,128)S(1)}, s32[168,256]{1,0:T(8,128)S(1)}, u32[]{:S(2)}, u32[]{:S(2)}) collective-permute-start(s32[168,256]{1,0:T(8,128)S(1)} %shard_map.76), channel_id=1, source_target_pairs={{0,32},{32,64},{64,96},{96,128},{128,160},{160,192},{192,224},{224... | collective-permute-start | bytes 516104 | tf_op jit(solution)/shard_map/ppermute | solution.py:453
  109.4 5.9 %collective-permute-done.24.refs_1_ = s32[168,256]{1,0:T(8,128)S(1)} collective-permute-done((s32[168,256]{1,0:T(8,128)S(1)}, s32[168,256]{1,0:T(8,128)S(1)}, u32[]{:S(2)}, u32[]{:S(2)}) %collective-permute-start.24) | collective-permute-done | bytes 172064 | tf_op jit(solution)/shard_map/ppermute | solution.py:453
  (60 shorter events, 22.3 us)
Async XLA Ops:
  3.2 24.9 %collective-permute-start = (bf16[768,512]{1,0:T(8,128)(2,1)}, bf16[768,512]{1,0:T(8,128)(2,1)S(1)}, u32[]{:S(2)}, u32[]{:S(2)}) collective-permute-start(bf16[768,512]{1,0:T(8,128)(2,1)} %get-tuple-element.32), channel_id=1, source_target_pairs={{0,1},{1,2},{2,3},{3,4},{4,5},{5,6},{6,7},{7,8},{8,9},{9,10},{10,1... | collective-permute-start | bytes 2359304 | tf_op jit(solution)/shard_map/ppermute | solution.py:431
  6.6 21.5 %collective-permute-start.1 = (bf16[768,512]{1,0:T(8,128)(2,1)S(1)}, bf16[768,512]{1,0:T(8,128)(2,1)S(1)}, u32[]{:S(2)}, u32[]{:S(2)}) collective-permute-start(bf16[768,512]{1,0:T(8,128)(2,1)S(1)} %get-tuple-element.33), channel_id=1, source_target_pairs={{1,0},{2,1},{3,2},{4,3},{5,4},{6,5},{7,6},{8,7},{9,8},{10,9},{11,1... | collective-permute-start | bytes 2359304 | tf_op jit(solution)/shard_map/ppermute | solution.py:432
  33.3 8.5 %collective-permute-start.2 = (s32[168,256]{1,0:T(8,128)S(1)}, s32[168,256]{1,0:T(8,128)S(1)}, u32[]{:S(2)}, u32[]{:S(2)}) collective-permute-start(s32[168,256]{1,0:T(8,128)S(1)} %get-tuple-element.40), channel_id=1, source_target_pairs={{0,32},{32,64},{64,96},{96,128},{128,160},{160,192},{192,224},{224... | collective-permute-start | bytes 516104 | tf_op jit(solution)/shard_map/ppermute | solution.py:447
  40.3 9.7 %collective-permute-start.4 = (s32[168,256]{1,0:T(8,128)S(1)}, s32[168,256]{1,0:T(8,128)S(1)}, u32[]{:S(2)}, u32[]{:S(2)}) collective-permute-start(s32[168,256]{1,0:T(8,128)S(1)} %get-tuple-element.41.turned_ref), channel_id=1, source_target_pairs={{480,0},{0,480},{481,1},{1,481},{482,2},{2,482},{483,3},{3,483},{4... | collective-permute-start | bytes 516104 | tf_op jit(solution)/shard_map/ppermute | solution.py:449
  42.0 8.5 %collective-permute-start.3 = (s32[168,256]{1,0:T(8,128)S(1)}, s32[168,256]{1,0:T(8,128)S(1)}, u32[]{:S(2)}, u32[]{:S(2)}) collective-permute-start(s32[168,256]{1,0:T(8,128)S(1)} %shard_map.62.refs_0_), channel_id=1, source_target_pairs={{0,32},{32,64},{64,96},{96,128},{128,160},{160,192},{192,224},{224... | collective-permute-start | bytes 516104 | tf_op jit(solution)/shard_map/ppermute | solution.py:453
  49.3 9.4 %collective-permute-start.7 = (s32[168,256]{1,0:T(8,128)S(1)}, s32[168,256]{1,0:T(8,128)S(1)}, u32[]{:S(2)}, u32[]{:S(2)}) collective-permute-start(s32[168,256]{1,0:T(8,128)S(1)} %get-tuple-element.48), channel_id=1, source_target_pairs={{480,0},{0,480},{481,1},{1,481},{482,2},{2,482},{483,3},{3,483},{4... | collective-permute-start | bytes 516104 | tf_op jit(solution)/shard_map/ppermute | solution.py:457
  50.8 8.5 %collective-permute-start.6 = (s32[168,256]{1,0:T(8,128)S(1)}, s32[168,256]{1,0:T(8,128)S(1)}, u32[]{:S(2)}, u32[]{:S(2)}) collective-permute-start(s32[168,256]{1,0:T(8,128)S(1)} %shard_map.64.refs_0_), channel_id=1, source_target_pairs={{0,32},{32,64},{64,96},{96,128},{128,160},{160,192},{192,224},{224... | collective-permute-start | bytes 516104 | tf_op jit(solution)/shard_map/ppermute | solution.py:453
  52.9 8.5 %collective-permute-start.11 = (s32[168,256]{1,0:T(8,128)S(1)}, s32[168,256]{1,0:T(8,128)S(1)}, u32[]{:S(2)}, u32[]{:S(2)}) collective-permute-start(s32[168,256]{1,0:T(8,128)S(1)} %get-tuple-element.49.refs_0_), channel_id=1, source_target_pairs={{32,0},{64,32},{96,64},{128,96},{160,128},{192,160},{224,192},{256... | collective-permute-start | bytes 516104 | tf_op jit(solution)/shard_map/ppermute | solution.py:456
  58.1 9.4 %collective-permute-start.10 = (s32[168,256]{1,0:T(8,128)S(1)}, s32[168,256]{1,0:T(8,128)S(1)}, u32[]{:S(2)}, u32[]{:S(2)}) collective-permute-start(s32[168,256]{1,0:T(8,128)S(1)} %get-tuple-element.50), channel_id=1, source_target_pairs={{480,0},{0,480},{481,1},{1,481},{482,2},{2,482},{483,3},{3,483},{4... | collective-permute-start | bytes 516104 | tf_op jit(solution)/shard_map/ppermute | solution.py:457
  59.5 8.7 %collective-permute-start.9 = (s32[168,256]{1,0:T(8,128)S(1)}, s32[168,256]{1,0:T(8,128)S(1)}, u32[]{:S(2)}, u32[]{:S(2)}) collective-permute-start(s32[168,256]{1,0:T(8,128)S(1)} %shard_map.66.refs_0_), channel_id=1, source_target_pairs={{0,32},{32,64},{64,96},{96,128},{128,160},{160,192},{192,224},{224... | collective-permute-start | bytes 516104 | tf_op jit(solution)/shard_map/ppermute | solution.py:453
  61.7 8.6 %collective-permute-start.14 = (s32[168,256]{1,0:T(8,128)S(1)}, s32[168,256]{1,0:T(8,128)S(1)}, u32[]{:S(2)}, u32[]{:S(2)}) collective-permute-start(s32[168,256]{1,0:T(8,128)S(1)} %get-tuple-element.51.refs_0_), channel_id=1, source_target_pairs={{32,0},{64,32},{96,64},{128,96},{160,128},{192,160},{224,192},{256... | collective-permute-start | bytes 516104 | tf_op jit(solution)/shard_map/ppermute | solution.py:456
  66.8 9.9 %collective-permute-start.13 = (s32[168,256]{1,0:T(8,128)S(1)}, s32[168,256]{1,0:T(8,128)S(1)}, u32[]{:S(2)}, u32[]{:S(2)}) collective-permute-start(s32[168,256]{1,0:T(8,128)S(1)} %get-tuple-element.52), channel_id=1, source_target_pairs={{480,0},{0,480},{481,1},{1,481},{482,2},{2,482},{483,3},{3,483},{4... | collective-permute-start | bytes 516104 | tf_op jit(solution)/shard_map/ppermute | solution.py:457
  68.4 9.9 %collective-permute-start.12 = (s32[168,256]{1,0:T(8,128)S(1)}, s32[168,256]{1,0:T(8,128)S(1)}, u32[]{:S(2)}, u32[]{:S(2)}) collective-permute-start(s32[168,256]{1,0:T(8,128)S(1)} %shard_map.68.refs_0_), channel_id=1, source_target_pairs={{0,32},{32,64},{64,96},{96,128},{128,160},{160,192},{192,224},{224... | collective-permute-start | bytes 516104 | tf_op jit(solution)/shard_map/ppermute | solution.py:453
  70.6 10.0 %collective-permute-start.17 = (s32[168,256]{1,0:T(8,128)S(1)}, s32[168,256]{1,0:T(8,128)S(1)}, u32[]{:S(2)}, u32[]{:S(2)}) collective-permute-start(s32[168,256]{1,0:T(8,128)S(1)} %get-tuple-element.53.refs_0_), channel_id=1, source_target_pairs={{32,0},{64,32},{96,64},{128,96},{160,128},{192,160},{224,192},{256... | collective-permute-start | bytes 516104 | tf_op jit(solution)/shard_map/ppermute | solution.py:456
  76.1 11.1 %collective-permute-start.16 = (s32[168,256]{1,0:T(8,128)S(1)}, s32[168,256]{1,0:T(8,128)S(1)}, u32[]{:S(2)}, u32[]{:S(2)}) collective-permute-start(s32[168,256]{1,0:T(8,128)S(1)} %get-tuple-element.54), channel_id=1, source_target_pairs={{480,0},{0,480},{481,1},{1,481},{482,2},{2,482},{483,3},{3,483},{4... | collective-permute-start | bytes 516104 | tf_op jit(solution)/shard_map/ppermute | solution.py:457
  78.5 9.7 %collective-permute-start.15 = (s32[168,256]{1,0:T(8,128)S(1)}, s32[168,256]{1,0:T(8,128)S(1)}, u32[]{:S(2)}, u32[]{:S(2)}) collective-permute-start(s32[168,256]{1,0:T(8,128)S(1)} %shard_map.70.refs_0_), channel_id=1, source_target_pairs={{0,32},{32,64},{64,96},{96,128},{128,160},{160,192},{192,224},{224... | collective-permute-start | bytes 516104 | tf_op jit(solution)/shard_map/ppermute | solution.py:453
  80.9 9.5 %collective-permute-start.20 = (s32[168,256]{1,0:T(8,128)S(1)}, s32[168,256]{1,0:T(8,128)S(1)}, u32[]{:S(2)}, u32[]{:S(2)}) collective-permute-start(s32[168,256]{1,0:T(8,128)S(1)} %get-tuple-element.55.refs_0_), channel_id=1, source_target_pairs={{32,0},{64,32},{96,64},{128,96},{160,128},{192,160},{224,192},{256... | collective-permute-start | bytes 516104 | tf_op jit(solution)/shard_map/ppermute | solution.py:456
  86.5 10.4 %collective-permute-start.19 = (s32[168,256]{1,0:T(8,128)S(1)}, s32[168,256]{1,0:T(8,128)S(1)}, u32[]{:S(2)}, u32[]{:S(2)}) collective-permute-start(s32[168,256]{1,0:T(8,128)S(1)} %get-tuple-element.56), channel_id=1, source_target_pairs={{480,0},{0,480},{481,1},{1,481},{482,2},{2,482},{483,3},{3,483},{4... | collective-permute-start | bytes 516104 | tf_op jit(solution)/shard_map/ppermute | solution.py:457
  88.4 8.9 %collective-permute-start.18 = (s32[168,256]{1,0:T(8,128)S(1)}, s32[168,256]{1,0:T(8,128)S(1)}, u32[]{:S(2)}, u32[]{:S(2)}) collective-permute-start(s32[168,256]{1,0:T(8,128)S(1)} %shard_map.72.refs_0_), channel_id=1, source_target_pairs={{0,32},{32,64},{64,96},{96,128},{128,160},{160,192},{192,224},{224... | collective-permute-start | bytes 516104 | tf_op jit(solution)/shard_map/ppermute | solution.py:453
  90.6 9.3 %collective-permute-start.23 = (s32[168,256]{1,0:T(8,128)S(1)}, s32[168,256]{1,0:T(8,128)S(1)}, u32[]{:S(2)}, u32[]{:S(2)}) collective-permute-start(s32[168,256]{1,0:T(8,128)S(1)} %get-tuple-element.57.refs_0_), channel_id=1, source_target_pairs={{32,0},{64,32},{96,64},{128,96},{160,128},{192,160},{224,192},{256... | collective-permute-start | bytes 516104 | tf_op jit(solution)/shard_map/ppermute | solution.py:456
  96.2 10.3 %collective-permute-start.22 = (s32[168,256]{1,0:T(8,128)S(1)}, s32[168,256]{1,0:T(8,128)S(1)}, u32[]{:S(2)}, u32[]{:S(2)}) collective-permute-start(s32[168,256]{1,0:T(8,128)S(1)} %get-tuple-element.58), channel_id=1, source_target_pairs={{480,0},{0,480},{481,1},{1,481},{482,2},{2,482},{483,3},{3,483},{4... | collective-permute-start | bytes 516104 | tf_op jit(solution)/shard_map/ppermute | solution.py:457
  97.5 9.0 %collective-permute-start.21 = (s32[168,256]{1,0:T(8,128)S(1)}, s32[168,256]{1,0:T(8,128)S(1)}, u32[]{:S(2)}, u32[]{:S(2)}) collective-permute-start(s32[168,256]{1,0:T(8,128)S(1)} %shard_map.74.refs_0_), channel_id=1, source_target_pairs={{0,32},{32,64},{64,96},{96,128},{128,160},{160,192},{192,224},{224... | collective-permute-start | bytes 516104 | tf_op jit(solution)/shard_map/ppermute | solution.py:453
  100.9 8.5 %collective-permute-start.26 = (s32[168,256]{1,0:T(8,128)S(1)}, s32[168,256]{1,0:T(8,128)S(1)}, u32[]{:S(2)}, u32[]{:S(2)}) collective-permute-start(s32[168,256]{1,0:T(8,128)S(1)} %get-tuple-element.59.refs_0_), channel_id=1, source_target_pairs={{32,0},{64,32},{96,64},{128,96},{160,128},{192,160},{224,192},{256... | collective-permute-start | bytes 516104 | tf_op jit(solution)/shard_map/ppermute | solution.py:456
  106.7 8.5 %collective-permute-start.24 = (s32[168,256]{1,0:T(8,128)S(1)}, s32[168,256]{1,0:T(8,128)S(1)}, u32[]{:S(2)}, u32[]{:S(2)}) collective-permute-start(s32[168,256]{1,0:T(8,128)S(1)} %shard_map.76), channel_id=1, source_target_pairs={{0,32},{32,64},{64,96},{96,128},{128,160},{160,192},{192,224},{224... | collective-permute-start | bytes 516104 | tf_op jit(solution)/shard_map/ppermute | solution.py:453
  (7 other events, 28.9 us)

commit v10 on v8

--- a/solution.py
+++ b/solution.py
@@ -73,10 +73,14 @@
     )(soft)
 
 
+def way():
+    return 1 - 2 * lax.rem(lax.axis_index("row"), 2)
+
+
 def spread(cov_ref, slot, tile, me):
     groups, _, share, _ = cov_ref.shape
     for d in range(groups):
-        at = lax.rem(d - me + groups, groups)
+        at = lax.rem((d - me) * way() + groups, groups)
         cov_ref[at, slot] = tile[d * share : (d + 1) * share, :]
 
 
@@ -293,7 +297,7 @@
     )
     others = picked(pick_ref, shift)
     factors = factors_of(came_ref, words)
-    dest = lax.rem(lax.axis_index("shot") + at, groups)
+    dest = lax.rem(lax.axis_index("shot") + way() * at + groups, groups)
     for block in range(blocks):
         column = column_of(shift[block + HALO : block + HALO + 1, :], dest * share, share)
         column = column * (float(SHOTS) * seen / (seen + 1))
@@ -414,17 +418,21 @@
     parts = (cov, edges, sums, pick)
 
     half = groups // 2
-    rise = [(i, (i + 1) % groups) for i in range(groups)]
+    rows = lax.axis_size("row")
+    rise = [
+        (z * rows + row, (z + 1 - 2 * (row % 2)) % groups * rows + row) for z in range(groups) for row in range(rows)
+    ]
     fall = [(b, a) for a, b in rise]
-    rising = lax.ppermute(up, "shot", rise)
-    falling = lax.ppermute(down, "shot", fall)
+    axes = ("shot", "row")
+    rising = lax.ppermute(up, axes, rise)
+    falling = lax.ppermute(down, axes, fall)
     order = down
     for step in range(1, half):
         order = hop_call(half - step, step, rising, parts, order)
-        rising = lax.ppermute(order, "shot", rise)
+        rising = lax.ppermute(order, axes, rise)
         if step < half - 1:
             order = hop_call(half + 1 + step, step, falling, parts, order)
-            falling = lax.ppermute(order, "shot", fall)
+            falling = lax.ppermute(order, axes, fall)
     return final_call(slots, incidence, rising, falling, parts, fit)
 
 

time: 114 us -> 115 us (level)
  no operation moved by 1% of the time
where the time goes in v10:
time: 115 us; the launch traced here: 114 us
  starting transfers between devices  65.6 us (57%)
  Pallas kernels  21.4 us (19%)
  waiting for transfers between devices  20.9 us (18%)
  local copies, waits for them, and re-layouts  4.5 us (4%)
    ppermute x6, starting transfers between devices, local(): falling = lax.ppermute(order, axes, fall)  31.2 us
    ppermute x7, waiting for transfers between devices, local(): rising = lax.ppermute(order, axes, rise)  17.1 us
    ppermute x7, starting transfers between devices, local(): rising = lax.ppermute(order, axes, rise)  13.4 us
    ppermute x1, starting transfers between devices, local(): falling = lax.ppermute(down, axes, fall)  9.49 us
    pallas_call x1, Pallas kernels, ready_call(): pl.pallas_call(functools.partial(ready_kernel, width), out_shape=[jax.Sha...  9.24 us
    pallas_call x1, Pallas kernels, pair_call(): pl.pallas_call(pair_kernel, out_shape=[jax.ShapeDtypeStruct(cov.shape, jn...  5.42 us
    unnamed x9, local copies, waits for them, and re-layouts  4.35 us
    ppermute x1, starting transfers between devices, local(): lax.ppermute(head, ('row', 'col'), [((i + 1) % sides, i) for i in range(s...  4.27 us
  transfers between devices with their start and end apart: 17, of which 10 were waited for; matrix products, arithmetic and copies ran while one was open for 2% of the time, Pallas kernels for 11%

profile of v10, /device:TPU:24, one launch (start us, length us, event | category | flops | bytes accessed | tf_op | source)
XLA Modules:
  0.0 114.0 jit_solution(16792512786704107537)
XLA Ops:
  0.6 2.6 %shard_map.59 = (bf16[768,512]{1,0:T(8,128)(2,1)}, bf16[768,512]{1,0:T(8,128)(2,1)}, f32[8,128]{1,0:T(8,128)}) custom-call(bf16[768,1024]{1,0:T(8,128)(2,1)} %own_ref.3), custom_call_target="tpu_custom_call" | custom-call | bytes 3000000 | tf_op jit(solution)/shard_map/pallas_call | solution.py:65
  3.2 3.4 %collective-permute-start = (bf16[768,512]{1,0:T(8,128)(2,1)}, bf16[768,512]{1,0:T(8,128)(2,1)S(1)}, u32[]{:S(2)}, u32[]{:S(2)}) collective-permute-start(bf16[768,512]{1,0:T(8,128)(2,1)} %get-tuple-element.17), channel_id=1, source_target_pairs={{0,1},{1,2},{2,3},{3,4},{4,5},{5,6},{6,7},{7,8},{8,9},{9,10},{10,1... | collective-permute-start | bytes 2359304 | tf_op jit(solution)/shard_map/ppermute | solution.py:410
  6.6 4.3 %collective-permute-start.1 = (bf16[768,512]{1,0:T(8,128)(2,1)}, bf16[768,512]{1,0:T(8,128)(2,1)S(1)}, u32[]{:S(2)}, u32[]{:S(2)}) collective-permute-start(bf16[768,512]{1,0:T(8,128)(2,1)} %get-tuple-element.18), channel_id=1, source_target_pairs={{1,0},{2,1},{3,2},{4,3},{5,4},{6,5},{7,6},{8,7},{9,8},{10,9},{11,1... | collective-permute-start | bytes 2359304 | tf_op jit(solution)/shard_map/ppermute | solution.py:411
  16.1 9.2 %shard_map.60 = (f32[4,512]{1,0:T(4,128)S(1)}, bf16[4,768,512]{2,1,0:T(8,128)(2,1)S(1)}, bf16[4,512,512]{2,1,0:T(8,128)(2,1)S(1)}, f32[16,16,16,256]{3,2,1,0:T(8...) custom-call(s32[4,4]{1,0:T(4,128)S(1)} %copy-done.2, ...), custom_call_target="tpu_custom_call" | custom-call | flops 20000000000 | bytes 12000000 | tf_op jit(solution)/shard_map/pallas_call | solution.py:156
  27.7 5.4 %shard_map.61 = (f32[16,16,16,256]{3,2,1,0:T(8,128)S(1)}, s32[24,256]{1,0:T(8,128)S(1)}, s32[8,256]{1,0:T(8,128)S(1)}, s32[168,256]{1,0:T(8,128)S(1)}, s32[168,256]{1,0:T(8,128)S(1)}) custom-call(s32[4,4]{1,0:T(4,128)S(1)} %copy-done.2, bf16[768,512]{1,0:T(8,128)(2,1)S(1)} %collective-permute-done.left_ref, ...), custom_call_target="tpu_custom_call", output_to_operand_aliasing={{0}: (8, {})} | custom-call | flops 2000000000 | bytes 4000000 | tf_op jit(solution)/shard_map/pallas_call | solution.py:263
  33.1 3.8 %collective-permute-start.2 = (s32[168,256]{1,0:T(8,128)S(1)}, s32[168,256]{1,0:T(8,128)S(1)}, u32[]{:S(2)}, u32[]{:S(2)}) collective-permute-start(s32[168,256]{1,0:T(8,128)S(1)} %get-tuple-element.25), channel_id=1, source_target_pairs={{0,32},{4,484},{8,40},{12,492},{16,48},{20,500},{24,56},{28,508},{... | collective-permute-start | bytes 516104 | tf_op jit(solution)/shard_map/ppermute | solution.py:427
  37.0 9.5 %collective-permute-start.4 = (s32[168,256]{1,0:T(8,128)S(1)}, s32[168,256]{1,0:T(8,128)S(1)}, u32[]{:S(2)}, u32[]{:S(2)}) collective-permute-start(s32[168,256]{1,0:T(8,128)S(1)} %get-tuple-element.30._), channel_id=1, source_target_pairs={{32,0},{484,4},{40,8},{492,12},{48,16},{500,20},{56,24},{508,28},{... | collective-permute-start | bytes 516104 | tf_op jit(solution)/shard_map/ppermute | solution.py:428
  48.2 1.9 %collective-permute-start.3 = (s32[168,256]{1,0:T(8,128)S(1)}, s32[168,256]{1,0:T(8,128)S(1)}, u32[]{:S(2)}, u32[]{:S(2)}) collective-permute-start(s32[168,256]{1,0:T(8,128)S(1)} %shard_map.62._), channel_id=1, source_target_pairs={{0,32},{4,484},{8,40},{12,492},{16,48},{20,500},{24,56},{28,508},{... | collective-permute-start | bytes 516104 | tf_op jit(solution)/shard_map/ppermute | solution.py:432
  50.3 5.5 %collective-permute-start.6 = (s32[168,256]{1,0:T(8,128)S(1)}, s32[168,256]{1,0:T(8,128)S(1)}, u32[]{:S(2)}, u32[]{:S(2)}) collective-permute-start(s32[168,256]{1,0:T(8,128)S(1)} %shard_map.63._), channel_id=1, source_target_pairs={{32,0},{484,4},{40,8},{492,12},{48,16},{500,20},{56,24},{508,28},{... | collective-permute-start | bytes 516104 | tf_op jit(solution)/shard_map/ppermute | solution.py:435
  55.8 1.8 %collective-permute-done.3.came_ref = s32[168,256]{1,0:T(8,128)S(1)} collective-permute-done((s32[168,256]{1,0:T(8,128)S(1)}, s32[168,256]{1,0:T(8,128)S(1)}, u32[]{:S(2)}, u32[]{:S(2)}) %collective-permute-start.3) | collective-permute-done | bytes 172064 | tf_op jit(solution)/shard_map/ppermute | solution.py:432
  57.9 1.9 %collective-permute-start.5 = (s32[168,256]{1,0:T(8,128)S(1)}, s32[168,256]{1,0:T(8,128)S(1)}, u32[]{:S(2)}, u32[]{:S(2)}) collective-permute-start(s32[168,256]{1,0:T(8,128)S(1)} %shard_map.64._), channel_id=1, source_target_pairs={{0,32},{4,484},{8,40},{12,492},{16,48},{20,500},{24,56},{28,508},{... | collective-permute-start | bytes 516104 | tf_op jit(solution)/shard_map/ppermute | solution.py:432
  60.1 5.1 %collective-permute-start.8 = (s32[168,256]{1,0:T(8,128)S(1)}, s32[168,256]{1,0:T(8,128)S(1)}, u32[]{:S(2)}, u32[]{:S(2)}) collective-permute-start(s32[168,256]{1,0:T(8,128)S(1)} %shard_map.65._), channel_id=1, source_target_pairs={{32,0},{484,4},{40,8},{492,12},{48,16},{500,20},{56,24},{508,28},{... | collective-permute-start | bytes 516104 | tf_op jit(solution)/shard_map/ppermute | solution.py:435
  65.2 2.9 %collective-permute-done.5.came_ref = s32[168,256]{1,0:T(8,128)S(1)} collective-permute-done((s32[168,256]{1,0:T(8,128)S(1)}, s32[168,256]{1,0:T(8,128)S(1)}, u32[]{:S(2)}, u32[]{:S(2)}) %collective-permute-start.5) | collective-permute-done | bytes 172064 | tf_op jit(solution)/shard_map/ppermute | solution.py:432
  68.4 1.9 %collective-permute-start.7 = (s32[168,256]{1,0:T(8,128)S(1)}, s32[168,256]{1,0:T(8,128)S(1)}, u32[]{:S(2)}, u32[]{:S(2)}) collective-permute-start(s32[168,256]{1,0:T(8,128)S(1)} %shard_map.66._), channel_id=1, source_target_pairs={{0,32},{4,484},{8,40},{12,492},{16,48},{20,500},{24,56},{28,508},{... | collective-permute-start | bytes 516104 | tf_op jit(solution)/shard_map/ppermute | solution.py:432
  70.6 5.1 %collective-permute-start.10 = (s32[168,256]{1,0:T(8,128)S(1)}, s32[168,256]{1,0:T(8,128)S(1)}, u32[]{:S(2)}, u32[]{:S(2)}) collective-permute-start(s32[168,256]{1,0:T(8,128)S(1)} %shard_map.67._), channel_id=1, source_target_pairs={{32,0},{484,4},{40,8},{492,12},{48,16},{500,20},{56,24},{508,28},{... | collective-permute-start | bytes 516104 | tf_op jit(solution)/shard_map/ppermute | solution.py:435
  75.7 2.2 %collective-permute-done.7.came_ref = s32[168,256]{1,0:T(8,128)S(1)} collective-permute-done((s32[168,256]{1,0:T(8,128)S(1)}, s32[168,256]{1,0:T(8,128)S(1)}, u32[]{:S(2)}, u32[]{:S(2)}) %collective-permute-start.7) | collective-permute-done | bytes 172064 | tf_op jit(solution)/shard_map/ppermute | solution.py:432
  78.1 1.9 %collective-permute-start.9 = (s32[168,256]{1,0:T(8,128)S(1)}, s32[168,256]{1,0:T(8,128)S(1)}, u32[]{:S(2)}, u32[]{:S(2)}) collective-permute-start(s32[168,256]{1,0:T(8,128)S(1)} %shard_map.68._), channel_id=1, source_target_pairs={{0,32},{4,484},{8,40},{12,492},{16,48},{20,500},{24,56},{28,508},{... | collective-permute-start | bytes 516104 | tf_op jit(solution)/shard_map/ppermute | solution.py:432
  80.3 5.1 %collective-permute-start.12 = (s32[168,256]{1,0:T(8,128)S(1)}, s32[168,256]{1,0:T(8,128)S(1)}, u32[]{:S(2)}, u32[]{:S(2)}) collective-permute-start(s32[168,256]{1,0:T(8,128)S(1)} %shard_map.69._), channel_id=1, source_target_pairs={{32,0},{484,4},{40,8},{492,12},{48,16},{500,20},{56,24},{508,28},{... | collective-permute-start | bytes 516104 | tf_op jit(solution)/shard_map/ppermute | solution.py:435
  87.0 1.9 %collective-permute-start.11 = (s32[168,256]{1,0:T(8,128)S(1)}, s32[168,256]{1,0:T(8,128)S(1)}, u32[]{:S(2)}, u32[]{:S(2)}) collective-permute-start(s32[168,256]{1,0:T(8,128)S(1)} %shard_map.70._), channel_id=1, source_target_pairs={{0,32},{4,484},{8,40},{12,492},{16,48},{20,500},{24,56},{28,508},{... | collective-permute-start | bytes 516104 | tf_op jit(solution)/shard_map/ppermute | solution.py:432
  89.2 5.1 %collective-permute-start.14 = (s32[168,256]{1,0:T(8,128)S(1)}, s32[168,256]{1,0:T(8,128)S(1)}, u32[]{:S(2)}, u32[]{:S(2)}) collective-permute-start(s32[168,256]{1,0:T(8,128)S(1)} %shard_map.71._), channel_id=1, source_target_pairs={{32,0},{484,4},{40,8},{492,12},{48,16},{500,20},{56,24},{508,28},{... | collective-permute-start | bytes 516104 | tf_op jit(solution)/shard_map/ppermute | solution.py:435
  95.8 1.9 %collective-permute-start.13 = (s32[168,256]{1,0:T(8,128)S(1)}, s32[168,256]{1,0:T(8,128)S(1)}, u32[]{:S(2)}, u32[]{:S(2)}) collective-permute-start(s32[168,256]{1,0:T(8,128)S(1)} %shard_map.72._), channel_id=1, source_target_pairs={{0,32},{4,484},{8,40},{12,492},{16,48},{20,500},{24,56},{28,508},{... | collective-permute-start | bytes 516104 | tf_op jit(solution)/shard_map/ppermute | solution.py:432
  98.0 5.1 %collective-permute-start.16 = (s32[168,256]{1,0:T(8,128)S(1)}, s32[168,256]{1,0:T(8,128)S(1)}, u32[]{:S(2)}, u32[]{:S(2)}) collective-permute-start(s32[168,256]{1,0:T(8,128)S(1)} %shard_map.73._), channel_id=1, source_target_pairs={{32,0},{484,4},{40,8},{492,12},{48,16},{500,20},{56,24},{508,28},{... | collective-permute-start | bytes 516104 | tf_op jit(solution)/shard_map/ppermute | solution.py:435
  104.5 1.9 %collective-permute-start.15 = (s32[168,256]{1,0:T(8,128)S(1)}, s32[168,256]{1,0:T(8,128)S(1)}, u32[]{:S(2)}, u32[]{:S(2)}) collective-permute-start(s32[168,256]{1,0:T(8,128)S(1)} %shard_map.74), channel_id=1, source_target_pairs={{0,32},{4,484},{8,40},{12,492},{16,48},{20,500},{24,56},{28,508},{... | collective-permute-start | bytes 516104 | tf_op jit(solution)/shard_map/ppermute | solution.py:432
  106.5 6.6 %collective-permute-done.15.rising_ref = s32[168,256]{1,0:T(8,128)S(1)} collective-permute-done((s32[168,256]{1,0:T(8,128)S(1)}, s32[168,256]{1,0:T(8,128)S(1)}, u32[]{:S(2)}, u32[]{:S(2)}) %collective-permute-start.15) | collective-permute-done | bytes 172064 | tf_op jit(solution)/shard_map/ppermute | solution.py:432
  (38 shorter events, 16.9 us)
Async XLA Ops:
  3.2 23.4 %collective-permute-start = (bf16[768,512]{1,0:T(8,128)(2,1)}, bf16[768,512]{1,0:T(8,128)(2,1)S(1)}, u32[]{:S(2)}, u32[]{:S(2)}) collective-permute-start(bf16[768,512]{1,0:T(8,128)(2,1)} %get-tuple-element.17), channel_id=1, source_target_pairs={{0,1},{1,2},{2,3},{3,4},{4,5},{5,6},{6,7},{7,8},{8,9},{9,10},{10,1... | collective-permute-start | bytes 2359304 | tf_op jit(solution)/shard_map/ppermute | solution.py:410
  6.6 21.1 %collective-permute-start.1 = (bf16[768,512]{1,0:T(8,128)(2,1)}, bf16[768,512]{1,0:T(8,128)(2,1)S(1)}, u32[]{:S(2)}, u32[]{:S(2)}) collective-permute-start(bf16[768,512]{1,0:T(8,128)(2,1)} %get-tuple-element.18), channel_id=1, source_target_pairs={{1,0},{2,1},{3,2},{4,3},{5,4},{6,5},{7,6},{8,7},{9,8},{10,9},{11,1... | collective-permute-start | bytes 2359304 | tf_op jit(solution)/shard_map/ppermute | solution.py:411
  12.6 1.4 %copy-start = (bf16[768,1024]{1,0:T(8,128)(2,1)S(1)}, bf16[768,1024]{1,0:T(8,128)(2,1)}, u32[]{:S(2)}) copy-start(bf16[768,1024]{1,0:T(8,128)(2,1)} %own_ref.3) | copy-start | bytes 4718596
  14.0 0.7 copy-start.1
  14.8 0.7 copy-start.2
  15.5 0.7 copy-start.3
  33.1 14.8 %collective-permute-start.2 = (s32[168,256]{1,0:T(8,128)S(1)}, s32[168,256]{1,0:T(8,128)S(1)}, u32[]{:S(2)}, u32[]{:S(2)}) collective-permute-start(s32[168,256]{1,0:T(8,128)S(1)} %get-tuple-element.25), channel_id=1, source_target_pairs={{0,32},{4,484},{8,40},{12,492},{16,48},{20,500},{24,56},{28,508},{... | collective-permute-start | bytes 516104 | tf_op jit(solution)/shard_map/ppermute | solution.py:427
  37.0 13.1 %collective-permute-start.4 = (s32[168,256]{1,0:T(8,128)S(1)}, s32[168,256]{1,0:T(8,128)S(1)}, u32[]{:S(2)}, u32[]{:S(2)}) collective-permute-start(s32[168,256]{1,0:T(8,128)S(1)} %get-tuple-element.30._), channel_id=1, source_target_pairs={{32,0},{484,4},{40,8},{492,12},{48,16},{500,20},{56,24},{508,28},{... | collective-permute-start | bytes 516104 | tf_op jit(solution)/shard_map/ppermute | solution.py:428
  48.2 9.5 %collective-permute-start.3 = (s32[168,256]{1,0:T(8,128)S(1)}, s32[168,256]{1,0:T(8,128)S(1)}, u32[]{:S(2)}, u32[]{:S(2)}) collective-permute-start(s32[168,256]{1,0:T(8,128)S(1)} %shard_map.62._), channel_id=1, source_target_pairs={{0,32},{4,484},{8,40},{12,492},{16,48},{20,500},{24,56},{28,508},{... | collective-permute-start | bytes 516104 | tf_op jit(solution)/shard_map/ppermute | solution.py:432
  50.3 9.5 %collective-permute-start.6 = (s32[168,256]{1,0:T(8,128)S(1)}, s32[168,256]{1,0:T(8,128)S(1)}, u32[]{:S(2)}, u32[]{:S(2)}) collective-permute-start(s32[168,256]{1,0:T(8,128)S(1)} %shard_map.63._), channel_id=1, source_target_pairs={{32,0},{484,4},{40,8},{492,12},{48,16},{500,20},{56,24},{508,28},{... | collective-permute-start | bytes 516104 | tf_op jit(solution)/shard_map/ppermute | solution.py:435
  57.9 10.2 %collective-permute-start.5 = (s32[168,256]{1,0:T(8,128)S(1)}, s32[168,256]{1,0:T(8,128)S(1)}, u32[]{:S(2)}, u32[]{:S(2)}) collective-permute-start(s32[168,256]{1,0:T(8,128)S(1)} %shard_map.64._), channel_id=1, source_target_pairs={{0,32},{4,484},{8,40},{12,492},{16,48},{20,500},{24,56},{28,508},{... | collective-permute-start | bytes 516104 | tf_op jit(solution)/shard_map/ppermute | solution.py:432
  60.1 10.2 %collective-permute-start.8 = (s32[168,256]{1,0:T(8,128)S(1)}, s32[168,256]{1,0:T(8,128)S(1)}, u32[]{:S(2)}, u32[]{:S(2)}) collective-permute-start(s32[168,256]{1,0:T(8,128)S(1)} %shard_map.65._), channel_id=1, source_target_pairs={{32,0},{484,4},{40,8},{492,12},{48,16},{500,20},{56,24},{508,28},{... | collective-permute-start | bytes 516104 | tf_op jit(solution)/shard_map/ppermute | solution.py:435
  68.4 9.5 %collective-permute-start.7 = (s32[168,256]{1,0:T(8,128)S(1)}, s32[168,256]{1,0:T(8,128)S(1)}, u32[]{:S(2)}, u32[]{:S(2)}) collective-permute-start(s32[168,256]{1,0:T(8,128)S(1)} %shard_map.66._), channel_id=1, source_target_pairs={{0,32},{4,484},{8,40},{12,492},{16,48},{20,500},{24,56},{28,508},{... | collective-permute-start | bytes 516104 | tf_op jit(solution)/shard_map/ppermute | solution.py:432
  70.6 9.5 %collective-permute-start.10 = (s32[168,256]{1,0:T(8,128)S(1)}, s32[168,256]{1,0:T(8,128)S(1)}, u32[]{:S(2)}, u32[]{:S(2)}) collective-permute-start(s32[168,256]{1,0:T(8,128)S(1)} %shard_map.67._), channel_id=1, source_target_pairs={{32,0},{484,4},{40,8},{492,12},{48,16},{500,20},{56,24},{508,28},{... | collective-permute-start | bytes 516104 | tf_op jit(solution)/shard_map/ppermute | solution.py:435
  78.1 8.7 %collective-permute-start.9 = (s32[168,256]{1,0:T(8,128)S(1)}, s32[168,256]{1,0:T(8,128)S(1)}, u32[]{:S(2)}, u32[]{:S(2)}) collective-permute-start(s32[168,256]{1,0:T(8,128)S(1)} %shard_map.68._), channel_id=1, source_target_pairs={{0,32},{4,484},{8,40},{12,492},{16,48},{20,500},{24,56},{28,508},{... | collective-permute-start | bytes 516104 | tf_op jit(solution)/shard_map/ppermute | solution.py:432
  80.3 8.7 %collective-permute-start.12 = (s32[168,256]{1,0:T(8,128)S(1)}, s32[168,256]{1,0:T(8,128)S(1)}, u32[]{:S(2)}, u32[]{:S(2)}) collective-permute-start(s32[168,256]{1,0:T(8,128)S(1)} %shard_map.69._), channel_id=1, source_target_pairs={{32,0},{484,4},{40,8},{492,12},{48,16},{500,20},{56,24},{508,28},{... | collective-permute-start | bytes 516104 | tf_op jit(solution)/shard_map/ppermute | solution.py:435
  87.0 8.5 %collective-permute-start.11 = (s32[168,256]{1,0:T(8,128)S(1)}, s32[168,256]{1,0:T(8,128)S(1)}, u32[]{:S(2)}, u32[]{:S(2)}) collective-permute-start(s32[168,256]{1,0:T(8,128)S(1)} %shard_map.70._), channel_id=1, source_target_pairs={{0,32},{4,484},{8,40},{12,492},{16,48},{20,500},{24,56},{28,508},{... | collective-permute-start | bytes 516104 | tf_op jit(solution)/shard_map/ppermute | solution.py:432
  89.2 8.5 %collective-permute-start.14 = (s32[168,256]{1,0:T(8,128)S(1)}, s32[168,256]{1,0:T(8,128)S(1)}, u32[]{:S(2)}, u32[]{:S(2)}) collective-permute-start(s32[168,256]{1,0:T(8,128)S(1)} %shard_map.71._), channel_id=1, source_target_pairs={{32,0},{484,4},{40,8},{492,12},{48,16},{500,20},{56,24},{508,28},{... | collective-permute-start | bytes 516104 | tf_op jit(solution)/shard_map/ppermute | solution.py:435
  95.8 8.5 %collective-permute-start.13 = (s32[168,256]{1,0:T(8,128)S(1)}, s32[168,256]{1,0:T(8,128)S(1)}, u32[]{:S(2)}, u32[]{:S(2)}) collective-permute-start(s32[168,256]{1,0:T(8,128)S(1)} %shard_map.72._), channel_id=1, source_target_pairs={{0,32},{4,484},{8,40},{12,492},{16,48},{20,500},{24,56},{28,508},{... | collective-permute-start | bytes 516104 | tf_op jit(solution)/shard_map/ppermute | solution.py:432
  98.0 8.5 %collective-permute-start.16 = (s32[168,256]{1,0:T(8,128)S(1)}, s32[168,256]{1,0:T(8,128)S(1)}, u32[]{:S(2)}, u32[]{:S(2)}) collective-permute-start(s32[168,256]{1,0:T(8,128)S(1)} %shard_map.73._), channel_id=1, source_target_pairs={{32,0},{484,4},{40,8},{492,12},{48,16},{500,20},{56,24},{508,28},{... | collective-permute-start | bytes 516104 | tf_op jit(solution)/shard_map/ppermute | solution.py:435
  104.5 8.5 %collective-permute-start.15 = (s32[168,256]{1,0:T(8,128)S(1)}, s32[168,256]{1,0:T(8,128)S(1)}, u32[]{:S(2)}, u32[]{:S(2)}) collective-permute-start(s32[168,256]{1,0:T(8,128)S(1)} %shard_map.74), channel_id=1, source_target_pairs={{0,32},{4,484},{8,40},{12,492},{16,48},{20,500},{24,56},{28,508},{... | collective-permute-start | bytes 516104 | tf_op jit(solution)/shard_map/ppermute | solution.py:432

commit v11 on v8

--- a/solution.py
+++ b/solution.py
@@ -66,9 +66,9 @@
         cut_kernel,
         out_shape=[shape, shape, jax.ShapeDtypeStruct((8, 128), jnp.float32)],
         in_specs=[HBM],
-        out_specs=[VMEM, VMEM, VMEM],
+        out_specs=[ANY, ANY, VMEM],
         scratch_shapes=[pltpu.SemaphoreType.DMA((2,))],
-        compiler_params=pltpu.CompilerParams(vmem_limit_bytes=58 * 1024 * 1024),
+        compiler_params=pltpu.CompilerParams(vmem_limit_bytes=51 * 1024 * 1024),
         cost_estimate=pl.CostEstimate(flops=0, bytes_accessed=3_000_000, transcendentals=0),
     )(soft)
 
@@ -86,8 +86,8 @@
 
 
 def ready_kernel(
-    width, partners_ref, own_ref, inc_ref, keyt_ref, probt_ref, _,
-    fit_ref, vals_ref, hot_ref, cov_ref, early_ref, sums_ref, pick_ref,
+    width, partners_ref, soft_ref, inc_ref, keyt_ref, probt_ref, _,
+    fit_ref, vals_ref, hot_ref, cov_ref, early_ref, sums_ref, pick_ref, own_ref, sem,
 ):
     blocks, slots = partners_ref.shape
     mine = blocks // 2
@@ -96,6 +96,13 @@
     pieces = edges // width
     me = lax.axis_index("shot")
     base = group_index() * blocks
+    fetch = pltpu.make_async_copy(soft_ref, own_ref, sem)
+    fetch.start()
+    for b in range(blocks):
+        key = inc_ref[1, b : b + 1, :] * (width * width) + inc_ref[0, b : b + 1, :] * width + inc_ref[2, b : b + 1, :]
+        same = keyt_ref[:, b : b + 1] == key
+        fit_ref[b : b + 1, :] = jnp.sum(jnp.where(same, probt_ref[:, b : b + 1], 0.0), axis=0, keepdims=True)
+    fetch.wait()
     lines = lax.broadcasted_iota(jnp.int32, (width, edges), 0)
     products, firsts, others = [], [], []
     for b in range(blocks):
@@ -138,9 +145,6 @@
         products += rows_of(jnp.sum(vals * other, axis=0, keepdims=True), pieces)
         firsts += rows_of(jnp.sum(vals, axis=0, keepdims=True), pieces)
         others += rows_of(jnp.sum(other, axis=0, keepdims=True), pieces)
-        key = slot_x * (width * width) + rows_x * width + cols_x
-        same = keyt_ref[:, b : b + 1] == key
-        fit_ref[b : b + 1, :] = jnp.sum(jnp.where(same, probt_ref[:, b : b + 1], 0.0), axis=0, keepdims=True)
     early_ref[...] = jnp.concatenate(products + firsts + others, axis=0)
     sums_ref[...] = jnp.concatenate(rows_of(row_sums(own_ref[...]), blocks), axis=0)
 
@@ -160,8 +164,9 @@
             jax.ShapeDtypeStruct((blocks, width), jnp.float32),
             jax.ShapeDtypeStruct((REACH + 1, blocks * slots, width), jnp.float32),
         ],
-        in_specs=[SMEM] + [VMEM] * 4 + [ANY],
+        in_specs=[SMEM, ANY] + [VMEM] * 3 + [ANY],
         out_specs=[VMEM] * 7,
+        scratch_shapes=[pltpu.VMEM(soft.shape, soft.dtype), pltpu.SemaphoreType.DMA],
         compiler_params=PARAMS,
         cost_estimate=pl.CostEstimate(flops=20_000_000_000, bytes_accessed=12_000_000, transcendentals=0),
     )(partners, soft, incidence, keys_t, prob_t, after)
@@ -235,7 +240,7 @@
                 def _():
                     spread(cov_ref, block * slots + k, tiles[:, n * width : (n + 1) * width], me)
 
-        other = jnp.dot(halo, hot_ref[block], preferred_element_type=jnp.float32)
+        other = jnp.dot(halo[:, first:last], hot_ref[block, first:last, :], preferred_element_type=jnp.float32)
         product = jnp.sum(vals_ref[block].astype(jnp.float32) * other, axis=0, keepdims=True)
         products += rows_of(product, pieces)
         others += rows_of(jnp.sum(other, axis=0, keepdims=True), pieces)

time: 114 us -> 136 us (1.19)
  Pallas kernels: 21.1 us -> 43.9 us
    pallas_call x1, Pallas kernels: 2.56 us -> 24.9 us  [cut_call(): pl.pallas_call(cut_kernel, out_shape=[shape, shape, jax.ShapeDtypeStruct(...]
    unnamed x9 -> x7, local copies, waits for them, and re-layouts: 4.35 us -> 3.66 us
  transfers between devices with their start and end apart: 17 -> 17, of which waited for: 10 -> 10; matrix products, arithmetic and copies ran while one was open for 2% -> 1% of each run, Pallas kernels for 11% -> 10%
where the time goes in v11:
time: 136 us; the launch traced here: 135 us
  starting transfers between devices  65.6 us (48%)
  Pallas kernels  43.9 us (32%)
  waiting for transfers between devices  20.2 us (15%)
  local copies, waits for them, and re-layouts  3.81 us (3%)
    ppermute x6, starting transfers between devices, local(): falling = lax.ppermute(order, 'shot', fall)  31.1 us
    pallas_call x1, Pallas kernels, cut_call(): pl.pallas_call(cut_kernel, out_shape=[shape, shape, jax.ShapeDtypeStruct(...  24.9 us
    ppermute x7, waiting for transfers between devices, local(): rising = lax.ppermute(order, 'shot', rise)  16.7 us
    ppermute x7, starting transfers between devices, local(): rising = lax.ppermute(order, 'shot', rise)  13.4 us
    pallas_call x1, Pallas kernels, ready_call(): pl.pallas_call(functools.partial(ready_kernel, width), out_shape=[jax.Sha...  9.97 us
    ppermute x1, starting transfers between devices, local(): falling = lax.ppermute(down, 'shot', fall)  9.5 us
    pallas_call x1, Pallas kernels, pair_call(): pl.pallas_call(pair_kernel, out_shape=[jax.ShapeDtypeStruct(cov.shape, jn...  4.82 us
    ppermute x1, starting transfers between devices, local(): lax.ppermute(head, ('row', 'col'), [((i + 1) % sides, i) for i in range(s...  4.27 us
  transfers between devices with their start and end apart: 17, of which 10 were waited for; matrix products, arithmetic and copies ran while one was open for 1% of the time, Pallas kernels for 10%

profile of v11, /device:TPU:24, one launch (start us, length us, event | category | flops | bytes accessed | tf_op | source)
XLA Modules:
  0.0 135.1 jit_solution(3333706446584268958)
XLA Ops:
  0.6 24.9 %shard_map.59 = (bf16[768,512]{1,0:T(8,128)(2,1)S(1)}, bf16[768,512]{1,0:T(8,128)(2,1)}, f32[8,128]{1,0:T(8,128)S(1)}) custom-call(bf16[768,1024]{1,0:T(8,128)(2,1)} %own_ref.1), custom_call_target="tpu_custom_call" | custom-call | bytes 3000000 | tf_op jit(solution)/shard_map/pallas_call | solution.py:65
  25.6 3.4 %collective-permute-start = (bf16[768,512]{1,0:T(8,128)(2,1)}, bf16[768,512]{1,0:T(8,128)(2,1)S(1)}, u32[]{:S(2)}, u32[]{:S(2)}) collective-permute-start(bf16[768,512]{1,0:T(8,128)(2,1)} %get-tuple-element.17), channel_id=1, source_target_pairs={{0,1},{1,2},{2,3},{3,4},{4,5},{5,6},{6,7},{7,8},{8,9},{9,10},{10,1... | collective-permute-start | bytes 2359304 | tf_op jit(solution)/shard_map/ppermute | solution.py:411
  29.0 4.3 %collective-permute-start.1 = (bf16[768,512]{1,0:T(8,128)(2,1)S(1)}, bf16[768,512]{1,0:T(8,128)(2,1)S(1)}, u32[]{:S(2)}, u32[]{:S(2)}) collective-permute-start(bf16[768,512]{1,0:T(8,128)(2,1)S(1)} %get-tuple-element.18), channel_id=1, source_target_pairs={{1,0},{2,1},{3,2},{4,3},{5,4},{6,5},{7,6},{8,7},{9,8},{10,9},{11,1... | collective-permute-start | bytes 2359304 | tf_op jit(solution)/shard_map/ppermute | solution.py:412
  37.8 10.0 %shard_map.60 = (f32[4,512]{1,0:T(4,128)S(1)}, bf16[4,768,512]{2,1,0:T(8,128)(2,1)S(1)}, bf16[4,512,512]{2,1,0:T(8,128)(2,1)S(1)}, f32[16,16,16,256]{3,2,1,0:T(8...) custom-call(s32[4,4]{1,0:T(4,128)S(1)} %copy-done.2, ...), custom_call_target="tpu_custom_call" | custom-call | flops 20000000000 | bytes 12000000 | tf_op jit(solution)/shard_map/pallas_call | solution.py:156
  49.9 4.8 %shard_map.61 = (f32[16,16,16,256]{3,2,1,0:T(8,128)S(1)}, s32[24,256]{1,0:T(8,128)S(1)}, s32[8,256]{1,0:T(8,128)S(1)}, s32[168,256]{1,0:T(8,128)S(1)}, s32[168,256]{1,0:T(8,128)S(1)}) custom-call(s32[4,4]{1,0:T(4,128)S(1)} %copy-done.2, bf16[768,512]{1,0:T(8,128)(2,1)S(1)} %collective-permute-done.left_ref, ...), custom_call_target="tpu_custom_call", output_to_operand_aliasing={{0}: (8, {})} | custom-call | flops 2000000000 | bytes 4000000 | tf_op jit(solution)/shard_map/pallas_call | solution.py:264
  54.7 3.8 %collective-permute-start.2 = (s32[168,256]{1,0:T(8,128)S(1)}, s32[168,256]{1,0:T(8,128)S(1)}, u32[]{:S(2)}, u32[]{:S(2)}) collective-permute-start(s32[168,256]{1,0:T(8,128)S(1)} %get-tuple-element.25), channel_id=1, source_target_pairs={{0,32},{32,64},{64,96},{96,128},{128,160},{160,192},{192,224},{224... | collective-permute-start | bytes 516104 | tf_op jit(solution)/shard_map/ppermute | solution.py:424
  58.5 9.5 %collective-permute-start.4 = (s32[168,256]{1,0:T(8,128)S(1)}, s32[168,256]{1,0:T(8,128)S(1)}, u32[]{:S(2)}, u32[]{:S(2)}) collective-permute-start(s32[168,256]{1,0:T(8,128)S(1)} %get-tuple-element.30._), channel_id=1, source_target_pairs={{32,0},{64,32},{96,64},{128,96},{160,128},{192,160},{224,192},{256... | collective-permute-start | bytes 516104 | tf_op jit(solution)/shard_map/ppermute | solution.py:425
  69.7 1.9 %collective-permute-start.3 = (s32[168,256]{1,0:T(8,128)S(1)}, s32[168,256]{1,0:T(8,128)S(1)}, u32[]{:S(2)}, u32[]{:S(2)}) collective-permute-start(s32[168,256]{1,0:T(8,128)S(1)} %shard_map.62._), channel_id=1, source_target_pairs={{0,32},{32,64},{64,96},{96,128},{128,160},{160,192},{192,224},{224... | collective-permute-start | bytes 516104 | tf_op jit(solution)/shard_map/ppermute | solution.py:429
  71.9 5.1 %collective-permute-start.6 = (s32[168,256]{1,0:T(8,128)S(1)}, s32[168,256]{1,0:T(8,128)S(1)}, u32[]{:S(2)}, u32[]{:S(2)}) collective-permute-start(s32[168,256]{1,0:T(8,128)S(1)} %shard_map.63._), channel_id=1, source_target_pairs={{32,0},{64,32},{96,64},{128,96},{160,128},{192,160},{224,192},{256... | collective-permute-start | bytes 516104 | tf_op jit(solution)/shard_map/ppermute | solution.py:432
  78.5 1.9 %collective-permute-start.5 = (s32[168,256]{1,0:T(8,128)S(1)}, s32[168,256]{1,0:T(8,128)S(1)}, u32[]{:S(2)}, u32[]{:S(2)}) collective-permute-start(s32[168,256]{1,0:T(8,128)S(1)} %shard_map.64._), channel_id=1, source_target_pairs={{0,32},{32,64},{64,96},{96,128},{128,160},{160,192},{192,224},{224... | collective-permute-start | bytes 516104 | tf_op jit(solution)/shard_map/ppermute | solution.py:429
  80.7 5.1 %collective-permute-start.8 = (s32[168,256]{1,0:T(8,128)S(1)}, s32[168,256]{1,0:T(8,128)S(1)}, u32[]{:S(2)}, u32[]{:S(2)}) collective-permute-start(s32[168,256]{1,0:T(8,128)S(1)} %shard_map.65._), channel_id=1, source_target_pairs={{32,0},{64,32},{96,64},{128,96},{160,128},{192,160},{224,192},{256... | collective-permute-start | bytes 516104 | tf_op jit(solution)/shard_map/ppermute | solution.py:432
  87.2 1.9 %collective-permute-start.7 = (s32[168,256]{1,0:T(8,128)S(1)}, s32[168,256]{1,0:T(8,128)S(1)}, u32[]{:S(2)}, u32[]{:S(2)}) collective-permute-start(s32[168,256]{1,0:T(8,128)S(1)} %shard_map.66._), channel_id=1, source_target_pairs={{0,32},{32,64},{64,96},{96,128},{128,160},{160,192},{192,224},{224... | collective-permute-start | bytes 516104 | tf_op jit(solution)/shard_map/ppermute | solution.py:429
  89.4 5.1 %collective-permute-start.10 = (s32[168,256]{1,0:T(8,128)S(1)}, s32[168,256]{1,0:T(8,128)S(1)}, u32[]{:S(2)}, u32[]{:S(2)}) collective-permute-start(s32[168,256]{1,0:T(8,128)S(1)} %shard_map.67._), channel_id=1, source_target_pairs={{32,0},{64,32},{96,64},{128,96},{160,128},{192,160},{224,192},{256... | collective-permute-start | bytes 516104 | tf_op jit(solution)/shard_map/ppermute | solution.py:432
  96.0 1.9 %collective-permute-start.9 = (s32[168,256]{1,0:T(8,128)S(1)}, s32[168,256]{1,0:T(8,128)S(1)}, u32[]{:S(2)}, u32[]{:S(2)}) collective-permute-start(s32[168,256]{1,0:T(8,128)S(1)} %shard_map.68._), channel_id=1, source_target_pairs={{0,32},{32,64},{64,96},{96,128},{128,160},{160,192},{192,224},{224... | collective-permute-start | bytes 516104 | tf_op jit(solution)/shard_map/ppermute | solution.py:429
  98.2 5.1 %collective-permute-start.12 = (s32[168,256]{1,0:T(8,128)S(1)}, s32[168,256]{1,0:T(8,128)S(1)}, u32[]{:S(2)}, u32[]{:S(2)}) collective-permute-start(s32[168,256]{1,0:T(8,128)S(1)} %shard_map.69._), channel_id=1, source_target_pairs={{32,0},{64,32},{96,64},{128,96},{160,128},{192,160},{224,192},{256... | collective-permute-start | bytes 516104 | tf_op jit(solution)/shard_map/ppermute | solution.py:432
  103.3 2.0 %collective-permute-done.9.came_ref = s32[168,256]{1,0:T(8,128)S(1)} collective-permute-done((s32[168,256]{1,0:T(8,128)S(1)}, s32[168,256]{1,0:T(8,128)S(1)}, u32[]{:S(2)}, u32[]{:S(2)}) %collective-permute-start.9) | collective-permute-done | bytes 172064 | tf_op jit(solution)/shard_map/ppermute | solution.py:429
  105.6 1.9 %collective-permute-start.11 = (s32[168,256]{1,0:T(8,128)S(1)}, s32[168,256]{1,0:T(8,128)S(1)}, u32[]{:S(2)}, u32[]{:S(2)}) collective-permute-start(s32[168,256]{1,0:T(8,128)S(1)} %shard_map.70._), channel_id=1, source_target_pairs={{0,32},{32,64},{64,96},{96,128},{128,160},{160,192},{192,224},{224... | collective-permute-start | bytes 516104 | tf_op jit(solution)/shard_map/ppermute | solution.py:429
  107.8 5.5 %collective-permute-start.14 = (s32[168,256]{1,0:T(8,128)S(1)}, s32[168,256]{1,0:T(8,128)S(1)}, u32[]{:S(2)}, u32[]{:S(2)}) collective-permute-start(s32[168,256]{1,0:T(8,128)S(1)} %shard_map.71._), channel_id=1, source_target_pairs={{32,0},{64,32},{96,64},{128,96},{160,128},{192,160},{224,192},{256... | collective-permute-start | bytes 516104 | tf_op jit(solution)/shard_map/ppermute | solution.py:432
  113.3 2.5 %collective-permute-done.11.came_ref = s32[168,256]{1,0:T(8,128)S(1)} collective-permute-done((s32[168,256]{1,0:T(8,128)S(1)}, s32[168,256]{1,0:T(8,128)S(1)}, u32[]{:S(2)}, u32[]{:S(2)}) %collective-permute-start.11) | collective-permute-done | bytes 172064 | tf_op jit(solution)/shard_map/ppermute | solution.py:429
  116.0 1.9 %collective-permute-start.13 = (s32[168,256]{1,0:T(8,128)S(1)}, s32[168,256]{1,0:T(8,128)S(1)}, u32[]{:S(2)}, u32[]{:S(2)}) collective-permute-start(s32[168,256]{1,0:T(8,128)S(1)} %shard_map.72._), channel_id=1, source_target_pairs={{0,32},{32,64},{64,96},{96,128},{128,160},{160,192},{192,224},{224... | collective-permute-start | bytes 516104 | tf_op jit(solution)/shard_map/ppermute | solution.py:429
  118.2 5.1 %collective-permute-start.16 = (s32[168,256]{1,0:T(8,128)S(1)}, s32[168,256]{1,0:T(8,128)S(1)}, u32[]{:S(2)}, u32[]{:S(2)}) collective-permute-start(s32[168,256]{1,0:T(8,128)S(1)} %shard_map.73._), channel_id=1, source_target_pairs={{32,0},{64,32},{96,64},{128,96},{160,128},{192,160},{224,192},{256... | collective-permute-start | bytes 516104 | tf_op jit(solution)/shard_map/ppermute | solution.py:432
  123.4 2.0 %collective-permute-done.13.came_ref = s32[168,256]{1,0:T(8,128)S(1)} collective-permute-done((s32[168,256]{1,0:T(8,128)S(1)}, s32[168,256]{1,0:T(8,128)S(1)}, u32[]{:S(2)}, u32[]{:S(2)}) %collective-permute-start.13) | collective-permute-done | bytes 172064 | tf_op jit(solution)/shard_map/ppermute | solution.py:429
  125.6 1.9 %collective-permute-start.15 = (s32[168,256]{1,0:T(8,128)S(1)}, s32[168,256]{1,0:T(8,128)S(1)}, u32[]{:S(2)}, u32[]{:S(2)}) collective-permute-start(s32[168,256]{1,0:T(8,128)S(1)} %shard_map.74), channel_id=1, source_target_pairs={{0,32},{32,64},{64,96},{96,128},{128,160},{160,192},{192,224},{224... | collective-permute-start | bytes 516104 | tf_op jit(solution)/shard_map/ppermute | solution.py:429
  127.6 6.6 %collective-permute-done.15.rising_ref = s32[168,256]{1,0:T(8,128)S(1)} collective-permute-done((s32[168,256]{1,0:T(8,128)S(1)}, s32[168,256]{1,0:T(8,128)S(1)}, u32[]{:S(2)}, u32[]{:S(2)}) %collective-permute-start.15) | collective-permute-done | bytes 172064 | tf_op jit(solution)/shard_map/ppermute | solution.py:429
  (36 shorter events, 15.7 us)
Async XLA Ops:
  25.6 23.4 %collective-permute-start = (bf16[768,512]{1,0:T(8,128)(2,1)}, bf16[768,512]{1,0:T(8,128)(2,1)S(1)}, u32[]{:S(2)}, u32[]{:S(2)}) collective-permute-start(bf16[768,512]{1,0:T(8,128)(2,1)} %get-tuple-element.17), channel_id=1, source_target_pairs={{0,1},{1,2},{2,3},{3,4},{4,5},{5,6},{6,7},{7,8},{8,9},{9,10},{10,1... | collective-permute-start | bytes 2359304 | tf_op jit(solution)/shard_map/ppermute | solution.py:411
  29.0 20.9 %collective-permute-start.1 = (bf16[768,512]{1,0:T(8,128)(2,1)S(1)}, bf16[768,512]{1,0:T(8,128)(2,1)S(1)}, u32[]{:S(2)}, u32[]{:S(2)}) collective-permute-start(bf16[768,512]{1,0:T(8,128)(2,1)S(1)} %get-tuple-element.18), channel_id=1, source_target_pairs={{1,0},{2,1},{3,2},{4,3},{5,4},{6,5},{7,6},{8,7},{9,8},{10,9},{11,1... | collective-permute-start | bytes 2359304 | tf_op jit(solution)/shard_map/ppermute | solution.py:412
  35.0 1.4 %copy-start = (bf16[768,1024]{1,0:T(8,128)(2,1)S(1)}, bf16[768,1024]{1,0:T(8,128)(2,1)}, u32[]{:S(2)}) copy-start(bf16[768,1024]{1,0:T(8,128)(2,1)} %own_ref.1) | copy-start | bytes 4718596
  36.4 0.7 copy-start.1
  37.2 0.7 copy-start.2
  54.7 14.8 %collective-permute-start.2 = (s32[168,256]{1,0:T(8,128)S(1)}, s32[168,256]{1,0:T(8,128)S(1)}, u32[]{:S(2)}, u32[]{:S(2)}) collective-permute-start(s32[168,256]{1,0:T(8,128)S(1)} %get-tuple-element.25), channel_id=1, source_target_pairs={{0,32},{32,64},{64,96},{96,128},{128,160},{160,192},{192,224},{224... | collective-permute-start | bytes 516104 | tf_op jit(solution)/shard_map/ppermute | solution.py:424
  58.5 13.1 %collective-permute-start.4 = (s32[168,256]{1,0:T(8,128)S(1)}, s32[168,256]{1,0:T(8,128)S(1)}, u32[]{:S(2)}, u32[]{:S(2)}) collective-permute-start(s32[168,256]{1,0:T(8,128)S(1)} %get-tuple-element.30._), channel_id=1, source_target_pairs={{32,0},{64,32},{96,64},{128,96},{160,128},{192,160},{224,192},{256... | collective-permute-start | bytes 516104 | tf_op jit(solution)/shard_map/ppermute | solution.py:425
  69.7 8.5 %collective-permute-start.3 = (s32[168,256]{1,0:T(8,128)S(1)}, s32[168,256]{1,0:T(8,128)S(1)}, u32[]{:S(2)}, u32[]{:S(2)}) collective-permute-start(s32[168,256]{1,0:T(8,128)S(1)} %shard_map.62._), channel_id=1, source_target_pairs={{0,32},{32,64},{64,96},{96,128},{128,160},{160,192},{192,224},{224... | collective-permute-start | bytes 516104 | tf_op jit(solution)/shard_map/ppermute | solution.py:429
  71.9 8.5 %collective-permute-start.6 = (s32[168,256]{1,0:T(8,128)S(1)}, s32[168,256]{1,0:T(8,128)S(1)}, u32[]{:S(2)}, u32[]{:S(2)}) collective-permute-start(s32[168,256]{1,0:T(8,128)S(1)} %shard_map.63._), channel_id=1, source_target_pairs={{32,0},{64,32},{96,64},{128,96},{160,128},{192,160},{224,192},{256... | collective-permute-start | bytes 516104 | tf_op jit(solution)/shard_map/ppermute | solution.py:432
  78.5 8.5 %collective-permute-start.5 = (s32[168,256]{1,0:T(8,128)S(1)}, s32[168,256]{1,0:T(8,128)S(1)}, u32[]{:S(2)}, u32[]{:S(2)}) collective-permute-start(s32[168,256]{1,0:T(8,128)S(1)} %shard_map.64._), channel_id=1, source_target_pairs={{0,32},{32,64},{64,96},{96,128},{128,160},{160,192},{192,224},{224... | collective-permute-start | bytes 516104 | tf_op jit(solution)/shard_map/ppermute | solution.py:429
  80.7 8.5 %collective-permute-start.8 = (s32[168,256]{1,0:T(8,128)S(1)}, s32[168,256]{1,0:T(8,128)S(1)}, u32[]{:S(2)}, u32[]{:S(2)}) collective-permute-start(s32[168,256]{1,0:T(8,128)S(1)} %shard_map.65._), channel_id=1, source_target_pairs={{32,0},{64,32},{96,64},{128,96},{160,128},{192,160},{224,192},{256... | collective-permute-start | bytes 516104 | tf_op jit(solution)/shard_map/ppermute | solution.py:432
  87.2 8.5 %collective-permute-start.7 = (s32[168,256]{1,0:T(8,128)S(1)}, s32[168,256]{1,0:T(8,128)S(1)}, u32[]{:S(2)}, u32[]{:S(2)}) collective-permute-start(s32[168,256]{1,0:T(8,128)S(1)} %shard_map.66._), channel_id=1, source_target_pairs={{0,32},{32,64},{64,96},{96,128},{128,160},{160,192},{192,224},{224... | collective-permute-start | bytes 516104 | tf_op jit(solution)/shard_map/ppermute | solution.py:429
  89.4 8.5 %collective-permute-start.10 = (s32[168,256]{1,0:T(8,128)S(1)}, s32[168,256]{1,0:T(8,128)S(1)}, u32[]{:S(2)}, u32[]{:S(2)}) collective-permute-start(s32[168,256]{1,0:T(8,128)S(1)} %shard_map.67._), channel_id=1, source_target_pairs={{32,0},{64,32},{96,64},{128,96},{160,128},{192,160},{224,192},{256... | collective-permute-start | bytes 516104 | tf_op jit(solution)/shard_map/ppermute | solution.py:432
  96.0 9.4 %collective-permute-start.9 = (s32[168,256]{1,0:T(8,128)S(1)}, s32[168,256]{1,0:T(8,128)S(1)}, u32[]{:S(2)}, u32[]{:S(2)}) collective-permute-start(s32[168,256]{1,0:T(8,128)S(1)} %shard_map.68._), channel_id=1, source_target_pairs={{0,32},{32,64},{64,96},{96,128},{128,160},{160,192},{192,224},{224... | collective-permute-start | bytes 516104 | tf_op jit(solution)/shard_map/ppermute | solution.py:429
  98.2 9.4 %collective-permute-start.12 = (s32[168,256]{1,0:T(8,128)S(1)}, s32[168,256]{1,0:T(8,128)S(1)}, u32[]{:S(2)}, u32[]{:S(2)}) collective-permute-start(s32[168,256]{1,0:T(8,128)S(1)} %shard_map.69._), channel_id=1, source_target_pairs={{32,0},{64,32},{96,64},{128,96},{160,128},{192,160},{224,192},{256... | collective-permute-start | bytes 516104 | tf_op jit(solution)/shard_map/ppermute | solution.py:432
  105.6 10.2 %collective-permute-start.11 = (s32[168,256]{1,0:T(8,128)S(1)}, s32[168,256]{1,0:T(8,128)S(1)}, u32[]{:S(2)}, u32[]{:S(2)}) collective-permute-start(s32[168,256]{1,0:T(8,128)S(1)} %shard_map.70._), channel_id=1, source_target_pairs={{0,32},{32,64},{64,96},{96,128},{128,160},{160,192},{192,224},{224... | collective-permute-start | bytes 516104 | tf_op jit(solution)/shard_map/ppermute | solution.py:429
  107.8 10.2 %collective-permute-start.14 = (s32[168,256]{1,0:T(8,128)S(1)}, s32[168,256]{1,0:T(8,128)S(1)}, u32[]{:S(2)}, u32[]{:S(2)}) collective-permute-start(s32[168,256]{1,0:T(8,128)S(1)} %shard_map.71._), channel_id=1, source_target_pairs={{32,0},{64,32},{96,64},{128,96},{160,128},{192,160},{224,192},{256... | collective-permute-start | bytes 516104 | tf_op jit(solution)/shard_map/ppermute | solution.py:432
  116.0 9.3 %collective-permute-start.13 = (s32[168,256]{1,0:T(8,128)S(1)}, s32[168,256]{1,0:T(8,128)S(1)}, u32[]{:S(2)}, u32[]{:S(2)}) collective-permute-start(s32[168,256]{1,0:T(8,128)S(1)} %shard_map.72._), channel_id=1, source_target_pairs={{0,32},{32,64},{64,96},{96,128},{128,160},{160,192},{192,224},{224... | collective-permute-start | bytes 516104 | tf_op jit(solution)/shard_map/ppermute | solution.py:429
  118.2 9.3 %collective-permute-start.16 = (s32[168,256]{1,0:T(8,128)S(1)}, s32[168,256]{1,0:T(8,128)S(1)}, u32[]{:S(2)}, u32[]{:S(2)}) collective-permute-start(s32[168,256]{1,0:T(8,128)S(1)} %shard_map.73._), channel_id=1, source_target_pairs={{32,0},{64,32},{96,64},{128,96},{160,128},{192,160},{224,192},{256... | collective-permute-start | bytes 516104 | tf_op jit(solution)/shard_map/ppermute | solution.py:432
  125.6 8.5 %collective-permute-start.15 = (s32[168,256]{1,0:T(8,128)S(1)}, s32[168,256]{1,0:T(8,128)S(1)}, u32[]{:S(2)}, u32[]{:S(2)}) collective-permute-start(s32[168,256]{1,0:T(8,128)S(1)} %shard_map.74), channel_id=1, source_target_pairs={{0,32},{32,64},{64,96},{96,128},{128,160},{160,192},{192,224},{224... | collective-permute-start | bytes 516104 | tf_op jit(solution)/shard_map/ppermute | solution.py:429

commit v12 on v11

--- a/solution.py
+++ b/solution.py
@@ -66,9 +66,9 @@
         cut_kernel,
         out_shape=[shape, shape, jax.ShapeDtypeStruct((8, 128), jnp.float32)],
         in_specs=[HBM],
-        out_specs=[ANY, ANY, VMEM],
+        out_specs=[VMEM, VMEM, VMEM],
         scratch_shapes=[pltpu.SemaphoreType.DMA((2,))],
-        compiler_params=pltpu.CompilerParams(vmem_limit_bytes=51 * 1024 * 1024),
+        compiler_params=pltpu.CompilerParams(vmem_limit_bytes=50 * 1024 * 1024),
         cost_estimate=pl.CostEstimate(flops=0, bytes_accessed=3_000_000, transcendentals=0),
     )(soft)
 

time: 136 us -> 114 us (0.84)
  Pallas kernels: 43.9 us -> 20 us
  local copies, waits for them, and re-layouts: 3.81 us -> 5.21 us
    pallas_call x1, Pallas kernels: 24.9 us -> 1.11 us  [cut_call(): pl.pallas_call(cut_kernel, out_shape=[shape, shape, jax.ShapeDtypeStruct(...]
    unnamed x7 -> x9, local copies, waits for them, and re-layouts: 3.66 us -> 5.07 us
  transfers between devices with their start and end apart: 17 -> 17, of which waited for: 10 -> 10; matrix products, arithmetic and copies ran while one was open for 1% -> 2% of each run, Pallas kernels for 10% -> 12%
where the time goes in v12:
time: 114 us; the launch traced here: 113 us
  starting transfers between devices  65.5 us (57%)
  waiting for transfers between devices  20.2 us (18%)
  Pallas kernels  20 us (18%)
  local copies, waits for them, and re-layouts  5.21 us (5%)
    ppermute x6, starting transfers between devices, local(): falling = lax.ppermute(order, 'shot', fall)  31.1 us
    ppermute x7, waiting for transfers between devices, local(): rising = lax.ppermute(order, 'shot', rise)  16.7 us
    ppermute x7, starting transfers between devices, local(): rising = lax.ppermute(order, 'shot', rise)  13.4 us
    pallas_call x1, Pallas kernels, ready_call(): pl.pallas_call(functools.partial(ready_kernel, width), out_shape=[jax.Sha...  9.98 us
    ppermute x1, starting transfers between devices, local(): falling = lax.ppermute(down, 'shot', fall)  9.5 us
    unnamed x9, local copies, waits for them, and re-layouts  5.07 us
    pallas_call x1, Pallas kernels, pair_call(): pl.pallas_call(pair_kernel, out_shape=[jax.ShapeDtypeStruct(cov.shape, jn...  4.83 us
    ppermute x1, starting transfers between devices, local(): lax.ppermute(head, ('row', 'col'), [((i + 1) % sides, i) for i in range(s...  4.27 us
  transfers between devices with their start and end apart: 17, of which 10 were waited for; matrix products, arithmetic and copies ran while one was open for 2% of the time, Pallas kernels for 12%

profile of v12, /device:TPU:24, one launch (start us, length us, event | category | flops | bytes accessed | tf_op | source)
XLA Modules:
  0.0 112.7 jit_solution(8613432482190220736)
XLA Ops:
  3.2 3.4 %collective-permute-start = (bf16[768,512]{1,0:T(8,128)(2,1)}, bf16[768,512]{1,0:T(8,128)(2,1)S(1)}, u32[]{:S(2)}, u32[]{:S(2)}) collective-permute-start(bf16[768,512]{1,0:T(8,128)(2,1)} %get-tuple-element.17), channel_id=1, source_target_pairs={{0,1},{1,2},{2,3},{3,4},{4,5},{5,6},{6,7},{7,8},{8,9},{9,10},{10,1... | collective-permute-start | bytes 2359304 | tf_op jit(solution)/shard_map/ppermute | solution.py:411
  6.6 4.3 %collective-permute-start.1 = (bf16[768,512]{1,0:T(8,128)(2,1)S(1)}, bf16[768,512]{1,0:T(8,128)(2,1)S(1)}, u32[]{:S(2)}, u32[]{:S(2)}) collective-permute-start(bf16[768,512]{1,0:T(8,128)(2,1)S(1)} %get-tuple-element.18), channel_id=1, source_target_pairs={{1,0},{2,1},{3,2},{4,3},{5,4},{6,5},{7,6},{8,7},{9,8},{10,9},{11,1... | collective-permute-start | bytes 2359304 | tf_op jit(solution)/shard_map/ppermute | solution.py:412
  15.4 10.0 %shard_map.60 = (f32[4,512]{1,0:T(4,128)S(1)}, bf16[4,768,512]{2,1,0:T(8,128)(2,1)S(1)}, bf16[4,512,512]{2,1,0:T(8,128)(2,1)S(1)}, f32[16,16,16,256]{3,2,1,0:T(8...) custom-call(s32[4,4]{1,0:T(4,128)S(1)} %copy-done.3, ...), custom_call_target="tpu_custom_call" | custom-call | flops 20000000000 | bytes 12000000 | tf_op jit(solution)/shard_map/pallas_call | solution.py:156
  27.5 4.8 %shard_map.61 = (f32[16,16,16,256]{3,2,1,0:T(8,128)S(1)}, s32[24,256]{1,0:T(8,128)S(1)}, s32[8,256]{1,0:T(8,128)S(1)}, s32[168,256]{1,0:T(8,128)S(1)}, s32[168,256]{1,0:T(8,128)S(1)}) custom-call(s32[4,4]{1,0:T(4,128)S(1)} %copy-done.3, bf16[768,512]{1,0:T(8,128)(2,1)S(1)} %collective-permute-done.left_ref, ...), custom_call_target="tpu_custom_call", output_to_operand_aliasing={{0}: (8, {})} | custom-call | flops 2000000000 | bytes 4000000 | tf_op jit(solution)/shard_map/pallas_call | solution.py:264
  32.3 3.8 %collective-permute-start.2 = (s32[168,256]{1,0:T(8,128)S(1)}, s32[168,256]{1,0:T(8,128)S(1)}, u32[]{:S(2)}, u32[]{:S(2)}) collective-permute-start(s32[168,256]{1,0:T(8,128)S(1)} %get-tuple-element.25), channel_id=1, source_target_pairs={{0,32},{32,64},{64,96},{96,128},{128,160},{160,192},{192,224},{224... | collective-permute-start | bytes 516104 | tf_op jit(solution)/shard_map/ppermute | solution.py:424
  36.1 9.5 %collective-permute-start.4 = (s32[168,256]{1,0:T(8,128)S(1)}, s32[168,256]{1,0:T(8,128)S(1)}, u32[]{:S(2)}, u32[]{:S(2)}) collective-permute-start(s32[168,256]{1,0:T(8,128)S(1)} %get-tuple-element.30._), channel_id=1, source_target_pairs={{32,0},{64,32},{96,64},{128,96},{160,128},{192,160},{224,192},{256... | collective-permute-start | bytes 516104 | tf_op jit(solution)/shard_map/ppermute | solution.py:425
  45.6 1.4 %collective-permute-done.2.came_ref = s32[168,256]{1,0:T(8,128)S(1)} collective-permute-done((s32[168,256]{1,0:T(8,128)S(1)}, s32[168,256]{1,0:T(8,128)S(1)}, u32[]{:S(2)}, u32[]{:S(2)}) %collective-permute-start.2) | collective-permute-done | bytes 172064 | tf_op jit(solution)/shard_map/ppermute | solution.py:424
  47.3 1.9 %collective-permute-start.3 = (s32[168,256]{1,0:T(8,128)S(1)}, s32[168,256]{1,0:T(8,128)S(1)}, u32[]{:S(2)}, u32[]{:S(2)}) collective-permute-start(s32[168,256]{1,0:T(8,128)S(1)} %shard_map.62._), channel_id=1, source_target_pairs={{0,32},{32,64},{64,96},{96,128},{128,160},{160,192},{192,224},{224... | collective-permute-start | bytes 516104 | tf_op jit(solution)/shard_map/ppermute | solution.py:429
  49.5 5.1 %collective-permute-start.6 = (s32[168,256]{1,0:T(8,128)S(1)}, s32[168,256]{1,0:T(8,128)S(1)}, u32[]{:S(2)}, u32[]{:S(2)}) collective-permute-start(s32[168,256]{1,0:T(8,128)S(1)} %shard_map.63._), channel_id=1, source_target_pairs={{32,0},{64,32},{96,64},{128,96},{160,128},{192,160},{224,192},{256... | collective-permute-start | bytes 516104 | tf_op jit(solution)/shard_map/ppermute | solution.py:432
  56.1 1.9 %collective-permute-start.5 = (s32[168,256]{1,0:T(8,128)S(1)}, s32[168,256]{1,0:T(8,128)S(1)}, u32[]{:S(2)}, u32[]{:S(2)}) collective-permute-start(s32[168,256]{1,0:T(8,128)S(1)} %shard_map.64._), channel_id=1, source_target_pairs={{0,32},{32,64},{64,96},{96,128},{128,160},{160,192},{192,224},{224... | collective-permute-start | bytes 516104 | tf_op jit(solution)/shard_map/ppermute | solution.py:429
  58.3 5.1 %collective-permute-start.8 = (s32[168,256]{1,0:T(8,128)S(1)}, s32[168,256]{1,0:T(8,128)S(1)}, u32[]{:S(2)}, u32[]{:S(2)}) collective-permute-start(s32[168,256]{1,0:T(8,128)S(1)} %shard_map.65._), channel_id=1, source_target_pairs={{32,0},{64,32},{96,64},{128,96},{160,128},{192,160},{224,192},{256... | collective-permute-start | bytes 516104 | tf_op jit(solution)/shard_map/ppermute | solution.py:432
  64.8 1.9 %collective-permute-start.7 = (s32[168,256]{1,0:T(8,128)S(1)}, s32[168,256]{1,0:T(8,128)S(1)}, u32[]{:S(2)}, u32[]{:S(2)}) collective-permute-start(s32[168,256]{1,0:T(8,128)S(1)} %shard_map.66._), channel_id=1, source_target_pairs={{0,32},{32,64},{64,96},{96,128},{128,160},{160,192},{192,224},{224... | collective-permute-start | bytes 516104 | tf_op jit(solution)/shard_map/ppermute | solution.py:429
  67.0 5.1 %collective-permute-start.10 = (s32[168,256]{1,0:T(8,128)S(1)}, s32[168,256]{1,0:T(8,128)S(1)}, u32[]{:S(2)}, u32[]{:S(2)}) collective-permute-start(s32[168,256]{1,0:T(8,128)S(1)} %shard_map.67._), channel_id=1, source_target_pairs={{32,0},{64,32},{96,64},{128,96},{160,128},{192,160},{224,192},{256... | collective-permute-start | bytes 516104 | tf_op jit(solution)/shard_map/ppermute | solution.py:432
  73.6 1.9 %collective-permute-start.9 = (s32[168,256]{1,0:T(8,128)S(1)}, s32[168,256]{1,0:T(8,128)S(1)}, u32[]{:S(2)}, u32[]{:S(2)}) collective-permute-start(s32[168,256]{1,0:T(8,128)S(1)} %shard_map.68._), channel_id=1, source_target_pairs={{0,32},{32,64},{64,96},{96,128},{128,160},{160,192},{192,224},{224... | collective-permute-start | bytes 516104 | tf_op jit(solution)/shard_map/ppermute | solution.py:429
  75.8 5.1 %collective-permute-start.12 = (s32[168,256]{1,0:T(8,128)S(1)}, s32[168,256]{1,0:T(8,128)S(1)}, u32[]{:S(2)}, u32[]{:S(2)}) collective-permute-start(s32[168,256]{1,0:T(8,128)S(1)} %shard_map.69._), channel_id=1, source_target_pairs={{32,0},{64,32},{96,64},{128,96},{160,128},{192,160},{224,192},{256... | collective-permute-start | bytes 516104 | tf_op jit(solution)/shard_map/ppermute | solution.py:432
  80.9 2.1 %collective-permute-done.9.came_ref = s32[168,256]{1,0:T(8,128)S(1)} collective-permute-done((s32[168,256]{1,0:T(8,128)S(1)}, s32[168,256]{1,0:T(8,128)S(1)}, u32[]{:S(2)}, u32[]{:S(2)}) %collective-permute-start.9) | collective-permute-done | bytes 172064 | tf_op jit(solution)/shard_map/ppermute | solution.py:429
  83.2 1.9 %collective-permute-start.11 = (s32[168,256]{1,0:T(8,128)S(1)}, s32[168,256]{1,0:T(8,128)S(1)}, u32[]{:S(2)}, u32[]{:S(2)}) collective-permute-start(s32[168,256]{1,0:T(8,128)S(1)} %shard_map.70._), channel_id=1, source_target_pairs={{0,32},{32,64},{64,96},{96,128},{128,160},{160,192},{192,224},{224... | collective-permute-start | bytes 516104 | tf_op jit(solution)/shard_map/ppermute | solution.py:429
  85.4 5.4 %collective-permute-start.14 = (s32[168,256]{1,0:T(8,128)S(1)}, s32[168,256]{1,0:T(8,128)S(1)}, u32[]{:S(2)}, u32[]{:S(2)}) collective-permute-start(s32[168,256]{1,0:T(8,128)S(1)} %shard_map.71._), channel_id=1, source_target_pairs={{32,0},{64,32},{96,64},{128,96},{160,128},{192,160},{224,192},{256... | collective-permute-start | bytes 516104 | tf_op jit(solution)/shard_map/ppermute | solution.py:432
  90.9 2.5 %collective-permute-done.11.came_ref = s32[168,256]{1,0:T(8,128)S(1)} collective-permute-done((s32[168,256]{1,0:T(8,128)S(1)}, s32[168,256]{1,0:T(8,128)S(1)}, u32[]{:S(2)}, u32[]{:S(2)}) %collective-permute-start.11) | collective-permute-done | bytes 172064 | tf_op jit(solution)/shard_map/ppermute | solution.py:429
  93.6 1.9 %collective-permute-start.13 = (s32[168,256]{1,0:T(8,128)S(1)}, s32[168,256]{1,0:T(8,128)S(1)}, u32[]{:S(2)}, u32[]{:S(2)}) collective-permute-start(s32[168,256]{1,0:T(8,128)S(1)} %shard_map.72._), channel_id=1, source_target_pairs={{0,32},{32,64},{64,96},{96,128},{128,160},{160,192},{192,224},{224... | collective-permute-start | bytes 516104 | tf_op jit(solution)/shard_map/ppermute | solution.py:429
  95.8 5.1 %collective-permute-start.16 = (s32[168,256]{1,0:T(8,128)S(1)}, s32[168,256]{1,0:T(8,128)S(1)}, u32[]{:S(2)}, u32[]{:S(2)}) collective-permute-start(s32[168,256]{1,0:T(8,128)S(1)} %shard_map.73._), channel_id=1, source_target_pairs={{32,0},{64,32},{96,64},{128,96},{160,128},{192,160},{224,192},{256... | collective-permute-start | bytes 516104 | tf_op jit(solution)/shard_map/ppermute | solution.py:432
  101.0 2.0 %collective-permute-done.13.came_ref = s32[168,256]{1,0:T(8,128)S(1)} collective-permute-done((s32[168,256]{1,0:T(8,128)S(1)}, s32[168,256]{1,0:T(8,128)S(1)}, u32[]{:S(2)}, u32[]{:S(2)}) %collective-permute-start.13) | collective-permute-done | bytes 172064 | tf_op jit(solution)/shard_map/ppermute | solution.py:429
  103.2 1.9 %collective-permute-start.15 = (s32[168,256]{1,0:T(8,128)S(1)}, s32[168,256]{1,0:T(8,128)S(1)}, u32[]{:S(2)}, u32[]{:S(2)}) collective-permute-start(s32[168,256]{1,0:T(8,128)S(1)} %shard_map.74), channel_id=1, source_target_pairs={{0,32},{32,64},{64,96},{96,128},{128,160},{160,192},{192,224},{224... | collective-permute-start | bytes 516104 | tf_op jit(solution)/shard_map/ppermute | solution.py:429
  105.1 6.6 %collective-permute-done.15.rising_ref = s32[168,256]{1,0:T(8,128)S(1)} collective-permute-done((s32[168,256]{1,0:T(8,128)S(1)}, s32[168,256]{1,0:T(8,128)S(1)}, u32[]{:S(2)}, u32[]{:S(2)}) %collective-permute-start.15) | collective-permute-done | bytes 172064 | tf_op jit(solution)/shard_map/ppermute | solution.py:429
  (38 shorter events, 16.8 us)
Async XLA Ops:
  0.6 1.4 %copy-start = (bf16[768,1024]{1,0:T(8,128)(2,1)S(1)}, bf16[768,1024]{1,0:T(8,128)(2,1)}, u32[]{:S(2)}) copy-start(bf16[768,1024]{1,0:T(8,128)(2,1)} %own_ref.1) | copy-start | bytes 4718596
  3.2 23.4 %collective-permute-start = (bf16[768,512]{1,0:T(8,128)(2,1)}, bf16[768,512]{1,0:T(8,128)(2,1)S(1)}, u32[]{:S(2)}, u32[]{:S(2)}) collective-permute-start(bf16[768,512]{1,0:T(8,128)(2,1)} %get-tuple-element.17), channel_id=1, source_target_pairs={{0,1},{1,2},{2,3},{3,4},{4,5},{5,6},{6,7},{7,8},{8,9},{9,10},{10,1... | collective-permute-start | bytes 2359304 | tf_op jit(solution)/shard_map/ppermute | solution.py:411
  6.6 20.9 %collective-permute-start.1 = (bf16[768,512]{1,0:T(8,128)(2,1)S(1)}, bf16[768,512]{1,0:T(8,128)(2,1)S(1)}, u32[]{:S(2)}, u32[]{:S(2)}) collective-permute-start(bf16[768,512]{1,0:T(8,128)(2,1)S(1)} %get-tuple-element.18), channel_id=1, source_target_pairs={{1,0},{2,1},{3,2},{4,3},{5,4},{6,5},{7,6},{8,7},{9,8},{10,9},{11,1... | collective-permute-start | bytes 2359304 | tf_op jit(solution)/shard_map/ppermute | solution.py:412
  12.6 1.4 %copy-start.1 = (bf16[768,1024]{1,0:T(8,128)(2,1)S(1)}, bf16[768,1024]{1,0:T(8,128)(2,1)}, u32[]{:S(2)}) copy-start(bf16[768,1024]{1,0:T(8,128)(2,1)} %own_ref.1) | copy-start | bytes 4718596
  14.0 0.7 copy-start.2
  14.7 0.7 copy-start.3
  32.3 14.8 %collective-permute-start.2 = (s32[168,256]{1,0:T(8,128)S(1)}, s32[168,256]{1,0:T(8,128)S(1)}, u32[]{:S(2)}, u32[]{:S(2)}) collective-permute-start(s32[168,256]{1,0:T(8,128)S(1)} %get-tuple-element.25), channel_id=1, source_target_pairs={{0,32},{32,64},{64,96},{96,128},{128,160},{160,192},{192,224},{224... | collective-permute-start | bytes 516104 | tf_op jit(solution)/shard_map/ppermute | solution.py:424
  36.1 13.1 %collective-permute-start.4 = (s32[168,256]{1,0:T(8,128)S(1)}, s32[168,256]{1,0:T(8,128)S(1)}, u32[]{:S(2)}, u32[]{:S(2)}) collective-permute-start(s32[168,256]{1,0:T(8,128)S(1)} %get-tuple-element.30._), channel_id=1, source_target_pairs={{32,0},{64,32},{96,64},{128,96},{160,128},{192,160},{224,192},{256... | collective-permute-start | bytes 516104 | tf_op jit(solution)/shard_map/ppermute | solution.py:425
  47.3 8.5 %collective-permute-start.3 = (s32[168,256]{1,0:T(8,128)S(1)}, s32[168,256]{1,0:T(8,128)S(1)}, u32[]{:S(2)}, u32[]{:S(2)}) collective-permute-start(s32[168,256]{1,0:T(8,128)S(1)} %shard_map.62._), channel_id=1, source_target_pairs={{0,32},{32,64},{64,96},{96,128},{128,160},{160,192},{192,224},{224... | collective-permute-start | bytes 516104 | tf_op jit(solution)/shard_map/ppermute | solution.py:429
  49.5 8.5 %collective-permute-start.6 = (s32[168,256]{1,0:T(8,128)S(1)}, s32[168,256]{1,0:T(8,128)S(1)}, u32[]{:S(2)}, u32[]{:S(2)}) collective-permute-start(s32[168,256]{1,0:T(8,128)S(1)} %shard_map.63._), channel_id=1, source_target_pairs={{32,0},{64,32},{96,64},{128,96},{160,128},{192,160},{224,192},{256... | collective-permute-start | bytes 516104 | tf_op jit(solution)/shard_map/ppermute | solution.py:432
  56.1 8.5 %collective-permute-start.5 = (s32[168,256]{1,0:T(8,128)S(1)}, s32[168,256]{1,0:T(8,128)S(1)}, u32[]{:S(2)}, u32[]{:S(2)}) collective-permute-start(s32[168,256]{1,0:T(8,128)S(1)} %shard_map.64._), channel_id=1, source_target_pairs={{0,32},{32,64},{64,96},{96,128},{128,160},{160,192},{192,224},{224... | collective-permute-start | bytes 516104 | tf_op jit(solution)/shard_map/ppermute | solution.py:429
  58.3 8.5 %collective-permute-start.8 = (s32[168,256]{1,0:T(8,128)S(1)}, s32[168,256]{1,0:T(8,128)S(1)}, u32[]{:S(2)}, u32[]{:S(2)}) collective-permute-start(s32[168,256]{1,0:T(8,128)S(1)} %shard_map.65._), channel_id=1, source_target_pairs={{32,0},{64,32},{96,64},{128,96},{160,128},{192,160},{224,192},{256... | collective-permute-start | bytes 516104 | tf_op jit(solution)/shard_map/ppermute | solution.py:432
  64.8 8.5 %collective-permute-start.7 = (s32[168,256]{1,0:T(8,128)S(1)}, s32[168,256]{1,0:T(8,128)S(1)}, u32[]{:S(2)}, u32[]{:S(2)}) collective-permute-start(s32[168,256]{1,0:T(8,128)S(1)} %shard_map.66._), channel_id=1, source_target_pairs={{0,32},{32,64},{64,96},{96,128},{128,160},{160,192},{192,224},{224... | collective-permute-start | bytes 516104 | tf_op jit(solution)/shard_map/ppermute | solution.py:429
  67.0 8.5 %collective-permute-start.10 = (s32[168,256]{1,0:T(8,128)S(1)}, s32[168,256]{1,0:T(8,128)S(1)}, u32[]{:S(2)}, u32[]{:S(2)}) collective-permute-start(s32[168,256]{1,0:T(8,128)S(1)} %shard_map.67._), channel_id=1, source_target_pairs={{32,0},{64,32},{96,64},{128,96},{160,128},{192,160},{224,192},{256... | collective-permute-start | bytes 516104 | tf_op jit(solution)/shard_map/ppermute | solution.py:432
  73.6 9.4 %collective-permute-start.9 = (s32[168,256]{1,0:T(8,128)S(1)}, s32[168,256]{1,0:T(8,128)S(1)}, u32[]{:S(2)}, u32[]{:S(2)}) collective-permute-start(s32[168,256]{1,0:T(8,128)S(1)} %shard_map.68._), channel_id=1, source_target_pairs={{0,32},{32,64},{64,96},{96,128},{128,160},{160,192},{192,224},{224... | collective-permute-start | bytes 516104 | tf_op jit(solution)/shard_map/ppermute | solution.py:429
  75.8 9.4 %collective-permute-start.12 = (s32[168,256]{1,0:T(8,128)S(1)}, s32[168,256]{1,0:T(8,128)S(1)}, u32[]{:S(2)}, u32[]{:S(2)}) collective-permute-start(s32[168,256]{1,0:T(8,128)S(1)} %shard_map.69._), channel_id=1, source_target_pairs={{32,0},{64,32},{96,64},{128,96},{160,128},{192,160},{224,192},{256... | collective-permute-start | bytes 516104 | tf_op jit(solution)/shard_map/ppermute | solution.py:432
  83.2 10.2 %collective-permute-start.11 = (s32[168,256]{1,0:T(8,128)S(1)}, s32[168,256]{1,0:T(8,128)S(1)}, u32[]{:S(2)}, u32[]{:S(2)}) collective-permute-start(s32[168,256]{1,0:T(8,128)S(1)} %shard_map.70._), channel_id=1, source_target_pairs={{0,32},{32,64},{64,96},{96,128},{128,160},{160,192},{192,224},{224... | collective-permute-start | bytes 516104 | tf_op jit(solution)/shard_map/ppermute | solution.py:429
  85.4 10.2 %collective-permute-start.14 = (s32[168,256]{1,0:T(8,128)S(1)}, s32[168,256]{1,0:T(8,128)S(1)}, u32[]{:S(2)}, u32[]{:S(2)}) collective-permute-start(s32[168,256]{1,0:T(8,128)S(1)} %shard_map.71._), channel_id=1, source_target_pairs={{32,0},{64,32},{96,64},{128,96},{160,128},{192,160},{224,192},{256... | collective-permute-start | bytes 516104 | tf_op jit(solution)/shard_map/ppermute | solution.py:432
  93.6 9.3 %collective-permute-start.13 = (s32[168,256]{1,0:T(8,128)S(1)}, s32[168,256]{1,0:T(8,128)S(1)}, u32[]{:S(2)}, u32[]{:S(2)}) collective-permute-start(s32[168,256]{1,0:T(8,128)S(1)} %shard_map.72._), channel_id=1, source_target_pairs={{0,32},{32,64},{64,96},{96,128},{128,160},{160,192},{192,224},{224... | collective-permute-start | bytes 516104 | tf_op jit(solution)/shard_map/ppermute | solution.py:429
  95.8 9.3 %collective-permute-start.16 = (s32[168,256]{1,0:T(8,128)S(1)}, s32[168,256]{1,0:T(8,128)S(1)}, u32[]{:S(2)}, u32[]{:S(2)}) collective-permute-start(s32[168,256]{1,0:T(8,128)S(1)} %shard_map.73._), channel_id=1, source_target_pairs={{32,0},{64,32},{96,64},{128,96},{160,128},{192,160},{224,192},{256... | collective-permute-start | bytes 516104 | tf_op jit(solution)/shard_map/ppermute | solution.py:432
  103.2 8.5 %collective-permute-start.15 = (s32[168,256]{1,0:T(8,128)S(1)}, s32[168,256]{1,0:T(8,128)S(1)}, u32[]{:S(2)}, u32[]{:S(2)}) collective-permute-start(s32[168,256]{1,0:T(8,128)S(1)} %shard_map.74), channel_id=1, source_target_pairs={{0,32},{32,64},{64,96},{96,128},{128,160},{160,192},{192,224},{224... | collective-permute-start | bytes 516104 | tf_op jit(solution)/shard_map/ppermute | solution.py:429

commit v13 on v12

--- a/solution.py
+++ b/solution.py
@@ -13,7 +13,7 @@
 SCALE = 131072.0
 UNIT = 1600.0 / 65535.0
 SHOTS = 768
-TAIL = 40
+TAIL = 32
 ANY = pl.BlockSpec(memory_space=pl.ANY)
 VMEM = pl.BlockSpec(memory_space=pltpu.VMEM)
 SMEM = pl.BlockSpec(memory_space=pltpu.SMEM)
@@ -104,7 +104,7 @@
         fit_ref[b : b + 1, :] = jnp.sum(jnp.where(same, probt_ref[:, b : b + 1], 0.0), axis=0, keepdims=True)
     fetch.wait()
     lines = lax.broadcasted_iota(jnp.int32, (width, edges), 0)
-    products, firsts, others = [], [], []
+    products, others = [], []
     for b in range(blocks):
         own = own_ref[:, b * width : (b + 1) * width]
         rows_x = inc_ref[0, b : b + 1, :]
@@ -143,9 +143,8 @@
         vals_ref[b] = vals.astype(jnp.bfloat16)
         other = jnp.dot(chosen, jnp.concatenate(hot, axis=0), preferred_element_type=jnp.float32)
         products += rows_of(jnp.sum(vals * other, axis=0, keepdims=True), pieces)
-        firsts += rows_of(jnp.sum(vals, axis=0, keepdims=True), pieces)
         others += rows_of(jnp.sum(other, axis=0, keepdims=True), pieces)
-    early_ref[...] = jnp.concatenate(products + firsts + others, axis=0)
+    early_ref[...] = jnp.concatenate(products + others, axis=0)
     sums_ref[...] = jnp.concatenate(rows_of(row_sums(own_ref[...]), blocks), axis=0)
 
 
@@ -160,7 +159,7 @@
             jax.ShapeDtypeStruct((blocks, shots, edges), jnp.bfloat16),
             jax.ShapeDtypeStruct((blocks, HALO * width, edges), jnp.bfloat16),
             jax.ShapeDtypeStruct((groups, blocks * slots, width // groups, width), jnp.float32),
-            jax.ShapeDtypeStruct((3 * blocks * edges // width, width), jnp.float32),
+            jax.ShapeDtypeStruct((2 * blocks * edges // width, width), jnp.float32),
             jax.ShapeDtypeStruct((blocks, width), jnp.float32),
             jax.ShapeDtypeStruct((REACH + 1, blocks * slots, width), jnp.float32),
         ],
@@ -244,13 +243,10 @@
         product = jnp.sum(vals_ref[block].astype(jnp.float32) * other, axis=0, keepdims=True)
         products += rows_of(product, pieces)
         others += rows_of(jnp.sum(other, axis=0, keepdims=True), pieces)
-    count = blocks * pieces
     sums = fixed(
         jnp.concatenate(rows_of(halo_sums[0], HALO) + [own_sums_ref[...]] + rows_of(halo_sums[1], HALO), axis=0)
     )
-    edges = early_ref[...] + jnp.concatenate(
-        products + [jnp.zeros((count, width), jnp.float32)] + others, axis=0
-    )
+    edges = early_ref[...] + jnp.concatenate(products + others, axis=0)
     edges = fixed(edges)
     sums_ref[...] = sums
     edge_ref[...] = edges
@@ -367,17 +363,20 @@
                 alone = total_column * alls[row, :]
                 entry = 0.5 - 0.5 * jnp.sqrt(alone / (alone + cov))
                 pair_ref[block, 2 * pair + i] = (entry * pick_ref[REACH, row, :]).astype(jnp.bfloat16)
+        column = column_of(totals[own, :], 0, width)
         for p in range(pieces):
             n = block * pieces + p
             at = slice(p * width, (p + 1) * width)
+            here = lax.broadcasted_iota(jnp.int32, (width, width), 0) == inc_ref[0, block : block + 1, at]
+            first = jnp.sum(jnp.where(here, column, 0.0), axis=0, keepdims=True)
             slot_x = inc_ref[1, block : block + 1, at]
             live = jnp.zeros((1, width), jnp.float32)
             for k in range(slots):
                 tile = block * slots + k
                 live = live + jnp.where(slot_x == k, pick_ref[REACH, tile : tile + 1, :], 0.0)
             rows = blocks * pieces
-            quotient = (edges[rows + n : rows + n + 1] / count) * (
-                edges[2 * rows + n : 2 * rows + n + 1] / count
+            quotient = (first / count) * (
+                edges[rows + n : rows + n + 1] / count
             ) * count / edges[n : n + 1]
             entry = (0.5 - 0.5 * jnp.sqrt(quotient)) * live
             residual = live * (entry - fit_ref[block : block + 1, at]) / NOISE_SPREAD

time: 114 us -> 113 us (level)
  no operation moved by 1% of the time
where the time goes in v13:
time: 113 us; the launch traced here: 112 us
  starting transfers between devices  65.6 us (58%)
  Pallas kernels  20.5 us (18%)
  waiting for transfers between devices  19.2 us (17%)
  local copies, waits for them, and re-layouts  5.21 us (5%)
    ppermute x6, starting transfers between devices, local(): falling = lax.ppermute(order, 'shot', fall)  31.1 us
    ppermute x7, waiting for transfers between devices, local(): rising = lax.ppermute(order, 'shot', rise)  15.8 us
    ppermute x7, starting transfers between devices, local(): rising = lax.ppermute(order, 'shot', rise)  13.4 us
    pallas_call x1, Pallas kernels, ready_call(): pl.pallas_call(functools.partial(ready_kernel, width), out_shape=[jax.Sha...  9.97 us
    ppermute x1, starting transfers between devices, local(): falling = lax.ppermute(down, 'shot', fall)  9.5 us
    unnamed x9, local copies, waits for them, and re-layouts  5.07 us
    pallas_call x1, Pallas kernels, pair_call(): pl.pallas_call(pair_kernel, out_shape=[jax.ShapeDtypeStruct(cov.shape, jn...  4.85 us
    ppermute x1, starting transfers between devices, local(): lax.ppermute(head, ('row', 'col'), [((i + 1) % sides, i) for i in range(s...  4.27 us
  transfers between devices with their start and end apart: 17, of which 10 were waited for; matrix products, arithmetic and copies ran while one was open for 2% of the time, Pallas kernels for 12%

profile of v13, /device:TPU:24, one launch (start us, length us, event | category | flops | bytes accessed | tf_op | source)
XLA Modules:
  0.0 112.1 jit_solution(16907999877513167797)
XLA Ops:
  3.2 3.4 %collective-permute-start = (bf16[768,512]{1,0:T(8,128)(2,1)}, bf16[768,512]{1,0:T(8,128)(2,1)S(1)}, u32[]{:S(2)}, u32[]{:S(2)}) collective-permute-start(bf16[768,512]{1,0:T(8,128)(2,1)} %get-tuple-element.17), channel_id=1, source_target_pairs={{0,1},{1,2},{2,3},{3,4},{4,5},{5,6},{6,7},{7,8},{8,9},{9,10},{10,1... | collective-permute-start | bytes 2359304 | tf_op jit(solution)/shard_map/ppermute | solution.py:410
  6.6 4.3 %collective-permute-start.1 = (bf16[768,512]{1,0:T(8,128)(2,1)S(1)}, bf16[768,512]{1,0:T(8,128)(2,1)S(1)}, u32[]{:S(2)}, u32[]{:S(2)}) collective-permute-start(bf16[768,512]{1,0:T(8,128)(2,1)S(1)} %get-tuple-element.18), channel_id=1, source_target_pairs={{1,0},{2,1},{3,2},{4,3},{5,4},{6,5},{7,6},{8,7},{9,8},{10,9},{11,1... | collective-permute-start | bytes 2359304 | tf_op jit(solution)/shard_map/ppermute | solution.py:411
  15.4 10.0 %shard_map.60 = (f32[4,512]{1,0:T(4,128)S(1)}, bf16[4,768,512]{2,1,0:T(8,128)(2,1)S(1)}, bf16[4,512,512]{2,1,0:T(8,128)(2,1)S(1)}, f32[16,16,16,256]{3,2,1,0:T(8...) custom-call(s32[4,4]{1,0:T(4,128)S(1)} %copy-done.3, ...), custom_call_target="tpu_custom_call" | custom-call | flops 20000000000 | bytes 12000000 | tf_op jit(solution)/shard_map/pallas_call | solution.py:155
  27.5 4.8 %shard_map.61 = (f32[16,16,16,256]{3,2,1,0:T(8,128)S(1)}, s32[16,256]{1,0:T(8,128)S(1)}, s32[8,256]{1,0:T(8,128)S(1)}, s32[160,256]{1,0:T(8,128)S(1)}, s32[160,256]{1,0:T(8,128)S(1)}) custom-call(s32[4,4]{1,0:T(4,128)S(1)} %copy-done.3, bf16[768,512]{1,0:T(8,128)(2,1)S(1)} %collective-permute-done.left_ref, ...), custom_call_target="tpu_custom_call", output_to_operand_aliasing={{0}: (8, {})} | custom-call | flops 2000000000 | bytes 4000000 | tf_op jit(solution)/shard_map/pallas_call | solution.py:260
  32.3 3.8 %collective-permute-start.2 = (s32[160,256]{1,0:T(8,128)S(1)}, s32[160,256]{1,0:T(8,128)S(1)}, u32[]{:S(2)}, u32[]{:S(2)}) collective-permute-start(s32[160,256]{1,0:T(8,128)S(1)} %get-tuple-element.25), channel_id=1, source_target_pairs={{0,32},{32,64},{64,96},{96,128},{128,160},{160,192},{192,224},{224... | collective-permute-start | bytes 491528 | tf_op jit(solution)/shard_map/ppermute | solution.py:423
  36.1 9.5 %collective-permute-start.4 = (s32[160,256]{1,0:T(8,128)S(1)}, s32[160,256]{1,0:T(8,128)S(1)}, u32[]{:S(2)}, u32[]{:S(2)}) collective-permute-start(s32[160,256]{1,0:T(8,128)S(1)} %get-tuple-element.30._), channel_id=1, source_target_pairs={{32,0},{64,32},{96,64},{128,96},{160,128},{192,160},{224,192},{256... | collective-permute-start | bytes 491528 | tf_op jit(solution)/shard_map/ppermute | solution.py:424
  47.2 1.9 %collective-permute-start.3 = (s32[160,256]{1,0:T(8,128)S(1)}, s32[160,256]{1,0:T(8,128)S(1)}, u32[]{:S(2)}, u32[]{:S(2)}) collective-permute-start(s32[160,256]{1,0:T(8,128)S(1)} %shard_map.62._), channel_id=1, source_target_pairs={{0,32},{32,64},{64,96},{96,128},{128,160},{160,192},{192,224},{224... | collective-permute-start | bytes 491528 | tf_op jit(solution)/shard_map/ppermute | solution.py:428
  49.4 5.1 %collective-permute-start.6 = (s32[160,256]{1,0:T(8,128)S(1)}, s32[160,256]{1,0:T(8,128)S(1)}, u32[]{:S(2)}, u32[]{:S(2)}) collective-permute-start(s32[160,256]{1,0:T(8,128)S(1)} %shard_map.63._), channel_id=1, source_target_pairs={{32,0},{64,32},{96,64},{128,96},{160,128},{192,160},{224,192},{256... | collective-permute-start | bytes 491528 | tf_op jit(solution)/shard_map/ppermute | solution.py:431
  55.9 1.9 %collective-permute-start.5 = (s32[160,256]{1,0:T(8,128)S(1)}, s32[160,256]{1,0:T(8,128)S(1)}, u32[]{:S(2)}, u32[]{:S(2)}) collective-permute-start(s32[160,256]{1,0:T(8,128)S(1)} %shard_map.64._), channel_id=1, source_target_pairs={{0,32},{32,64},{64,96},{96,128},{128,160},{160,192},{192,224},{224... | collective-permute-start | bytes 491528 | tf_op jit(solution)/shard_map/ppermute | solution.py:428
  58.1 5.1 %collective-permute-start.8 = (s32[160,256]{1,0:T(8,128)S(1)}, s32[160,256]{1,0:T(8,128)S(1)}, u32[]{:S(2)}, u32[]{:S(2)}) collective-permute-start(s32[160,256]{1,0:T(8,128)S(1)} %shard_map.65._), channel_id=1, source_target_pairs={{32,0},{64,32},{96,64},{128,96},{160,128},{192,160},{224,192},{256... | collective-permute-start | bytes 491528 | tf_op jit(solution)/shard_map/ppermute | solution.py:431
  64.6 1.9 %collective-permute-start.7 = (s32[160,256]{1,0:T(8,128)S(1)}, s32[160,256]{1,0:T(8,128)S(1)}, u32[]{:S(2)}, u32[]{:S(2)}) collective-permute-start(s32[160,256]{1,0:T(8,128)S(1)} %shard_map.66._), channel_id=1, source_target_pairs={{0,32},{32,64},{64,96},{96,128},{128,160},{160,192},{192,224},{224... | collective-permute-start | bytes 491528 | tf_op jit(solution)/shard_map/ppermute | solution.py:428
  66.8 5.1 %collective-permute-start.10 = (s32[160,256]{1,0:T(8,128)S(1)}, s32[160,256]{1,0:T(8,128)S(1)}, u32[]{:S(2)}, u32[]{:S(2)}) collective-permute-start(s32[160,256]{1,0:T(8,128)S(1)} %shard_map.67._), channel_id=1, source_target_pairs={{32,0},{64,32},{96,64},{128,96},{160,128},{192,160},{224,192},{256... | collective-permute-start | bytes 491528 | tf_op jit(solution)/shard_map/ppermute | solution.py:431
  73.2 1.9 %collective-permute-start.9 = (s32[160,256]{1,0:T(8,128)S(1)}, s32[160,256]{1,0:T(8,128)S(1)}, u32[]{:S(2)}, u32[]{:S(2)}) collective-permute-start(s32[160,256]{1,0:T(8,128)S(1)} %shard_map.68._), channel_id=1, source_target_pairs={{0,32},{32,64},{64,96},{96,128},{128,160},{160,192},{192,224},{224... | collective-permute-start | bytes 491528 | tf_op jit(solution)/shard_map/ppermute | solution.py:428
  75.4 5.1 %collective-permute-start.12 = (s32[160,256]{1,0:T(8,128)S(1)}, s32[160,256]{1,0:T(8,128)S(1)}, u32[]{:S(2)}, u32[]{:S(2)}) collective-permute-start(s32[160,256]{1,0:T(8,128)S(1)} %shard_map.69._), channel_id=1, source_target_pairs={{32,0},{64,32},{96,64},{128,96},{160,128},{192,160},{224,192},{256... | collective-permute-start | bytes 491528 | tf_op jit(solution)/shard_map/ppermute | solution.py:431
  80.6 1.9 %collective-permute-done.9.came_ref = s32[160,256]{1,0:T(8,128)S(1)} collective-permute-done((s32[160,256]{1,0:T(8,128)S(1)}, s32[160,256]{1,0:T(8,128)S(1)}, u32[]{:S(2)}, u32[]{:S(2)}) %collective-permute-start.9) | collective-permute-done | bytes 163872 | tf_op jit(solution)/shard_map/ppermute | solution.py:428
  82.8 1.9 %collective-permute-start.11 = (s32[160,256]{1,0:T(8,128)S(1)}, s32[160,256]{1,0:T(8,128)S(1)}, u32[]{:S(2)}, u32[]{:S(2)}) collective-permute-start(s32[160,256]{1,0:T(8,128)S(1)} %shard_map.70._), channel_id=1, source_target_pairs={{0,32},{32,64},{64,96},{96,128},{128,160},{160,192},{192,224},{224... | collective-permute-start | bytes 491528 | tf_op jit(solution)/shard_map/ppermute | solution.py:428
  84.9 5.5 %collective-permute-start.14 = (s32[160,256]{1,0:T(8,128)S(1)}, s32[160,256]{1,0:T(8,128)S(1)}, u32[]{:S(2)}, u32[]{:S(2)}) collective-permute-start(s32[160,256]{1,0:T(8,128)S(1)} %shard_map.71._), channel_id=1, source_target_pairs={{32,0},{64,32},{96,64},{128,96},{160,128},{192,160},{224,192},{256... | collective-permute-start | bytes 491528 | tf_op jit(solution)/shard_map/ppermute | solution.py:431
  90.4 2.3 %collective-permute-done.11.came_ref = s32[160,256]{1,0:T(8,128)S(1)} collective-permute-done((s32[160,256]{1,0:T(8,128)S(1)}, s32[160,256]{1,0:T(8,128)S(1)}, u32[]{:S(2)}, u32[]{:S(2)}) %collective-permute-start.11) | collective-permute-done | bytes 163872 | tf_op jit(solution)/shard_map/ppermute | solution.py:428
  92.9 1.9 %collective-permute-start.13 = (s32[160,256]{1,0:T(8,128)S(1)}, s32[160,256]{1,0:T(8,128)S(1)}, u32[]{:S(2)}, u32[]{:S(2)}) collective-permute-start(s32[160,256]{1,0:T(8,128)S(1)} %shard_map.72._), channel_id=1, source_target_pairs={{0,32},{32,64},{64,96},{96,128},{128,160},{160,192},{192,224},{224... | collective-permute-start | bytes 491528 | tf_op jit(solution)/shard_map/ppermute | solution.py:428
  95.1 5.2 %collective-permute-start.16 = (s32[160,256]{1,0:T(8,128)S(1)}, s32[160,256]{1,0:T(8,128)S(1)}, u32[]{:S(2)}, u32[]{:S(2)}) collective-permute-start(s32[160,256]{1,0:T(8,128)S(1)} %shard_map.73._), channel_id=1, source_target_pairs={{32,0},{64,32},{96,64},{128,96},{160,128},{192,160},{224,192},{256... | collective-permute-start | bytes 491528 | tf_op jit(solution)/shard_map/ppermute | solution.py:431
  100.3 1.7 %collective-permute-done.13.came_ref = s32[160,256]{1,0:T(8,128)S(1)} collective-permute-done((s32[160,256]{1,0:T(8,128)S(1)}, s32[160,256]{1,0:T(8,128)S(1)}, u32[]{:S(2)}, u32[]{:S(2)}) %collective-permute-start.13) | collective-permute-done | bytes 163872 | tf_op jit(solution)/shard_map/ppermute | solution.py:428
  102.3 1.9 %collective-permute-start.15 = (s32[160,256]{1,0:T(8,128)S(1)}, s32[160,256]{1,0:T(8,128)S(1)}, u32[]{:S(2)}, u32[]{:S(2)}) collective-permute-start(s32[160,256]{1,0:T(8,128)S(1)} %shard_map.74), channel_id=1, source_target_pairs={{0,32},{32,64},{64,96},{96,128},{128,160},{160,192},{192,224},{224... | collective-permute-start | bytes 491528 | tf_op jit(solution)/shard_map/ppermute | solution.py:428
  104.2 6.5 %collective-permute-done.15.rising_ref = s32[160,256]{1,0:T(8,128)S(1)} collective-permute-done((s32[160,256]{1,0:T(8,128)S(1)}, s32[160,256]{1,0:T(8,128)S(1)}, u32[]{:S(2)}, u32[]{:S(2)}) %collective-permute-start.15) | collective-permute-done | bytes 163872 | tf_op jit(solution)/shard_map/ppermute | solution.py:428
  110.7 1.4 %shard_map.75 = (bf16[4,4,16,256]{3,2,1,0:T(8,128)(2,1)}, f32[4,512]{1,0:T(4,128)}) custom-call(s32[3,4,512]{2,1,0:T(4,128)S(1)} %copy-done.2, s32[160,256]{1,0:T(8,128)S(1)} %collective-permute-done.15.rising_ref, s32[160,256]{1,0:T(8,128)S(1)} %collective-permute-done.16.falling_ref, f32[16,16,16,256]{3,2,1,0:T(8,128)S(1)} %get-tuple-element.26.cov_ref, ...), custom_call_target="tpu_custom_call" | custom-call | flops 1000000 | bytes 2000000 | tf_op jit(solution)/shard_map/pallas_call | solution.py:389
  (38 shorter events, 16.9 us)
Async XLA Ops:
  0.6 1.4 %copy-start = (bf16[768,1024]{1,0:T(8,128)(2,1)S(1)}, bf16[768,1024]{1,0:T(8,128)(2,1)}, u32[]{:S(2)}) copy-start(bf16[768,1024]{1,0:T(8,128)(2,1)} %own_ref.1) | copy-start | bytes 4718596
  3.2 23.4 %collective-permute-start = (bf16[768,512]{1,0:T(8,128)(2,1)}, bf16[768,512]{1,0:T(8,128)(2,1)S(1)}, u32[]{:S(2)}, u32[]{:S(2)}) collective-permute-start(bf16[768,512]{1,0:T(8,128)(2,1)} %get-tuple-element.17), channel_id=1, source_target_pairs={{0,1},{1,2},{2,3},{3,4},{4,5},{5,6},{6,7},{7,8},{8,9},{9,10},{10,1... | collective-permute-start | bytes 2359304 | tf_op jit(solution)/shard_map/ppermute | solution.py:410
  6.6 20.9 %collective-permute-start.1 = (bf16[768,512]{1,0:T(8,128)(2,1)S(1)}, bf16[768,512]{1,0:T(8,128)(2,1)S(1)}, u32[]{:S(2)}, u32[]{:S(2)}) collective-permute-start(bf16[768,512]{1,0:T(8,128)(2,1)S(1)} %get-tuple-element.18), channel_id=1, source_target_pairs={{1,0},{2,1},{3,2},{4,3},{5,4},{6,5},{7,6},{8,7},{9,8},{10,9},{11,1... | collective-permute-start | bytes 2359304 | tf_op jit(solution)/shard_map/ppermute | solution.py:411
  12.6 1.4 %copy-start.1 = (bf16[768,1024]{1,0:T(8,128)(2,1)S(1)}, bf16[768,1024]{1,0:T(8,128)(2,1)}, u32[]{:S(2)}) copy-start(bf16[768,1024]{1,0:T(8,128)(2,1)} %own_ref.1) | copy-start | bytes 4718596
  14.0 0.7 copy-start.2
  14.7 0.7 copy-start.3
  32.3 14.7 %collective-permute-start.2 = (s32[160,256]{1,0:T(8,128)S(1)}, s32[160,256]{1,0:T(8,128)S(1)}, u32[]{:S(2)}, u32[]{:S(2)}) collective-permute-start(s32[160,256]{1,0:T(8,128)S(1)} %get-tuple-element.25), channel_id=1, source_target_pairs={{0,32},{32,64},{64,96},{96,128},{128,160},{160,192},{192,224},{224... | collective-permute-start | bytes 491528 | tf_op jit(solution)/shard_map/ppermute | solution.py:423
  36.1 13.0 %collective-permute-start.4 = (s32[160,256]{1,0:T(8,128)S(1)}, s32[160,256]{1,0:T(8,128)S(1)}, u32[]{:S(2)}, u32[]{:S(2)}) collective-permute-start(s32[160,256]{1,0:T(8,128)S(1)} %get-tuple-element.30._), channel_id=1, source_target_pairs={{32,0},{64,32},{96,64},{128,96},{160,128},{192,160},{224,192},{256... | collective-permute-start | bytes 491528 | tf_op jit(solution)/shard_map/ppermute | solution.py:424
  47.2 8.4 %collective-permute-start.3 = (s32[160,256]{1,0:T(8,128)S(1)}, s32[160,256]{1,0:T(8,128)S(1)}, u32[]{:S(2)}, u32[]{:S(2)}) collective-permute-start(s32[160,256]{1,0:T(8,128)S(1)} %shard_map.62._), channel_id=1, source_target_pairs={{0,32},{32,64},{64,96},{96,128},{128,160},{160,192},{192,224},{224... | collective-permute-start | bytes 491528 | tf_op jit(solution)/shard_map/ppermute | solution.py:428
  49.4 8.4 %collective-permute-start.6 = (s32[160,256]{1,0:T(8,128)S(1)}, s32[160,256]{1,0:T(8,128)S(1)}, u32[]{:S(2)}, u32[]{:S(2)}) collective-permute-start(s32[160,256]{1,0:T(8,128)S(1)} %shard_map.63._), channel_id=1, source_target_pairs={{32,0},{64,32},{96,64},{128,96},{160,128},{192,160},{224,192},{256... | collective-permute-start | bytes 491528 | tf_op jit(solution)/shard_map/ppermute | solution.py:431
  55.9 8.4 %collective-permute-start.5 = (s32[160,256]{1,0:T(8,128)S(1)}, s32[160,256]{1,0:T(8,128)S(1)}, u32[]{:S(2)}, u32[]{:S(2)}) collective-permute-start(s32[160,256]{1,0:T(8,128)S(1)} %shard_map.64._), channel_id=1, source_target_pairs={{0,32},{32,64},{64,96},{96,128},{128,160},{160,192},{192,224},{224... | collective-permute-start | bytes 491528 | tf_op jit(solution)/shard_map/ppermute | solution.py:428
  58.1 8.4 %collective-permute-start.8 = (s32[160,256]{1,0:T(8,128)S(1)}, s32[160,256]{1,0:T(8,128)S(1)}, u32[]{:S(2)}, u32[]{:S(2)}) collective-permute-start(s32[160,256]{1,0:T(8,128)S(1)} %shard_map.65._), channel_id=1, source_target_pairs={{32,0},{64,32},{96,64},{128,96},{160,128},{192,160},{224,192},{256... | collective-permute-start | bytes 491528 | tf_op jit(solution)/shard_map/ppermute | solution.py:431
  64.6 8.4 %collective-permute-start.7 = (s32[160,256]{1,0:T(8,128)S(1)}, s32[160,256]{1,0:T(8,128)S(1)}, u32[]{:S(2)}, u32[]{:S(2)}) collective-permute-start(s32[160,256]{1,0:T(8,128)S(1)} %shard_map.66._), channel_id=1, source_target_pairs={{0,32},{32,64},{64,96},{96,128},{128,160},{160,192},{192,224},{224... | collective-permute-start | bytes 491528 | tf_op jit(solution)/shard_map/ppermute | solution.py:428
  66.8 8.4 %collective-permute-start.10 = (s32[160,256]{1,0:T(8,128)S(1)}, s32[160,256]{1,0:T(8,128)S(1)}, u32[]{:S(2)}, u32[]{:S(2)}) collective-permute-start(s32[160,256]{1,0:T(8,128)S(1)} %shard_map.67._), channel_id=1, source_target_pairs={{32,0},{64,32},{96,64},{128,96},{160,128},{192,160},{224,192},{256... | collective-permute-start | bytes 491528 | tf_op jit(solution)/shard_map/ppermute | solution.py:431
  73.2 9.3 %collective-permute-start.9 = (s32[160,256]{1,0:T(8,128)S(1)}, s32[160,256]{1,0:T(8,128)S(1)}, u32[]{:S(2)}, u32[]{:S(2)}) collective-permute-start(s32[160,256]{1,0:T(8,128)S(1)} %shard_map.68._), channel_id=1, source_target_pairs={{0,32},{32,64},{64,96},{96,128},{128,160},{160,192},{192,224},{224... | collective-permute-start | bytes 491528 | tf_op jit(solution)/shard_map/ppermute | solution.py:428
  75.4 9.3 %collective-permute-start.12 = (s32[160,256]{1,0:T(8,128)S(1)}, s32[160,256]{1,0:T(8,128)S(1)}, u32[]{:S(2)}, u32[]{:S(2)}) collective-permute-start(s32[160,256]{1,0:T(8,128)S(1)} %shard_map.69._), channel_id=1, source_target_pairs={{32,0},{64,32},{96,64},{128,96},{160,128},{192,160},{224,192},{256... | collective-permute-start | bytes 491528 | tf_op jit(solution)/shard_map/ppermute | solution.py:431
  82.8 9.9 %collective-permute-start.11 = (s32[160,256]{1,0:T(8,128)S(1)}, s32[160,256]{1,0:T(8,128)S(1)}, u32[]{:S(2)}, u32[]{:S(2)}) collective-permute-start(s32[160,256]{1,0:T(8,128)S(1)} %shard_map.70._), channel_id=1, source_target_pairs={{0,32},{32,64},{64,96},{96,128},{128,160},{160,192},{192,224},{224... | collective-permute-start | bytes 491528 | tf_op jit(solution)/shard_map/ppermute | solution.py:428
  84.9 9.9 %collective-permute-start.14 = (s32[160,256]{1,0:T(8,128)S(1)}, s32[160,256]{1,0:T(8,128)S(1)}, u32[]{:S(2)}, u32[]{:S(2)}) collective-permute-start(s32[160,256]{1,0:T(8,128)S(1)} %shard_map.71._), channel_id=1, source_target_pairs={{32,0},{64,32},{96,64},{128,96},{160,128},{192,160},{224,192},{256... | collective-permute-start | bytes 491528 | tf_op jit(solution)/shard_map/ppermute | solution.py:431
  92.9 9.1 %collective-permute-start.13 = (s32[160,256]{1,0:T(8,128)S(1)}, s32[160,256]{1,0:T(8,128)S(1)}, u32[]{:S(2)}, u32[]{:S(2)}) collective-permute-start(s32[160,256]{1,0:T(8,128)S(1)} %shard_map.72._), channel_id=1, source_target_pairs={{0,32},{32,64},{64,96},{96,128},{128,160},{160,192},{192,224},{224... | collective-permute-start | bytes 491528 | tf_op jit(solution)/shard_map/ppermute | solution.py:428
  95.1 9.1 %collective-permute-start.16 = (s32[160,256]{1,0:T(8,128)S(1)}, s32[160,256]{1,0:T(8,128)S(1)}, u32[]{:S(2)}, u32[]{:S(2)}) collective-permute-start(s32[160,256]{1,0:T(8,128)S(1)} %shard_map.73._), channel_id=1, source_target_pairs={{32,0},{64,32},{96,64},{128,96},{160,128},{192,160},{224,192},{256... | collective-permute-start | bytes 491528 | tf_op jit(solution)/shard_map/ppermute | solution.py:431
  102.3 8.4 %collective-permute-start.15 = (s32[160,256]{1,0:T(8,128)S(1)}, s32[160,256]{1,0:T(8,128)S(1)}, u32[]{:S(2)}, u32[]{:S(2)}) collective-permute-start(s32[160,256]{1,0:T(8,128)S(1)} %shard_map.74), channel_id=1, source_target_pairs={{0,32},{32,64},{64,96},{96,128},{128,160},{160,192},{192,224},{224... | collective-permute-start | bytes 491528 | tf_op jit(solution)/shard_map/ppermute | solution.py:428
